TPU v7x, 128 devices: a whole 4x4x4 slice. The times are simulated.
128 devices in a mesh: au: 16 (over z_lo, y, core), aa: 8 (over x, z_hi).
Axes of the slice: x: 4, y: 4, z: 4 (z_hi: 2, z_lo: 2; z = z_hi * 2 + z_lo), core: 2. Of those that a mesh axis runs over, the one named last changes fastest.
Arguments:
- users: bfloat16 [32768, 256], P(('au', 'aa')), may hold values from -16 to 16
- ads: bfloat16 [32768, 256], P(('aa', 'au')), may hold values from -16 to 16
- counts: int32 [32768], P('aa'), may hold values from 1 to 999
- positives: int32 [32768], P('au'), may hold values from 0 to 32767
- weights: float32 [32768], P('au'), may hold values from 0.25 to 4
Outputs:
- grad_users: float32 [32768, 256], P(('au', 'aa'))
- grad_ads: float32 [32768, 256], P(('aa', 'au'))
- loss: float32 [], replicated
All inputs are finite; a program needn't handle non-finite values.
Results may differ from a plain program's by a relative error of at most 0.015.
Values may be sent and summed in bfloat16 or wider, within the bound.
No kernel may reach another device: no remote copies, remote signals or barrier semaphores. Data moves between devices by JAX's collectives and lax.ppermute only.
A program may use at most 64 MiB of HBM per device.

v0:
```python
import jax
import jax.numpy as jnp
from jax import lax
from jax.sharding import PartitionSpec as P


def local(users, ads, counts, positives, weights):
    width = users.shape[1]
    inv = width ** (-0.5)
    user_rows = lax.all_gather(users, "aa", axis=0, tiled=True)
    total_rows = user_rows.shape[0]
    block = min(total_rows, 256)
    nblocks = total_rows // block
    user_split = user_rows.reshape(nblocks, block, width)
    pos_split = positives.reshape(nblocks, block)
    weight_split = weights.reshape(nblocks, block)
    log_counts = jnp.log(counts.astype(jnp.float32))
    ad_count = counts.shape[0]
    ad_offset = lax.axis_index("aa") * ad_count

    def piece_logits(block_users, piece):
        length = piece.shape[0]
        columns = ad_offset + jnp.arange(length, dtype=jnp.int32)
        scores = jnp.einsum("re,ce->rc", block_users, piece, preferred_element_type=jnp.float32)
        return (inv * scores - log_counts[None, :], columns)

    start_stats = (
        jnp.full((total_rows,), -jnp.inf, jnp.float32),
        jnp.zeros((total_rows,), jnp.float32),
        jnp.zeros((total_rows,), jnp.float32),
    )
    ad_rows = lax.all_gather(ads, "au", axis=0, tiled=True)

    def stats_one_block(inputs):
        block_users, block_pos, top, total, positive = inputs
        logits, columns = piece_logits(block_users, ad_rows)
        newtop = jnp.maximum(top, jnp.max(logits, axis=1))
        total = total * jnp.exp(top - newtop) + jnp.sum(jnp.exp(logits - newtop[:, None]), axis=1)
        hit = columns[None, :] == block_pos[:, None]
        positive = positive + jnp.sum(jnp.where(hit, logits, jnp.float32(0.0)), axis=1)
        return (newtop, total, positive)

    split_carry = tuple((value.reshape(nblocks, block) for value in start_stats))
    results = lax.map(stats_one_block, (user_split, pos_split) + split_carry)
    local_top, local_total, local_positive = tuple((value.reshape(total_rows) for value in results))
    row_top = lax.pmax(local_top, "aa")
    row_total, row_positive = lax.psum(
        (local_total * jnp.exp(local_top - row_top), local_positive), "aa"
    )
    lse = row_top + jnp.log(row_total)
    lse_split = lse.reshape(nblocks, block)
    length = ad_rows.shape[0]

    def grad_one_block(acc, inputs):
        block_users, block_pos, block_weight, block_lse = inputs
        logits, columns = piece_logits(block_users, ad_rows)
        hit = (columns[None, :] == block_pos[:, None]).astype(jnp.float32)
        dlogits = (block_weight[:, None] * (jnp.exp(logits - block_lse[:, None]) - hit)).astype(
            jnp.bfloat16
        )
        user_part = inv * jnp.dot(dlogits, ad_rows, preferred_element_type=jnp.float32)
        acc = acc + inv * lax.dot_general(
            dlogits, block_users, (((0,), (0,)), ((), ())), preferred_element_type=jnp.float32
        )
        return (acc, user_part)

    piece_grad, user_parts = lax.scan(
        grad_one_block,
        jnp.zeros((length, width), jnp.float32),
        (user_split, pos_split, weight_split, lse_split),
    )
    grad_rows = user_parts.reshape(total_rows, width)
    grad_cols = piece_grad
    grad_rows, grad_cols = (grad_rows, grad_cols)
    grad_users = lax.psum_scatter(
        grad_rows.astype(jnp.bfloat16), "aa", scatter_dimension=0, tiled=True
    ).astype(jnp.float32)
    grad_ads = lax.psum_scatter(
        grad_cols.astype(jnp.bfloat16), "au", scatter_dimension=0, tiled=True
    ).astype(jnp.float32)
    share = total_rows // lax.axis_size("aa")
    own_start = lax.axis_index("aa") * share
    terms = weights * (lse - row_positive)
    own_terms = lax.dynamic_slice_in_dim(terms, own_start, share)
    loss = lax.psum(jnp.sum(own_terms), ("au", "aa"))
    return (grad_users, grad_ads, loss)


def solution(mesh):
    return jax.shard_map(
        local,
        mesh=mesh,
        in_specs=(P(("au", "aa"), None), P(("aa", "au"), None), P("aa"), P("au"), P("au")),
        out_specs=(P(("au", "aa"), None), P(("aa", "au"), None), P()),
        check_vma=False,
    )
```

profile of v0, /device:TPU:0, one launch (start us, length us, event | category | flops | bytes accessed | tf_op | source)
XLA Modules:
  0.0 406.9 jit_solution(3314122203605554116)
XLA Ops:
  10.9 49.3 %all-gather.3.cloned.1.call-done = bf16[2048,256]{1,0:T(8,128)(2,1)} async-done(((bf16[256,256]{1,0:T(8,128)(2,1)}), bf16[2048,256]{1,0:T(8,128)(2,1)}) %all-gather.3.cloned.1.call-update) | async-done | bytes 1048592 | tf_op jit(solution)/shard_map/all_gather | solution.py:10
  60.2 34.3 %all-gather.5.cloned.1.call-done = bf16[4096,256]{1,0:T(8,128)(2,1)} async-done(((bf16[256,256]{1,0:T(8,128)(2,1)}), bf16[4096,256]{1,0:T(8,128)(2,1)}) %all-gather.5.cloned.1.call-update) | async-done | bytes 2097168 | tf_op jit(solution)/shard_map/all_gather | solution.py:32
  94.5 31.9 %while.27 = (s32[]{:T(128)}, f32[8,256]{1,0:T(8,128)S(1)}, f32[8,256]{1,0:T(8,128)S(1)}, f32[8,256]{1,0:T(8,128)S(1)}, bf16[8,256,256]{2,1,0:T(8,128)(2,1)}, /*i...) while((s32[]{:T(128)}, f32[8,256]{1,0:T(8,128)S(1)}, ...), condition=%wide.region_4.5_spmd, body=%wide.region_0.4_spmd.sunk | while | flops 545263616 | bytes 10683009 | solution.py:44
  98.5 2.5 fusion.38
  102.5 2.5 fusion.38
  106.5 2.5 fusion.38
  110.5 2.5 fusion.38
  114.5 2.5 fusion.38
  118.5 2.5 fusion.38
  122.5 2.5 fusion.38
  126.5 24.3 %pmax.7 = f32[2048]{0:T(1024)S(1)} all-reduce(f32[2048]{0:T(1024)S(1)} %bitcast.73), channel_id=1, replica_groups=mesh['au'=16,'aa'=8] {'aa'}, use_global_device_ids=true, to_apply=%region_5.6 | all-reduce | flops 2048 | bytes 16384 | tf_op jit(solution)/shard_map/pmax | solution.py:46
  150.9 36.7 %all-reduce = (f32[2048]{0:T(1024)S(1)}, f32[2048]{0:T(1024)S(1)}) all-reduce(f32[2048]{0:T(1024)S(1)} %exponential_multiply_fusion, f32[2048]{0:T(1024)S(1)} %bitcast.75), channel_id=1, replica_groups=mesh['au'=16,'aa'=8] {'aa'}, use_global_device_ids=true, to_apply=%region_6.7 | all-reduce | flops 4096 | bytes 32768 | tf_op jit(solution)/shard_map/psum | solution.py:47
  187.5 77.8 %while.28 = (s32[]{:T(128)}, f32[4096,256]{1,0:T(8,128)}, bf16[8,256,256]{2,1,0:T(8,128)(2,1)}, f32[8,256]{1,0:T(8,128)S(1)}, bf16[8,256,256]{2,1,0:T(8,128)(2,1...) while((s32[]{:T(128)}, f32[4096,256]{1,0:T(8,128)}, ...), condition=%wide.region_8.9_spmd.clone, body=%wide.region_7.8_spmd.clone.sunk | while | flops 1622216704 | bytes 27847336 | solution.py:67
  187.6 3.3 fusion.45
  190.9 3.8 fusion.46
  196.2 3.3 fusion.45
  199.5 5.2 %fusion.46 = f32[4096,256]{1,0:T(8,128)} fusion(bf16[256,4096]{1,0:T(8,128)(2,1)S(1)} %fusion.45, f32[4096,256]{1,0:T(8,128)} %get-tuple-element.363, pred[]{:T(512)S(6)} %compare.3, bf16[8,256,256]{2,1,0:T(8,128)(2,1)} %get-tuple-element.378, s32[]{:T(128)} %get-tuple-element.362), kind=kOutput, calls=%fused_computation.11.clone.1 | convolution fusion | flops 540016640 | bytes 10617345 | tf_op jit(solution)/shard_map/while/body/eval_jaxpr/dot_general | solution.py:62
  206.0 3.3 fusion.45
  209.4 5.2 %fusion.46 = f32[4096,256]{1,0:T(8,128)} fusion(bf16[256,4096]{1,0:T(8,128)(2,1)S(1)} %fusion.45, f32[4096,256]{1,0:T(8,128)} %get-tuple-element.363, pred[]{:T(512)S(6)} %compare.3, bf16[8,256,256]{2,1,0:T(8,128)(2,1)} %get-tuple-element.378, s32[]{:T(128)} %get-tuple-element.362), kind=kOutput, calls=%fused_computation.11.clone.1 | convolution fusion | flops 540016640 | bytes 10617345 | tf_op jit(solution)/shard_map/while/body/eval_jaxpr/dot_general | solution.py:62
  215.9 3.3 fusion.45
  219.2 5.2 %fusion.46 = f32[4096,256]{1,0:T(8,128)} fusion(bf16[256,4096]{1,0:T(8,128)(2,1)S(1)} %fusion.45, f32[4096,256]{1,0:T(8,128)} %get-tuple-element.363, pred[]{:T(512)S(6)} %compare.3, bf16[8,256,256]{2,1,0:T(8,128)(2,1)} %get-tuple-element.378, s32[]{:T(128)} %get-tuple-element.362), kind=kOutput, calls=%fused_computation.11.clone.1 | convolution fusion | flops 540016640 | bytes 10617345 | tf_op jit(solution)/shard_map/while/body/eval_jaxpr/dot_general | solution.py:62
  225.8 3.3 fusion.45
  229.1 5.2 %fusion.46 = f32[4096,256]{1,0:T(8,128)} fusion(bf16[256,4096]{1,0:T(8,128)(2,1)S(1)} %fusion.45, f32[4096,256]{1,0:T(8,128)} %get-tuple-element.363, pred[]{:T(512)S(6)} %compare.3, bf16[8,256,256]{2,1,0:T(8,128)(2,1)} %get-tuple-element.378, s32[]{:T(128)} %get-tuple-element.362), kind=kOutput, calls=%fused_computation.11.clone.1 | convolution fusion | flops 540016640 | bytes 10617345 | tf_op jit(solution)/shard_map/while/body/eval_jaxpr/dot_general | solution.py:62
  235.7 3.3 fusion.45
  239.0 5.2 %fusion.46 = f32[4096,256]{1,0:T(8,128)} fusion(bf16[256,4096]{1,0:T(8,128)(2,1)S(1)} %fusion.45, f32[4096,256]{1,0:T(8,128)} %get-tuple-element.363, pred[]{:T(512)S(6)} %compare.3, bf16[8,256,256]{2,1,0:T(8,128)(2,1)} %get-tuple-element.378, s32[]{:T(128)} %get-tuple-element.362), kind=kOutput, calls=%fused_computation.11.clone.1 | convolution fusion | flops 540016640 | bytes 10617345 | tf_op jit(solution)/shard_map/while/body/eval_jaxpr/dot_general | solution.py:62
  245.6 3.3 fusion.45
  248.9 5.2 %fusion.46 = f32[4096,256]{1,0:T(8,128)} fusion(bf16[256,4096]{1,0:T(8,128)(2,1)S(1)} %fusion.45, f32[4096,256]{1,0:T(8,128)} %get-tuple-element.363, pred[]{:T(512)S(6)} %compare.3, bf16[8,256,256]{2,1,0:T(8,128)(2,1)} %get-tuple-element.378, s32[]{:T(128)} %get-tuple-element.362), kind=kOutput, calls=%fused_computation.11.clone.1 | convolution fusion | flops 540016640 | bytes 10617345 | tf_op jit(solution)/shard_map/while/body/eval_jaxpr/dot_general | solution.py:62
  255.5 3.3 fusion.45
  258.8 5.2 %fusion.46 = f32[4096,256]{1,0:T(8,128)} fusion(bf16[256,4096]{1,0:T(8,128)(2,1)S(1)} %fusion.45, f32[4096,256]{1,0:T(8,128)} %get-tuple-element.363, pred[]{:T(512)S(6)} %compare.3, bf16[8,256,256]{2,1,0:T(8,128)(2,1)} %get-tuple-element.378, s32[]{:T(128)} %get-tuple-element.362), kind=kOutput, calls=%fused_computation.11.clone.1 | convolution fusion | flops 540016640 | bytes 10617345 | tf_op jit(solution)/shard_map/while/body/eval_jaxpr/dot_general | solution.py:62
  265.4 3.7 convert_element_type.28
  270.6 63.3 %psum.23 = f32[]{:T(128)} all-reduce(f32[]{:T(128)} %fusion.19), channel_id=1, replica_groups=mesh['au'=16,'aa'=8] {'au','aa'}, use_global_device_ids=true, to_apply=%region_13.14 | all-reduce | flops 1 | bytes 8 | tf_op jit(solution)/shard_map/psum | solution.py:85
  335.7 63.0 %reduce-scatter.5.cloned.1.call-done = bf16[256,256]{1,0:T(8,128)(2,1)} async-done(((bf16[4096,256]{1,0:T(8,128)(2,1)}), bf16[256,256]{1,0:T(8,128)(2,1)}) %reduce-scatter.5.cloned.1.call-update) | async-done | bytes 131088 | tf_op jit(solution)/shard_map/reduce_scatter | solution.py:78
  (131 shorter events, 33.9 us)
Async XLA Ops:
  7.2 53.1 %all-gather.3.cloned.1.call-start = ((), (), s32[]{:S(2)}) async-start(), calls=%async_computation.2 | async-start | bytes 1179648 | tf_op jit(solution)/shard_map/all_gather | solution.py:10
  7.9 86.6 %all-gather.5.cloned.1.call-start = ((), (), s32[]{:S(2)}) async-start(), calls=%async_computation.3 | async-start | bytes 2228224 | tf_op jit(solution)/shard_map/all_gather | solution.py:32
  8.6 325.5 %reduce-scatter.3.cloned.1.call-start = ((), (), s32[]{:S(2)}) async-start(), calls=%async_computation.4 | async-start | bytes 1179648 | tf_op jit(solution)/shard_map/reduce_scatter | solution.py:75
  190.9 3.8 copy-start
  199.4 5.2 %copy-start = (bf16[4096,256]{1,0:T(8,128)(2,1)S(1)}, bf16[4096,256]{1,0:T(8,128)(2,1)}, u32[]{:S(2)}) copy-start(bf16[4096,256]{1,0:T(8,128)(2,1)} %get-tuple-element.379) | copy-start | bytes 6291460 | tf_op jit(solution)/shard_map/while
  209.3 5.2 %copy-start = (bf16[4096,256]{1,0:T(8,128)(2,1)S(1)}, bf16[4096,256]{1,0:T(8,128)(2,1)}, u32[]{:S(2)}) copy-start(bf16[4096,256]{1,0:T(8,128)(2,1)} %get-tuple-element.379) | copy-start | bytes 6291460 | tf_op jit(solution)/shard_map/while
  219.2 5.2 %copy-start = (bf16[4096,256]{1,0:T(8,128)(2,1)S(1)}, bf16[4096,256]{1,0:T(8,128)(2,1)}, u32[]{:S(2)}) copy-start(bf16[4096,256]{1,0:T(8,128)(2,1)} %get-tuple-element.379) | copy-start | bytes 6291460 | tf_op jit(solution)/shard_map/while
  229.1 5.2 %copy-start = (bf16[4096,256]{1,0:T(8,128)(2,1)S(1)}, bf16[4096,256]{1,0:T(8,128)(2,1)}, u32[]{:S(2)}) copy-start(bf16[4096,256]{1,0:T(8,128)(2,1)} %get-tuple-element.379) | copy-start | bytes 6291460 | tf_op jit(solution)/shard_map/while
  239.0 5.2 %copy-start = (bf16[4096,256]{1,0:T(8,128)(2,1)S(1)}, bf16[4096,256]{1,0:T(8,128)(2,1)}, u32[]{:S(2)}) copy-start(bf16[4096,256]{1,0:T(8,128)(2,1)} %get-tuple-element.379) | copy-start | bytes 6291460 | tf_op jit(solution)/shard_map/while
  248.9 5.2 %copy-start = (bf16[4096,256]{1,0:T(8,128)(2,1)S(1)}, bf16[4096,256]{1,0:T(8,128)(2,1)}, u32[]{:S(2)}) copy-start(bf16[4096,256]{1,0:T(8,128)(2,1)} %get-tuple-element.379) | copy-start | bytes 6291460 | tf_op jit(solution)/shard_map/while
  258.8 5.2 %copy-start = (bf16[4096,256]{1,0:T(8,128)(2,1)S(1)}, bf16[4096,256]{1,0:T(8,128)(2,1)}, u32[]{:S(2)}) copy-start(bf16[4096,256]{1,0:T(8,128)(2,1)} %get-tuple-element.379) | copy-start | bytes 6291460 | tf_op jit(solution)/shard_map/while
  265.4 133.4 %reduce-scatter.5.cloned.1.call-start = ((), (), s32[]{:S(2)}) async-start(), calls=%async_computation.5 | async-start | bytes 2228224 | tf_op jit(solution)/shard_map/reduce_scatter | solution.py:78
Sparse Core Ops, SparseCore 0:
  10.3 49.8 all-gather.2
  61.9 32.5 all-gather.4
  265.5 68.5 reduce-scatter.2
  336.5 62.2 reduce-scatter.4
where the time goes:
time: 408 us; the launch traced here: 407 us
  waiting for transfers between devices  148 us (36%)
  blocking collectives  124 us (30%)
  matrix products  97.5 us (24%)
  other arithmetic  19.5 us (5%)
  between operations  13.9 us (3%)
    psum x1, blocking collectives, local(): loss = lax.psum(jnp.sum(own_terms), ('au', 'aa'))  63.3 us
    reduce_scatter x1, waiting for transfers between devices, local(): lax.psum_scatter(grad_cols.astype(jnp.bfloat16), 'au', scatter_dimension=...  63 us
    all_gather x1, waiting for transfers between devices, local(): user_rows = lax.all_gather(users, 'aa', axis=0, tiled=True)  49.3 us
    dot_general x16, matrix products, piece_logits(): jnp.einsum('re,ce->rc', block_users, piece, preferred_element_type=jnp.fl...  46.4 us
    dot_general x8, matrix products, grad_one_block(): lax.dot_general(dlogits, block_users, (((0,), (0,)), ((), ())), preferred...  39.9 us
    psum x1, blocking collectives, local(): lax.psum((local_total * jnp.exp(local_top - row_top), local_positive), 'aa')  36.7 us
    all_gather x1, waiting for transfers between devices, local(): ad_rows = lax.all_gather(ads, 'au', axis=0, tiled=True)  34.3 us
    pmax x1, blocking collectives, local(): row_top = lax.pmax(local_top, 'aa')  24.3 us
  transfers between devices with their start and end apart: 4, of which 4 were waited for; matrix products, arithmetic and copies ran while one was open for 2% of the time, Pallas kernels for 0%

commit v1 on v0

v1 whole, which is shorter than its diff:
```python
import jax
import jax.numpy as jnp
from jax import lax
from jax.experimental import pallas as pl
from jax.experimental.pallas import tpu as pltpu
from jax.sharding import PartitionSpec as P

F32 = jnp.float32
BF16 = jnp.bfloat16
T = 256
LANES = 128
EXTRA = 16
NX, NZ, NY, NC = 4, 2, 4, 2
VMEM_LIMIT = 32 * 2**20


def params():
    return pltpu.CompilerParams(vmem_limit_bytes=VMEM_LIMIT)


def whole(shape):
    return pl.BlockSpec(shape, lambda *_: (0,) * len(shape))


def user_block(j, zr):
    me = lax.axis_index("aa")
    x, z = me // NZ, me % NZ
    return lax.rem(x + NX - j, NX) * NZ + (z + zr - 2 * z * zr)


def ads_block(t, cr):
    me = lax.axis_index("au")
    k, zr = t // NZ, t % NZ
    z, y, c = me // (NY * NC), (me // NC) % NY, me % NC
    return (z + zr - 2 * z * zr) * (NY * NC) + lax.rem(y + NY - k, NY) * NC + (c + cr - 2 * c * cr)


def stage_users(user_refs, staged, inv):
    for j in range(NX):
        for zr in range(NZ):
            spot = pl.multiple_of(user_block(j, zr) * T, T)
            block = user_refs[j][zr * T : (zr + 1) * T, :].astype(F32) * inv
            staged[pl.ds(spot, T), :] = block.astype(BF16)


def split(value):
    high = value.astype(BF16).astype(F32)
    mid = (value - high).astype(BF16).astype(F32)
    return high, mid, value - high - mid


def loss_rows(loss, width):
    high, mid, low = split(loss)
    lane = lax.broadcasted_iota(jnp.int32, (EXTRA, width), 1)
    return jnp.where(lane == 0, high, jnp.where(lane == 1, mid, jnp.where(lane == 2, low, 0.0))).astype(BF16)


def read_loss(rows):
    return jnp.sum(rows[:1, :LANES].astype(F32), axis=1, keepdims=True)


def logits_kernel(cr, steps, inv, *refs):
    n = NX * NZ
    chunks = 2 * steps
    user_refs = refs[:NX]
    ads_ref, logc_ref, pos_ref = refs[NX : NX + 3]
    rest = refs[NX + 3 :]
    if cr:
        m_in, t_in, hit_in = rest[:3]
        p_ref, m_ref, hit_ref, stats_ref, staged, s0, s1, total_ref = rest[3:]
    else:
        p_ref, m_ref, total_ref, hit_ref, staged, s0, s1 = rest
    step = pl.program_id(0)
    aa = lax.axis_index("aa")
    per_aa = NY * NZ * NC

    def product(chunk, dst, b):
        cols = slice(b * T, (b + 1) * T)
        ads = ads_ref[pl.ds(pl.multiple_of(chunk * T, T), T), :]
        logc = logc_ref[pl.ds(pl.multiple_of(ads_block(chunk, cr) * T, T), T), :]
        prod = lax.dot_general(
            ads, staged[cols, :], (((1,), (1,)), ((), ())), preferred_element_type=F32
        )
        dst[:, cols] = prod - jnp.concatenate([logc] * (T // LANES), axis=1)

    def tile(chunk, src, b, half):
        cols = slice(b * T, (b + 1) * T)
        logits = src[:, cols]
        rows = lax.broadcasted_iota(jnp.int32, (T, T), 0)
        base = (aa * per_aa + ads_block(chunk, cr)) * T
        hit = rows == pos_ref[:, cols] - base
        top = jnp.max(logits, axis=0, keepdims=True)
        hit_ref[:, cols] += jnp.sum(jnp.where(hit, logits, 0.0), axis=0, keepdims=True)
        e = jnp.exp(logits - top)
        total_ref[pl.ds(chunk, 1), cols] = jnp.sum(e, axis=0, keepdims=True)
        m_ref[pl.ds(chunk, 1), cols] = top
        p_ref[half * T : (half + 1) * T, cols] = e.astype(BF16)

    @pl.when(step == 0)
    def _():
        stage_users(user_refs, staged, inv)
        hit_ref[...] = hit_in[...] if cr else jnp.zeros_like(hit_ref)
        for b in range(n):
            product(0, s0, b)

    first = 2 * step
    for b in range(n):
        product(first + 1, s1, b)
        tile(first, s0, b, 0)
    after = jnp.minimum(first + 2, chunks - 1)
    for b in range(n):
        product(after, s0, b)
        tile(first + 1, s1, b, 1)

    if cr:

        @pl.when(step == steps - 1)
        def _():
            top = jnp.maximum(
                jnp.max(m_in[...], axis=0, keepdims=True), jnp.max(m_ref[...], axis=0, keepdims=True)
            )
            total = jnp.sum(t_in[...] * jnp.exp(m_in[...] - top), axis=0, keepdims=True)
            total += jnp.sum(total_ref[...] * jnp.exp(m_ref[...] - top), axis=0, keepdims=True)
            lse = top + jnp.log(total)
            width = n * T // LANES
            for r in range(width):
                cols = slice(r * LANES, (r + 1) * LANES)
                stats_ref[r : r + 1, :] = lse[:, cols]
                stats_ref[width + r : width + r + 1, :] = hit_ref[:, cols]


def run_logits(cr, users, ads, logc, positives, inv, before=()):
    width = ads.shape[1]
    count = ads.shape[0]
    chunks = count // T
    steps = chunks // 2
    total = NX * NZ * T
    rows = 2 * total // LANES
    p_spec = pl.BlockSpec((2 * T, total), lambda i: (i, 0))
    p_shape = jax.ShapeDtypeStruct((count, total), BF16)
    per_chunk = jax.ShapeDtypeStruct((chunks, total), F32)
    per_user = jax.ShapeDtypeStruct((1, total), F32)
    scratch = [pltpu.VMEM((total, width), BF16), pltpu.VMEM((T, total), F32), pltpu.VMEM((T, total), F32)]
    if cr:
        out_specs = [p_spec, whole((chunks, total)), whole((1, total)), whole((rows, LANES))]
        out_shape = [p_shape, per_chunk, per_user, jax.ShapeDtypeStruct((rows, LANES), F32)]
        scratch.append(pltpu.VMEM((chunks, total), F32))
    else:
        out_specs = [p_spec, whole((chunks, total)), whole((chunks, total)), whole((1, total))]
        out_shape = [p_shape, per_chunk, per_chunk, per_user]
    args = (*users, ads, logc, positives, *before)
    return pl.pallas_call(
        lambda *refs: logits_kernel(cr, steps, inv, *refs),
        grid=(steps,),
        in_specs=[whole(x.shape) for x in args],
        out_specs=out_specs,
        out_shape=out_shape,
        scratch_shapes=scratch,
        compiler_params=params(),
        name="logits_far" if cr else "logits_near",
    )(*args)


def grads_kernel(cr, steps, inv, *refs):
    n = NX * NZ
    user_refs = refs[:NX]
    ads_ref, p_ref, m_ref, hit_ref, pos_ref, weight_ref, stats_ref = refs[NX : NX + 7]
    rest = refs[NX + 7 :]
    if cr:
        da_ref, loss_ref, acc, staged, lse_row, coef_row = rest[:6]
        qs = rest[6:]
    else:
        acc_in, da_ref = rest[:2]
        du_refs = rest[2 : 2 + NX]
        acc, staged, lse_row, coef_row = rest[2 + NX : 6 + NX]
        qs = rest[6 + NX :]
    step = pl.program_id(0)
    aa = lax.axis_index("aa")
    per_aa = NY * NZ * NC
    width = n * T // LANES
    deep = 2 * T

    @pl.when(step == 0)
    def _():
        stage_users(user_refs, staged, inv)
        acc[...] = jnp.zeros_like(acc) if cr else acc_in[...]
        tops = stats_ref[:, :width, :]
        top = jnp.max(tops, axis=0)
        lse = top + jnp.log(jnp.sum(jnp.exp(tops - top[None]), axis=0))
        for r in range(width):
            lse_row[:, r * LANES : (r + 1) * LANES] = lse[r : r + 1, :]
        if cr:
            diff = lse - jnp.sum(stats_ref[:, width:, :], axis=0)
            loss = jnp.zeros((1, LANES), F32)
            for r in range(width):
                loss += weight_ref[:, r * LANES : (r + 1) * LANES] * diff[r : r + 1, :]
            loss_ref[...] = loss_rows(jnp.sum(loss, axis=1, keepdims=True), loss_ref.shape[1])
        coef_row[...] = weight_ref[...] * (jnp.exp(hit_ref[...] - lse_row[...]) - 1.0)

    ads = ads_ref[...]
    ads_t = ads.T
    rows = lax.broadcasted_iota(jnp.int32, (T, deep), 0)
    scales, bases = [], []
    for half in range(2):
        chunk = 2 * step + half
        scales.append(weight_ref[...] * jnp.exp(m_ref[pl.ds(chunk, 1), :] - lse_row[...]))
        bases.append((aa * per_aa + ads_block(chunk, cr)) * T)

    def build(b):
        cols = slice(b * deep, (b + 1) * deep)
        for half in range(2):
            part = slice(half * T, (half + 1) * T)
            hit = rows == pos_ref[:, cols] - bases[half]
            scaled = p_ref[part, cols].astype(F32) * scales[half][:, cols]
            qs[b][part, :] = jnp.where(hit, coef_row[:, cols], scaled).astype(BF16)

    def products(b, da):
        cols = slice(b * deep, (b + 1) * deep)
        q = qs[b][...]
        acc[:, cols] += jnp.dot(ads_t, q, preferred_element_type=F32)
        return da + jnp.dot(q, staged[cols, :], preferred_element_type=F32)

    tiles = n // 2
    da = jnp.zeros((deep, ads.shape[1]), F32)
    build(0)
    for b in range(tiles):
        if b + 1 < tiles:
            build(b + 1)
        da = products(b, da)
    da_ref[...] = da.astype(BF16)

    if not cr:

        @pl.when(step == steps - 1)
        def _():
            for j in range(NX):
                for zr in range(NZ):
                    spot = pl.multiple_of(user_block((NX - j) % NX, zr) * T, T)
                    du_refs[j][zr * T : (zr + 1) * T, :] = (acc[:, pl.ds(spot, T)] * inv).astype(BF16)


def run_grads(cr, users, ads, p, tops, hits, positives, weights, stats, inv, before=()):
    width = ads.shape[1]
    count = ads.shape[0]
    steps = count // (2 * T)
    total = NX * NZ * T
    args = (*users, ads, p, tops, hits, positives, weights, stats, *before)
    in_specs = [whole(x.shape) for x in args]
    in_specs[NX] = pl.BlockSpec((2 * T, width), lambda i: (i, 0))
    in_specs[NX + 1] = pl.BlockSpec((2 * T, total), lambda i: (i, 0))
    da_spec = pl.BlockSpec((2 * T, width), lambda i: (i, 0))
    acc_shape = jax.ShapeDtypeStruct((width, total), F32)
    da_shape = jax.ShapeDtypeStruct((count, width), BF16)
    scratch = [
        pltpu.VMEM((total, width), BF16),
        pltpu.VMEM((1, total), F32),
        pltpu.VMEM((1, total), F32),
    ] + [pltpu.VMEM((2 * T, 2 * T), BF16)] * (NX * NZ // 2)
    if cr:
        out_specs = [da_spec, whole((EXTRA, width)), whole((width, total))]
        out_shape = [da_shape, jax.ShapeDtypeStruct((EXTRA, width), BF16), acc_shape]
    else:
        out_specs = [da_spec] + [whole((NZ * width, T))] * NX
        out_shape = [da_shape] + [jax.ShapeDtypeStruct((NZ * width, T), BF16)] * NX
        scratch = [pltpu.VMEM((width, total), F32)] + scratch
    return pl.pallas_call(
        lambda *refs: grads_kernel(cr, steps, inv, *refs),
        grid=(steps,),
        in_specs=in_specs,
        out_specs=out_specs,
        out_shape=out_shape,
        scratch_shapes=scratch,
        compiler_params=params(),
        name="grads_far" if cr else "grads_near",
    )(*args)


def simple_call(kernel, name, out_shape, *args):
    return pl.pallas_call(
        kernel,
        in_specs=[whole(x.shape) for x in args],
        out_specs=[whole(x.shape) for x in out_shape],
        out_shape=out_shape,
        grid=(1,),
        compiler_params=params(),
        name=name,
    )(*args)


def add_cores(da, loss, da_far, loss_far):
    width = da.shape[1]
    rows = NZ * T

    def kernel(da_ref, loss_ref, far_ref, loss_far_ref, *outs):
        both = read_loss(loss_ref[...]) + read_loss(loss_far_ref[...])
        for k in range(NY):
            part = slice(k * rows, (k + 1) * rows)
            outs[k][:rows, :] = (da_ref[part, :].astype(F32) + far_ref[part, :].astype(F32)).astype(BF16)
            outs[k][rows:, :] = loss_rows(both, width)

    shape = jax.ShapeDtypeStruct((rows + EXTRA, width), BF16)
    return simple_call(kernel, "add_cores", [shape] * NY, da, loss, da_far, loss_far)


def add_rows(parts):
    width = parts[0].shape[1]

    def kernel(*refs):
        ins, (keep, kept_loss, send) = refs[:NY], refs[NY:]
        loss = sum(read_loss(r[NZ * T :, :]) for r in ins)
        keep[...] = sum(r[:T, :].astype(F32) for r in ins)
        kept_loss[...] = jnp.broadcast_to(loss, kept_loss.shape)
        send[:T, :] = sum(r[T : NZ * T, :].astype(F32) for r in ins).astype(BF16)
        send[T:, :] = loss_rows(loss, width)

    shapes = [
        jax.ShapeDtypeStruct((T, width), F32),
        jax.ShapeDtypeStruct((8, LANES), F32),
        jax.ShapeDtypeStruct((T + EXTRA, width), BF16),
    ]
    return simple_call(kernel, "add_rows", shapes, *parts)


def finish_ads(keep, kept_loss, received):
    def kernel(keep_ref, loss_ref, received_ref, grad, loss):
        grad[...] = keep_ref[...] + received_ref[:T, :].astype(F32)
        loss[...] = loss_ref[...] + read_loss(received_ref[T:, :])

    shapes = [jax.ShapeDtypeStruct(keep.shape, F32), jax.ShapeDtypeStruct(kept_loss.shape, F32)]
    return simple_call(kernel, "finish_ads", shapes, keep, kept_loss, received)


def add_users(parts):
    width = parts[0].shape[0] // NZ

    def kernel(*refs):
        ins, (keep, send) = refs[:NX], refs[NX:]
        keep[...] = sum(r[:width, :].astype(F32) for r in ins)
        send[...] = sum(r[width:, :].astype(F32) for r in ins).astype(BF16)

    shapes = [jax.ShapeDtypeStruct((width, T), F32), jax.ShapeDtypeStruct((width, T), BF16)]
    return simple_call(kernel, "add_users", shapes, *parts)


def finish_users(keep, received):
    def kernel(keep_ref, received_ref, grad):
        grad[...] = (keep_ref[...] + received_ref[...].astype(F32)).T

    shapes = [jax.ShapeDtypeStruct(keep.shape[::-1], F32)]
    return simple_call(kernel, "finish_users", shapes, keep, received)[0]


def move(x, axis, target):
    return lax.ppermute(x, axis, [(i, target(i)) for i in range(lax.axis_size(axis))])


def shift_x(x, j):
    return move(x, "aa", lambda i: (i + j * NZ) % (NX * NZ))


def swap_z_hi(x):
    return move(x, "aa", lambda i: i ^ 1)


def shift_y(x, k):
    return move(x, "au", lambda i: i // 8 * 8 + (i % 8 + k * NC) % 8)


def swap_core(x):
    return move(x, "au", lambda i: i ^ 1)


def swap_z_lo(x):
    return move(x, "au", lambda i: i ^ 8)


def local(users, ads, counts, positives, weights):
    inv = users.shape[1] ** (-0.5)
    ads_z, users_z = lax.optimization_barrier((swap_z_lo(ads), swap_z_hi(users)))
    ads_pair = jnp.concatenate([ads, ads_z], axis=0)
    user_pair = jnp.concatenate([users, users_z], axis=0)
    moved = [shift_y(ads_pair, k) for k in range(1, NY)] + [shift_x(user_pair, j) for j in range(1, NX)]
    moved = lax.optimization_barrier(tuple(moved))
    near = jnp.concatenate([ads_pair, *moved[: NY - 1]], axis=0)
    user_pairs = [user_pair, *moved[NY - 1 :]]
    far = swap_core(near)
    logc = jnp.broadcast_to(jnp.log(counts.astype(F32))[:, None], (counts.shape[0], LANES))
    pos_row = positives[None, :]
    weight_row = weights[None, :]

    p_near, m_near, t_near, h_near = run_logits(0, user_pairs, near, logc, pos_row, inv)
    p_far, m_far, hits, stats = run_logits(1, user_pairs, far, logc, pos_row, inv, (m_near, t_near, h_near))
    n_aa = lax.axis_size("aa")
    stats = lax.all_to_all(
        jnp.broadcast_to(stats[None], (n_aa,) + stats.shape), "aa", split_axis=0, concat_axis=0, tiled=True
    )
    da_far, loss, acc = run_grads(1, user_pairs, far, p_far, m_far, hits, pos_row, weight_row, stats, inv)
    da_back, loss_back = swap_core(da_far), swap_core(loss)
    da_near, *du = run_grads(0, user_pairs, near, p_near, m_near, hits, pos_row, weight_row, stats, inv, (acc,))

    da = add_cores(da_near, loss, da_back, loss_back)
    da = [da[0]] + [shift_y(da[k], -k) for k in range(1, NY)]
    du = [du[0]] + [shift_x(du[j], j) for j in range(1, NX)]
    keep, kept_loss, send = add_rows(da)
    keep_u, send_u = add_users(du)
    grad_ads, loss = finish_ads(keep, kept_loss, swap_z_lo(send))
    grad_users = finish_users(keep_u, swap_z_hi(send_u))
    return grad_users, grad_ads, loss[0, 0]


def solution(mesh):
    return jax.shard_map(
        local,
        mesh=mesh,
        in_specs=(P(("au", "aa"), None), P(("aa", "au"), None), P("aa"), P("au"), P("au")),
        out_specs=(P(("au", "aa"), None), P(("aa", "au"), None), P()),
        check_vma=False,
    )
```

time: 408 us -> 111 us (0.27)
  waiting for transfers between devices: 148 us -> 34.7 us
  blocking collectives: 124 us -> 12.4 us
  matrix products: 97.5 us -> 0 us
  Pallas kernels: 0 us -> 33.8 us
  starting transfers between devices: 0.16 us -> 23.9 us
  other arithmetic: 19.5 us -> 0.73 us
  between operations: 13.9 us -> 0.82 us
    psum x2 -> x0, blocking collectives: 100 us -> none  [the longest x1 63.3 us: local(): loss = lax.psum(jnp.sum(own_terms), ('au', 'aa'))]
    dot_general x32 -> x0, matrix products: 97.5 us -> none  [the longest x16 46.4 us: piece_logits(): jnp.einsum('re,ce->rc', block_users, piece, preferred_element_type=jnp.fl...]
    all_gather x2 -> x0, waiting for transfers between devices: 83.6 us -> none  [the longest x1 49.3 us: local(): user_rows = lax.all_gather(users, 'aa', axis=0, tiled=True)]
    reduce_scatter x2 -> x0, waiting for transfers between devices: 63.3 us -> none  [the longest x1 63 us: local(): lax.psum_scatter(grad_cols.astype(jnp.bfloat16), 'au', scatter_dimension=...]
    ppermute x0 -> x19, waiting for transfers between devices: none -> 34.7 us  [move(): lax.ppermute(x, axis, [(i, target(i)) for i in range(lax.axis_size(axis))])]
    pallas_call x0 -> x9, Pallas kernels: none -> 33.8 us  [the longest x2 17.9 us: run_logits(): pl.pallas_call(lambda *refs: logits_kernel(cr, steps, inv, *refs), grid=(...]
    pmax x1 -> x0, blocking collectives: 24.3 us -> none  [local(): row_top = lax.pmax(local_top, 'aa')]
    ppermute x0 -> x19, starting transfers between devices: none -> 23.9 us  [move(): lax.ppermute(x, axis, [(i, target(i)) for i in range(lax.axis_size(axis))])]
  transfers between devices with their start and end apart: 4 -> 19, of which waited for: 4 -> 11; matrix products, arithmetic and copies ran while one was open for 2% -> 3% of each run, Pallas kernels for 0% -> 15%
where the time goes in v1:
time: 111 us; the launch traced here: 110 us
  waiting for transfers between devices  34.7 us (31%)
  Pallas kernels  33.8 us (30%)
  starting transfers between devices  23.9 us (22%)
  blocking collectives  12.4 us (11%)
  local copies, waits for them, and re-layouts  3.74 us (3%)
    ppermute x19, waiting for transfers between devices, move(): lax.ppermute(x, axis, [(i, target(i)) for i in range(lax.axis_size(axis))])  34.7 us
    ppermute x19, starting transfers between devices, move(): lax.ppermute(x, axis, [(i, target(i)) for i in range(lax.axis_size(axis))])  23.9 us
    pallas_call x2, Pallas kernels, run_logits(): pl.pallas_call(lambda *refs: logits_kernel(cr, steps, inv, *refs), grid=(...  17.9 us
    pallas_call x2, Pallas kernels, run_grads(): pl.pallas_call(lambda *refs: grads_kernel(cr, steps, inv, *refs), grid=(s...  13.6 us
    all_to_all x1, blocking collectives, local(): lax.all_to_all(jnp.broadcast_to(stats[None], (n_aa,) + stats.shape), 'aa'...  12.4 us
    unnamed x11, local copies, waits for them, and re-layouts  2.6 us
    pallas_call x5, Pallas kernels, simple_call(): pl.pallas_call(kernel, in_specs=[whole(x.shape) for x in args], out_specs...  2.33 us
  transfers between devices with their start and end apart: 19, of which 11 were waited for; matrix products, arithmetic and copies ran while one was open for 3% of the time, Pallas kernels for 15%

profile of v1, /device:TPU:0, one launch (start us, length us, event | category | flops | bytes accessed | tf_op | source)
XLA Modules:
  0.0 110.0 jit_solution(18164623413634060377)
XLA Ops:
  0.7 4.0 %collective-permute-start.1 = (bf16[256,256]{1,0:T(8,128)(2,1)}, bf16[256,256]{1,0:T(8,128)(2,1)S(1)}, u32[]{:S(2)}, u32[]{:S(2)}) collective-permute-start(bf16[256,256]{1,0:T(8,128)(2,1)} %param.5), channel_id=1, source_target_pairs={{0,1},{1,0},{2,3},{3,2},{4,5},{5,4},{6,7},{7,6},{8,9},{9,8},{10,11... | collective-permute-start | bytes 393224 | tf_op jit(solution)/shard_map/ppermute | solution.py:354
  4.7 1.0 collective-permute-start
  5.7 0.9 constant_dynamic-update-slice_fusion.1
  6.6 2.6 %collective-permute-done.1 = bf16[256,256]{1,0:T(8,128)(2,1)S(1)} collective-permute-done((bf16[256,256]{1,0:T(8,128)(2,1)}, bf16[256,256]{1,0:T(8,128)(2,1)S(1)}, u32[]{:S(2)}, u32[]{:S(2)}) %collective-permute-start.1) | collective-permute-done | bytes 131104 | tf_op jit(solution)/shard_map/ppermute | solution.py:354
  9.2 2.7 %collective-permute-done = bf16[256,256]{1,0:T(8,128)(2,1)S(1)} collective-permute-done((bf16[256,256]{1,0:T(8,128)(2,1)}, bf16[256,256]{1,0:T(8,128)(2,1)S(1)}, u32[]{:S(2)}, u32[]{:S(2)}) %collective-permute-start) | collective-permute-done | bytes 131104 | tf_op jit(solution)/shard_map/ppermute | solution.py:354
  12.0 2.8 %collective-permute-start.7 = (bf16[512,256]{1,0:T(8,128)(2,1)S(1)}, bf16[512,256]{1,0:T(8,128)(2,1)S(1)}, u32[]{:S(2)}, u32[]{:S(2)}) collective-permute-start(bf16[512,256]{1,0:T(8,128)(2,1)S(1)} %constant_dynamic-update-slice_fusion.refs_0_), channel_id=1, source_target_pairs={{0,6},{1,7},{2,0},{3,1},{4,2},{5,3},{6,4},{7,5},{8,14},{9,15},{10,... | collective-permute-start | bytes 786440 | tf_op jit(solution)/shard_map/ppermute | solution.py:354
  14.8 0.9 constant_dynamic-update-slice_fusion.8
  15.7 0.9 collective-permute-start.6
  16.6 0.9 collective-permute-start.5
  17.5 3.1 %collective-permute-start.4 = (bf16[512,256]{1,0:T(8,128)(2,1)S(1)}, bf16[512,256]{1,0:T(8,128)(2,1)S(1)}, u32[]{:S(2)}, u32[]{:S(2)}) collective-permute-start(bf16[512,256]{1,0:T(8,128)(2,1)S(1)} %get-tuple-element.74), channel_id=1, source_target_pairs={{0,48},{8,56},{16,0},{24,8},{32,16},{40,24},{48,32},{56,40},{64,11... | collective-permute-start | bytes 786440 | tf_op jit(solution)/shard_map/ppermute | solution.py:354
  21.2 3.9 %collective-permute-done.7.refs_3_ = bf16[512,256]{1,0:T(8,128)(2,1)S(1)} collective-permute-done((bf16[512,256]{1,0:T(8,128)(2,1)S(1)}, bf16[512,256]{1,0:T(8,128)(2,1)S(1)}, u32[]{:S(2)}, u32[]{:S(2)}) %collective-permute-start.7) | collective-permute-done | bytes 262176 | tf_op jit(solution)/shard_map/ppermute | solution.py:354
  25.1 1.6 %collective-permute-start.2 = (bf16[512,256]{1,0:T(8,128)(2,1)S(1)}, bf16[512,256]{1,0:T(8,128)(2,1)S(1)}, u32[]{:S(2)}, u32[]{:S(2)}) collective-permute-start(bf16[512,256]{1,0:T(8,128)(2,1)S(1)} %get-tuple-element.74), channel_id=1, source_target_pairs={{0,16},{8,24},{16,32},{24,40},{32,48},{40,56},{48,0},{56,8},{64,80... | collective-permute-start | bytes 786440 | tf_op jit(solution)/shard_map/ppermute | solution.py:354
  26.7 3.1 %collective-permute-done.5.refs_1_ = bf16[512,256]{1,0:T(8,128)(2,1)S(1)} collective-permute-done((bf16[512,256]{1,0:T(8,128)(2,1)S(1)}, bf16[512,256]{1,0:T(8,128)(2,1)S(1)}, u32[]{:S(2)}, u32[]{:S(2)}) %collective-permute-start.5) | collective-permute-done | bytes 262176 | tf_op jit(solution)/shard_map/ppermute | solution.py:354
  30.0 1.0 collective-permute-done.3
  31.0 2.7 %collective-permute-done.2 = bf16[512,256]{1,0:T(8,128)(2,1)S(1)} collective-permute-done((bf16[512,256]{1,0:T(8,128)(2,1)S(1)}, bf16[512,256]{1,0:T(8,128)(2,1)S(1)}, u32[]{:S(2)}, u32[]{:S(2)}) %collective-permute-start.2) | collective-permute-done | bytes 262176 | tf_op jit(solution)/shard_map/ppermute | solution.py:354
  33.9 0.7 convert_log_fusion
  36.0 8.8 %logits_near.1 = (bf16[2048,2048]{1,0:T(8,128)(2,1)S(1)}, f32[8,2048]{1,0:T(8,128)S(1)}, f32[8,2048]{1,0:T(8,128)S(1)}, f32[1,2048]{1,0:T(1,128)S(1)}) custom-call(bf16[512,256]{1,0:T(8,128)(2,1)S(1)} %constant_dynamic-update-slice_fusion.refs_0_, bf16[512,256]{1,0:T(8,128)(2,1)S(1)} %collective-permute-done.5.refs_1_, ...), custom_call_target="tpu_custom_call" | custom-call | tf_op jit(solution)/shard_map/logits_near/pallas_call | solution.py:152
  44.8 9.0 %logits_far.1 = (bf16[2048,2048]{1,0:T(8,128)(2,1)S(1)}, f32[8,2048]{1,0:T(8,128)S(1)}, f32[1,2048]{1,0:T(1,128)S(1)}, f32[32,128]{1,0:T(8,128)S(1)}) custom-call(bf16[512,256]{1,0:T(8,128)(2,1)S(1)} %constant_dynamic-update-slice_fusion.refs_0_, bf16[512,256]{1,0:T(8,128)(2,1)S(1)} %collective-permute-done.5.refs_1_, ...), custom_call_target="tpu_custom_call" | custom-call | tf_op jit(solution)/shard_map/logits_far/pallas_call | solution.py:152
  53.9 12.4 %all_to_all.5.refs_10_ = f32[8,32,128]{2,1,0:T(8,128)S(1)} all-to-all(f32[8,32,128]{2,1,0:T(8,128)S(1)} %broadcast_in_dim.21), channel_id=1, replica_groups=mesh['au'=16,'aa'=8] {'aa'}, dimensions={0} | all-to-all | bytes 262144 | tf_op jit(solution)/shard_map/all_to_all | solution.py:394
  66.3 6.7 %grads_far.1 = (bf16[2048,256]{1,0:T(8,128)(2,1)S(1)}, bf16[16,256]{1,0:T(8,128)(2,1)S(1)}, f32[256,2048]{1,0:T(8,128)S(1)}) custom-call(bf16[512,256]{1,0:T(8,128)(2,1)S(1)} %constant_dynamic-update-slice_fusion.refs_0_, bf16[512,256]{1,0:T(8,128)(2,1)S(1)} %collective-permute-done.5.refs_1_, bf16[512,256]{1,0:T(8,128)(2,1)S(1)} %collective-permute-done.6.refs_2_, ...), custom_call_target="tpu_custom_call" | custom-call | tf_op jit(solution)/shard_map/grads_far/pallas_call | solution.py:266
  73.6 6.8 %grads_near.1 = (bf16[2048,256]{1,0:T(8,128)(2,1)S(1)}, bf16[512,256]{1,0:T(8,128)(2,1)S(1)}, bf16[512,256]{1,0:T(8,128)(2,1)S(1)}, bf16[512,256]{1,0:T(8,128)(2,1)S(1)}, bf16[512,256]{1,0:T(8,128)(2,1)S(1)}) custom-call(bf16[512,256]{1,0:T(8,128)(2,1)S(1)} %constant_dynamic-update-slice_fusion.refs_0_, bf16[512,256]{1,0:T(8,128)(2,1)S(1)} %collective-permute-done.5.refs_1_, ...), custom_call_target="tpu_custom_call" | custom-call | tf_op jit(solution)/shard_map/grads_near/pallas_call | solution.py:266
  80.9 1.9 %collective-permute-start.15 = (bf16[528,256]{1,0:T(8,128)(2,1)S(1)}, bf16[528,256]{1,0:T(8,128)(2,1)S(1)}, u32[]{:S(2)}, u32[]{:S(2)}) collective-permute-start(bf16[528,256]{1,0:T(8,128)(2,1)S(1)} %get-tuple-element.65), channel_id=1, source_target_pairs={{0,48},{8,56},{16,0},{24,8},{32,16},{40,24},{48,32},{56,40},{64,11... | collective-permute-start | bytes 811016 | tf_op jit(solution)/shard_map/ppermute | solution.py:354
  83.4 1.0 collective-permute-start.17
  84.8 2.1 %collective-permute-start.10 = (bf16[512,256]{1,0:T(8,128)(2,1)S(1)}, bf16[512,256]{1,0:T(8,128)(2,1)S(1)}, u32[]{:S(2)}, u32[]{:S(2)}) collective-permute-start(bf16[512,256]{1,0:T(8,128)(2,1)S(1)} %get-tuple-element.57), channel_id=1, source_target_pairs={{0,4},{1,5},{2,6},{3,7},{4,0},{5,1},{6,2},{7,3},{8,12},{9,13},{10,... | collective-permute-start | bytes 786440 | tf_op jit(solution)/shard_map/ppermute | solution.py:354
  86.8 8.0 %collective-permute-done.15.refs_1_ = bf16[528,256]{1,0:T(8,128)(2,1)S(1)} collective-permute-done((bf16[528,256]{1,0:T(8,128)(2,1)S(1)}, bf16[528,256]{1,0:T(8,128)(2,1)S(1)}, u32[]{:S(2)}, u32[]{:S(2)}) %collective-permute-start.15) | collective-permute-done | bytes 270368 | tf_op jit(solution)/shard_map/ppermute | solution.py:354
  94.8 0.9 collective-permute-start.11
  95.8 2.7 %collective-permute-done.17.refs_3_ = bf16[528,256]{1,0:T(8,128)(2,1)S(1)} collective-permute-done((bf16[528,256]{1,0:T(8,128)(2,1)S(1)}, bf16[528,256]{1,0:T(8,128)(2,1)S(1)}, u32[]{:S(2)}, u32[]{:S(2)}) %collective-permute-start.17) | collective-permute-done | bytes 270368 | tf_op jit(solution)/shard_map/ppermute | solution.py:354
  99.2 2.0 %collective-permute-done.11.refs_3_ = bf16[512,256]{1,0:T(8,128)(2,1)S(1)} collective-permute-done((bf16[512,256]{1,0:T(8,128)(2,1)S(1)}, bf16[512,256]{1,0:T(8,128)(2,1)S(1)}, u32[]{:S(2)}, u32[]{:S(2)}) %collective-permute-start.11) | collective-permute-done | bytes 262176 | tf_op jit(solution)/shard_map/ppermute | solution.py:354
  101.3 0.9 collective-permute-start.12
  102.3 5.6 %collective-permute-done.12.received_ref = bf16[256,256]{1,0:T(8,128)(2,1)S(1)} collective-permute-done((bf16[256,256]{1,0:T(8,128)(2,1)S(1)}, bf16[256,256]{1,0:T(8,128)(2,1)S(1)}, u32[]{:S(2)}, u32[]{:S(2)}) %collective-permute-start.12) | collective-permute-done | bytes 131104 | tf_op jit(solution)/shard_map/ppermute | solution.py:354
  107.9 0.8 finish_users.1
  108.7 0.7 finish_ads.1
  (33 shorter events, 5.7 us)
Async XLA Ops:
  0.6 44.2 %copy-start.1 = (s32[2048]{0:T(1024)S(1)}, s32[2048]{0:T(1024)}, u32[]{:S(2)}) copy-start(s32[2048]{0:T(1024)} %param.8) | copy-start | bytes 24580
  0.6 65.6 %copy-start.2 = (f32[2048]{0:T(1024)S(1)}, f32[2048]{0:T(1024)}, u32[]{:S(2)}) copy-start(f32[2048]{0:T(1024)} %param.9) | copy-start | bytes 24580
  0.7 8.6 %collective-permute-start.1 = (bf16[256,256]{1,0:T(8,128)(2,1)}, bf16[256,256]{1,0:T(8,128)(2,1)S(1)}, u32[]{:S(2)}, u32[]{:S(2)}) collective-permute-start(bf16[256,256]{1,0:T(8,128)(2,1)} %param.5), channel_id=1, source_target_pairs={{0,1},{1,0},{2,3},{3,2},{4,5},{5,4},{6,7},{7,6},{8,9},{9,8},{10,11... | collective-permute-start | bytes 393224 | tf_op jit(solution)/shard_map/ppermute | solution.py:354
  4.7 7.2 %collective-permute-start = (bf16[256,256]{1,0:T(8,128)(2,1)}, bf16[256,256]{1,0:T(8,128)(2,1)S(1)}, u32[]{:S(2)}, u32[]{:S(2)}) collective-permute-start(bf16[256,256]{1,0:T(8,128)(2,1)} %param.6), channel_id=1, source_target_pairs={{0,64},{8,72},{16,80},{24,88},{32,96},{40,104},{48,112},{56,120},{... | collective-permute-start | bytes 393224 | tf_op jit(solution)/shard_map/ppermute | solution.py:354
  12.0 13.2 %collective-permute-start.7 = (bf16[512,256]{1,0:T(8,128)(2,1)S(1)}, bf16[512,256]{1,0:T(8,128)(2,1)S(1)}, u32[]{:S(2)}, u32[]{:S(2)}) collective-permute-start(bf16[512,256]{1,0:T(8,128)(2,1)S(1)} %constant_dynamic-update-slice_fusion.refs_0_), channel_id=1, source_target_pairs={{0,6},{1,7},{2,0},{3,1},{4,2},{5,3},{6,4},{7,5},{8,14},{9,15},{10,... | collective-permute-start | bytes 786440 | tf_op jit(solution)/shard_map/ppermute | solution.py:354
  15.7 11.0 %collective-permute-start.6 = (bf16[512,256]{1,0:T(8,128)(2,1)S(1)}, bf16[512,256]{1,0:T(8,128)(2,1)S(1)}, u32[]{:S(2)}, u32[]{:S(2)}) collective-permute-start(bf16[512,256]{1,0:T(8,128)(2,1)S(1)} %constant_dynamic-update-slice_fusion.refs_0_), channel_id=1, source_target_pairs={{0,4},{1,5},{2,6},{3,7},{4,0},{5,1},{6,2},{7,3},{8,12},{9,13},{10,... | collective-permute-start | bytes 786440 | tf_op jit(solution)/shard_map/ppermute | solution.py:354
  16.6 13.2 %collective-permute-start.5 = (bf16[512,256]{1,0:T(8,128)(2,1)S(1)}, bf16[512,256]{1,0:T(8,128)(2,1)S(1)}, u32[]{:S(2)}, u32[]{:S(2)}) collective-permute-start(bf16[512,256]{1,0:T(8,128)(2,1)S(1)} %constant_dynamic-update-slice_fusion.refs_0_), channel_id=1, source_target_pairs={{0,2},{1,3},{2,4},{3,5},{4,6},{5,7},{6,0},{7,1},{8,10},{9,11},{10,... | collective-permute-start | bytes 786440 | tf_op jit(solution)/shard_map/ppermute | solution.py:354
  17.5 12.6 %collective-permute-start.4 = (bf16[512,256]{1,0:T(8,128)(2,1)S(1)}, bf16[512,256]{1,0:T(8,128)(2,1)S(1)}, u32[]{:S(2)}, u32[]{:S(2)}) collective-permute-start(bf16[512,256]{1,0:T(8,128)(2,1)S(1)} %get-tuple-element.74), channel_id=1, source_target_pairs={{0,48},{8,56},{16,0},{24,8},{32,16},{40,24},{48,32},{56,40},{64,11... | collective-permute-start | bytes 786440 | tf_op jit(solution)/shard_map/ppermute | solution.py:354
  20.6 10.4 %collective-permute-start.3 = (bf16[512,256]{1,0:T(8,128)(2,1)S(1)}, bf16[512,256]{1,0:T(8,128)(2,1)S(1)}, u32[]{:S(2)}, u32[]{:S(2)}) collective-permute-start(bf16[512,256]{1,0:T(8,128)(2,1)S(1)} %get-tuple-element.74), channel_id=1, source_target_pairs={{0,32},{8,40},{16,48},{24,56},{32,0},{40,8},{48,16},{56,24},{64,96... | collective-permute-start | bytes 786440 | tf_op jit(solution)/shard_map/ppermute | solution.py:354
  25.1 8.6 %collective-permute-start.2 = (bf16[512,256]{1,0:T(8,128)(2,1)S(1)}, bf16[512,256]{1,0:T(8,128)(2,1)S(1)}, u32[]{:S(2)}, u32[]{:S(2)}) collective-permute-start(bf16[512,256]{1,0:T(8,128)(2,1)S(1)} %get-tuple-element.74), channel_id=1, source_target_pairs={{0,16},{8,24},{16,32},{24,40},{32,48},{40,56},{48,0},{56,8},{64,80... | collective-permute-start | bytes 786440 | tf_op jit(solution)/shard_map/ppermute | solution.py:354
  33.8 11.0 %collective-permute-start.8 = (bf16[2048,256]{1,0:T(8,128)(2,1)S(1)}, bf16[2048,256]{1,0:T(8,128)(2,1)S(1)}, u32[]{:S(2)}, u32[]{:S(2)}) collective-permute-start(bf16[2048,256]{1,0:T(8,128)(2,1)S(1)} %constant_dynamic-update-slice_fusion.4.refs_4_), channel_id=1, source_target_pairs={{0,8},{8,0},{16,24},{24,16},{32,40},{40,32},{48,56},{56,48},{64,72... | collective-permute-start | bytes 3145736 | tf_op jit(solution)/shard_map/ppermute | solution.py:354
  35.3 0.7 copy-start
  73.0 7.4 %collective-permute-start.13 = (bf16[2048,256]{1,0:T(8,128)(2,1)S(1)}, bf16[2048,256]{1,0:T(8,128)(2,1)S(1)}, u32[]{:S(2)}, u32[]{:S(2)}) collective-permute-start(bf16[2048,256]{1,0:T(8,128)(2,1)S(1)} %get-tuple-element.63), channel_id=1, source_target_pairs={{0,8},{8,0},{16,24},{24,16},{32,40},{40,32},{48,56},{56,48},{64,72... | collective-permute-start | bytes 3145736 | tf_op jit(solution)/shard_map/ppermute | solution.py:354
  73.1 7.3 %collective-permute-start.14 = (bf16[16,256]{1,0:T(8,128)(2,1)S(1)}, bf16[16,256]{1,0:T(8,128)(2,1)S(1)}, u32[]{:S(2)}, u32[]{:S(2)}) collective-permute-start(bf16[16,256]{1,0:T(8,128)(2,1)S(1)} %get-tuple-element.62.loss_ref), channel_id=1, source_target_pairs={{0,8},{8,0},{16,24},{24,16},{32,40},{40,32},{48,56},{56,48},{64,72... | collective-permute-start | bytes 24584 | tf_op jit(solution)/shard_map/ppermute | solution.py:354
  80.9 13.9 %collective-permute-start.15 = (bf16[528,256]{1,0:T(8,128)(2,1)S(1)}, bf16[528,256]{1,0:T(8,128)(2,1)S(1)}, u32[]{:S(2)}, u32[]{:S(2)}) collective-permute-start(bf16[528,256]{1,0:T(8,128)(2,1)S(1)} %get-tuple-element.65), channel_id=1, source_target_pairs={{0,48},{8,56},{16,0},{24,8},{32,16},{40,24},{48,32},{56,40},{64,11... | collective-permute-start | bytes 811016 | tf_op jit(solution)/shard_map/ppermute | solution.py:354
  82.8 13.0 %collective-permute-start.16 = (bf16[528,256]{1,0:T(8,128)(2,1)S(1)}, bf16[528,256]{1,0:T(8,128)(2,1)S(1)}, u32[]{:S(2)}, u32[]{:S(2)}) collective-permute-start(bf16[528,256]{1,0:T(8,128)(2,1)S(1)} %get-tuple-element.66), channel_id=1, source_target_pairs={{0,32},{8,40},{16,48},{24,56},{32,0},{40,8},{48,16},{56,24},{64,96... | collective-permute-start | bytes 811016 | tf_op jit(solution)/shard_map/ppermute | solution.py:354
  83.4 15.1 %collective-permute-start.17 = (bf16[528,256]{1,0:T(8,128)(2,1)S(1)}, bf16[528,256]{1,0:T(8,128)(2,1)S(1)}, u32[]{:S(2)}, u32[]{:S(2)}) collective-permute-start(bf16[528,256]{1,0:T(8,128)(2,1)S(1)} %get-tuple-element.67), channel_id=1, source_target_pairs={{0,16},{8,24},{16,32},{24,40},{32,48},{40,56},{48,0},{56,8},{64,80... | collective-permute-start | bytes 811016 | tf_op jit(solution)/shard_map/ppermute | solution.py:354
  84.4 14.8 %collective-permute-start.9 = (bf16[512,256]{1,0:T(8,128)(2,1)S(1)}, bf16[512,256]{1,0:T(8,128)(2,1)S(1)}, u32[]{:S(2)}, u32[]{:S(2)}) collective-permute-start(bf16[512,256]{1,0:T(8,128)(2,1)S(1)} %get-tuple-element.56), channel_id=1, source_target_pairs={{0,2},{1,3},{2,4},{3,5},{4,6},{5,7},{6,0},{7,1},{8,10},{9,11},{10,... | collective-permute-start | bytes 786440 | tf_op jit(solution)/shard_map/ppermute | solution.py:354
  84.8 14.4 %collective-permute-start.10 = (bf16[512,256]{1,0:T(8,128)(2,1)S(1)}, bf16[512,256]{1,0:T(8,128)(2,1)S(1)}, u32[]{:S(2)}, u32[]{:S(2)}) collective-permute-start(bf16[512,256]{1,0:T(8,128)(2,1)S(1)} %get-tuple-element.57), channel_id=1, source_target_pairs={{0,4},{1,5},{2,6},{3,7},{4,0},{5,1},{6,2},{7,3},{8,12},{9,13},{10,... | collective-permute-start | bytes 786440 | tf_op jit(solution)/shard_map/ppermute | solution.py:354
  94.8 6.4 %collective-permute-start.11 = (bf16[512,256]{1,0:T(8,128)(2,1)S(1)}, bf16[512,256]{1,0:T(8,128)(2,1)S(1)}, u32[]{:S(2)}, u32[]{:S(2)}) collective-permute-start(bf16[512,256]{1,0:T(8,128)(2,1)S(1)} %get-tuple-element.58), channel_id=1, source_target_pairs={{0,6},{1,7},{2,0},{3,1},{4,2},{5,3},{6,4},{7,5},{8,14},{9,15},{10,... | collective-permute-start | bytes 786440 | tf_op jit(solution)/shard_map/ppermute | solution.py:354
  98.7 10.0 %collective-permute-start.18 = (bf16[272,256]{1,0:T(8,128)(2,1)S(1)}, bf16[272,256]{1,0:T(8,128)(2,1)S(1)}, u32[]{:S(2)}, u32[]{:S(2)}) collective-permute-start(bf16[272,256]{1,0:T(8,128)(2,1)S(1)} %get-tuple-element.70), channel_id=1, source_target_pairs={{0,64},{8,72},{16,80},{24,88},{32,96},{40,104},{48,112},{56,120},{... | collective-permute-start | bytes 417800 | tf_op jit(solution)/shard_map/ppermute | solution.py:354
  101.3 6.6 %collective-permute-start.12 = (bf16[256,256]{1,0:T(8,128)(2,1)S(1)}, bf16[256,256]{1,0:T(8,128)(2,1)S(1)}, u32[]{:S(2)}, u32[]{:S(2)}) collective-permute-start(bf16[256,256]{1,0:T(8,128)(2,1)S(1)} %get-tuple-element.60), channel_id=1, source_target_pairs={{0,1},{1,0},{2,3},{3,2},{4,5},{5,4},{6,7},{7,6},{8,9},{9,8},{10,11... | collective-permute-start | bytes 393224 | tf_op jit(solution)/shard_map/ppermute | solution.py:354

commit v2 on v1

v2 whole, which is shorter than its diff:
```python
import jax
import jax.numpy as jnp
from jax import lax
from jax.experimental import pallas as pl
from jax.experimental.pallas import tpu as pltpu
from jax.sharding import PartitionSpec as P

F32 = jnp.float32
BF16 = jnp.bfloat16
T = 256
LANES = 128
EXTRA = 16
NX, NZ, NY, NC = 4, 2, 4, 2
VMEM_LIMIT = 32 * 2**20


def params():
    return pltpu.CompilerParams(vmem_limit_bytes=VMEM_LIMIT)


def whole(shape):
    return pl.BlockSpec(shape, lambda *_: (0,) * len(shape))


def user_block(j, zr):
    me = lax.axis_index("aa")
    x, z = me // NZ, me % NZ
    return lax.rem(x + NX - j, NX) * NZ + (z + zr - 2 * z * zr)


def ads_block(group, chunk):
    pair, zr = chunk // NZ, chunk % NZ
    k, cr = {"near": (pair + pair // 2, 0), "far": (pair + pair // 2, 1), "mid": (2, pair)}[group]
    me = lax.axis_index("au")
    z, y, c = me // (NY * NC), (me // NC) % NY, me % NC
    return (z + zr - 2 * z * zr) * (NY * NC) + lax.rem(y + NY - k, NY) * NC + (c + cr - 2 * c * cr)


USER_PARTS = 5


def stage_users(user_refs, staged, inv):
    places = [(0, 0, 0, 0), (0, 1, 0, 1), (1, 0, 1, 0), (1, 1, 1, 1), (3, 0, 2, 0), (3, 1, 2, 1), (2, 0, 3, 0), (2, 1, 4, 0)]
    for j, zr, part, half in places:
        spot = pl.multiple_of(user_block(j, zr) * T, T)
        block = user_refs[part][half * T : (half + 1) * T, :].astype(F32) * inv
        staged[pl.ds(spot, T), :] = block.astype(BF16)


def split(value):
    high = value.astype(BF16).astype(F32)
    mid = (value - high).astype(BF16).astype(F32)
    return high, mid, value - high - mid


def loss_rows(loss, width):
    high, mid, low = split(loss)
    lane = lax.broadcasted_iota(jnp.int32, (EXTRA, width), 1)
    return jnp.where(lane == 0, high, jnp.where(lane == 1, mid, jnp.where(lane == 2, low, 0.0))).astype(BF16)


def read_loss(rows):
    return jnp.sum(rows[:1, :LANES].astype(F32), axis=1, keepdims=True)


def logits_kernel(group, n_ads, first_call, last_call, steps, inv, *refs):
    n = NX * NZ
    chunks = 2 * steps
    user_refs, refs = refs[:USER_PARTS], refs[USER_PARTS:]
    ads_refs, refs = refs[:n_ads], refs[n_ads:]
    (count_ref, pos_ref), refs = refs[:2], refs[2:]
    hit_in = None
    olds = []
    if not first_call:
        hit_in, refs = refs[0], refs[1:]
    if last_call:
        olds, refs = refs[:4], refs[4:]
    p_ref, m_ref, total_ref, hit_ref = refs[:4]
    refs = refs[4:]
    if last_call:
        stats_ref, refs = refs[0], refs[1:]
    staged, ads_all, s0, s1 = refs
    step = pl.program_id(0)
    aa = lax.axis_index("aa")
    per_aa = NY * NZ * NC

    def product(chunk, dst, b):
        cols = slice(b * T, (b + 1) * T)
        ads = ads_all[pl.ds(pl.multiple_of(chunk * T, T), T), :]
        counts = count_ref[:, pl.ds(pl.multiple_of(ads_block(group, chunk) * T, T), T)]
        logc = jnp.broadcast_to(jnp.log(counts.astype(F32)), (LANES, T)).T
        prod = lax.dot_general(
            ads, staged[cols, :], (((1,), (1,)), ((), ())), preferred_element_type=F32
        )
        dst[:, cols] = prod - jnp.concatenate([logc] * (T // LANES), axis=1)

    def tile(chunk, src, b, half):
        cols = slice(b * T, (b + 1) * T)
        base = (aa * per_aa + ads_block(group, chunk)) * T
        ahead = pos_ref[:, cols] - base - lax.broadcasted_iota(jnp.int32, (8, T), 0)
        best = src[:8, cols]
        found = jnp.where(ahead == 0, best, 0.0)
        for r in range(8, T, 8):
            x = src[r : r + 8, cols]
            best = jnp.maximum(best, x)
            found = jnp.where(ahead == r, x, found)
        top = jnp.max(best, axis=0, keepdims=True)
        hit_ref[:, cols] += jnp.sum(found, axis=0, keepdims=True)
        total = jnp.zeros((8, T), F32)
        for r in range(0, T, 16):
            e = jnp.exp(src[r : r + 16, cols] - top)
            total += e[:8] + e[8:]
            p_ref[half * T + r : half * T + r + 16, cols] = e.astype(BF16)
        total_ref[pl.ds(chunk, 1), cols] = jnp.sum(total, axis=0, keepdims=True)
        m_ref[pl.ds(chunk, 1), cols] = top

    @pl.when(step == 0)
    def _():
        stage_users(user_refs, staged, inv)
        spot = 0
        for r in ads_refs:
            ads_all[spot : spot + r.shape[0], :] = r[...]
            spot += r.shape[0]
        hit_ref[...] = jnp.zeros_like(hit_ref) if first_call else hit_in[...]
        m_ref[...] = jnp.full(m_ref.shape, -jnp.inf, F32)
        total_ref[...] = jnp.zeros_like(total_ref)
        for b in range(n):
            product(0, s0, b)

    first = 2 * step
    for b in range(n):
        product(first + 1, s1, b)
        tile(first, s0, b, 0)
    after = jnp.minimum(first + 2, chunks - 1)
    for b in range(n):
        product(after, s0, b)
        tile(first + 1, s1, b, 1)

    if last_call:

        @pl.when(step == steps - 1)
        def _():
            ms = [olds[0][...], olds[2][...], m_ref[...]]
            ts = [olds[1][...], olds[3][...], total_ref[...]]
            top = jnp.max(jnp.maximum(jnp.maximum(ms[0], ms[1]), ms[2]), axis=0, keepdims=True)
            total = jnp.sum(sum(t * jnp.exp(m - top) for m, t in zip(ms, ts)), axis=0, keepdims=True)
            lse = top + jnp.log(total)
            width = n * T // LANES
            for r in range(width):
                cols = slice(r * LANES, (r + 1) * LANES)
                stats_ref[r : r + 1, :] = lse[:, cols]
                stats_ref[width + r : width + r + 1, :] = hit_ref[:, cols]


STATS = 8


def cost(rows, total, width, products):
    return pl.CostEstimate(
        flops=2 * products * rows * total * width, bytes_accessed=2 * rows * total, transcendentals=rows * total
    )


def run_logits(group, users, ads, counts, positives, inv, hits=(), olds=()):
    width = ads[0].shape[1]
    count = sum(x.shape[0] for x in ads)
    steps = count // (2 * T)
    total = NX * NZ * T
    rows = 2 * total // LANES
    out_specs = [
        pl.BlockSpec((2 * T, total), lambda i: (i, 0)),
        whole((STATS, total)),
        whole((STATS, total)),
        whole((1, total)),
    ]
    out_shape = [
        jax.ShapeDtypeStruct((count, total), BF16),
        jax.ShapeDtypeStruct((STATS, total), F32),
        jax.ShapeDtypeStruct((STATS, total), F32),
        jax.ShapeDtypeStruct((1, total), F32),
    ]
    if olds:
        out_specs.append(whole((rows, LANES)))
        out_shape.append(jax.ShapeDtypeStruct((rows, LANES), F32))
    args = (*users, *ads, counts, positives, *hits, *olds)
    return pl.pallas_call(
        lambda *refs: logits_kernel(group, len(ads), not hits, bool(olds), steps, inv, *refs),
        grid=(steps,),
        in_specs=[whole(x.shape) for x in args],
        out_specs=out_specs,
        out_shape=out_shape,
        scratch_shapes=[
            pltpu.VMEM((total, width), BF16),
            pltpu.VMEM((count, width), BF16),
            pltpu.VMEM((T, total), F32),
            pltpu.VMEM((T, total), F32),
        ],
        compiler_params=params(),
        cost_estimate=cost(count, total, width, 4),
        name="logits_" + group,
    )(*args)


def grads_kernel(group, n_ads, steps, inv, *refs):
    n = NX * NZ
    user_refs, refs = refs[:USER_PARTS], refs[USER_PARTS:]
    ads_refs, refs = refs[:n_ads], refs[n_ads:]
    (p_ref, m_ref, hit_ref, pos_ref, weight_ref, stats_ref), refs = refs[:6], refs[6:]
    if group == "mid":
        (near_ref, far_ref, loss_ref, acc), refs = refs[:4], refs[4:]
    elif group == "far":
        (acc_in, da_ref, acc), refs = refs[:3], refs[3:]
    else:
        (acc_in, da_ref), refs = refs[:2], refs[2:]
        du_refs, acc, refs = refs[:USER_PARTS], refs[USER_PARTS], refs[USER_PARTS + 1 :]
    staged, ads_all, lse_row, coef_row = refs[:4]
    qs = refs[4:]
    step = pl.program_id(0)
    aa = lax.axis_index("aa")
    per_aa = NY * NZ * NC
    width = n * T // LANES
    deep = 2 * T

    @pl.when(step == 0)
    def _():
        stage_users(user_refs, staged, inv)
        spot = 0
        for r in ads_refs:
            ads_all[spot : spot + r.shape[0], :] = r[...]
            spot += r.shape[0]
        acc[...] = jnp.zeros_like(acc) if group == "mid" else acc_in[...]
        tops = stats_ref[:, :width, :]
        top = jnp.max(tops, axis=0)
        lse = top + jnp.log(jnp.sum(jnp.exp(tops - top[None]), axis=0))
        for r in range(width):
            lse_row[:, r * LANES : (r + 1) * LANES] = lse[r : r + 1, :]
        if group == "mid":
            diff = lse - jnp.sum(stats_ref[:, width:, :], axis=0)
            loss = jnp.zeros((1, LANES), F32)
            for r in range(width):
                loss += weight_ref[:, r * LANES : (r + 1) * LANES] * diff[r : r + 1, :]
            rows = loss_rows(jnp.sum(loss, axis=1, keepdims=True), loss_ref.shape[1])
            loss_ref[...] = rows
            far_ref[deep:, :] = rows
        coef_row[...] = weight_ref[...] * (jnp.exp(hit_ref[...] - lse_row[...]) - 1.0)

    ads_t = ads_all[pl.ds(pl.multiple_of(step * deep, deep), deep), :].T
    rows = lax.broadcasted_iota(jnp.int32, (T, deep), 0)
    scales, bases = [], []
    for half in range(2):
        chunk = 2 * step + half
        scales.append(weight_ref[...] * jnp.exp(m_ref[pl.ds(chunk, 1), :] - lse_row[...]))
        bases.append((aa * per_aa + ads_block(group, chunk)) * T)

    def build(b):
        cols = slice(b * deep, (b + 1) * deep)
        for half in range(2):
            part = slice(half * T, (half + 1) * T)
            hit = rows == pos_ref[:, cols] - bases[half]
            scaled = p_ref[part, cols].astype(F32) * scales[half][:, cols]
            qs[b][part, :] = jnp.where(hit, coef_row[:, cols], scaled).astype(BF16)

    def products(b, da):
        cols = slice(b * deep, (b + 1) * deep)
        q = qs[b][...]
        acc[:, cols] += jnp.dot(ads_t, q, preferred_element_type=F32)
        return da + jnp.dot(q, staged[cols, :], preferred_element_type=F32)

    tiles = n // 2
    da = jnp.zeros((deep, ads_all.shape[1]), F32)
    build(0)
    for b in range(tiles):
        if b + 1 < tiles:
            build(b + 1)
        da = products(b, da)

    if group == "mid":

        @pl.when(step == 0)
        def _():
            near_ref[...] = da.astype(BF16)

        @pl.when(step == 1)
        def _():
            far_ref[:deep, :] = da.astype(BF16)

    else:
        da_ref[...] = da.astype(BF16)

    if group == "near":

        @pl.when(step == steps - 1)
        def _():
            def users_at(j, zr):
                spot = pl.multiple_of(user_block((NX - j) % NX, zr) * T, T)
                return (acc[:, pl.ds(spot, T)] * inv).astype(BF16)

            for part, j in enumerate((0, 1, 3)):
                for zr in range(NZ):
                    du_refs[part][zr * T : (zr + 1) * T, :] = users_at(j, zr)
            du_refs[3][...] = users_at(2, 0)
            du_refs[4][...] = users_at(2, 1)


def run_grads(group, users, ads, p, tops, hits, positives, weights, stats, inv, before=()):
    width = ads[0].shape[1]
    count = sum(x.shape[0] for x in ads)
    deep = 2 * T
    steps = count // deep
    total = NX * NZ * T
    args = (*users, *ads, p, tops, hits, positives, weights, stats, *before)
    in_specs = [whole(x.shape) for x in args]
    in_specs[len(users) + len(ads)] = pl.BlockSpec((deep, total), lambda i: (i, 0))
    da_spec = pl.BlockSpec((deep, width), lambda i: (i, 0))
    acc_shape = jax.ShapeDtypeStruct((width, total), F32)
    da_shape = jax.ShapeDtypeStruct((count, width), BF16)
    scratch = [
        pltpu.VMEM((total, width), BF16),
        pltpu.VMEM((count, width), BF16),
        pltpu.VMEM((1, total), F32),
        pltpu.VMEM((1, total), F32),
    ] + [pltpu.VMEM((deep, deep), BF16)] * (total // deep)
    if group == "mid":
        shapes = [(deep, width), (deep + EXTRA, width), (EXTRA, width)]
        out_shape = [jax.ShapeDtypeStruct(x, BF16) for x in shapes] + [acc_shape]
        out_specs = [whole(x.shape) for x in out_shape]
    elif group == "far":
        out_specs = [da_spec, whole((width, total))]
        out_shape = [da_shape, acc_shape]
    else:
        shapes = [(NZ * width, T)] * 3 + [(width, T)] * 2
        out_specs = [da_spec] + [whole(x) for x in shapes]
        out_shape = [da_shape] + [jax.ShapeDtypeStruct(x, BF16) for x in shapes]
        scratch = [pltpu.VMEM((width, total), F32)] + scratch
    return pl.pallas_call(
        lambda *refs: grads_kernel(group, len(ads), steps, inv, *refs),
        grid=(steps,),
        in_specs=in_specs,
        out_specs=out_specs,
        out_shape=out_shape,
        scratch_shapes=scratch,
        compiler_params=params(),
        cost_estimate=cost(count, total, width, 4),
        name="grads_" + group,
    )(*args)


def simple_call(kernel, name, out_shape, *args):
    return pl.pallas_call(
        kernel,
        in_specs=[whole(x.shape) for x in args],
        out_specs=[whole(x.shape) for x in out_shape],
        out_shape=out_shape,
        grid=(1,),
        compiler_params=params(),
        name=name,
    )(*args)


def add_mid(near, loss, back):
    width = near.shape[1]

    def kernel(near_ref, loss_ref, back_ref, first, second, both_ref):
        both = read_loss(loss_ref[...]) + read_loss(back_ref[NZ * T :, :])
        first[:T, :] = (near_ref[:T, :].astype(F32) + back_ref[:T, :].astype(F32)).astype(BF16)
        first[T:, :] = loss_rows(both, width)
        second[...] = (near_ref[T:, :].astype(F32) + back_ref[T : NZ * T, :].astype(F32)).astype(BF16)
        both_ref[...] = jnp.broadcast_to(both, both_ref.shape)

    shapes = [
        jax.ShapeDtypeStruct((T + EXTRA, width), BF16),
        jax.ShapeDtypeStruct((T, width), BF16),
        jax.ShapeDtypeStruct((8, LANES), F32),
    ]
    return simple_call(kernel, "add_mid", shapes, near, loss, back)


def add_near(near, back, both, first, second):
    width = near.shape[1]
    rows = NZ * T

    def kernel(near_ref, back_ref, both_ref, first_ref, second_ref, keep, one, three):
        both = both_ref[:1, :1]
        total = near_ref[...].astype(F32) + back_ref[...].astype(F32)
        keep[...] = total[:rows]
        one[:T, :] = (total[rows : rows + T] + first_ref[:T, :].astype(F32)).astype(BF16)
        one[T:rows, :] = total[rows + T : 2 * rows].astype(BF16)
        one[rows:, :] = loss_rows(both + read_loss(first_ref[T:, :]), width)
        three[:T, :] = total[2 * rows : 2 * rows + T].astype(BF16)
        three[T:rows, :] = (total[2 * rows + T :] + second_ref[...].astype(F32)).astype(BF16)
        three[rows:, :] = loss_rows(both, width)

    shape = jax.ShapeDtypeStruct((rows + EXTRA, width), BF16)
    return simple_call(
        kernel, "add_near", [jax.ShapeDtypeStruct((rows, width), F32), shape, shape], near, back, both, first, second
    )


def add_rows(kept, both, parts):
    width = kept.shape[1]

    def kernel(kept_ref, both_ref, r1, r3, keep, loss_ref, send):
        loss = both_ref[:1, :1] + read_loss(r1[NZ * T :, :]) + read_loss(r3[NZ * T :, :])
        keep[...] = kept_ref[:T, :] + r1[:T, :].astype(F32) + r3[:T, :].astype(F32)
        loss_ref[...] = jnp.broadcast_to(loss, loss_ref.shape)
        two = slice(T, NZ * T)
        send[:T, :] = (kept_ref[two, :] + r1[two, :].astype(F32) + r3[two, :].astype(F32)).astype(BF16)
        send[T:, :] = loss_rows(loss, width)

    shapes = [
        jax.ShapeDtypeStruct((T, width), F32),
        jax.ShapeDtypeStruct((8, LANES), F32),
        jax.ShapeDtypeStruct((T + EXTRA, width), BF16),
    ]
    return simple_call(kernel, "add_rows", shapes, kept, both, *parts)


def add_halves(one, three, first, second):
    half = one.shape[0] // NZ

    def kernel(one_ref, three_ref, first_ref, second_ref, out1, out3):
        out1[:half, :] = (one_ref[:half, :].astype(F32) + first_ref[...].astype(F32)).astype(BF16)
        out1[half:, :] = one_ref[half:, :]
        out3[:half, :] = three_ref[:half, :]
        out3[half:, :] = (three_ref[half:, :].astype(F32) + second_ref[...].astype(F32)).astype(BF16)

    shapes = [jax.ShapeDtypeStruct(one.shape, BF16)] * 2
    return simple_call(kernel, "add_halves", shapes, one, three, first, second)


def add_users(parts):
    width = parts[0].shape[0] // NZ

    def kernel(*refs):
        ins, (keep, send) = refs[:-2], refs[-2:]
        keep[...] = sum(r[:width, :].astype(F32) for r in ins)
        send[...] = sum(r[width:, :].astype(F32) for r in ins).astype(BF16)

    shapes = [jax.ShapeDtypeStruct((width, T), F32), jax.ShapeDtypeStruct((width, T), BF16)]
    return simple_call(kernel, "add_users", shapes, *parts)


def finish(keep_u, received_u, keep, kept_loss, received):
    def kernel(keep_u_ref, received_u_ref, keep_ref, loss_ref, received_ref, grad_u, grad, loss):
        grad_u[...] = (keep_u_ref[...] + received_u_ref[...].astype(F32)).T
        grad[...] = keep_ref[...] + received_ref[:T, :].astype(F32)
        loss[...] = loss_ref[:1, :1] + read_loss(received_ref[T:, :])

    shapes = [
        jax.ShapeDtypeStruct(keep_u.shape[::-1], F32),
        jax.ShapeDtypeStruct(keep.shape, F32),
        jax.ShapeDtypeStruct((1, 1), F32),
    ]
    return simple_call(kernel, "finish", shapes, keep_u, received_u, keep, kept_loss, received)


def move(x, axis, target):
    return lax.ppermute(x, axis, [(i, target(i)) for i in range(lax.axis_size(axis))])


def shift_x(x, j):
    return move(x, "aa", lambda i: (i + j * NZ) % (NX * NZ))


def swap_z_hi(x):
    return move(x, "aa", lambda i: i ^ 1)


def shift_y(x, k):
    return move(x, "au", lambda i: i // 8 * 8 + (i % 8 + k * NC) % 8)


def swap_core(x):
    return move(x, "au", lambda i: i ^ 1)


def swap_z_lo(x):
    return move(x, "au", lambda i: i ^ 8)


def local(users, ads, counts, positives, weights):
    inv = users.shape[1] ** (-0.5)
    count_row, pos_row, weight_row = counts[None, :], positives[None, :], weights[None, :]
    users_z, ads_z = lax.optimization_barrier((swap_z_hi(users), swap_z_lo(ads)))
    user_pair = jnp.concatenate([users, users_z], axis=0)
    ads_pair = jnp.concatenate([ads, ads_z], axis=0)
    user_1, user_3, ads_1, ads_3 = lax.optimization_barrier(
        (shift_x(user_pair, 1), shift_x(user_pair, -1), shift_y(ads_pair, 1), shift_y(ads_pair, -1))
    )
    user_2a, user_2b = shift_x(user_1[:T], 1), shift_x(user_3[T:], -1)
    ads_2a, ads_2b = shift_y(ads_1[:T], 1), shift_y(ads_3[T:], -1)
    near = jnp.concatenate([ads_pair, ads_1, ads_3], axis=0)
    far = swap_core(near)
    user_2a, user_2b, ads_2a, ads_2b = lax.optimization_barrier((user_2a, user_2b, ads_2a, ads_2b))
    near_2 = jnp.concatenate([ads_2a, ads_2b], axis=0)
    far_2 = swap_core(near_2)
    parts = (user_pair, user_1, user_3, user_2a, user_2b)

    p_near, m_near, t_near, hits = run_logits("near", parts, (near,), count_row, pos_row, inv)
    p_far, m_far, t_far, hits = run_logits("far", parts, (far,), count_row, pos_row, inv, (hits,))
    p_mid, m_mid, _, hits, stats = run_logits(
        "mid", parts, (near_2, far_2), count_row, pos_row, inv, (hits,), (m_near, t_near, m_far, t_far)
    )
    n_aa = lax.axis_size("aa")
    stats = lax.all_to_all(
        jnp.broadcast_to(stats[None], (n_aa,) + stats.shape), "aa", split_axis=0, concat_axis=0, tiled=True
    )
    tail = (hits, pos_row, weight_row, stats, inv)
    da_2, pay_2, loss, acc = run_grads("mid", parts, (near_2, far_2), p_mid, m_mid, *tail)
    back_2 = swap_core(pay_2)
    da_far, acc = run_grads("far", parts, (far,), p_far, m_far, *tail, (acc,))
    back = swap_core(da_far)
    first, second, both = add_mid(da_2, loss, back_2)
    first, second = shift_y(first, -1), shift_y(second, 1)
    da_near, du_0, du_1, du_3, du_2a, du_2b = run_grads("near", parts, (near,), p_near, m_near, *tail, (acc,))
    du_2a, du_2b = shift_x(du_2a, 1), shift_x(du_2b, -1)
    kept, one, three = add_near(da_near, back, both, first, second)
    one, three = shift_y(one, -1), shift_y(three, 1)
    du_1, du_3 = add_halves(du_1, du_3, du_2a, du_2b)
    du_1, du_3 = shift_x(du_1, 1), shift_x(du_3, -1)
    keep, kept_loss, send = add_rows(kept, both, (one, three))
    keep_u, send_u = add_users((du_0, du_1, du_3))
    grad_users, grad_ads, loss = finish(keep_u, swap_z_hi(send_u), keep, kept_loss, swap_z_lo(send))
    return grad_users, grad_ads, loss.reshape(())


def solution(mesh):
    return jax.shard_map(
        local,
        mesh=mesh,
        in_specs=(P(("au", "aa"), None), P(("aa", "au"), None), P("aa"), P("au"), P("au")),
        out_specs=(P(("au", "aa"), None), P(("aa", "au"), None), P()),
        check_vma=False,
    )
```

time: 111 us -> 107 us (0.964)
  waiting for transfers between devices: 34.7 us -> 26.2 us
  starting transfers between devices: 23.9 us -> 30.5 us
    ppermute x19 -> x24, waiting for transfers between devices: 34.7 us -> 26.2 us  [move(): lax.ppermute(x, axis, [(i, target(i)) for i in range(lax.axis_size(axis))])]
    ppermute x19 -> x24, starting transfers between devices: 23.9 us -> 30.5 us  [move(): lax.ppermute(x, axis, [(i, target(i)) for i in range(lax.axis_size(axis))])]
    unnamed x11 -> x13, local copies, waits for them, and re-layouts: 2.6 us -> 3.3 us
    pallas_call x5 -> x6, Pallas kernels: 2.33 us -> 1.79 us  [simple_call(): pl.pallas_call(kernel, in_specs=[whole(x.shape) for x in args], out_specs...]
    pallas_call x4 -> x6, Pallas kernels: 31.5 us -> 31.3 us  [the longest x3 17.1 us: run_logits(): pl.pallas_call(lambda *refs: logits_kernel(group, len(ads), not hits, boo...]
  transfers between devices with their start and end apart: 19 -> 24, of which waited for: 11 -> 13; matrix products, arithmetic and copies ran while one was open for 3% -> 2% of each run, Pallas kernels for 15% -> 22%
where the time goes in v2:
time: 107 us
  Pallas kernels  33.1 us (31%)
  starting transfers between devices  30.5 us (29%)
  waiting for transfers between devices  26.2 us (24%)
  blocking collectives  13 us (12%)
  local copies, waits for them, and re-layouts  3.39 us (3%)
    ppermute x24, starting transfers between devices, move(): lax.ppermute(x, axis, [(i, target(i)) for i in range(lax.axis_size(axis))])  30.5 us
    ppermute x24, waiting for transfers between devices, move(): lax.ppermute(x, axis, [(i, target(i)) for i in range(lax.axis_size(axis))])  26.2 us
    pallas_call x3, Pallas kernels, run_logits(): pl.pallas_call(lambda *refs: logits_kernel(group, len(ads), not hits, boo...  17.1 us
    pallas_call x3, Pallas kernels, run_grads(): pl.pallas_call(lambda *refs: grads_kernel(group, len(ads), steps, inv, *r...  14.2 us
    all_to_all x1, blocking collectives, local(): lax.all_to_all(jnp.broadcast_to(stats[None], (n_aa,) + stats.shape), 'aa'...  13 us
    unnamed x13, local copies, waits for them, and re-layouts  3.3 us
  transfers between devices with their start and end apart: 24, of which 13 were waited for; matrix products, arithmetic and copies ran while one was open for 2% of the time, Pallas kernels for 22%

profile of v2, /device:TPU:0, one launch (start us, length us, event | category | flops | bytes accessed | tf_op | source)
XLA Modules:
  0.0 106.9 jit_solution(12971877470282025351)
XLA Ops:
  0.6 4.0 %collective-permute-start = (bf16[256,256]{1,0:T(8,128)(2,1)}, bf16[256,256]{1,0:T(8,128)(2,1)S(1)}, u32[]{:S(2)}, u32[]{:S(2)}) collective-permute-start(bf16[256,256]{1,0:T(8,128)(2,1)} %param.5), channel_id=1, source_target_pairs={{0,1},{1,0},{2,3},{3,2},{4,5},{5,4},{6,7},{7,6},{8,9},{9,8},{10,11... | collective-permute-start | bytes 393224 | tf_op jit(solution)/shard_map/ppermute | solution.py:458
  4.7 1.0 collective-permute-start.1
  5.7 0.9 constant_dynamic-update-slice_fusion.1
  6.6 0.9 constant_dynamic-update-slice_fusion.7
  7.5 1.7 %collective-permute-done = bf16[256,256]{1,0:T(8,128)(2,1)S(1)} collective-permute-done((bf16[256,256]{1,0:T(8,128)(2,1)}, bf16[256,256]{1,0:T(8,128)(2,1)S(1)}, u32[]{:S(2)}, u32[]{:S(2)}) %collective-permute-start) | collective-permute-done | bytes 131104 | tf_op jit(solution)/shard_map/ppermute | solution.py:458
  9.2 2.7 %collective-permute-done.1 = bf16[256,256]{1,0:T(8,128)(2,1)S(1)} collective-permute-done((bf16[256,256]{1,0:T(8,128)(2,1)}, bf16[256,256]{1,0:T(8,128)(2,1)S(1)}, u32[]{:S(2)}, u32[]{:S(2)}) %collective-permute-start.1) | collective-permute-done | bytes 131104 | tf_op jit(solution)/shard_map/ppermute | solution.py:458
  11.9 2.8 %collective-permute-start.3 = (bf16[512,256]{1,0:T(8,128)(2,1)S(1)}, bf16[512,256]{1,0:T(8,128)(2,1)S(1)}, u32[]{:S(2)}, u32[]{:S(2)}) collective-permute-start(bf16[512,256]{1,0:T(8,128)(2,1)S(1)} %constant_dynamic-update-slice_fusion.refs_0_), channel_id=1, source_target_pairs={{0,6},{1,7},{2,0},{3,1},{4,2},{5,3},{6,4},{7,5},{8,14},{9,15},{10,... | collective-permute-start | bytes 786440 | tf_op jit(solution)/shard_map/ppermute | solution.py:458
  14.8 3.1 %collective-permute-start.5 = (bf16[512,256]{1,0:T(8,128)(2,1)S(1)}, bf16[512,256]{1,0:T(8,128)(2,1)S(1)}, u32[]{:S(2)}, u32[]{:S(2)}) collective-permute-start(bf16[512,256]{1,0:T(8,128)(2,1)S(1)} %get-tuple-element.104), channel_id=1, source_target_pairs={{0,48},{8,56},{16,0},{24,8},{32,16},{40,24},{48,32},{56,40},{64,11... | collective-permute-start | bytes 786440 | tf_op jit(solution)/shard_map/ppermute | solution.py:458
  17.9 1.6 %collective-permute-done.3.refs_2_ = bf16[512,256]{1,0:T(8,128)(2,1)S(1)} collective-permute-done((bf16[512,256]{1,0:T(8,128)(2,1)S(1)}, bf16[512,256]{1,0:T(8,128)(2,1)S(1)}, u32[]{:S(2)}, u32[]{:S(2)}) %collective-permute-start.3) | collective-permute-done | bytes 262176 | tf_op jit(solution)/shard_map/ppermute | solution.py:458
  19.5 3.4 %collective-permute-done.2.refs_1_ = bf16[512,256]{1,0:T(8,128)(2,1)S(1)} collective-permute-done((bf16[512,256]{1,0:T(8,128)(2,1)S(1)}, bf16[512,256]{1,0:T(8,128)(2,1)S(1)}, u32[]{:S(2)}, u32[]{:S(2)}) %collective-permute-start.2) | collective-permute-done | bytes 262176 | tf_op jit(solution)/shard_map/ppermute | solution.py:458
  22.9 2.8 %collective-permute-done.4 = bf16[512,256]{1,0:T(8,128)(2,1)S(1)} collective-permute-done((bf16[512,256]{1,0:T(8,128)(2,1)S(1)}, bf16[512,256]{1,0:T(8,128)(2,1)S(1)}, u32[]{:S(2)}, u32[]{:S(2)}) %collective-permute-start.4) | collective-permute-done | bytes 262176 | tf_op jit(solution)/shard_map/ppermute | solution.py:458
  25.8 3.1 %collective-permute-start.7 = (bf16[256,256]{1,0:T(8,128)(2,1)S(1)}, bf16[256,256]{1,0:T(8,128)(2,1)S(1)}, u32[]{:S(2)}, u32[]{:S(2)}) collective-permute-start(bf16[256,256]{1,0:T(8,128)(2,1)S(1)} %slice.13), channel_id=1, source_target_pairs={{0,6},{1,7},{2,0},{3,1},{4,2},{5,3},{6,4},{7,5},{8,14},{9,15},{10,... | collective-permute-start | bytes 393224 | tf_op jit(solution)/shard_map/ppermute | solution.py:458
  29.1 1.8 %collective-permute-start.8 = (bf16[256,256]{1,0:T(8,128)(2,1)S(1)}, bf16[256,256]{1,0:T(8,128)(2,1)S(1)}, u32[]{:S(2)}, u32[]{:S(2)}) collective-permute-start(bf16[256,256]{1,0:T(8,128)(2,1)S(1)} %slice.14), channel_id=1, source_target_pairs={{0,16},{8,24},{16,32},{24,40},{32,48},{40,56},{48,0},{56,8},{64,80... | collective-permute-start | bytes 393224 | tf_op jit(solution)/shard_map/ppermute | solution.py:458
  31.3 3.7 %collective-permute-done.6.refs_3_ = bf16[256,256]{1,0:T(8,128)(2,1)S(1)} collective-permute-done((bf16[256,256]{1,0:T(8,128)(2,1)S(1)}, bf16[256,256]{1,0:T(8,128)(2,1)S(1)}, u32[]{:S(2)}, u32[]{:S(2)}) %collective-permute-start.6) | collective-permute-done | bytes 131104 | tf_op jit(solution)/shard_map/ppermute | solution.py:458
  35.4 0.7 copy-done
  36.8 6.0 %logits_near.1 = (bf16[1536,2048]{1,0:T(8,128)(2,1)S(1)}, f32[8,2048]{1,0:T(8,128)S(1)}, f32[8,2048]{1,0:T(8,128)S(1)}, f32[1,2048]{1,0:T(1,128)S(1)}) custom-call(bf16[512,256]{1,0:T(8,128)(2,1)S(1)} %constant_dynamic-update-slice_fusion.refs_0_, bf16[512,256]{1,0:T(8,128)(2,1)S(1)} %collective-permute-done.2.refs_1_, ...), custom_call_target="tpu_custom_call" | custom-call | flops 6442450944 | bytes 6291456 | tf_op jit(solution)/shard_map/logits_near/pallas_call | solution.py:186
  42.8 6.1 %logits_far.1 = (bf16[1536,2048]{1,0:T(8,128)(2,1)S(1)}, f32[8,2048]{1,0:T(8,128)S(1)}, f32[8,2048]{1,0:T(8,128)S(1)}, f32[1,2048]{1,0:T(1,128)S(1)}) custom-call(bf16[512,256]{1,0:T(8,128)(2,1)S(1)} %constant_dynamic-update-slice_fusion.refs_0_, bf16[512,256]{1,0:T(8,128)(2,1)S(1)} %collective-permute-done.2.refs_1_, ...), custom_call_target="tpu_custom_call" | custom-call | flops 6442450944 | bytes 6291456 | tf_op jit(solution)/shard_map/logits_far/pallas_call | solution.py:186
  48.9 5.0 %logits_mid.1 = (bf16[1024,2048]{1,0:T(8,128)(2,1)S(1)}, f32[8,2048]{1,0:T(8,128)S(1)}, f32[8,2048]{1,0:T(8,128)}, f32[1,2048]{1,0:T(1,128)S(1)}, f32[32,128]{1,0:T(8,128)S(1)}) custom-call(bf16[512,256]{1,0:T(8,128)(2,1)S(1)} %constant_dynamic-update-slice_fusion.refs_0_, bf16[512,256]{1,0:T(8,128)(2,1)S(1)} %collective-permute-done.2.refs_1_, ...), custom_call_target="tpu_custom_call" | custom-call | flops 4294967296 | bytes 4194304 | tf_op jit(solution)/shard_map/logits_mid/pallas_call | solution.py:186
  53.9 13.0 %all_to_all.5.refs_12_.refs_11_ = f32[8,32,128]{2,1,0:T(8,128)S(1)} all-to-all(f32[8,32,128]{2,1,0:T(8,128)S(1)} %broadcast_in_dim.18), channel_id=1, replica_groups=mesh['au'=16,'aa'=8] {'aa'}, dimensions={0} | all-to-all | bytes 262144 | tf_op jit(solution)/shard_map/all_to_all | solution.py:505
  66.9 3.7 %grads_mid.1 = (bf16[512,256]{1,0:T(8,128)(2,1)S(1)}, bf16[528,256]{1,0:T(8,128)(2,1)S(1)}, bf16[16,256]{1,0:T(8,128)(2,1)S(1)}, f32[256,2048]{1,0:T(8,128)S(1)}) custom-call(bf16[512,256]{1,0:T(8,128)(2,1)S(1)} %constant_dynamic-update-slice_fusion.refs_0_, bf16[512,256]{1,0:T(8,128)(2,1)S(1)} %collective-permute-done.2.refs_1_, ...), custom_call_target="tpu_custom_call" | custom-call | flops 4294967296 | bytes 4194304 | tf_op jit(solution)/shard_map/grads_mid/pallas_call | solution.py:335
  70.7 5.2 %grads_far.1 = (bf16[1536,256]{1,0:T(8,128)(2,1)S(1)}, f32[256,2048]{1,0:T(8,128)S(1)}) custom-call(bf16[512,256]{1,0:T(8,128)(2,1)S(1)} %constant_dynamic-update-slice_fusion.refs_0_, bf16[512,256]{1,0:T(8,128)(2,1)S(1)} %collective-permute-done.2.refs_1_, bf16[512,256]{1,0:T(8,128)(2,1)S(1)} %collective-permute-done.3.refs_2_, ...), custom_call_target="tpu_custom_call" | custom-call | flops 6442450944 | bytes 6291456 | tf_op jit(solution)/shard_map/grads_far/pallas_call | solution.py:335
  77.2 2.6 %collective-permute-start.19 = (bf16[272,256]{1,0:T(8,128)(2,1)S(1)}, bf16[272,256]{1,0:T(8,128)(2,1)S(1)}, u32[]{:S(2)}, u32[]{:S(2)}) collective-permute-start(bf16[272,256]{1,0:T(8,128)(2,1)S(1)} %get-tuple-element.92), channel_id=1, source_target_pairs={{0,48},{8,56},{16,0},{24,8},{32,16},{40,24},{48,32},{56,40},{64,11... | collective-permute-start | bytes 417800 | tf_op jit(solution)/shard_map/ppermute | solution.py:458
  79.9 5.3 %grads_near.1 = (bf16[1536,256]{1,0:T(8,128)(2,1)S(1)}, bf16[512,256]{1,0:T(8,128)(2,1)S(1)}, bf16[512,256]{1,0:T(8,128)(2,1)S(1)}, bf16[512,256]{1,0:T(8,128)(2...) custom-call(bf16[512,256]{1,0:T(8,128)(2,1)S(1)} %constant_dynamic-update-slice_fusion.refs_0_, ...), custom_call_target="tpu_custom_call" | custom-call | flops 6442450944 | bytes 6291456 | tf_op jit(solution)/shard_map/grads_near/pallas_call | solution.py:335
  85.6 2.9 %collective-permute-start.13 = (bf16[256,256]{1,0:T(8,128)(2,1)S(1)}, bf16[256,256]{1,0:T(8,128)(2,1)S(1)}, u32[]{:S(2)}, u32[]{:S(2)}) collective-permute-start(bf16[256,256]{1,0:T(8,128)(2,1)S(1)} %get-tuple-element.81), channel_id=1, source_target_pairs={{0,6},{1,7},{2,0},{3,1},{4,2},{5,3},{6,4},{7,5},{8,14},{9,15},{10,... | collective-permute-start | bytes 393224 | tf_op jit(solution)/shard_map/ppermute | solution.py:458
  89.1 2.0 %collective-permute-start.22 = (bf16[528,256]{1,0:T(8,128)(2,1)S(1)}, bf16[528,256]{1,0:T(8,128)(2,1)S(1)}, u32[]{:S(2)}, u32[]{:S(2)}) collective-permute-start(bf16[528,256]{1,0:T(8,128)(2,1)S(1)} %get-tuple-element.96), channel_id=1, source_target_pairs={{0,16},{8,24},{16,32},{24,40},{32,48},{40,56},{48,0},{56,8},{64,80... | collective-permute-start | bytes 811016 | tf_op jit(solution)/shard_map/ppermute | solution.py:458
  91.6 3.3 %collective-permute-start.15 = (bf16[512,256]{1,0:T(8,128)(2,1)S(1)}, bf16[512,256]{1,0:T(8,128)(2,1)S(1)}, u32[]{:S(2)}, u32[]{:S(2)}) collective-permute-start(bf16[512,256]{1,0:T(8,128)(2,1)S(1)} %get-tuple-element.83), channel_id=1, source_target_pairs={{0,6},{1,7},{2,0},{3,1},{4,2},{5,3},{6,4},{7,5},{8,14},{9,15},{10,... | collective-permute-start | bytes 786440 | tf_op jit(solution)/shard_map/ppermute | solution.py:458
  94.9 1.4 %collective-permute-done.21.r1 = bf16[528,256]{1,0:T(8,128)(2,1)S(1)} collective-permute-done((bf16[528,256]{1,0:T(8,128)(2,1)S(1)}, bf16[528,256]{1,0:T(8,128)(2,1)S(1)}, u32[]{:S(2)}, u32[]{:S(2)}) %collective-permute-start.21) | collective-permute-done | bytes 270368 | tf_op jit(solution)/shard_map/ppermute | solution.py:458
  96.3 1.3 %collective-permute-done.22.r3 = bf16[528,256]{1,0:T(8,128)(2,1)S(1)} collective-permute-done((bf16[528,256]{1,0:T(8,128)(2,1)S(1)}, bf16[528,256]{1,0:T(8,128)(2,1)S(1)}, u32[]{:S(2)}, u32[]{:S(2)}) %collective-permute-start.22) | collective-permute-done | bytes 270368 | tf_op jit(solution)/shard_map/ppermute | solution.py:458
  98.4 1.0 collective-permute-done.14.refs_1_
  99.4 1.0 collective-permute-start.16
  100.4 5.6 %collective-permute-done.16.received_u_ref = bf16[256,256]{1,0:T(8,128)(2,1)S(1)} collective-permute-done((bf16[256,256]{1,0:T(8,128)(2,1)S(1)}, bf16[256,256]{1,0:T(8,128)(2,1)S(1)}, u32[]{:S(2)}, u32[]{:S(2)}) %collective-permute-start.16) | collective-permute-done | bytes 131104 | tf_op jit(solution)/shard_map/ppermute | solution.py:458
  106.0 0.9 finish.1
  (50 shorter events, 5.6 us)
Async XLA Ops:
  0.6 8.6 %collective-permute-start = (bf16[256,256]{1,0:T(8,128)(2,1)}, bf16[256,256]{1,0:T(8,128)(2,1)S(1)}, u32[]{:S(2)}, u32[]{:S(2)}) collective-permute-start(bf16[256,256]{1,0:T(8,128)(2,1)} %param.5), channel_id=1, source_target_pairs={{0,1},{1,0},{2,3},{3,2},{4,5},{5,4},{6,7},{7,6},{8,9},{9,8},{10,11... | collective-permute-start | bytes 393224 | tf_op jit(solution)/shard_map/ppermute | solution.py:458
  4.7 7.2 %collective-permute-start.1 = (bf16[256,256]{1,0:T(8,128)(2,1)}, bf16[256,256]{1,0:T(8,128)(2,1)S(1)}, u32[]{:S(2)}, u32[]{:S(2)}) collective-permute-start(bf16[256,256]{1,0:T(8,128)(2,1)} %param.6), channel_id=1, source_target_pairs={{0,64},{8,72},{16,80},{24,88},{32,96},{40,104},{48,112},{56,120},{... | collective-permute-start | bytes 393224 | tf_op jit(solution)/shard_map/ppermute | solution.py:458
  11.9 7.5 %collective-permute-start.3 = (bf16[512,256]{1,0:T(8,128)(2,1)S(1)}, bf16[512,256]{1,0:T(8,128)(2,1)S(1)}, u32[]{:S(2)}, u32[]{:S(2)}) collective-permute-start(bf16[512,256]{1,0:T(8,128)(2,1)S(1)} %constant_dynamic-update-slice_fusion.refs_0_), channel_id=1, source_target_pairs={{0,6},{1,7},{2,0},{3,1},{4,2},{5,3},{6,4},{7,5},{8,14},{9,15},{10,... | collective-permute-start | bytes 786440 | tf_op jit(solution)/shard_map/ppermute | solution.py:458
  14.8 8.1 %collective-permute-start.2 = (bf16[512,256]{1,0:T(8,128)(2,1)S(1)}, bf16[512,256]{1,0:T(8,128)(2,1)S(1)}, u32[]{:S(2)}, u32[]{:S(2)}) collective-permute-start(bf16[512,256]{1,0:T(8,128)(2,1)S(1)} %constant_dynamic-update-slice_fusion.refs_0_), channel_id=1, source_target_pairs={{0,2},{1,3},{2,4},{3,5},{4,6},{5,7},{6,0},{7,1},{8,10},{9,11},{10,... | collective-permute-start | bytes 786440 | tf_op jit(solution)/shard_map/ppermute | solution.py:458
  14.8 8.1 %collective-permute-start.5 = (bf16[512,256]{1,0:T(8,128)(2,1)S(1)}, bf16[512,256]{1,0:T(8,128)(2,1)S(1)}, u32[]{:S(2)}, u32[]{:S(2)}) collective-permute-start(bf16[512,256]{1,0:T(8,128)(2,1)S(1)} %get-tuple-element.104), channel_id=1, source_target_pairs={{0,48},{8,56},{16,0},{24,8},{32,16},{40,24},{48,32},{56,40},{64,11... | collective-permute-start | bytes 786440 | tf_op jit(solution)/shard_map/ppermute | solution.py:458
  17.9 7.8 %collective-permute-start.4 = (bf16[512,256]{1,0:T(8,128)(2,1)S(1)}, bf16[512,256]{1,0:T(8,128)(2,1)S(1)}, u32[]{:S(2)}, u32[]{:S(2)}) collective-permute-start(bf16[512,256]{1,0:T(8,128)(2,1)S(1)} %get-tuple-element.104), channel_id=1, source_target_pairs={{0,16},{8,24},{16,32},{24,40},{32,48},{40,56},{48,0},{56,8},{64,80... | collective-permute-start | bytes 786440 | tf_op jit(solution)/shard_map/ppermute | solution.py:458
  25.8 5.6 %collective-permute-start.7 = (bf16[256,256]{1,0:T(8,128)(2,1)S(1)}, bf16[256,256]{1,0:T(8,128)(2,1)S(1)}, u32[]{:S(2)}, u32[]{:S(2)}) collective-permute-start(bf16[256,256]{1,0:T(8,128)(2,1)S(1)} %slice.13), channel_id=1, source_target_pairs={{0,6},{1,7},{2,0},{3,1},{4,2},{5,3},{6,4},{7,5},{8,14},{9,15},{10,... | collective-permute-start | bytes 393224 | tf_op jit(solution)/shard_map/ppermute | solution.py:458
  28.8 6.2 %collective-permute-start.6 = (bf16[256,256]{1,0:T(8,128)(2,1)S(1)}, bf16[256,256]{1,0:T(8,128)(2,1)S(1)}, u32[]{:S(2)}, u32[]{:S(2)}) collective-permute-start(bf16[256,256]{1,0:T(8,128)(2,1)S(1)} %slice.12), channel_id=1, source_target_pairs={{0,2},{1,3},{2,4},{3,5},{4,6},{5,7},{6,0},{7,1},{8,10},{9,11},{10,... | collective-permute-start | bytes 393224 | tf_op jit(solution)/shard_map/ppermute | solution.py:458
  28.8 6.2 %collective-permute-start.9 = (bf16[256,256]{1,0:T(8,128)(2,1)S(1)}, bf16[256,256]{1,0:T(8,128)(2,1)S(1)}, u32[]{:S(2)}, u32[]{:S(2)}) collective-permute-start(bf16[256,256]{1,0:T(8,128)(2,1)S(1)} %slice.15), channel_id=1, source_target_pairs={{0,48},{8,56},{16,0},{24,8},{32,16},{40,24},{48,32},{56,40},{64,11... | collective-permute-start | bytes 393224 | tf_op jit(solution)/shard_map/ppermute | solution.py:458
  29.1 6.2 %collective-permute-start.8 = (bf16[256,256]{1,0:T(8,128)(2,1)S(1)}, bf16[256,256]{1,0:T(8,128)(2,1)S(1)}, u32[]{:S(2)}, u32[]{:S(2)}) collective-permute-start(bf16[256,256]{1,0:T(8,128)(2,1)S(1)} %slice.14), channel_id=1, source_target_pairs={{0,16},{8,24},{16,32},{24,40},{32,48},{40,56},{48,0},{56,8},{64,80... | collective-permute-start | bytes 393224 | tf_op jit(solution)/shard_map/ppermute | solution.py:458
  30.9 11.9 %collective-permute-start.11 = (bf16[1536,256]{1,0:T(8,128)(2,1)S(1)}, bf16[1536,256]{1,0:T(8,128)(2,1)S(1)}, u32[]{:S(2)}, u32[]{:S(2)}) collective-permute-start(bf16[1536,256]{1,0:T(8,128)(2,1)S(1)} %constant_dynamic-update-slice_fusion.4.refs_5_), channel_id=1, source_target_pairs={{0,8},{8,0},{16,24},{24,16},{32,40},{40,32},{48,56},{56,48},{64,72... | collective-permute-start | bytes 2359304 | tf_op jit(solution)/shard_map/ppermute | solution.py:458
  35.3 13.6 %collective-permute-start.10 = (bf16[512,256]{1,0:T(8,128)(2,1)S(1)}, bf16[512,256]{1,0:T(8,128)(2,1)S(1)}, u32[]{:S(2)}, u32[]{:S(2)}) collective-permute-start(bf16[512,256]{1,0:T(8,128)(2,1)S(1)} %constant_dynamic-update-slice_fusion.8.refs_5_), channel_id=1, source_target_pairs={{0,8},{8,0},{16,24},{24,16},{32,40},{40,32},{48,56},{56,48},{64,72... | collective-permute-start | bytes 786440 | tf_op jit(solution)/shard_map/ppermute | solution.py:458
  35.4 0.7 copy-start
  36.1 0.7 copy-start.1
  48.9 18.0 %copy-start.2 = (s32[2048]{0:T(1024)S(1)}, s32[2048]{0:T(1024)}, u32[]{:S(2)}) copy-start(s32[2048]{0:T(1024)} %param.8) | copy-start | bytes 24580
  48.9 18.0 %copy-start.3 = (f32[2048]{0:T(1024)S(1)}, f32[2048]{0:T(1024)}, u32[]{:S(2)}) copy-start(f32[2048]{0:T(1024)} %param.9) | copy-start | bytes 24580
  70.6 5.9 %collective-permute-start.18 = (bf16[528,256]{1,0:T(8,128)(2,1)S(1)}, bf16[528,256]{1,0:T(8,128)(2,1)S(1)}, u32[]{:S(2)}, u32[]{:S(2)}) collective-permute-start(bf16[528,256]{1,0:T(8,128)(2,1)S(1)} %get-tuple-element.90), channel_id=1, source_target_pairs={{0,8},{8,0},{16,24},{24,16},{32,40},{40,32},{48,56},{56,48},{64,72... | collective-permute-start | bytes 811016 | tf_op jit(solution)/shard_map/ppermute | solution.py:458
  75.9 12.6 %collective-permute-start.17 = (bf16[1536,256]{1,0:T(8,128)(2,1)S(1)}, bf16[1536,256]{1,0:T(8,128)(2,1)S(1)}, u32[]{:S(2)}, u32[]{:S(2)}) collective-permute-start(bf16[1536,256]{1,0:T(8,128)(2,1)S(1)} %get-tuple-element.87), channel_id=1, source_target_pairs={{0,8},{8,0},{16,24},{24,16},{32,40},{40,32},{48,56},{56,48},{64,72... | collective-permute-start | bytes 2359304 | tf_op jit(solution)/shard_map/ppermute | solution.py:458
  76.6 11.9 %collective-permute-start.20 = (bf16[256,256]{1,0:T(8,128)(2,1)S(1)}, bf16[256,256]{1,0:T(8,128)(2,1)S(1)}, u32[]{:S(2)}, u32[]{:S(2)}) collective-permute-start(bf16[256,256]{1,0:T(8,128)(2,1)S(1)} %get-tuple-element.93), channel_id=1, source_target_pairs={{0,16},{8,24},{16,32},{24,40},{32,48},{40,56},{48,0},{56,8},{64,80... | collective-permute-start | bytes 393224 | tf_op jit(solution)/shard_map/ppermute | solution.py:458
  77.2 11.3 %collective-permute-start.19 = (bf16[272,256]{1,0:T(8,128)(2,1)S(1)}, bf16[272,256]{1,0:T(8,128)(2,1)S(1)}, u32[]{:S(2)}, u32[]{:S(2)}) collective-permute-start(bf16[272,256]{1,0:T(8,128)(2,1)S(1)} %get-tuple-element.92), channel_id=1, source_target_pairs={{0,48},{8,56},{16,0},{24,8},{32,16},{40,24},{48,32},{56,40},{64,11... | collective-permute-start | bytes 417800 | tf_op jit(solution)/shard_map/ppermute | solution.py:458
  85.2 6.2 %collective-permute-start.12 = (bf16[256,256]{1,0:T(8,128)(2,1)S(1)}, bf16[256,256]{1,0:T(8,128)(2,1)S(1)}, u32[]{:S(2)}, u32[]{:S(2)}) collective-permute-start(bf16[256,256]{1,0:T(8,128)(2,1)S(1)} %get-tuple-element.80), channel_id=1, source_target_pairs={{0,2},{1,3},{2,4},{3,5},{4,6},{5,7},{6,0},{7,1},{8,10},{9,11},{10,... | collective-permute-start | bytes 393224 | tf_op jit(solution)/shard_map/ppermute | solution.py:458
  85.6 5.8 %collective-permute-start.13 = (bf16[256,256]{1,0:T(8,128)(2,1)S(1)}, bf16[256,256]{1,0:T(8,128)(2,1)S(1)}, u32[]{:S(2)}, u32[]{:S(2)}) collective-permute-start(bf16[256,256]{1,0:T(8,128)(2,1)S(1)} %get-tuple-element.81), channel_id=1, source_target_pairs={{0,6},{1,7},{2,0},{3,1},{4,2},{5,3},{6,4},{7,5},{8,14},{9,15},{10,... | collective-permute-start | bytes 393224 | tf_op jit(solution)/shard_map/ppermute | solution.py:458
  89.0 7.4 %collective-permute-start.21 = (bf16[528,256]{1,0:T(8,128)(2,1)S(1)}, bf16[528,256]{1,0:T(8,128)(2,1)S(1)}, u32[]{:S(2)}, u32[]{:S(2)}) collective-permute-start(bf16[528,256]{1,0:T(8,128)(2,1)S(1)} %get-tuple-element.95), channel_id=1, source_target_pairs={{0,48},{8,56},{16,0},{24,8},{32,16},{40,24},{48,32},{56,40},{64,11... | collective-permute-start | bytes 811016 | tf_op jit(solution)/shard_map/ppermute | solution.py:458
  89.1 8.6 %collective-permute-start.22 = (bf16[528,256]{1,0:T(8,128)(2,1)S(1)}, bf16[528,256]{1,0:T(8,128)(2,1)S(1)}, u32[]{:S(2)}, u32[]{:S(2)}) collective-permute-start(bf16[528,256]{1,0:T(8,128)(2,1)S(1)} %get-tuple-element.96), channel_id=1, source_target_pairs={{0,16},{8,24},{16,32},{24,40},{32,48},{40,56},{48,0},{56,8},{64,80... | collective-permute-start | bytes 811016 | tf_op jit(solution)/shard_map/ppermute | solution.py:458
  91.5 7.8 %collective-permute-start.14 = (bf16[512,256]{1,0:T(8,128)(2,1)S(1)}, bf16[512,256]{1,0:T(8,128)(2,1)S(1)}, u32[]{:S(2)}, u32[]{:S(2)}) collective-permute-start(bf16[512,256]{1,0:T(8,128)(2,1)S(1)} %get-tuple-element.82), channel_id=1, source_target_pairs={{0,2},{1,3},{2,4},{3,5},{4,6},{5,7},{6,0},{7,1},{8,10},{9,11},{10,... | collective-permute-start | bytes 786440 | tf_op jit(solution)/shard_map/ppermute | solution.py:458
  91.6 7.7 %collective-permute-start.15 = (bf16[512,256]{1,0:T(8,128)(2,1)S(1)}, bf16[512,256]{1,0:T(8,128)(2,1)S(1)}, u32[]{:S(2)}, u32[]{:S(2)}) collective-permute-start(bf16[512,256]{1,0:T(8,128)(2,1)S(1)} %get-tuple-element.83), channel_id=1, source_target_pairs={{0,6},{1,7},{2,0},{3,1},{4,2},{5,3},{6,4},{7,5},{8,14},{9,15},{10,... | collective-permute-start | bytes 786440 | tf_op jit(solution)/shard_map/ppermute | solution.py:458
  97.8 8.2 %collective-permute-start.23 = (bf16[272,256]{1,0:T(8,128)(2,1)S(1)}, bf16[272,256]{1,0:T(8,128)(2,1)S(1)}, u32[]{:S(2)}, u32[]{:S(2)}) collective-permute-start(bf16[272,256]{1,0:T(8,128)(2,1)S(1)} %get-tuple-element.99), channel_id=1, source_target_pairs={{0,64},{8,72},{16,80},{24,88},{32,96},{40,104},{48,112},{56,120},{... | collective-permute-start | bytes 417800 | tf_op jit(solution)/shard_map/ppermute | solution.py:458
  99.4 6.6 %collective-permute-start.16 = (bf16[256,256]{1,0:T(8,128)(2,1)S(1)}, bf16[256,256]{1,0:T(8,128)(2,1)S(1)}, u32[]{:S(2)}, u32[]{:S(2)}) collective-permute-start(bf16[256,256]{1,0:T(8,128)(2,1)S(1)} %get-tuple-element.85), channel_id=1, source_target_pairs={{0,1},{1,0},{2,3},{3,2},{4,5},{5,4},{6,7},{7,6},{8,9},{9,8},{10,11... | collective-permute-start | bytes 393224 | tf_op jit(solution)/shard_map/ppermute | solution.py:458

commit v3 on v0

v3 whole, which is shorter than its diff:
```python
import jax
import jax.numpy as jnp
from jax import lax
from jax.experimental import pallas as pl
from jax.experimental.pallas import tpu as pltpu
from jax.sharding import PartitionSpec as P

F32 = jnp.float32
BF16 = jnp.bfloat16
T = 256
LANES = 128
EXTRA = 16
NX, NZ, NY, NC = 4, 2, 4, 2
VMEM_LIMIT = 32 * 2**20


def params():
    return pltpu.CompilerParams(vmem_limit_bytes=VMEM_LIMIT)


def whole(shape):
    return pl.BlockSpec(shape, lambda *_: (0,) * len(shape))


def user_block(j, zr):
    me = lax.axis_index("aa")
    x, z = me // NZ, me % NZ
    return lax.rem(x + NX - j, NX) * NZ + (z + zr - 2 * z * zr)


def ads_block(group, chunk):
    pair, zr = chunk // NZ, chunk % NZ
    k, cr = {"near": (pair + pair // 2, 0), "far": (pair + pair // 2, 1), "mid": (2, pair)}[group]
    me = lax.axis_index("au")
    z, y, c = me // (NY * NC), (me // NC) % NY, me % NC
    return (z + zr - 2 * z * zr) * (NY * NC) + lax.rem(y + NY - k, NY) * NC + (c + cr - 2 * c * cr)


USER_PARTS = 5


def stage_users(user_refs, staged, inv):
    places = [(0, 0, 0, 0), (0, 1, 0, 1), (1, 0, 1, 0), (1, 1, 1, 1), (3, 0, 2, 0), (3, 1, 2, 1), (2, 0, 3, 0), (2, 1, 4, 0)]
    for j, zr, part, half in places:
        spot = pl.multiple_of(user_block(j, zr) * T, T)
        block = user_refs[part][half * T : (half + 1) * T, :].astype(F32) * inv
        staged[pl.ds(spot, T), :] = block.astype(BF16)


def first_row(group, chunk):
    return pl.multiple_of(ads_block(group, chunk) * T, T)


def split(value):
    high = value.astype(BF16).astype(F32)
    mid = (value - high).astype(BF16).astype(F32)
    return high, mid, value - high - mid


def loss_rows(loss, width):
    high, mid, low = split(loss)
    lane = lax.broadcasted_iota(jnp.int32, (EXTRA, width), 1) - 3 * lax.axis_index("au")
    return jnp.where(lane == 0, high, jnp.where(lane == 1, mid, jnp.where(lane == 2, low, 0.0))).astype(BF16)


def plus(*values):
    return sum(v.astype(F32) for v in values)


def logits_kernel(group, n_ads, rows, inv, *refs):
    n = NX * NZ
    steps = n // 2
    chunks = rows // T
    first_call = group == "near"
    last_call = group == "mid"
    if first_call:
        user_refs, refs = refs[:USER_PARTS], refs[USER_PARTS:]
    else:
        (users_t,), refs = refs[:1], refs[1:]
    ads_refs, refs = refs[:n_ads], refs[n_ads:]
    (logc_ref, pos_ref), refs = refs[:2], refs[2:]
    if not first_call:
        (acc_in, m_in, total_in, hit_in), refs = refs[:4], refs[4:]
    (p_ref, top_ref, ads_t, acc_ref, m_ref, total_ref, hit_ref), refs = refs[:7], refs[7:]
    if first_call:
        (staged, users_t), refs = refs[:2], refs[2:]
    if last_call:
        (stats_ref,), refs = refs[:1], refs[1:]
    ads_all, logc_all, s0, s1, late = refs
    step = pl.program_id(0)

    @pl.when(step == 0)
    def _():
        if first_call:
            stage_users(user_refs, staged, inv)
            for b in range(n):
                users_t[:, b * T : (b + 1) * T] = staged[b * T : (b + 1) * T, :].T
        spot = 0
        for r in ads_refs:
            ads_all[spot : spot + r.shape[0], :] = r[...]
            spot += r.shape[0]
        for c in range(chunks):
            part = slice(c * T, (c + 1) * T)
            ads_t[:, part] = ads_all[part, :].T
            logc = logc_ref[:, pl.ds(first_row(group, c), T)]
            logc_all[part, :] = jnp.broadcast_to(logc, (LANES, T)).T

    def product(tile, dst):
        cols = pl.ds(pl.multiple_of(tile * T, T), T)
        side = users_t[:, cols]
        pos = pos_ref[:, cols] - lax.broadcasted_iota(jnp.int32, (8, T), 0)
        best = jnp.full((8, T), -jnp.inf, F32)
        found = jnp.zeros((8, T), F32)
        for c in range(chunks):
            ahead = pos - first_row(group, c)
            prod = jnp.dot(ads_all[c * T : (c + 1) * T, :], side, preferred_element_type=F32)
            for r in range(0, T, 8):
                row = c * T + r
                logc = logc_all[row : row + 8, :]
                x = prod[r : r + 8, :] - jnp.concatenate([logc] * (T // LANES), axis=1)
                dst[row : row + 8, :] = x
                best = jnp.maximum(best, x)
                found = jnp.where(ahead == r, x, found)
        top_ref[:, cols] = jnp.max(best, axis=0, keepdims=True)
        hit = jnp.sum(found, axis=0, keepdims=True)
        hit_ref[:, cols] = hit if first_call else hit + hit_in[:, cols]

    def exps(tile, src, half, extra):
        cols = pl.ds(pl.multiple_of(tile * T, T), T)
        top = top_ref[:, cols]
        total = jnp.zeros((8, T), F32)
        for r in range(0, rows, 16):
            e = jnp.exp(src[r : r + 16, :] - top)
            total += e[:8] + e[8:]
            e = e.astype(BF16)
            p_ref[r : r + 16, half * T : (half + 1) * T] = e
            if extra is not None:
                extra[r : r + 16, :] = e
        total = jnp.sum(total, axis=0, keepdims=True)
        if first_call:
            m_ref[:, cols] = top
            total_ref[:, cols] = total
        else:
            m = jnp.maximum(m_in[:, cols], top)
            m_ref[:, cols] = m
            total_ref[:, cols] = total_in[:, cols] * jnp.exp(m_in[:, cols] - m) + total * jnp.exp(top - m)

    def gather(tile, e):
        cols = pl.ds(pl.multiple_of(tile * T, T), T)
        new = jnp.dot(ads_t[...], e, preferred_element_type=F32)
        if first_call:
            acc_ref[:, cols] = new
        else:
            m = m_ref[:, cols]
            acc_ref[:, cols] = acc_in[:, cols] * jnp.exp(m_in[:, cols] - m) + new * jnp.exp(top_ref[:, cols] - m)

    @pl.when(step == 0)
    def _():
        product(0, s0)
        late[...] = jnp.zeros_like(late)

    first = 2 * step
    gather(jnp.maximum(first - 1, 0), late[...])
    product(first + 1, s1)
    exps(first, s0, 0, None)
    gather(first, p_ref[:, :T])
    product(jnp.minimum(first + 2, n - 1), s0)
    exps(first + 1, s1, 1, late)

    @pl.when(step == steps - 1)
    def _():
        gather(n - 1, late[...])
        if last_call:
            lse = m_ref[...] + jnp.log(total_ref[...])
            width = n * T // LANES
            for r in range(width):
                cols = slice(r * LANES, (r + 1) * LANES)
                stats_ref[r : r + 1, :] = lse[:, cols]
                stats_ref[width + r : width + r + 1, :] = hit_ref[:, cols]


def cost(rows, total, width):
    return pl.CostEstimate(flops=rows * total * width // 8, bytes_accessed=rows * total // 8, transcendentals=0)


def run_logits(group, users, ads, logc, positives, inv, before=()):
    width = ads[0].shape[1]
    count = sum(x.shape[0] for x in ads)
    total = NX * NZ * T
    stats_rows = 2 * total // LANES
    row = jax.ShapeDtypeStruct((1, total), F32)
    out_shape = [
        jax.ShapeDtypeStruct((count, total), BF16),
        row,
        jax.ShapeDtypeStruct((width, count), BF16),
        jax.ShapeDtypeStruct((width, total), F32),
        row,
        row,
        row,
    ]
    if group == "near":
        out_shape.append(jax.ShapeDtypeStruct((total, width), BF16))
        out_shape.append(jax.ShapeDtypeStruct((width, total), BF16))
    if group == "mid":
        out_shape.append(jax.ShapeDtypeStruct((stats_rows, LANES), F32))
    out_specs = [whole(x.shape) for x in out_shape]
    out_specs[0] = pl.BlockSpec((count, 2 * T), lambda i: (0, i))
    args = (*users, *ads, logc, positives, *before)
    return pl.pallas_call(
        lambda *refs: logits_kernel(group, len(ads), count, inv, *refs),
        grid=(total // (2 * T),),
        in_specs=[whole(x.shape) for x in args],
        out_specs=out_specs,
        out_shape=out_shape,
        scratch_shapes=[
            pltpu.VMEM((count, width), BF16),
            pltpu.VMEM((count, LANES), F32),
            pltpu.VMEM((count, T), F32),
            pltpu.VMEM((count, T), F32),
            pltpu.VMEM((count, T), BF16),
        ],
        compiler_params=params(),
        cost_estimate=cost(count, total, width),
        name="logits_" + group,
    )(*args)


GROUPS = ("near", "far", "mid")


def rows_kernel(sizes, start, *refs):
    ads_refs, (pos_ref, out_ref, h0, h1) = refs[: len(sizes)], refs[len(sizes) :]
    step = pl.program_id(0)
    steps = out_ref.shape[1] // (2 * T)

    def build(tile, dst):
        cols = pl.ds(pl.multiple_of(start + tile * T, T), T)
        pos = pos_ref[:, cols] - lax.broadcasted_iota(jnp.int32, (16, T), 0)
        spot = 0
        for group, size in zip(GROUPS, sizes):
            for c in range(size // T):
                ahead = pos - first_row(group, c)
                for r in range(0, T, 16):
                    dst[spot + r : spot + r + 16, :] = jnp.where(ahead == r, 1.0, 0.0).astype(BF16)
                spot += T

    def product(tile, src):
        cols = pl.ds(pl.multiple_of(tile * T, T), T)
        out = jnp.zeros((out_ref.shape[0], T), F32)
        spot = 0
        for ads, size in zip(ads_refs, sizes):
            out += jnp.dot(ads[...], src[spot : spot + size, :], preferred_element_type=F32)
            spot += size
        out_ref[:, cols] = out.astype(BF16)

    @pl.when(step == 0)
    def _():
        h1[...] = jnp.zeros_like(h1)

    first = 2 * step
    product(jnp.maximum(first - 1, 0), h1)
    build(first, h0)
    product(first, h0)
    build(first + 1, h1)

    @pl.when(step == steps - 1)
    def _():
        product(first + 1, h1)


def run_rows(ads_t, positives, start, total):
    width = ads_t[0].shape[0]
    sizes = [x.shape[1] for x in ads_t]
    args = (*ads_t, positives)
    return pl.pallas_call(
        lambda *refs: rows_kernel(sizes, start, *refs),
        grid=(total // (2 * T),),
        in_specs=[whole(x.shape) for x in args],
        out_specs=whole((width, total)),
        out_shape=jax.ShapeDtypeStruct((width, total), BF16),
        scratch_shapes=[pltpu.VMEM((sum(sizes), T), BF16)] * 2,
        compiler_params=params(),
        cost_estimate=cost(sum(sizes), total, width),
        name="positive_rows",
    )(*args)


def users_kernel(inv, acc_ref, m_ref, rows_a, rows_b, hit_ref, weight_ref, *rest):
    stats_in, rest = rest[:NX], rest[NX:]
    du_refs, (lse_ref, coef_ref, loss_ref, stats_ref, rows_ref) = rest[:USER_PARTS], rest[USER_PARTS:]
    n = NX * NZ
    width = n * T // LANES
    for j in range(NX):
        stats_ref[pl.ds(lax.rem(lax.axis_index("aa") // NZ + NX - j, NX), 1)] = stats_in[j][...][None]
    rows_ref[:, : n * T // 2] = rows_a[...]
    rows_ref[:, n * T // 2 :] = rows_b[...]
    tops = stats_ref[:, :width, :]
    top = jnp.max(tops, axis=0)
    lse = top + jnp.log(jnp.sum(jnp.exp(tops - top[None]), axis=0))
    diff = lse - jnp.sum(stats_ref[:, width:, :], axis=0)
    loss = jnp.zeros((1, LANES), F32)
    for r in range(width):
        cols = slice(r * LANES, (r + 1) * LANES)
        lse_ref[:, cols] = lse[r : r + 1, :]
        loss += weight_ref[:, cols] * diff[r : r + 1, :]
    loss_ref[...] = loss_rows(jnp.sum(loss, axis=1, keepdims=True), loss_ref.shape[1])
    coef_ref[...] = weight_ref[...] * (jnp.exp(hit_ref[...] - lse_ref[...]) - 1.0)

    def users_at(j, zr):
        cols = pl.ds(pl.multiple_of(user_block((NX - j) % NX, zr) * T, T), T)
        weight = weight_ref[:, cols] * inv
        scale = weight * jnp.exp(m_ref[:, cols] - lse_ref[:, cols])
        return (acc_ref[:, cols] * scale - rows_ref[:, cols].astype(F32) * weight).astype(BF16)

    for part, j in enumerate((0, 1, 3)):
        for zr in range(NZ):
            du_refs[part][zr * T : (zr + 1) * T, :] = users_at(j, zr)
    du_refs[3][...] = users_at(2, 0)
    du_refs[4][...] = users_at(2, 1)


def run_users(acc, m, rows_a, rows_b, hits, weights, stats, inv):
    width, total = acc.shape
    row = jax.ShapeDtypeStruct((1, total), F32)
    shapes = [(NZ * width, T)] * 3 + [(width, T)] * 2
    out_shape = [jax.ShapeDtypeStruct(x, BF16) for x in shapes]
    out_shape += [row, row, jax.ShapeDtypeStruct((EXTRA, width), BF16)]
    args = (acc, m, rows_a, rows_b, hits, weights, *stats)
    return pl.pallas_call(
        lambda *refs: users_kernel(inv, *refs),
        grid=(1,),
        in_specs=[whole(x.shape) for x in args],
        out_specs=[whole(x.shape) for x in out_shape],
        out_shape=out_shape,
        scratch_shapes=[pltpu.VMEM((NX, *stats[0].shape), F32), pltpu.VMEM((width, total), BF16)],
        compiler_params=params(),
        name="grad_users",
    )(*args)


def grads_kernel(group, steps, users_ref, p_ref, top_ref, lse_ref, coef_ref, weight_ref, pos_ref, loss_in, *refs):
    if group == "mid":
        near_ref, far_ref, da_ref, q0, q1, scale_row = refs
    else:
        da_ref, q0, q1, scale_row = refs
    step = pl.program_id(0)
    deep = 2 * T
    total = p_ref.shape[1]

    @pl.when(step == 0)
    def _():
        scale_row[...] = weight_ref[...] * jnp.exp(top_ref[...] - lse_ref[...])
        q1[...] = jnp.zeros_like(q1)

    def build(half, dst):
        base = first_row(group, 2 * step + half)
        for b in range(total // T):
            cols = slice(b * T, (b + 1) * T)
            ahead = pos_ref[:, cols] - base - lax.broadcasted_iota(jnp.int32, (16, T), 0)
            scale, coef = scale_row[:, cols], coef_ref[:, cols]
            for r in range(0, T, 16):
                scaled = p_ref[half * T + r : half * T + r + 16, cols].astype(F32) * scale
                dst[r : r + 16, cols] = jnp.where(ahead == r, coef, scaled).astype(BF16)

    def product(chunk, src):
        da = jnp.dot(src[...], users_ref[...], preferred_element_type=F32)
        da_ref[pl.ds(pl.multiple_of(chunk * T, T), T), :] = da.astype(BF16)

    first = 2 * step
    product(jnp.maximum(first - 1, 0), q1)
    build(0, q0)
    product(first, q0)
    build(1, q1)

    @pl.when(step == steps - 1)
    def _():
        product(first + 1, q1)
        if group == "mid":
            near_ref[...] = da_ref[:deep, :]
            far_ref[:deep, :] = da_ref[deep:, :]
            far_ref[deep:, :] = loss_in[...]


def run_grads(group, users, p, top, lse, coefs, weights, positives, loss):
    count, total = p.shape
    width = users.shape[1]
    deep = 2 * T
    steps = count // deep
    args = (users, p, top, lse, coefs, weights, positives, loss)
    in_specs = [whole(x.shape) for x in args]
    in_specs[1] = pl.BlockSpec((deep, total), lambda i: (i, 0))
    da = pltpu.VMEM((count, width), BF16)
    scratch = [pltpu.VMEM((T, total), BF16)] * 2 + [pltpu.VMEM((1, total), F32)]
    shapes = [(deep, width), (deep + EXTRA, width)] if group == "mid" else [(count, width)]
    return pl.pallas_call(
        lambda *refs: grads_kernel(group, steps, *refs),
        grid=(steps,),
        in_specs=in_specs,
        out_specs=[whole(x) for x in shapes],
        out_shape=[jax.ShapeDtypeStruct(x, BF16) for x in shapes],
        scratch_shapes=([da] if group == "mid" else []) + scratch,
        compiler_params=params(),
        cost_estimate=cost(count, total, width),
        name="grads_" + group,
    )(*args)


def simple_call(kernel, name, out_shape, *args):
    return pl.pallas_call(
        kernel,
        in_specs=[whole(x.shape) for x in args],
        out_specs=[whole(x.shape) for x in out_shape],
        out_shape=out_shape,
        grid=(1,),
        compiler_params=params(),
        name=name,
    )(*args)


def add_mid(near, loss, back):
    width = near.shape[1]

    def kernel(near_ref, loss_ref, back_ref, first, second, both_ref):
        both = plus(loss_ref[...], back_ref[NZ * T :, :]).astype(BF16)
        first[:T, :] = plus(near_ref[:T, :], back_ref[:T, :]).astype(BF16)
        first[T:, :] = both
        second[...] = plus(near_ref[T:, :], back_ref[T : NZ * T, :]).astype(BF16)
        both_ref[...] = both

    shapes = [(T + EXTRA, width), (T, width), (EXTRA, width)]
    shapes = [jax.ShapeDtypeStruct(x, BF16) for x in shapes]
    return simple_call(kernel, "add_mid", shapes, near, loss, back)


def add_near(near, back, both, first, second):
    width = near.shape[1]
    rows = NZ * T

    def kernel(near_ref, back_ref, both_ref, first_ref, second_ref, keep, one, three):
        total = plus(near_ref[...], back_ref[...])
        keep[:rows, :] = total[:rows]
        keep[rows:, :] = both_ref[...].astype(F32)
        one[:T, :] = plus(total[rows : rows + T], first_ref[:T, :]).astype(BF16)
        one[T:rows, :] = total[rows + T : 2 * rows].astype(BF16)
        one[rows:, :] = plus(both_ref[...], first_ref[T:, :]).astype(BF16)
        three[:T, :] = total[2 * rows : 2 * rows + T].astype(BF16)
        three[T:rows, :] = plus(total[2 * rows + T :], second_ref[...]).astype(BF16)
        three[rows:, :] = both_ref[...]

    shape = jax.ShapeDtypeStruct((rows + EXTRA, width), BF16)
    shapes = [jax.ShapeDtypeStruct((rows + EXTRA, width), F32), shape, shape]
    return simple_call(kernel, "add_near", shapes, near, back, both, first, second)


def add_rows(*parts):
    width = parts[0].shape[1]

    def kernel(*refs):
        ins, (keep, send) = refs[:3], refs[3:]
        loss = plus(*(r[NZ * T :, :] for r in ins))
        keep[:T, :] = plus(*(r[:T, :] for r in ins))
        keep[T:, :] = loss
        send[:T, :] = plus(*(r[T : NZ * T, :] for r in ins)).astype(BF16)
        send[T:, :] = loss.astype(BF16)

    shapes = [jax.ShapeDtypeStruct((T + EXTRA, width), F32), jax.ShapeDtypeStruct((T + EXTRA, width), BF16)]
    return simple_call(kernel, "add_rows", shapes, *parts)


def add_halves(one, three, first, second):
    half = one.shape[0] // NZ

    def kernel(one_ref, three_ref, first_ref, second_ref, out1, out3):
        out1[:half, :] = (one_ref[:half, :].astype(F32) + first_ref[...].astype(F32)).astype(BF16)
        out1[half:, :] = one_ref[half:, :]
        out3[:half, :] = three_ref[:half, :]
        out3[half:, :] = (three_ref[half:, :].astype(F32) + second_ref[...].astype(F32)).astype(BF16)

    shapes = [jax.ShapeDtypeStruct(one.shape, BF16)] * 2
    return simple_call(kernel, "add_halves", shapes, one, three, first, second)


def add_users(parts):
    width = parts[0].shape[0] // NZ

    def kernel(*refs):
        ins, (keep, send) = refs[:-2], refs[-2:]
        keep[...] = sum(r[:width, :].astype(F32) for r in ins)
        send[...] = sum(r[width:, :].astype(F32) for r in ins).astype(BF16)

    shapes = [jax.ShapeDtypeStruct((width, T), F32), jax.ShapeDtypeStruct((width, T), BF16)]
    return simple_call(kernel, "add_users", shapes, *parts)


def finish(keep_u, received_u, keep, received):
    def kernel(keep_u_ref, received_u_ref, keep_ref, received_ref, grad_u, grad, loss):
        grad_u[...] = plus(keep_u_ref[...], received_u_ref[...]).T
        grad[...] = plus(keep_ref[:T, :], received_ref[:T, :])
        loss[...] = jnp.sum(plus(keep_ref[T : T + 1, :], received_ref[T : T + 1, :]), axis=1, keepdims=True)

    shapes = [(T, keep_u.shape[0]), (T, keep.shape[1]), (1, 1)]
    shapes = [jax.ShapeDtypeStruct(x, F32) for x in shapes]
    return simple_call(kernel, "finish", shapes, keep_u, received_u, keep, received)


def join_stats(own, other):
    half = own.shape[0] // 2

    def kernel(own_ref, other_ref, out_ref):
        a, b = own_ref[:half, :], other_ref[:half, :]
        top = jnp.maximum(a, b)
        out_ref[:half, :] = top + jnp.log(jnp.exp(a - top) + jnp.exp(b - top))
        out_ref[half:, :] = own_ref[half:, :] + other_ref[half:, :]

    return simple_call(kernel, "join_stats", [jax.ShapeDtypeStruct(own.shape, F32)], own, other)[0]


def move(x, axis, target):
    return lax.ppermute(x, axis, [(i, target(i)) for i in range(lax.axis_size(axis))])


def shift_x(x, j):
    return move(x, "aa", lambda i: (i + j * NZ) % (NX * NZ))


def swap_z_hi(x):
    return move(x, "aa", lambda i: i ^ 1)


def shift_y(x, k):
    return move(x, "au", lambda i: i // 8 * 8 + (i % 8 + k * NC) % 8)


def swap_core(x):
    return move(x, "au", lambda i: i ^ 1)


def swap_z_lo(x):
    return move(x, "au", lambda i: i ^ 8)


def local(users, ads, counts, positives, weights):
    inv = users.shape[1] ** (-0.5)
    pos_row = (positives - lax.axis_index("aa") * counts.shape[0])[None, :]
    logc = jnp.log(counts.astype(F32))[None, :]
    weight_row = weights[None, :]
    users_z, ads_z, pos_row, logc = lax.optimization_barrier((swap_z_hi(users), swap_z_lo(ads), pos_row, logc))
    user_pair = jnp.concatenate([users, users_z], axis=0)
    ads_pair = jnp.concatenate([ads, ads_z], axis=0)
    user_1, user_3, ads_1, ads_3 = lax.optimization_barrier(
        (shift_x(user_pair, 1), shift_x(user_pair, -1), shift_y(ads_pair, 1), shift_y(ads_pair, -1))
    )
    user_2a, user_2b = shift_x(user_1[:T], 1), shift_x(user_3[T:], -1)
    ads_2a, ads_2b = shift_y(ads_1[:T], 1), shift_y(ads_3[T:], -1)
    near = jnp.concatenate([ads_pair, ads_1, ads_3], axis=0)
    far = swap_core(near)
    parts = (user_pair, user_1, user_3, user_2a, user_2b)

    p_near, top_near, at_near, acc, m, total, hits, staged, users_t = run_logits(
        "near", parts, (near,), logc, pos_row, inv
    )
    ads_2a, ads_2b, hits = lax.optimization_barrier((ads_2a, ads_2b, hits))
    near_2 = jnp.concatenate([ads_2a, ads_2b], axis=0)
    far_2 = swap_core(near_2)
    p_far, top_far, at_far, acc, m, total, hits = run_logits(
        "far", (users_t,), (far,), logc, pos_row, inv, (acc, m, total, hits)
    )
    p_mid, top_mid, at_mid, acc, m, total, hits, stats = run_logits(
        "mid", (users_t,), (near_2, far_2), logc, pos_row, inv, (acc, m, total, hits)
    )
    half = stats.shape[0] * LANES // 4
    ads_t = (at_near, at_far, at_mid)
    stats_z, rows_a = lax.optimization_barrier((swap_z_hi(stats), run_rows(ads_t, pos_row, 0, half)))
    stats = join_stats(stats, stats_z)
    moved = tuple(shift_x(stats, j) for j in range(1, NX))
    moved, rows_b = lax.optimization_barrier((moved, run_rows(ads_t, pos_row, half, half)))
    du_0, du_1, du_3, du_2a, du_2b, lse, coefs, loss = run_users(
        acc, m, rows_a, rows_b, hits, weight_row, (stats, *moved), inv
    )
    tail = (lse, coefs, weight_row, pos_row, loss)
    du_2a, du_2b = shift_x(du_2a, 1), shift_x(du_2b, -1)
    da_2, pay_2 = run_grads("mid", staged, p_mid, top_mid, *tail)
    back_2 = swap_core(pay_2)
    da_2, staged = lax.optimization_barrier((da_2, staged))
    (da_far,) = run_grads("far", staged, p_far, top_far, *tail)
    da_far, back_2, du_2a, du_2b = lax.optimization_barrier((da_far, back_2, du_2a, du_2b))
    du_1, du_3 = add_halves(du_1, du_3, du_2a, du_2b)
    back = swap_core(da_far)
    first, second, both = add_mid(da_2, loss, back_2)
    first, second, du_1, du_3, staged = lax.optimization_barrier((first, second, du_1, du_3, staged))
    first, second = shift_y(first, -1), shift_y(second, 1)
    du_1, du_3 = shift_x(du_1, 1), shift_x(du_3, -1)
    (da_near,) = run_grads("near", staged, p_near, top_near, *tail)
    da_near, first, second = lax.optimization_barrier((da_near, first, second))
    kept, one, three = add_near(da_near, back, both, first, second)
    one, three = shift_y(one, -1), shift_y(three, 1)
    keep_u, send_u = add_users((du_0, du_1, du_3))
    one, three, received_u = lax.optimization_barrier((one, three, swap_z_hi(send_u)))
    keep, send = add_rows(kept, one, three)
    grad_users, grad_ads, loss = finish(keep_u, received_u, keep, swap_z_lo(send))
    return grad_users, grad_ads, loss.reshape(())


def solution(mesh):
    return jax.shard_map(
        local,
        mesh=mesh,
        in_specs=(P(("au", "aa"), None), P(("aa", "au"), None), P("aa"), P("au"), P("au")),
        out_specs=(P(("au", "aa"), None), P(("aa", "au"), None), P()),
        check_vma=False,
    )
```

time: 408 us -> 105 us (0.26)
  blocking collectives: 124 us -> 0 us
  waiting for transfers between devices: 148 us -> 28.2 us
  matrix products: 97.5 us -> 0 us
  Pallas kernels: 0 us -> 39 us
  starting transfers between devices: 0.16 us -> 33.3 us
  other arithmetic: 19.5 us -> 1.43 us
  between operations: 13.9 us -> 0.92 us
    psum x2 -> x0, blocking collectives: 100 us -> none  [the longest x1 63.3 us: local(): loss = lax.psum(jnp.sum(own_terms), ('au', 'aa'))]
    dot_general x32 -> x0, matrix products: 97.5 us -> none  [the longest x16 46.4 us: piece_logits(): jnp.einsum('re,ce->rc', block_users, piece, preferred_element_type=jnp.fl...]
    all_gather x2 -> x0, waiting for transfers between devices: 83.6 us -> none  [the longest x1 49.3 us: local(): user_rows = lax.all_gather(users, 'aa', axis=0, tiled=True)]
    reduce_scatter x2 -> x0, waiting for transfers between devices: 63.3 us -> none  [the longest x1 63 us: local(): lax.psum_scatter(grad_cols.astype(jnp.bfloat16), 'au', scatter_dimension=...]
    pallas_call x0 -> x16, Pallas kernels: none -> 39 us  [the longest x3 21.7 us: run_logits(): pl.pallas_call(lambda *refs: logits_kernel(group, len(ads), count, inv, *...]
    ppermute x0 -> x28, starting transfers between devices: none -> 33.3 us  [move(): lax.ppermute(x, axis, [(i, target(i)) for i in range(lax.axis_size(axis))])]
    ppermute x0 -> x28, waiting for transfers between devices: none -> 28.2 us  [move(): lax.ppermute(x, axis, [(i, target(i)) for i in range(lax.axis_size(axis))])]
    pmax x1 -> x0, blocking collectives: 24.3 us -> none  [local(): row_top = lax.pmax(local_top, 'aa')]
  transfers between devices with their start and end apart: 4 -> 28, of which waited for: 4 -> 16; matrix products, arithmetic and copies ran while one was open for 2% -> 3% of each run, Pallas kernels for 0% -> 27%
where the time goes in v3:
time: 105 us
  Pallas kernels  39 us (37%)
  starting transfers between devices  33.3 us (32%)
  waiting for transfers between devices  28.2 us (27%)
  local copies, waits for them, and re-layouts  1.97 us (2%)
  other arithmetic  1.43 us (1%)
    ppermute x28, starting transfers between devices, move(): lax.ppermute(x, axis, [(i, target(i)) for i in range(lax.axis_size(axis))])  33.3 us
    ppermute x28, waiting for transfers between devices, move(): lax.ppermute(x, axis, [(i, target(i)) for i in range(lax.axis_size(axis))])  28.2 us
    pallas_call x3, Pallas kernels, run_logits(): pl.pallas_call(lambda *refs: logits_kernel(group, len(ads), count, inv, *...  21.7 us
    pallas_call x3, Pallas kernels, run_grads(): pl.pallas_call(lambda *refs: grads_kernel(group, steps, *refs), grid=(ste...  8.34 us
    pallas_call x2, Pallas kernels, run_rows(): pl.pallas_call(lambda *refs: rows_kernel(sizes, start, *refs), grid=(tota...  6.85 us
  transfers between devices with their start and end apart: 28, of which 16 were waited for; matrix products, arithmetic and copies ran while one was open for 3% of the time, Pallas kernels for 27%

profile of v3, /device:TPU:0, one launch (start us, length us, event | category | flops | bytes accessed | tf_op | source)
XLA Modules:
  0.0 104.8 jit_solution(4941072470042230642)
XLA Ops:
  0.6 4.0 %collective-permute-start = (bf16[256,256]{1,0:T(8,128)(2,1)}, bf16[256,256]{1,0:T(8,128)(2,1)S(1)}, u32[]{:S(2)}, u32[]{:S(2)}) collective-permute-start(bf16[256,256]{1,0:T(8,128)(2,1)} %param.5), channel_id=1, source_target_pairs={{0,1},{1,0},{2,3},{3,2},{4,5},{5,4},{6,7},{7,6},{8,9},{9,8},{10,11... | collective-permute-start | bytes 393224 | tf_op jit(solution)/shard_map/ppermute | solution.py:519
  4.7 1.0 collective-permute-start.1
  9.2 2.7 %collective-permute-done.1 = bf16[256,256]{1,0:T(8,128)(2,1)S(1)} collective-permute-done((bf16[256,256]{1,0:T(8,128)(2,1)}, bf16[256,256]{1,0:T(8,128)(2,1)S(1)}, u32[]{:S(2)}, u32[]{:S(2)}) %collective-permute-start.1) | collective-permute-done | bytes 131104 | tf_op jit(solution)/shard_map/ppermute | solution.py:519
  11.9 2.8 %collective-permute-start.3 = (bf16[512,256]{1,0:T(8,128)(2,1)S(1)}, bf16[512,256]{1,0:T(8,128)(2,1)S(1)}, u32[]{:S(2)}, u32[]{:S(2)}) collective-permute-start(bf16[512,256]{1,0:T(8,128)(2,1)S(1)} %constant_dynamic-update-slice_fusion.refs_0_), channel_id=1, source_target_pairs={{0,6},{1,7},{2,0},{3,1},{4,2},{5,3},{6,4},{7,5},{8,14},{9,15},{10,... | collective-permute-start | bytes 786440 | tf_op jit(solution)/shard_map/ppermute | solution.py:519
  14.8 3.1 %collective-permute-start.5 = (bf16[512,256]{1,0:T(8,128)(2,1)S(1)}, bf16[512,256]{1,0:T(8,128)(2,1)S(1)}, u32[]{:S(2)}, u32[]{:S(2)}) collective-permute-start(bf16[512,256]{1,0:T(8,128)(2,1)S(1)} %get-tuple-element.168), channel_id=1, source_target_pairs={{0,48},{8,56},{16,0},{24,8},{32,16},{40,24},{48,32},{56,40},{64,11... | collective-permute-start | bytes 786440 | tf_op jit(solution)/shard_map/ppermute | solution.py:519
  17.9 1.6 %collective-permute-done.3.refs_2_ = bf16[512,256]{1,0:T(8,128)(2,1)S(1)} collective-permute-done((bf16[512,256]{1,0:T(8,128)(2,1)S(1)}, bf16[512,256]{1,0:T(8,128)(2,1)S(1)}, u32[]{:S(2)}, u32[]{:S(2)}) %collective-permute-start.3) | collective-permute-done | bytes 262176 | tf_op jit(solution)/shard_map/ppermute | solution.py:519
  19.5 3.4 %collective-permute-done.2.refs_1_ = bf16[512,256]{1,0:T(8,128)(2,1)S(1)} collective-permute-done((bf16[512,256]{1,0:T(8,128)(2,1)S(1)}, bf16[512,256]{1,0:T(8,128)(2,1)S(1)}, u32[]{:S(2)}, u32[]{:S(2)}) %collective-permute-start.2) | collective-permute-done | bytes 262176 | tf_op jit(solution)/shard_map/ppermute | solution.py:519
  22.9 2.8 %collective-permute-done.4 = bf16[512,256]{1,0:T(8,128)(2,1)S(1)} collective-permute-done((bf16[512,256]{1,0:T(8,128)(2,1)S(1)}, bf16[512,256]{1,0:T(8,128)(2,1)S(1)}, u32[]{:S(2)}, u32[]{:S(2)}) %collective-permute-start.4) | collective-permute-done | bytes 262176 | tf_op jit(solution)/shard_map/ppermute | solution.py:519
  25.9 3.1 %collective-permute-start.7 = (bf16[256,256]{1,0:T(8,128)(2,1)S(1)}, bf16[256,256]{1,0:T(8,128)(2,1)S(1)}, u32[]{:S(2)}, u32[]{:S(2)}) collective-permute-start(bf16[256,256]{1,0:T(8,128)(2,1)S(1)} %slice.13), channel_id=1, source_target_pairs={{0,6},{1,7},{2,0},{3,1},{4,2},{5,3},{6,4},{7,5},{8,14},{9,15},{10,... | collective-permute-start | bytes 393224 | tf_op jit(solution)/shard_map/ppermute | solution.py:519
  29.3 1.8 %collective-permute-start.8 = (bf16[256,256]{1,0:T(8,128)(2,1)S(1)}, bf16[256,256]{1,0:T(8,128)(2,1)S(1)}, u32[]{:S(2)}, u32[]{:S(2)}) collective-permute-start(bf16[256,256]{1,0:T(8,128)(2,1)S(1)} %slice.14), channel_id=1, source_target_pairs={{0,16},{8,24},{16,32},{24,40},{32,48},{40,56},{48,0},{56,8},{64,80... | collective-permute-start | bytes 393224 | tf_op jit(solution)/shard_map/ppermute | solution.py:519
  31.1 1.3 %collective-permute-done.7.refs_4_ = bf16[256,256]{1,0:T(8,128)(2,1)S(1)} collective-permute-done((bf16[256,256]{1,0:T(8,128)(2,1)S(1)}, bf16[256,256]{1,0:T(8,128)(2,1)S(1)}, u32[]{:S(2)}, u32[]{:S(2)}) %collective-permute-start.7) | collective-permute-done | bytes 131104 | tf_op jit(solution)/shard_map/ppermute | solution.py:519
  32.3 3.4 %collective-permute-done.6.refs_3_ = bf16[256,256]{1,0:T(8,128)(2,1)S(1)} collective-permute-done((bf16[256,256]{1,0:T(8,128)(2,1)S(1)}, bf16[256,256]{1,0:T(8,128)(2,1)S(1)}, u32[]{:S(2)}, u32[]{:S(2)}) %collective-permute-start.6) | collective-permute-done | bytes 131104 | tf_op jit(solution)/shard_map/ppermute | solution.py:519
  35.8 7.8 %logits_near.1 = (bf16[1536,2048]{1,0:T(8,128)(2,1)S(1)}, f32[1,2048]{1,0:T(1,128)S(1)}, bf16[256,1536]{1,0:T(8,128)(2,1)S(1)}, f32[256,2048]{1,0:T(8,128)S(1)},...) custom-call(bf16[512,256]{1,0:T(8,128)(2,1)S(1)} %constant_dynamic-u, ...), custom_call_target="tpu_custom_call" | custom-call | flops 100663296 | bytes 393216 | tf_op jit(solution)/shard_map/logits_near/pallas_call | solution.py:209
  43.7 7.4 %logits_far.1 = (bf16[1536,2048]{1,0:T(8,128)(2,1)S(1)}, f32[1,2048]{1,0:T(1,128)S(1)}, bf16[256,1536]{1,0:T(8,128)(2,1)S(1)}, f32[256,2048]{1,0:T(8,128)S(1)}, ...) custom-call(bf16[256,2048]{1,0:T(8,128)(2,1)S(1)} %get-tuple-element.93.refs_0_, ...), custom_call_target="tpu_custom_call" | custom-call | flops 100663296 | bytes 393216 | tf_op jit(solution)/shard_map/logits_far/pallas_call | solution.py:209
  51.2 6.5 %logits_mid.1 = (bf16[1024,2048]{1,0:T(8,128)(2,1)S(1)}, f32[1,2048]{1,0:T(1,128)S(1)}, bf16[256,1024]{1,0:T(8,128)(2,1)S(1)}, f32[256,2048]{1,0:T(8,128)S(1)}, ...) custom-call(bf16[256,2048]{1,0:T(8,128)(2,1)S(1)} %get-tuple-element.93.refs_0_, ...), custom_call_target="tpu_custom_call" | custom-call | flops 67108864 | bytes 262144 | tf_op jit(solution)/shard_map/logits_mid/pallas_call | solution.py:209
  57.6 1.2 %collective-permute-start.12 = (f32[32,128]{1,0:T(8,128)S(1)}, f32[32,128]{1,0:T(8,128)S(1)}, u32[]{:S(2)}, u32[]{:S(2)}) collective-permute-start(f32[32,128]{1,0:T(8,128)S(1)} %get-tuple-element.107.own_ref), channel_id=1, source_target_pairs={{0,1},{1,0},{2,3},{3,2},{4,5},{5,4},{6,7},{7,6},{8,9},{9,8},{10,11... | collective-permute-start | bytes 49160 | tf_op jit(solution)/shard_map/ppermute | solution.py:519
  58.8 3.4 %positive_rows.2.refs_2_ = bf16[256,1024]{1,0:T(8,128)(2,1)S(1)} custom-call(bf16[256,1536]{1,0:T(8,128)(2,1)S(1)} %get-tuple-element.108.refs_0_, bf16[256,1536]{1,0:T(8,128)(2,1)S(1)} %get-tuple-element.109.refs_1_, bf16[256,1024]{1,0:T(8,128)(2,1)S(1)} %get-tuple-element.110.refs_2_, s32[1,2048]{1,0:T(1,128)S(1)} %bitcast.7), custom_call_target="tpu_custom_call" | custom-call | flops 134217728 | bytes 524288 | tf_op jit(solution)/shard_map/positive_rows/pallas_call | solution.py:275
  65.0 3.4 %positive_rows.3.refs_3_ = bf16[256,1024]{1,0:T(8,128)(2,1)S(1)} custom-call(bf16[256,1536]{1,0:T(8,128)(2,1)S(1)} %get-tuple-element.108.refs_0_, bf16[256,1536]{1,0:T(8,128)(2,1)S(1)} %get-tuple-element.109.refs_1_, bf16[256,1024]{1,0:T(8,128)(2,1)S(1)} %get-tuple-element.110.refs_2_, s32[1,2048]{1,0:T(1,128)S(1)} %bitcast.8), custom_call_target="tpu_custom_call" | custom-call | flops 134217728 | bytes 524288 | tf_op jit(solution)/shard_map/positive_rows/pallas_call | solution.py:275
  70.1 2.2 %grads_mid.1 = (bf16[512,256]{1,0:T(8,128)(2,1)S(1)}, bf16[528,256]{1,0:T(8,128)(2,1)S(1)}) custom-call(bf16[2048,256]{1,0:T(8,128)(2,1)S(1)} %get-tuple-element.145.refs_0_, bf16[1024,2048]{1,0:T(8,128)(2,1)S(1)} %get-tuple-element.120.refs_1_, f32[1,2048]{1,0:T(1,128)S(1)} %get-tuple-element.121.refs_2_, f32[1,2048]{1,0:T(1,128)S(1)} %get-tuple-element.122.refs_3_, ...), custom_call_target="tpu_custom_call" | custom-call | flops 67108864 | bytes 262144 | tf_op jit(solution)/shard_map/grads_mid/pallas_call | solution.py:395
  72.4 0.9 collective-permute-start.17
  73.4 2.4 %collective-permute-start.18 = (bf16[256,256]{1,0:T(8,128)(2,1)S(1)}, bf16[256,256]{1,0:T(8,128)(2,1)S(1)}, u32[]{:S(2)}, u32[]{:S(2)}) collective-permute-start(bf16[256,256]{1,0:T(8,128)(2,1)S(1)} %get-tuple-element.132), channel_id=1, source_target_pairs={{0,6},{1,7},{2,0},{3,1},{4,2},{5,3},{6,4},{7,5},{8,14},{9,15},{10,... | collective-permute-start | bytes 393224 | tf_op jit(solution)/shard_map/ppermute | solution.py:519
  75.7 3.1 %grads_far.1 = bf16[1536,256]{1,0:T(8,128)(2,1)S(1)} custom-call(bf16[2048,256]{1,0:T(8,128)(2,1)S(1)} %get-tuple-element.145.refs_0_, bf16[1536,2048]{1,0:T(8,128)(2,1)S(1)} %get-tuple-element.128.refs_1_, f32[1,2048]{1,0:T(1,128)S(1)} %get-tuple-element.129.refs_2_, f32[1,2048]{1,0:T(1,128)S(1)} %get-tuple-element.122.refs_3_, ...), custom_call_target="tpu_custom_call" | custom-call | flops 100663296 | bytes 393216 | tf_op jit(solution)/shard_map/grads_far/pallas_call | solution.py:395
  80.0 1.8 %collective-permute-start.22 = (bf16[256,256]{1,0:T(8,128)(2,1)S(1)}, bf16[256,256]{1,0:T(8,128)(2,1)S(1)}, u32[]{:S(2)}, u32[]{:S(2)}) collective-permute-start(bf16[256,256]{1,0:T(8,128)(2,1)S(1)} %get-tuple-element.149), channel_id=1, source_target_pairs={{0,16},{8,24},{16,32},{24,40},{32,48},{40,56},{48,0},{56,8},{64,80... | collective-permute-start | bytes 393224 | tf_op jit(solution)/shard_map/ppermute | solution.py:519
  81.8 1.7 %collective-permute-start.19 = (bf16[512,256]{1,0:T(8,128)(2,1)S(1)}, bf16[512,256]{1,0:T(8,128)(2,1)S(1)}, u32[]{:S(2)}, u32[]{:S(2)}) collective-permute-start(bf16[512,256]{1,0:T(8,128)(2,1)S(1)} %get-tuple-element.142), channel_id=1, source_target_pairs={{0,2},{1,3},{2,4},{3,5},{4,6},{5,7},{6,0},{7,1},{8,10},{9,11},{10,... | collective-permute-start | bytes 786440 | tf_op jit(solution)/shard_map/ppermute | solution.py:519
  83.5 1.6 %collective-permute-start.20 = (bf16[512,256]{1,0:T(8,128)(2,1)S(1)}, bf16[512,256]{1,0:T(8,128)(2,1)S(1)}, u32[]{:S(2)}, u32[]{:S(2)}) collective-permute-start(bf16[512,256]{1,0:T(8,128)(2,1)S(1)} %get-tuple-element.143), channel_id=1, source_target_pairs={{0,6},{1,7},{2,0},{3,1},{4,2},{5,3},{6,4},{7,5},{8,14},{9,15},{10,... | collective-permute-start | bytes 786440 | tf_op jit(solution)/shard_map/ppermute | solution.py:519
  85.0 3.0 %grads_near.1.near_ref = bf16[1536,256]{1,0:T(8,128)(2,1)S(1)} custom-call(bf16[2048,256]{1,0:T(8,128)(2,1)S(1)} %get-tuple-element.145.refs_0_, bf16[1536,2048]{1,0:T(8,128)(2,1)S(1)} %get-tuple-element.146.refs_1_, f32[1,2048]{1,0:T(1,128)S(1)} %get-tuple-element.147.refs_2_, f32[1,2048]{1,0:T(1,128)S(1)} %get-tuple-element.122.refs_3_, ...), custom_call_target="tpu_custom_call" | custom-call | flops 100663296 | bytes 393216 | tf_op jit(solution)/shard_map/grads_near/pallas_call | solution.py:395
  88.3 1.5 %collective-permute-start.24 = (bf16[528,256]{1,0:T(8,128)(2,1)S(1)}, bf16[528,256]{1,0:T(8,128)(2,1)S(1)}, u32[]{:S(2)}, u32[]{:S(2)}) collective-permute-start(bf16[528,256]{1,0:T(8,128)(2,1)S(1)} %get-tuple-element.155), channel_id=1, source_target_pairs={{0,48},{8,56},{16,0},{24,8},{32,16},{40,24},{48,32},{56,40},{64,11... | collective-permute-start | bytes 811016 | tf_op jit(solution)/shard_map/ppermute | solution.py:519
  91.5 1.8 %collective-permute-start.26 = (bf16[256,256]{1,0:T(8,128)(2,1)S(1)}, bf16[256,256]{1,0:T(8,128)(2,1)S(1)}, u32[]{:S(2)}, u32[]{:S(2)}) collective-permute-start(bf16[256,256]{1,0:T(8,128)(2,1)S(1)} %get-tuple-element.157), channel_id=1, source_target_pairs={{0,1},{1,0},{2,3},{3,2},{4,5},{5,4},{6,7},{7,6},{8,9},{9,8},{10,11... | collective-permute-start | bytes 393224 | tf_op jit(solution)/shard_map/ppermute | solution.py:519
  93.3 4.7 %collective-permute-done.26.received_u_ref = bf16[256,256]{1,0:T(8,128)(2,1)S(1)} collective-permute-done((bf16[256,256]{1,0:T(8,128)(2,1)S(1)}, bf16[256,256]{1,0:T(8,128)(2,1)S(1)}, u32[]{:S(2)}, u32[]{:S(2)}) %collective-permute-start.26) | collective-permute-done | bytes 131104 | tf_op jit(solution)/shard_map/ppermute | solution.py:519
  98.8 1.1 %collective-permute-start.27 = (bf16[272,256]{1,0:T(8,128)(2,1)S(1)}, bf16[272,256]{1,0:T(8,128)(2,1)S(1)}, u32[]{:S(2)}, u32[]{:S(2)}) collective-permute-start(bf16[272,256]{1,0:T(8,128)(2,1)S(1)} %get-tuple-element.163), channel_id=1, source_target_pairs={{0,64},{8,72},{16,80},{24,88},{32,96},{40,104},{48,112},{56,120},{... | collective-permute-start | bytes 417800 | tf_op jit(solution)/shard_map/ppermute | solution.py:519
  99.9 4.1 %collective-permute-done.27.received_ref = bf16[272,256]{1,0:T(8,128)(2,1)S(1)} collective-permute-done((bf16[272,256]{1,0:T(8,128)(2,1)S(1)}, bf16[272,256]{1,0:T(8,128)(2,1)S(1)}, u32[]{:S(2)}, u32[]{:S(2)}) %collective-permute-start.27) | collective-permute-done | bytes 139296 | tf_op jit(solution)/shard_map/ppermute | solution.py:519
  103.9 0.9 finish.1
  (56 shorter events, 12.4 us)
Async XLA Ops:
  0.6 8.6 %collective-permute-start = (bf16[256,256]{1,0:T(8,128)(2,1)}, bf16[256,256]{1,0:T(8,128)(2,1)S(1)}, u32[]{:S(2)}, u32[]{:S(2)}) collective-permute-start(bf16[256,256]{1,0:T(8,128)(2,1)} %param.5), channel_id=1, source_target_pairs={{0,1},{1,0},{2,3},{3,2},{4,5},{5,4},{6,7},{7,6},{8,9},{9,8},{10,11... | collective-permute-start | bytes 393224 | tf_op jit(solution)/shard_map/ppermute | solution.py:519
  4.7 7.2 %collective-permute-start.1 = (bf16[256,256]{1,0:T(8,128)(2,1)}, bf16[256,256]{1,0:T(8,128)(2,1)S(1)}, u32[]{:S(2)}, u32[]{:S(2)}) collective-permute-start(bf16[256,256]{1,0:T(8,128)(2,1)} %param.6), channel_id=1, source_target_pairs={{0,64},{8,72},{16,80},{24,88},{32,96},{40,104},{48,112},{56,120},{... | collective-permute-start | bytes 393224 | tf_op jit(solution)/shard_map/ppermute | solution.py:519
  11.9 7.5 %collective-permute-start.3 = (bf16[512,256]{1,0:T(8,128)(2,1)S(1)}, bf16[512,256]{1,0:T(8,128)(2,1)S(1)}, u32[]{:S(2)}, u32[]{:S(2)}) collective-permute-start(bf16[512,256]{1,0:T(8,128)(2,1)S(1)} %constant_dynamic-update-slice_fusion.refs_0_), channel_id=1, source_target_pairs={{0,6},{1,7},{2,0},{3,1},{4,2},{5,3},{6,4},{7,5},{8,14},{9,15},{10,... | collective-permute-start | bytes 786440 | tf_op jit(solution)/shard_map/ppermute | solution.py:519
  14.8 8.1 %collective-permute-start.2 = (bf16[512,256]{1,0:T(8,128)(2,1)S(1)}, bf16[512,256]{1,0:T(8,128)(2,1)S(1)}, u32[]{:S(2)}, u32[]{:S(2)}) collective-permute-start(bf16[512,256]{1,0:T(8,128)(2,1)S(1)} %constant_dynamic-update-slice_fusion.refs_0_), channel_id=1, source_target_pairs={{0,2},{1,3},{2,4},{3,5},{4,6},{5,7},{6,0},{7,1},{8,10},{9,11},{10,... | collective-permute-start | bytes 786440 | tf_op jit(solution)/shard_map/ppermute | solution.py:519
  14.8 8.1 %collective-permute-start.5 = (bf16[512,256]{1,0:T(8,128)(2,1)S(1)}, bf16[512,256]{1,0:T(8,128)(2,1)S(1)}, u32[]{:S(2)}, u32[]{:S(2)}) collective-permute-start(bf16[512,256]{1,0:T(8,128)(2,1)S(1)} %get-tuple-element.168), channel_id=1, source_target_pairs={{0,48},{8,56},{16,0},{24,8},{32,16},{40,24},{48,32},{56,40},{64,11... | collective-permute-start | bytes 786440 | tf_op jit(solution)/shard_map/ppermute | solution.py:519
  17.9 7.8 %collective-permute-start.4 = (bf16[512,256]{1,0:T(8,128)(2,1)S(1)}, bf16[512,256]{1,0:T(8,128)(2,1)S(1)}, u32[]{:S(2)}, u32[]{:S(2)}) collective-permute-start(bf16[512,256]{1,0:T(8,128)(2,1)S(1)} %get-tuple-element.168), channel_id=1, source_target_pairs={{0,16},{8,24},{16,32},{24,40},{32,48},{40,56},{48,0},{56,8},{64,80... | collective-permute-start | bytes 786440 | tf_op jit(solution)/shard_map/ppermute | solution.py:519
  25.7 17.9 %collective-permute-start.11 = (bf16[1536,256]{1,0:T(8,128)(2,1)S(1)}, bf16[1536,256]{1,0:T(8,128)(2,1)S(1)}, u32[]{:S(2)}, u32[]{:S(2)}) collective-permute-start(bf16[1536,256]{1,0:T(8,128)(2,1)S(1)} %constant_dynamic-update-slice_fusion.4.refs_5_), channel_id=1, source_target_pairs={{0,8},{8,0},{16,24},{24,16},{32,40},{40,32},{48,56},{56,48},{64,72... | collective-permute-start | bytes 2359304 | tf_op jit(solution)/shard_map/ppermute | solution.py:519
  25.9 6.5 %collective-permute-start.7 = (bf16[256,256]{1,0:T(8,128)(2,1)S(1)}, bf16[256,256]{1,0:T(8,128)(2,1)S(1)}, u32[]{:S(2)}, u32[]{:S(2)}) collective-permute-start(bf16[256,256]{1,0:T(8,128)(2,1)S(1)} %slice.13), channel_id=1, source_target_pairs={{0,6},{1,7},{2,0},{3,1},{4,2},{5,3},{6,4},{7,5},{8,14},{9,15},{10,... | collective-permute-start | bytes 393224 | tf_op jit(solution)/shard_map/ppermute | solution.py:519
  28.9 6.8 %collective-permute-start.6 = (bf16[256,256]{1,0:T(8,128)(2,1)S(1)}, bf16[256,256]{1,0:T(8,128)(2,1)S(1)}, u32[]{:S(2)}, u32[]{:S(2)}) collective-permute-start(bf16[256,256]{1,0:T(8,128)(2,1)S(1)} %slice.12), channel_id=1, source_target_pairs={{0,2},{1,3},{2,4},{3,5},{4,6},{5,7},{6,0},{7,1},{8,10},{9,11},{10,... | collective-permute-start | bytes 393224 | tf_op jit(solution)/shard_map/ppermute | solution.py:519
  29.0 14.6 %collective-permute-start.9 = (bf16[256,256]{1,0:T(8,128)(2,1)S(1)}, bf16[256,256]{1,0:T(8,128)(2,1)S(1)}, u32[]{:S(2)}, u32[]{:S(2)}) collective-permute-start(bf16[256,256]{1,0:T(8,128)(2,1)S(1)} %slice.15), channel_id=1, source_target_pairs={{0,48},{8,56},{16,0},{24,8},{32,16},{40,24},{48,32},{56,40},{64,11... | collective-permute-start | bytes 393224 | tf_op jit(solution)/shard_map/ppermute | solution.py:519
  29.3 14.3 %collective-permute-start.8 = (bf16[256,256]{1,0:T(8,128)(2,1)S(1)}, bf16[256,256]{1,0:T(8,128)(2,1)S(1)}, u32[]{:S(2)}, u32[]{:S(2)}) collective-permute-start(bf16[256,256]{1,0:T(8,128)(2,1)S(1)} %slice.14), channel_id=1, source_target_pairs={{0,16},{8,24},{16,32},{24,40},{32,48},{40,56},{48,0},{56,8},{64,80... | collective-permute-start | bytes 393224 | tf_op jit(solution)/shard_map/ppermute | solution.py:519
  43.6 7.6 %collective-permute-start.10 = (bf16[512,256]{1,0:T(8,128)(2,1)S(1)}, bf16[512,256]{1,0:T(8,128)(2,1)S(1)}, u32[]{:S(2)}, u32[]{:S(2)}) collective-permute-start(bf16[512,256]{1,0:T(8,128)(2,1)S(1)} %constant_dynamic-update-slice_fusion.8.refs_1_), channel_id=1, source_target_pairs={{0,8},{8,0},{16,24},{24,16},{32,40},{40,32},{48,56},{56,48},{64,72... | collective-permute-start | bytes 786440 | tf_op jit(solution)/shard_map/ppermute | solution.py:519
  51.2 18.2 %copy-start = (f32[2048]{0:T(1024)S(1)}, f32[2048]{0:T(1024)}, u32[]{:S(2)}) copy-start(f32[2048]{0:T(1024)} %param.9) | copy-start | bytes 24580
  57.6 5.2 %collective-permute-start.12 = (f32[32,128]{1,0:T(8,128)S(1)}, f32[32,128]{1,0:T(8,128)S(1)}, u32[]{:S(2)}, u32[]{:S(2)}) collective-permute-start(f32[32,128]{1,0:T(8,128)S(1)} %get-tuple-element.107.own_ref), channel_id=1, source_target_pairs={{0,1},{1,0},{2,3},{3,2},{4,5},{5,4},{6,7},{7,6},{8,9},{9,8},{10,11... | collective-permute-start | bytes 49160 | tf_op jit(solution)/shard_map/ppermute | solution.py:519
  62.9 5.5 %collective-permute-start.15 = (f32[32,128]{1,0:T(8,128)S(1)}, f32[32,128]{1,0:T(8,128)S(1)}, u32[]{:S(2)}, u32[]{:S(2)}) collective-permute-start(f32[32,128]{1,0:T(8,128)S(1)} %join_stats.1.refs_6_), channel_id=1, source_target_pairs={{0,6},{1,7},{2,0},{3,1},{4,2},{5,3},{6,4},{7,5},{8,14},{9,15},{10,... | collective-permute-start | bytes 49160 | tf_op jit(solution)/shard_map/ppermute | solution.py:519
  63.3 5.2 %collective-permute-start.14 = (f32[32,128]{1,0:T(8,128)S(1)}, f32[32,128]{1,0:T(8,128)S(1)}, u32[]{:S(2)}, u32[]{:S(2)}) collective-permute-start(f32[32,128]{1,0:T(8,128)S(1)} %join_stats.1.refs_6_), channel_id=1, source_target_pairs={{0,4},{1,5},{2,6},{3,7},{4,0},{5,1},{6,2},{7,3},{8,12},{9,13},{10,... | collective-permute-start | bytes 49160 | tf_op jit(solution)/shard_map/ppermute | solution.py:519
  64.1 5.3 %collective-permute-start.13 = (f32[32,128]{1,0:T(8,128)S(1)}, f32[32,128]{1,0:T(8,128)S(1)}, u32[]{:S(2)}, u32[]{:S(2)}) collective-permute-start(f32[32,128]{1,0:T(8,128)S(1)} %join_stats.1.refs_6_), channel_id=1, source_target_pairs={{0,2},{1,3},{2,4},{3,5},{4,6},{5,7},{6,0},{7,1},{8,10},{9,11},{10,... | collective-permute-start | bytes 49160 | tf_op jit(solution)/shard_map/ppermute | solution.py:519
  72.3 7.2 %collective-permute-start.16 = (bf16[528,256]{1,0:T(8,128)(2,1)S(1)}, bf16[528,256]{1,0:T(8,128)(2,1)S(1)}, u32[]{:S(2)}, u32[]{:S(2)}) collective-permute-start(bf16[528,256]{1,0:T(8,128)(2,1)S(1)} %get-tuple-element.130), channel_id=1, source_target_pairs={{0,8},{8,0},{16,24},{24,16},{32,40},{40,32},{48,56},{56,48},{64,72... | collective-permute-start | bytes 811016 | tf_op jit(solution)/shard_map/ppermute | solution.py:519
  72.4 7.1 %collective-permute-start.17 = (bf16[256,256]{1,0:T(8,128)(2,1)S(1)}, bf16[256,256]{1,0:T(8,128)(2,1)S(1)}, u32[]{:S(2)}, u32[]{:S(2)}) collective-permute-start(bf16[256,256]{1,0:T(8,128)(2,1)S(1)} %get-tuple-element.131), channel_id=1, source_target_pairs={{0,2},{1,3},{2,4},{3,5},{4,6},{5,7},{6,0},{7,1},{8,10},{9,11},{10,... | collective-permute-start | bytes 393224 | tf_op jit(solution)/shard_map/ppermute | solution.py:519
  73.4 6.2 %collective-permute-start.18 = (bf16[256,256]{1,0:T(8,128)(2,1)S(1)}, bf16[256,256]{1,0:T(8,128)(2,1)S(1)}, u32[]{:S(2)}, u32[]{:S(2)}) collective-permute-start(bf16[256,256]{1,0:T(8,128)(2,1)S(1)} %get-tuple-element.132), channel_id=1, source_target_pairs={{0,6},{1,7},{2,0},{3,1},{4,2},{5,3},{6,4},{7,5},{8,14},{9,15},{10,... | collective-permute-start | bytes 393224 | tf_op jit(solution)/shard_map/ppermute | solution.py:519
  79.5 8.6 %collective-permute-start.23 = (bf16[1536,256]{1,0:T(8,128)(2,1)S(1)}, bf16[1536,256]{1,0:T(8,128)(2,1)S(1)}, u32[]{:S(2)}, u32[]{:S(2)}) collective-permute-start(bf16[1536,256]{1,0:T(8,128)(2,1)S(1)} %grads_far.1), channel_id=1, source_target_pairs={{0,8},{8,0},{16,24},{24,16},{32,40},{40,32},{48,56},{56,48},{64,72... | collective-permute-start | bytes 2359304 | tf_op jit(solution)/shard_map/ppermute | solution.py:519
  79.7 8.4 %collective-permute-start.21 = (bf16[272,256]{1,0:T(8,128)(2,1)S(1)}, bf16[272,256]{1,0:T(8,128)(2,1)S(1)}, u32[]{:S(2)}, u32[]{:S(2)}) collective-permute-start(bf16[272,256]{1,0:T(8,128)(2,1)S(1)} %get-tuple-element.148), channel_id=1, source_target_pairs={{0,48},{8,56},{16,0},{24,8},{32,16},{40,24},{48,32},{56,40},{64,11... | collective-permute-start | bytes 417800 | tf_op jit(solution)/shard_map/ppermute | solution.py:519
  80.0 8.1 %collective-permute-start.22 = (bf16[256,256]{1,0:T(8,128)(2,1)S(1)}, bf16[256,256]{1,0:T(8,128)(2,1)S(1)}, u32[]{:S(2)}, u32[]{:S(2)}) collective-permute-start(bf16[256,256]{1,0:T(8,128)(2,1)S(1)} %get-tuple-element.149), channel_id=1, source_target_pairs={{0,16},{8,24},{16,32},{24,40},{32,48},{40,56},{48,0},{56,8},{64,80... | collective-permute-start | bytes 393224 | tf_op jit(solution)/shard_map/ppermute | solution.py:519
  81.8 9.4 %collective-permute-start.19 = (bf16[512,256]{1,0:T(8,128)(2,1)S(1)}, bf16[512,256]{1,0:T(8,128)(2,1)S(1)}, u32[]{:S(2)}, u32[]{:S(2)}) collective-permute-start(bf16[512,256]{1,0:T(8,128)(2,1)S(1)} %get-tuple-element.142), channel_id=1, source_target_pairs={{0,2},{1,3},{2,4},{3,5},{4,6},{5,7},{6,0},{7,1},{8,10},{9,11},{10,... | collective-permute-start | bytes 786440 | tf_op jit(solution)/shard_map/ppermute | solution.py:519
  83.5 7.9 %collective-permute-start.20 = (bf16[512,256]{1,0:T(8,128)(2,1)S(1)}, bf16[512,256]{1,0:T(8,128)(2,1)S(1)}, u32[]{:S(2)}, u32[]{:S(2)}) collective-permute-start(bf16[512,256]{1,0:T(8,128)(2,1)S(1)} %get-tuple-element.143), channel_id=1, source_target_pairs={{0,6},{1,7},{2,0},{3,1},{4,2},{5,3},{6,4},{7,5},{8,14},{9,15},{10,... | collective-permute-start | bytes 786440 | tf_op jit(solution)/shard_map/ppermute | solution.py:519
  88.3 9.7 %collective-permute-start.24 = (bf16[528,256]{1,0:T(8,128)(2,1)S(1)}, bf16[528,256]{1,0:T(8,128)(2,1)S(1)}, u32[]{:S(2)}, u32[]{:S(2)}) collective-permute-start(bf16[528,256]{1,0:T(8,128)(2,1)S(1)} %get-tuple-element.155), channel_id=1, source_target_pairs={{0,48},{8,56},{16,0},{24,8},{32,16},{40,24},{48,32},{56,40},{64,11... | collective-permute-start | bytes 811016 | tf_op jit(solution)/shard_map/ppermute | solution.py:519
  89.9 8.8 %collective-permute-start.25 = (bf16[528,256]{1,0:T(8,128)(2,1)S(1)}, bf16[528,256]{1,0:T(8,128)(2,1)S(1)}, u32[]{:S(2)}, u32[]{:S(2)}) collective-permute-start(bf16[528,256]{1,0:T(8,128)(2,1)S(1)} %get-tuple-element.156), channel_id=1, source_target_pairs={{0,16},{8,24},{16,32},{24,40},{32,48},{40,56},{48,0},{56,8},{64,80... | collective-permute-start | bytes 811016 | tf_op jit(solution)/shard_map/ppermute | solution.py:519
  91.5 6.6 %collective-permute-start.26 = (bf16[256,256]{1,0:T(8,128)(2,1)S(1)}, bf16[256,256]{1,0:T(8,128)(2,1)S(1)}, u32[]{:S(2)}, u32[]{:S(2)}) collective-permute-start(bf16[256,256]{1,0:T(8,128)(2,1)S(1)} %get-tuple-element.157), channel_id=1, source_target_pairs={{0,1},{1,0},{2,3},{3,2},{4,5},{5,4},{6,7},{7,6},{8,9},{9,8},{10,11... | collective-permute-start | bytes 393224 | tf_op jit(solution)/shard_map/ppermute | solution.py:519
  98.8 5.1 %collective-permute-start.27 = (bf16[272,256]{1,0:T(8,128)(2,1)S(1)}, bf16[272,256]{1,0:T(8,128)(2,1)S(1)}, u32[]{:S(2)}, u32[]{:S(2)}) collective-permute-start(bf16[272,256]{1,0:T(8,128)(2,1)S(1)} %get-tuple-element.163), channel_id=1, source_target_pairs={{0,64},{8,72},{16,80},{24,88},{32,96},{40,104},{48,112},{56,120},{... | collective-permute-start | bytes 417800 | tf_op jit(solution)/shard_map/ppermute | solution.py:519

commit v4 on v3

--- a/solution.py
+++ b/solution.py
@@ -11,15 +11,25 @@
 LANES = 128
 EXTRA = 16
 NX, NZ, NY, NC = 4, 2, 4, 2
-VMEM_LIMIT = 32 * 2**20
+VMEM_LIMIT = 24 * 2**20
 
 
 def params():
     return pltpu.CompilerParams(vmem_limit_bytes=VMEM_LIMIT)
 
 
-def whole(shape):
-    return pl.BlockSpec(shape, lambda *_: (0,) * len(shape))
+def call(kernel, name, out_shape, scratch, args, estimate=None):
+    vmem = pl.BlockSpec(memory_space=pltpu.VMEM)
+    return pl.pallas_call(
+        kernel,
+        in_specs=[vmem] * len(args),
+        out_specs=[vmem] * len(out_shape),
+        out_shape=out_shape,
+        scratch_shapes=scratch,
+        compiler_params=params(),
+        cost_estimate=estimate,
+        name=name,
+    )(*args)
 
 
 def user_block(j, zr):
@@ -86,97 +96,113 @@
         (staged, users_t), refs = refs[:2], refs[2:]
     if last_call:
         (stats_ref,), refs = refs[:1], refs[1:]
-    ads_all, logc_all, s0, s1, late = refs
-    step = pl.program_id(0)
-
-    @pl.when(step == 0)
-    def _():
-        if first_call:
-            stage_users(user_refs, staged, inv)
-            for b in range(n):
-                users_t[:, b * T : (b + 1) * T] = staged[b * T : (b + 1) * T, :].T
-        spot = 0
-        for r in ads_refs:
-            ads_all[spot : spot + r.shape[0], :] = r[...]
-            spot += r.shape[0]
-        for c in range(chunks):
-            part = slice(c * T, (c + 1) * T)
-            ads_t[:, part] = ads_all[part, :].T
-            logc = logc_ref[:, pl.ds(first_row(group, c), T)]
-            logc_all[part, :] = jnp.broadcast_to(logc, (LANES, T)).T
-
-    def product(tile, dst):
-        cols = pl.ds(pl.multiple_of(tile * T, T), T)
-        side = users_t[:, cols]
-        pos = pos_ref[:, cols] - lax.broadcasted_iota(jnp.int32, (8, T), 0)
-        best = jnp.full((8, T), -jnp.inf, F32)
-        found = jnp.zeros((8, T), F32)
-        for c in range(chunks):
-            ahead = pos - first_row(group, c)
-            prod = jnp.dot(ads_all[c * T : (c + 1) * T, :], side, preferred_element_type=F32)
+    ads_all, logc_all, s0, s1, *late = refs
+
+    if first_call:
+        stage_users(user_refs, staged, inv)
+        for b in range(n):
+            users_t[:, b * T : (b + 1) * T] = staged[b * T : (b + 1) * T, :].T
+    spot = 0
+    for r in ads_refs:
+        ads_all[spot : spot + r.shape[0], :] = r[...]
+        spot += r.shape[0]
+    for c in range(chunks):
+        part = slice(c * T, (c + 1) * T)
+        ads_t[:, part] = ads_all[part, :].T
+        logc = logc_ref[:, pl.ds(first_row(group, c), T)]
+        logc_all[part, :] = jnp.broadcast_to(logc, (LANES, T)).T
+
+    def columns(tile):
+        return pl.ds(pl.multiple_of(tile * T, T), T)
+
+    class Product:
+        def __init__(self, tile, dst):
+            self.cols, self.dst = columns(tile), dst
+            self.side = users_t[:, self.cols]
+            self.pos = pos_ref[:, self.cols] - lax.broadcasted_iota(jnp.int32, (8, T), 0)
+            self.best = jnp.full((8, T), -jnp.inf, F32)
+            self.found = jnp.zeros((8, T), F32)
+
+        def chunk(self, c):
+            ahead = self.pos - first_row(group, c)
+            prod = jnp.dot(ads_all[c * T : (c + 1) * T, :], self.side, preferred_element_type=F32)
             for r in range(0, T, 8):
                 row = c * T + r
                 logc = logc_all[row : row + 8, :]
                 x = prod[r : r + 8, :] - jnp.concatenate([logc] * (T // LANES), axis=1)
-                dst[row : row + 8, :] = x
-                best = jnp.maximum(best, x)
-                found = jnp.where(ahead == r, x, found)
-        top_ref[:, cols] = jnp.max(best, axis=0, keepdims=True)
-        hit = jnp.sum(found, axis=0, keepdims=True)
-        hit_ref[:, cols] = hit if first_call else hit + hit_in[:, cols]
-
-    def exps(tile, src, half, extra):
-        cols = pl.ds(pl.multiple_of(tile * T, T), T)
-        top = top_ref[:, cols]
-        total = jnp.zeros((8, T), F32)
-        for r in range(0, rows, 16):
-            e = jnp.exp(src[r : r + 16, :] - top)
-            total += e[:8] + e[8:]
-            e = e.astype(BF16)
-            p_ref[r : r + 16, half * T : (half + 1) * T] = e
-            if extra is not None:
-                extra[r : r + 16, :] = e
-        total = jnp.sum(total, axis=0, keepdims=True)
-        if first_call:
-            m_ref[:, cols] = top
-            total_ref[:, cols] = total
-        else:
-            m = jnp.maximum(m_in[:, cols], top)
-            m_ref[:, cols] = m
-            total_ref[:, cols] = total_in[:, cols] * jnp.exp(m_in[:, cols] - m) + total * jnp.exp(top - m)
+                self.dst[row : row + 8, :] = x
+                self.best = jnp.maximum(self.best, x)
+                self.found = jnp.where(ahead == r, x, self.found)
+
+        def end(self):
+            top_ref[:, self.cols] = jnp.max(self.best, axis=0, keepdims=True)
+            hit = jnp.sum(self.found, axis=0, keepdims=True)
+            hit_ref[:, self.cols] = hit if first_call else hit + hit_in[:, self.cols]
+
+    class Exps:
+        def __init__(self, tile, src, extra):
+            self.cols, self.src, self.extra = columns(tile), src, extra
+            self.top = top_ref[:, self.cols]
+            self.total = jnp.zeros((8, T), F32)
+
+        def chunk(self, c):
+            for r in range(c * T, (c + 1) * T, 16):
+                e = jnp.exp(self.src[r : r + 16, :] - self.top)
+                self.total += e[:8] + e[8:]
+                e = e.astype(BF16)
+                p_ref[r : r + 16, self.cols] = e
+                self.extra[r : r + 16, :] = e
+
+        def end(self):
+            cols, top = self.cols, self.top
+            total = jnp.sum(self.total, axis=0, keepdims=True)
+            if first_call:
+                m_ref[:, cols] = top
+                total_ref[:, cols] = total
+            else:
+                m = jnp.maximum(m_in[:, cols], top)
+                m_ref[:, cols] = m
+                total_ref[:, cols] = total_in[:, cols] * jnp.exp(m_in[:, cols] - m) + total * jnp.exp(top - m)
 
     def gather(tile, e):
-        cols = pl.ds(pl.multiple_of(tile * T, T), T)
-        new = jnp.dot(ads_t[...], e, preferred_element_type=F32)
+        cols = columns(tile)
+        new = jnp.dot(ads_t[...], e[...], preferred_element_type=F32)
         if first_call:
             acc_ref[:, cols] = new
         else:
             m = m_ref[:, cols]
             acc_ref[:, cols] = acc_in[:, cols] * jnp.exp(m_in[:, cols] - m) + new * jnp.exp(top_ref[:, cols] - m)
 
-    @pl.when(step == 0)
-    def _():
-        product(0, s0)
-        late[...] = jnp.zeros_like(late)
-
-    first = 2 * step
-    gather(jnp.maximum(first - 1, 0), late[...])
-    product(first + 1, s1)
-    exps(first, s0, 0, None)
-    gather(first, p_ref[:, :T])
-    product(jnp.minimum(first + 2, n - 1), s0)
-    exps(first + 1, s1, 1, late)
-
-    @pl.when(step == steps - 1)
-    def _():
-        gather(n - 1, late[...])
-        if last_call:
-            lse = m_ref[...] + jnp.log(total_ref[...])
-            width = n * T // LANES
-            for r in range(width):
-                cols = slice(r * LANES, (r + 1) * LANES)
-                stats_ref[r : r + 1, :] = lse[:, cols]
-                stats_ref[width + r : width + r + 1, :] = hit_ref[:, cols]
+    def turn(tile, src, dst, e_now, e_before):
+        gather(jnp.maximum(tile - 1, 0), e_before)
+        product, exps = Product(jnp.minimum(tile + 1, n - 1), dst), Exps(tile, src, e_now)
+        for c in range(chunks):
+            product.chunk(c)
+            exps.chunk(c)
+        product.end()
+        exps.end()
+
+    opening = Product(0, s0)
+    for c in range(chunks):
+        opening.chunk(c)
+    opening.end()
+    e0, e1 = late
+    e1[...] = jnp.zeros_like(e1)
+    m_ref[...] = jnp.zeros_like(m_ref) if first_call else m_in[...]
+
+    @pl.loop(0, steps)
+    def _(step):
+        turn(2 * step, s0, s1, e0, e1)
+        turn(2 * step + 1, s1, s0, e1, e0)
+
+    gather(n - 1, e1)
+    if last_call:
+        lse = m_ref[...] + jnp.log(total_ref[...])
+        width = n * T // LANES
+        for r in range(width):
+            cols = slice(r * LANES, (r + 1) * LANES)
+            stats_ref[r : r + 1, :] = lse[:, cols]
+            stats_ref[width + r : width + r + 1, :] = hit_ref[:, cols]
 
 
 def cost(rows, total, width):
@@ -203,26 +229,22 @@
         out_shape.append(jax.ShapeDtypeStruct((width, total), BF16))
     if group == "mid":
         out_shape.append(jax.ShapeDtypeStruct((stats_rows, LANES), F32))
-    out_specs = [whole(x.shape) for x in out_shape]
-    out_specs[0] = pl.BlockSpec((count, 2 * T), lambda i: (0, i))
-    args = (*users, *ads, logc, positives, *before)
-    return pl.pallas_call(
+    scratch = [
+        pltpu.VMEM((count, width), BF16),
+        pltpu.VMEM((count, LANES), F32),
+        pltpu.VMEM((count, T), F32),
+        pltpu.VMEM((count, T), F32),
+        pltpu.VMEM((count, T), BF16),
+        pltpu.VMEM((count, T), BF16),
+    ]
+    return call(
         lambda *refs: logits_kernel(group, len(ads), count, inv, *refs),
-        grid=(total // (2 * T),),
-        in_specs=[whole(x.shape) for x in args],
-        out_specs=out_specs,
-        out_shape=out_shape,
-        scratch_shapes=[
-            pltpu.VMEM((count, width), BF16),
-            pltpu.VMEM((count, LANES), F32),
-            pltpu.VMEM((count, T), F32),
-            pltpu.VMEM((count, T), F32),
-            pltpu.VMEM((count, T), BF16),
-        ],
-        compiler_params=params(),
-        cost_estimate=cost(count, total, width),
-        name="logits_" + group,
-    )(*args)
+        "logits_" + group,
+        out_shape,
+        scratch,
+        (*users, *ads, logc, positives, *before),
+        cost(count, total, width),
+    )
 
 
 GROUPS = ("near", "far", "mid")
@@ -230,8 +252,7 @@
 
 def rows_kernel(sizes, start, *refs):
     ads_refs, (pos_ref, out_ref, h0, h1) = refs[: len(sizes)], refs[len(sizes) :]
-    step = pl.program_id(0)
-    steps = out_ref.shape[1] // (2 * T)
+    tiles = out_ref.shape[1] // T
 
     def build(tile, dst):
         cols = pl.ds(pl.multiple_of(start + tile * T, T), T)
@@ -253,36 +274,27 @@
             spot += size
         out_ref[:, cols] = out.astype(BF16)
 
-    @pl.when(step == 0)
-    def _():
-        h1[...] = jnp.zeros_like(h1)
-
-    first = 2 * step
-    product(jnp.maximum(first - 1, 0), h1)
-    build(first, h0)
-    product(first, h0)
-    build(first + 1, h1)
-
-    @pl.when(step == steps - 1)
-    def _():
-        product(first + 1, h1)
+    build(0, h0)
+
+    @pl.loop(0, tiles // 2)
+    def _(step):
+        product(2 * step, h0)
+        build(2 * step + 1, h1)
+        product(2 * step + 1, h1)
+        build(jnp.minimum(2 * step + 2, tiles - 1), h0)
 
 
 def run_rows(ads_t, positives, start, total):
     width = ads_t[0].shape[0]
     sizes = [x.shape[1] for x in ads_t]
-    args = (*ads_t, positives)
-    return pl.pallas_call(
+    return call(
         lambda *refs: rows_kernel(sizes, start, *refs),
-        grid=(total // (2 * T),),
-        in_specs=[whole(x.shape) for x in args],
-        out_specs=whole((width, total)),
-        out_shape=jax.ShapeDtypeStruct((width, total), BF16),
-        scratch_shapes=[pltpu.VMEM((sum(sizes), T), BF16)] * 2,
-        compiler_params=params(),
-        cost_estimate=cost(sum(sizes), total, width),
-        name="positive_rows",
-    )(*args)
+        "positive_rows",
+        [jax.ShapeDtypeStruct((width, total), BF16)],
+        [pltpu.VMEM((sum(sizes), T), BF16)] * 2,
+        (*ads_t, positives),
+        cost(sum(sizes), total, width),
+    )[0]
 
 
 def users_kernel(inv, acc_ref, m_ref, rows_a, rows_b, hit_ref, weight_ref, *rest):
@@ -325,96 +337,67 @@
     shapes = [(NZ * width, T)] * 3 + [(width, T)] * 2
     out_shape = [jax.ShapeDtypeStruct(x, BF16) for x in shapes]
     out_shape += [row, row, jax.ShapeDtypeStruct((EXTRA, width), BF16)]
-    args = (acc, m, rows_a, rows_b, hits, weights, *stats)
-    return pl.pallas_call(
+    return call(
         lambda *refs: users_kernel(inv, *refs),
-        grid=(1,),
-        in_specs=[whole(x.shape) for x in args],
-        out_specs=[whole(x.shape) for x in out_shape],
-        out_shape=out_shape,
-        scratch_shapes=[pltpu.VMEM((NX, *stats[0].shape), F32), pltpu.VMEM((width, total), BF16)],
-        compiler_params=params(),
-        name="grad_users",
-    )(*args)
-
-
-def grads_kernel(group, steps, users_ref, p_ref, top_ref, lse_ref, coef_ref, weight_ref, pos_ref, loss_in, *refs):
-    if group == "mid":
-        near_ref, far_ref, da_ref, q0, q1, scale_row = refs
-    else:
-        da_ref, q0, q1, scale_row = refs
-    step = pl.program_id(0)
+        "grad_users",
+        out_shape,
+        [pltpu.VMEM((NX, *stats[0].shape), F32), pltpu.VMEM((width, total), BF16)],
+        (acc, m, rows_a, rows_b, hits, weights, *stats),
+    )
+
+
+def grads_kernel(group, users_ref, p_ref, top_ref, lse_ref, coef_ref, weight_ref, pos_ref, loss_in, *refs):
+    outs, qs = refs[:-2], refs[-2:]
     deep = 2 * T
-    total = p_ref.shape[1]
-
-    @pl.when(step == 0)
-    def _():
-        scale_row[...] = weight_ref[...] * jnp.exp(top_ref[...] - lse_ref[...])
-        q1[...] = jnp.zeros_like(q1)
-
-    def build(half, dst):
-        base = first_row(group, 2 * step + half)
+    count, total = p_ref.shape
+
+    def build(unit, dst):
         for b in range(total // T):
             cols = slice(b * T, (b + 1) * T)
-            ahead = pos_ref[:, cols] - base - lax.broadcasted_iota(jnp.int32, (16, T), 0)
-            scale, coef = scale_row[:, cols], coef_ref[:, cols]
-            for r in range(0, T, 16):
-                scaled = p_ref[half * T + r : half * T + r + 16, cols].astype(F32) * scale
-                dst[r : r + 16, cols] = jnp.where(ahead == r, coef, scaled).astype(BF16)
-
-    def product(chunk, src):
-        da = jnp.dot(src[...], users_ref[...], preferred_element_type=F32)
-        da_ref[pl.ds(pl.multiple_of(chunk * T, T), T), :] = da.astype(BF16)
-
-    first = 2 * step
-    product(jnp.maximum(first - 1, 0), q1)
-    build(0, q0)
-    product(first, q0)
-    build(1, q1)
-
-    @pl.when(step == steps - 1)
-    def _():
-        product(first + 1, q1)
+            scale = weight_ref[:, cols] * jnp.exp(top_ref[:, cols] - lse_ref[:, cols])
+            coef = coef_ref[:, cols]
+            pos = pos_ref[:, cols] - lax.broadcasted_iota(jnp.int32, (16, T), 0)
+            for half in range(2):
+                ahead = pos - first_row(group, 2 * unit + half)
+                for r in range(0, T, 16):
+                    row = half * T + r
+                    scaled = p_ref[unit * deep + row : unit * deep + row + 16, cols].astype(F32) * scale
+                    dst[row : row + 16, cols] = jnp.where(ahead == r, coef, scaled).astype(BF16)
+
+    def product(unit, src):
+        da = jnp.dot(src[...], users_ref[...], preferred_element_type=F32).astype(BF16)
         if group == "mid":
-            near_ref[...] = da_ref[:deep, :]
-            far_ref[:deep, :] = da_ref[deep:, :]
-            far_ref[deep:, :] = loss_in[...]
+            outs[unit][:deep, :] = da
+        else:
+            outs[0][unit * deep : (unit + 1) * deep, :] = da
+
+    units = count // deep
+    build(0, qs[0])
+    for unit in range(units):
+        product(unit, qs[unit % 2])
+        if unit + 1 < units:
+            build(unit + 1, qs[(unit + 1) % 2])
+    if group == "mid":
+        outs[1][deep:, :] = loss_in[...]
 
 
 def run_grads(group, users, p, top, lse, coefs, weights, positives, loss):
     count, total = p.shape
     width = users.shape[1]
     deep = 2 * T
-    steps = count // deep
-    args = (users, p, top, lse, coefs, weights, positives, loss)
-    in_specs = [whole(x.shape) for x in args]
-    in_specs[1] = pl.BlockSpec((deep, total), lambda i: (i, 0))
-    da = pltpu.VMEM((count, width), BF16)
-    scratch = [pltpu.VMEM((T, total), BF16)] * 2 + [pltpu.VMEM((1, total), F32)]
     shapes = [(deep, width), (deep + EXTRA, width)] if group == "mid" else [(count, width)]
-    return pl.pallas_call(
-        lambda *refs: grads_kernel(group, steps, *refs),
-        grid=(steps,),
-        in_specs=in_specs,
-        out_specs=[whole(x) for x in shapes],
-        out_shape=[jax.ShapeDtypeStruct(x, BF16) for x in shapes],
-        scratch_shapes=([da] if group == "mid" else []) + scratch,
-        compiler_params=params(),
-        cost_estimate=cost(count, total, width),
-        name="grads_" + group,
-    )(*args)
+    return call(
+        lambda *refs: grads_kernel(group, *refs),
+        "grads_" + group,
+        [jax.ShapeDtypeStruct(x, BF16) for x in shapes],
+        [pltpu.VMEM((deep, total), BF16)] * 2,
+        (users, p, top, lse, coefs, weights, positives, loss),
+        cost(count, total, width),
+    )
 
 
 def simple_call(kernel, name, out_shape, *args):
-    return pl.pallas_call(
-        kernel,
-        in_specs=[whole(x.shape) for x in args],
-        out_specs=[whole(x.shape) for x in out_shape],
-        out_shape=out_shape,
-        grid=(1,),
-        compiler_params=params(),
-        name=name,
-    )(*args)
+    return call(kernel, name, out_shape, [], args)
 
 
 def add_mid(near, loss, back):
@@ -591,7 +574,7 @@
     first, second = shift_y(first, -1), shift_y(second, 1)
     du_1, du_3 = shift_x(du_1, 1), shift_x(du_3, -1)
     (da_near,) = run_grads("near", staged, p_near, top_near, *tail)
-    da_near, first, second = lax.optimization_barrier((da_near, first, second))
+    da_near, first, second, du_1, du_3 = lax.optimization_barrier((da_near, first, second, du_1, du_3))
     kept, one, three = add_near(da_near, back, both, first, second)
     one, three = shift_y(one, -1), shift_y(three, 1)
     keep_u, send_u = add_users((du_0, du_1, du_3))

time: 105 us -> 103 us (0.981)
  Pallas kernels: 39 us -> 33.2 us
  waiting for transfers between devices: 28.2 us -> 32.3 us
    pallas_call x16, Pallas kernels: 39 us -> 33.2 us  [call(): pl.pallas_call(kernel, in_specs=[vmem] * len(args), out_specs=[vmem] * le...]
    ppermute x28, waiting for transfers between devices: 28.2 us -> 32.3 us  [move(): lax.ppermute(x, axis, [(i, target(i)) for i in range(lax.axis_size(axis))])]
  transfers between devices with their start and end apart: 28 -> 28, of which waited for: 16 -> 15; matrix products, arithmetic and copies ran while one was open for 3% -> 3% of each run, Pallas kernels for 27% -> 24%
where the time goes in v4:
time: 103 us
  Pallas kernels  33.2 us (32%)
  starting transfers between devices  32.8 us (32%)
  waiting for transfers between devices  32.3 us (31%)
  local copies, waits for them, and re-layouts  1.97 us (2%)
  other arithmetic  1.43 us (1%)
    pallas_call x16, Pallas kernels, call(): pl.pallas_call(kernel, in_specs=[vmem] * len(args), out_specs=[vmem] * le...  33.2 us
    ppermute x28, starting transfers between devices, move(): lax.ppermute(x, axis, [(i, target(i)) for i in range(lax.axis_size(axis))])  32.8 us
    ppermute x28, waiting for transfers between devices, move(): lax.ppermute(x, axis, [(i, target(i)) for i in range(lax.axis_size(axis))])  32.3 us
  transfers between devices with their start and end apart: 28, of which 15 were waited for; matrix products, arithmetic and copies ran while one was open for 3% of the time, Pallas kernels for 24%

profile of v4, /device:TPU:0, one launch (start us, length us, event | category | flops | bytes accessed | tf_op | source)
XLA Modules:
  0.0 102.6 jit_solution(12315596645971124765)
XLA Ops:
  0.6 4.0 %collective-permute-start = (bf16[256,256]{1,0:T(8,128)(2,1)}, bf16[256,256]{1,0:T(8,128)(2,1)S(1)}, u32[]{:S(2)}, u32[]{:S(2)}) collective-permute-start(bf16[256,256]{1,0:T(8,128)(2,1)} %param.5), channel_id=1, source_target_pairs={{0,1},{1,0},{2,3},{3,2},{4,5},{5,4},{6,7},{7,6},{8,9},{9,8},{10,11... | collective-permute-start | bytes 393224 | tf_op jit(solution)/shard_map/ppermute | solution.py:502
  9.2 2.7 %collective-permute-done.1 = bf16[256,256]{1,0:T(8,128)(2,1)S(1)} collective-permute-done((bf16[256,256]{1,0:T(8,128)(2,1)}, bf16[256,256]{1,0:T(8,128)(2,1)S(1)}, u32[]{:S(2)}, u32[]{:S(2)}) %collective-permute-start.1) | collective-permute-done | bytes 131104 | tf_op jit(solution)/shard_map/ppermute | solution.py:502
  11.9 2.8 %collective-permute-start.3 = (bf16[512,256]{1,0:T(8,128)(2,1)S(1)}, bf16[512,256]{1,0:T(8,128)(2,1)S(1)}, u32[]{:S(2)}, u32[]{:S(2)}) collective-permute-start(bf16[512,256]{1,0:T(8,128)(2,1)S(1)} %constant_dynamic-update-slice_fusion.refs_0_), channel_id=1, source_target_pairs={{0,6},{1,7},{2,0},{3,1},{4,2},{5,3},{6,4},{7,5},{8,14},{9,15},{10,... | collective-permute-start | bytes 786440 | tf_op jit(solution)/shard_map/ppermute | solution.py:502
  14.8 3.1 %collective-permute-start.5 = (bf16[512,256]{1,0:T(8,128)(2,1)S(1)}, bf16[512,256]{1,0:T(8,128)(2,1)S(1)}, u32[]{:S(2)}, u32[]{:S(2)}) collective-permute-start(bf16[512,256]{1,0:T(8,128)(2,1)S(1)} %get-tuple-element.172), channel_id=1, source_target_pairs={{0,48},{8,56},{16,0},{24,8},{32,16},{40,24},{48,32},{56,40},{64,11... | collective-permute-start | bytes 786440 | tf_op jit(solution)/shard_map/ppermute | solution.py:502
  17.9 1.6 %collective-permute-done.3.refs_2_ = bf16[512,256]{1,0:T(8,128)(2,1)S(1)} collective-permute-done((bf16[512,256]{1,0:T(8,128)(2,1)S(1)}, bf16[512,256]{1,0:T(8,128)(2,1)S(1)}, u32[]{:S(2)}, u32[]{:S(2)}) %collective-permute-start.3) | collective-permute-done | bytes 262176 | tf_op jit(solution)/shard_map/ppermute | solution.py:502
  19.5 3.4 %collective-permute-done.2.refs_1_ = bf16[512,256]{1,0:T(8,128)(2,1)S(1)} collective-permute-done((bf16[512,256]{1,0:T(8,128)(2,1)S(1)}, bf16[512,256]{1,0:T(8,128)(2,1)S(1)}, u32[]{:S(2)}, u32[]{:S(2)}) %collective-permute-start.2) | collective-permute-done | bytes 262176 | tf_op jit(solution)/shard_map/ppermute | solution.py:502
  22.9 2.8 %collective-permute-done.4 = bf16[512,256]{1,0:T(8,128)(2,1)S(1)} collective-permute-done((bf16[512,256]{1,0:T(8,128)(2,1)S(1)}, bf16[512,256]{1,0:T(8,128)(2,1)S(1)}, u32[]{:S(2)}, u32[]{:S(2)}) %collective-permute-start.4) | collective-permute-done | bytes 262176 | tf_op jit(solution)/shard_map/ppermute | solution.py:502
  25.9 3.1 %collective-permute-start.7 = (bf16[256,256]{1,0:T(8,128)(2,1)S(1)}, bf16[256,256]{1,0:T(8,128)(2,1)S(1)}, u32[]{:S(2)}, u32[]{:S(2)}) collective-permute-start(bf16[256,256]{1,0:T(8,128)(2,1)S(1)} %slice.13), channel_id=1, source_target_pairs={{0,6},{1,7},{2,0},{3,1},{4,2},{5,3},{6,4},{7,5},{8,14},{9,15},{10,... | collective-permute-start | bytes 393224 | tf_op jit(solution)/shard_map/ppermute | solution.py:502
  29.3 1.8 %collective-permute-start.8 = (bf16[256,256]{1,0:T(8,128)(2,1)S(1)}, bf16[256,256]{1,0:T(8,128)(2,1)S(1)}, u32[]{:S(2)}, u32[]{:S(2)}) collective-permute-start(bf16[256,256]{1,0:T(8,128)(2,1)S(1)} %slice.14), channel_id=1, source_target_pairs={{0,16},{8,24},{16,32},{24,40},{32,48},{40,56},{48,0},{56,8},{64,80... | collective-permute-start | bytes 393224 | tf_op jit(solution)/shard_map/ppermute | solution.py:502
  31.1 1.3 %collective-permute-done.7.refs_4_ = bf16[256,256]{1,0:T(8,128)(2,1)S(1)} collective-permute-done((bf16[256,256]{1,0:T(8,128)(2,1)S(1)}, bf16[256,256]{1,0:T(8,128)(2,1)S(1)}, u32[]{:S(2)}, u32[]{:S(2)}) %collective-permute-start.7) | collective-permute-done | bytes 131104 | tf_op jit(solution)/shard_map/ppermute | solution.py:502
  32.3 3.4 %collective-permute-done.6.refs_3_ = bf16[256,256]{1,0:T(8,128)(2,1)S(1)} collective-permute-done((bf16[256,256]{1,0:T(8,128)(2,1)S(1)}, bf16[256,256]{1,0:T(8,128)(2,1)S(1)}, u32[]{:S(2)}, u32[]{:S(2)}) %collective-permute-start.6) | collective-permute-done | bytes 131104 | tf_op jit(solution)/shard_map/ppermute | solution.py:502
  35.8 7.2 %logits_near.1 = (bf16[1536,2048]{1,0:T(8,128)(2,1)S(1)}, f32[1,2048]{1,0:T(1,128)S(1)}, bf16[256,1536]{1,0:T(8,128)(2,1)S(1)}, f32[256,2048]{1,0:T(8,128)S(1)},...) custom-call(bf16[512,256]{1,0:T(8,128)(2,1)S(1)} %constant_dynamic-u, ...), custom_call_target="tpu_custom_call" | custom-call | flops 100663296 | bytes 393216 | tf_op jit(solution)/shard_map/logits_near/pallas_call | solution.py:23
  43.1 6.8 %logits_far.1 = (bf16[1536,2048]{1,0:T(8,128)(2,1)S(1)}, f32[1,2048]{1,0:T(1,128)S(1)}, bf16[256,1536]{1,0:T(8,128)(2,1)S(1)}, f32[256,2048]{1,0:T(8,128)S(1)}, ...) custom-call(bf16[256,2048]{1,0:T(8,128)(2,1)S(1)} %get-tuple-element.95.refs_0_, ...), custom_call_target="tpu_custom_call" | custom-call | flops 100663296 | bytes 393216 | tf_op jit(solution)/shard_map/logits_far/pallas_call | solution.py:23
  50.0 5.5 %logits_mid.1 = (bf16[1024,2048]{1,0:T(8,128)(2,1)S(1)}, f32[1,2048]{1,0:T(1,128)S(1)}, bf16[256,1024]{1,0:T(8,128)(2,1)S(1)}, f32[256,2048]{1,0:T(8,128)S(1)}, ...) custom-call(bf16[256,2048]{1,0:T(8,128)(2,1)S(1)} %get-tuple-element.95.refs_0_, ...), custom_call_target="tpu_custom_call" | custom-call | flops 67108864 | bytes 262144 | tf_op jit(solution)/shard_map/logits_mid/pallas_call | solution.py:23
  55.5 1.2 %collective-permute-start.12 = (f32[32,128]{1,0:T(8,128)S(1)}, f32[32,128]{1,0:T(8,128)S(1)}, u32[]{:S(2)}, u32[]{:S(2)}) collective-permute-start(f32[32,128]{1,0:T(8,128)S(1)} %get-tuple-element.109.own_ref), channel_id=1, source_target_pairs={{0,1},{1,0},{2,3},{3,2},{4,5},{5,4},{6,7},{7,6},{8,9},{9,8},{10,11... | collective-permute-start | bytes 49160 | tf_op jit(solution)/shard_map/ppermute | solution.py:502
  56.6 2.9 %positive_rows.2.refs_2_ = bf16[256,1024]{1,0:T(8,128)(2,1)S(1)} custom-call(bf16[256,1536]{1,0:T(8,128)(2,1)S(1)} %get-tuple-element.110.refs_0_, bf16[256,1536]{1,0:T(8,128)(2,1)S(1)} %get-tuple-element.111.refs_1_, bf16[256,1024]{1,0:T(8,128)(2,1)S(1)} %get-tuple-element.112.refs_2_, s32[1,2048]{1,0:T(1,128)S(1)} %bitcast.7), custom_call_target="tpu_custom_call" | custom-call | flops 134217728 | bytes 524288 | tf_op jit(solution)/shard_map/positive_rows/pallas_call | solution.py:23
  59.5 1.2 %collective-permute-done.12.other_ref = f32[32,128]{1,0:T(8,128)S(1)} collective-permute-done((f32[32,128]{1,0:T(8,128)S(1)}, f32[32,128]{1,0:T(8,128)S(1)}, u32[]{:S(2)}, u32[]{:S(2)}) %collective-permute-start.12) | collective-permute-done | bytes 16416 | tf_op jit(solution)/shard_map/ppermute | solution.py:502
  62.8 2.9 %positive_rows.3.refs_3_ = bf16[256,1024]{1,0:T(8,128)(2,1)S(1)} custom-call(bf16[256,1536]{1,0:T(8,128)(2,1)S(1)} %get-tuple-element.110.refs_0_, bf16[256,1536]{1,0:T(8,128)(2,1)S(1)} %get-tuple-element.111.refs_1_, bf16[256,1024]{1,0:T(8,128)(2,1)S(1)} %get-tuple-element.112.refs_2_, s32[1,2048]{1,0:T(1,128)S(1)} %bitcast.8), custom_call_target="tpu_custom_call" | custom-call | flops 134217728 | bytes 524288 | tf_op jit(solution)/shard_map/positive_rows/pallas_call | solution.py:23
  67.9 1.5 %grads_mid.1 = (bf16[512,256]{1,0:T(8,128)(2,1)S(1)}, bf16[528,256]{1,0:T(8,128)(2,1)S(1)}) custom-call(bf16[2048,256]{1,0:T(8,128)(2,1)S(1)} %get-tuple-element.144.refs_0_, bf16[1024,2048]{1,0:T(8,128)(2,1)S(1)} %get-tuple-element.122.refs_1_, f32[1,2048]{1,0:T(1,128)S(1)} %get-tuple-element.123.refs_2_, f32[1,2048]{1,0:T(1,128)S(1)} %get-tuple-element.124.refs_3_, ...), custom_call_target="tpu_custom_call" | custom-call | flops 67108864 | bytes 262144 | tf_op jit(solution)/shard_map/grads_mid/pallas_call | solution.py:23
  70.4 2.4 %collective-permute-start.18 = (bf16[256,256]{1,0:T(8,128)(2,1)S(1)}, bf16[256,256]{1,0:T(8,128)(2,1)S(1)}, u32[]{:S(2)}, u32[]{:S(2)}) collective-permute-start(bf16[256,256]{1,0:T(8,128)(2,1)S(1)} %get-tuple-element.134), channel_id=1, source_target_pairs={{0,6},{1,7},{2,0},{3,1},{4,2},{5,3},{6,4},{7,5},{8,14},{9,15},{10,... | collective-permute-start | bytes 393224 | tf_op jit(solution)/shard_map/ppermute | solution.py:502
  72.8 2.1 %grads_far.1 = bf16[1536,256]{1,0:T(8,128)(2,1)S(1)} custom-call(bf16[2048,256]{1,0:T(8,128)(2,1)S(1)} %get-tuple-element.144.refs_0_, bf16[1536,2048]{1,0:T(8,128)(2,1)S(1)} %get-tuple-element.130.refs_1_, f32[1,2048]{1,0:T(1,128)S(1)} %get-tuple-element.131.refs_2_, f32[1,2048]{1,0:T(1,128)S(1)} %get-tuple-element.124.refs_3_, ...), custom_call_target="tpu_custom_call" | custom-call | flops 100663296 | bytes 393216 | tf_op jit(solution)/shard_map/grads_far/pallas_call | solution.py:23
  74.9 1.7 %collective-permute-done.17.first_ref = bf16[256,256]{1,0:T(8,128)(2,1)S(1)} collective-permute-done((bf16[256,256]{1,0:T(8,128)(2,1)S(1)}, bf16[256,256]{1,0:T(8,128)(2,1)S(1)}, u32[]{:S(2)}, u32[]{:S(2)}) %collective-permute-start.17) | collective-permute-done | bytes 131104 | tf_op jit(solution)/shard_map/ppermute | solution.py:502
  76.7 1.2 %collective-permute-start.21 = (bf16[512,256]{1,0:T(8,128)(2,1)S(1)}, bf16[512,256]{1,0:T(8,128)(2,1)S(1)}, u32[]{:S(2)}, u32[]{:S(2)}) collective-permute-start(bf16[512,256]{1,0:T(8,128)(2,1)S(1)} %get-tuple-element.149), channel_id=1, source_target_pairs={{0,2},{1,3},{2,4},{3,5},{4,6},{5,7},{6,0},{7,1},{8,10},{9,11},{10,... | collective-permute-start | bytes 786440 | tf_op jit(solution)/shard_map/ppermute | solution.py:502
  78.0 2.1 %collective-permute-start.22 = (bf16[512,256]{1,0:T(8,128)(2,1)S(1)}, bf16[512,256]{1,0:T(8,128)(2,1)S(1)}, u32[]{:S(2)}, u32[]{:S(2)}) collective-permute-start(bf16[512,256]{1,0:T(8,128)(2,1)S(1)} %get-tuple-element.150), channel_id=1, source_target_pairs={{0,6},{1,7},{2,0},{3,1},{4,2},{5,3},{6,4},{7,5},{8,14},{9,15},{10,... | collective-permute-start | bytes 786440 | tf_op jit(solution)/shard_map/ppermute | solution.py:502
  80.3 1.8 %collective-permute-start.20 = (bf16[256,256]{1,0:T(8,128)(2,1)S(1)}, bf16[256,256]{1,0:T(8,128)(2,1)S(1)}, u32[]{:S(2)}, u32[]{:S(2)}) collective-permute-start(bf16[256,256]{1,0:T(8,128)(2,1)S(1)} %get-tuple-element.148), channel_id=1, source_target_pairs={{0,16},{8,24},{16,32},{24,40},{32,48},{40,56},{48,0},{56,8},{64,80... | collective-permute-start | bytes 393224 | tf_op jit(solution)/shard_map/ppermute | solution.py:502
  82.1 2.1 %grads_near.1.near_ref = bf16[1536,256]{1,0:T(8,128)(2,1)S(1)} custom-call(bf16[2048,256]{1,0:T(8,128)(2,1)S(1)} %get-tuple-element.144.refs_0_, bf16[1536,2048]{1,0:T(8,128)(2,1)S(1)} %get-tuple-element.145.refs_1_, f32[1,2048]{1,0:T(1,128)S(1)} %get-tuple-element.146.refs_2_, f32[1,2048]{1,0:T(1,128)S(1)} %get-tuple-element.124.refs_3_, ...), custom_call_target="tpu_custom_call" | custom-call | flops 100663296 | bytes 393216 | tf_op jit(solution)/shard_map/grads_near/pallas_call | solution.py:23
  84.2 2.5 %collective-permute-done.20.second_ref = bf16[256,256]{1,0:T(8,128)(2,1)S(1)} collective-permute-done((bf16[256,256]{1,0:T(8,128)(2,1)S(1)}, bf16[256,256]{1,0:T(8,128)(2,1)S(1)}, u32[]{:S(2)}, u32[]{:S(2)}) %collective-permute-start.20) | collective-permute-done | bytes 131104 | tf_op jit(solution)/shard_map/ppermute | solution.py:502
  87.4 1.6 %collective-permute-start.25 = (bf16[528,256]{1,0:T(8,128)(2,1)S(1)}, bf16[528,256]{1,0:T(8,128)(2,1)S(1)}, u32[]{:S(2)}, u32[]{:S(2)}) collective-permute-start(bf16[528,256]{1,0:T(8,128)(2,1)S(1)} %get-tuple-element.160), channel_id=1, source_target_pairs={{0,16},{8,24},{16,32},{24,40},{32,48},{40,56},{48,0},{56,8},{64,80... | collective-permute-start | bytes 811016 | tf_op jit(solution)/shard_map/ppermute | solution.py:502
  89.1 1.3 %collective-permute-start.26 = (bf16[256,256]{1,0:T(8,128)(2,1)S(1)}, bf16[256,256]{1,0:T(8,128)(2,1)S(1)}, u32[]{:S(2)}, u32[]{:S(2)}) collective-permute-start(bf16[256,256]{1,0:T(8,128)(2,1)S(1)} %get-tuple-element.161), channel_id=1, source_target_pairs={{0,1},{1,0},{2,3},{3,2},{4,5},{5,4},{6,7},{7,6},{8,9},{9,8},{10,11... | collective-permute-start | bytes 393224 | tf_op jit(solution)/shard_map/ppermute | solution.py:502
  90.4 5.3 %collective-permute-done.26.received_u_ref = bf16[256,256]{1,0:T(8,128)(2,1)S(1)} collective-permute-done((bf16[256,256]{1,0:T(8,128)(2,1)S(1)}, bf16[256,256]{1,0:T(8,128)(2,1)S(1)}, u32[]{:S(2)}, u32[]{:S(2)}) %collective-permute-start.26) | collective-permute-done | bytes 131104 | tf_op jit(solution)/shard_map/ppermute | solution.py:502
  96.5 1.1 %collective-permute-start.27 = (bf16[272,256]{1,0:T(8,128)(2,1)S(1)}, bf16[272,256]{1,0:T(8,128)(2,1)S(1)}, u32[]{:S(2)}, u32[]{:S(2)}) collective-permute-start(bf16[272,256]{1,0:T(8,128)(2,1)S(1)} %get-tuple-element.167), channel_id=1, source_target_pairs={{0,64},{8,72},{16,80},{24,88},{32,96},{40,104},{48,112},{56,120},{... | collective-permute-start | bytes 417800 | tf_op jit(solution)/shard_map/ppermute | solution.py:502
  97.6 4.0 %collective-permute-done.27.received_ref = bf16[272,256]{1,0:T(8,128)(2,1)S(1)} collective-permute-done((bf16[272,256]{1,0:T(8,128)(2,1)S(1)}, bf16[272,256]{1,0:T(8,128)(2,1)S(1)}, u32[]{:S(2)}, u32[]{:S(2)}) %collective-permute-start.27) | collective-permute-done | bytes 139296 | tf_op jit(solution)/shard_map/ppermute | solution.py:502
  (56 shorter events, 13.4 us)
Async XLA Ops:
  0.6 8.6 %collective-permute-start = (bf16[256,256]{1,0:T(8,128)(2,1)}, bf16[256,256]{1,0:T(8,128)(2,1)S(1)}, u32[]{:S(2)}, u32[]{:S(2)}) collective-permute-start(bf16[256,256]{1,0:T(8,128)(2,1)} %param.5), channel_id=1, source_target_pairs={{0,1},{1,0},{2,3},{3,2},{4,5},{5,4},{6,7},{7,6},{8,9},{9,8},{10,11... | collective-permute-start | bytes 393224 | tf_op jit(solution)/shard_map/ppermute | solution.py:502
  4.7 7.2 %collective-permute-start.1 = (bf16[256,256]{1,0:T(8,128)(2,1)}, bf16[256,256]{1,0:T(8,128)(2,1)S(1)}, u32[]{:S(2)}, u32[]{:S(2)}) collective-permute-start(bf16[256,256]{1,0:T(8,128)(2,1)} %param.6), channel_id=1, source_target_pairs={{0,64},{8,72},{16,80},{24,88},{32,96},{40,104},{48,112},{56,120},{... | collective-permute-start | bytes 393224 | tf_op jit(solution)/shard_map/ppermute | solution.py:502
  11.9 7.5 %collective-permute-start.3 = (bf16[512,256]{1,0:T(8,128)(2,1)S(1)}, bf16[512,256]{1,0:T(8,128)(2,1)S(1)}, u32[]{:S(2)}, u32[]{:S(2)}) collective-permute-start(bf16[512,256]{1,0:T(8,128)(2,1)S(1)} %constant_dynamic-update-slice_fusion.refs_0_), channel_id=1, source_target_pairs={{0,6},{1,7},{2,0},{3,1},{4,2},{5,3},{6,4},{7,5},{8,14},{9,15},{10,... | collective-permute-start | bytes 786440 | tf_op jit(solution)/shard_map/ppermute | solution.py:502
  14.8 8.1 %collective-permute-start.2 = (bf16[512,256]{1,0:T(8,128)(2,1)S(1)}, bf16[512,256]{1,0:T(8,128)(2,1)S(1)}, u32[]{:S(2)}, u32[]{:S(2)}) collective-permute-start(bf16[512,256]{1,0:T(8,128)(2,1)S(1)} %constant_dynamic-update-slice_fusion.refs_0_), channel_id=1, source_target_pairs={{0,2},{1,3},{2,4},{3,5},{4,6},{5,7},{6,0},{7,1},{8,10},{9,11},{10,... | collective-permute-start | bytes 786440 | tf_op jit(solution)/shard_map/ppermute | solution.py:502
  14.8 8.1 %collective-permute-start.5 = (bf16[512,256]{1,0:T(8,128)(2,1)S(1)}, bf16[512,256]{1,0:T(8,128)(2,1)S(1)}, u32[]{:S(2)}, u32[]{:S(2)}) collective-permute-start(bf16[512,256]{1,0:T(8,128)(2,1)S(1)} %get-tuple-element.172), channel_id=1, source_target_pairs={{0,48},{8,56},{16,0},{24,8},{32,16},{40,24},{48,32},{56,40},{64,11... | collective-permute-start | bytes 786440 | tf_op jit(solution)/shard_map/ppermute | solution.py:502
  17.9 7.8 %collective-permute-start.4 = (bf16[512,256]{1,0:T(8,128)(2,1)S(1)}, bf16[512,256]{1,0:T(8,128)(2,1)S(1)}, u32[]{:S(2)}, u32[]{:S(2)}) collective-permute-start(bf16[512,256]{1,0:T(8,128)(2,1)S(1)} %get-tuple-element.172), channel_id=1, source_target_pairs={{0,16},{8,24},{16,32},{24,40},{32,48},{40,56},{48,0},{56,8},{64,80... | collective-permute-start | bytes 786440 | tf_op jit(solution)/shard_map/ppermute | solution.py:502
  25.7 17.3 %collective-permute-start.11 = (bf16[1536,256]{1,0:T(8,128)(2,1)S(1)}, bf16[1536,256]{1,0:T(8,128)(2,1)S(1)}, u32[]{:S(2)}, u32[]{:S(2)}) collective-permute-start(bf16[1536,256]{1,0:T(8,128)(2,1)S(1)} %constant_dynamic-update-slice_fusion.4.refs_5_), channel_id=1, source_target_pairs={{0,8},{8,0},{16,24},{24,16},{32,40},{40,32},{48,56},{56,48},{64,72... | collective-permute-start | bytes 2359304 | tf_op jit(solution)/shard_map/ppermute | solution.py:502
  25.9 6.5 %collective-permute-start.7 = (bf16[256,256]{1,0:T(8,128)(2,1)S(1)}, bf16[256,256]{1,0:T(8,128)(2,1)S(1)}, u32[]{:S(2)}, u32[]{:S(2)}) collective-permute-start(bf16[256,256]{1,0:T(8,128)(2,1)S(1)} %slice.13), channel_id=1, source_target_pairs={{0,6},{1,7},{2,0},{3,1},{4,2},{5,3},{6,4},{7,5},{8,14},{9,15},{10,... | collective-permute-start | bytes 393224 | tf_op jit(solution)/shard_map/ppermute | solution.py:502
  28.9 6.8 %collective-permute-start.6 = (bf16[256,256]{1,0:T(8,128)(2,1)S(1)}, bf16[256,256]{1,0:T(8,128)(2,1)S(1)}, u32[]{:S(2)}, u32[]{:S(2)}) collective-permute-start(bf16[256,256]{1,0:T(8,128)(2,1)S(1)} %slice.12), channel_id=1, source_target_pairs={{0,2},{1,3},{2,4},{3,5},{4,6},{5,7},{6,0},{7,1},{8,10},{9,11},{10,... | collective-permute-start | bytes 393224 | tf_op jit(solution)/shard_map/ppermute | solution.py:502
  29.0 14.0 %collective-permute-start.9 = (bf16[256,256]{1,0:T(8,128)(2,1)S(1)}, bf16[256,256]{1,0:T(8,128)(2,1)S(1)}, u32[]{:S(2)}, u32[]{:S(2)}) collective-permute-start(bf16[256,256]{1,0:T(8,128)(2,1)S(1)} %slice.15), channel_id=1, source_target_pairs={{0,48},{8,56},{16,0},{24,8},{32,16},{40,24},{48,32},{56,40},{64,11... | collective-permute-start | bytes 393224 | tf_op jit(solution)/shard_map/ppermute | solution.py:502
  29.3 13.7 %collective-permute-start.8 = (bf16[256,256]{1,0:T(8,128)(2,1)S(1)}, bf16[256,256]{1,0:T(8,128)(2,1)S(1)}, u32[]{:S(2)}, u32[]{:S(2)}) collective-permute-start(bf16[256,256]{1,0:T(8,128)(2,1)S(1)} %slice.14), channel_id=1, source_target_pairs={{0,16},{8,24},{16,32},{24,40},{32,48},{40,56},{48,0},{56,8},{64,80... | collective-permute-start | bytes 393224 | tf_op jit(solution)/shard_map/ppermute | solution.py:502
  43.0 7.0 %collective-permute-start.10 = (bf16[512,256]{1,0:T(8,128)(2,1)S(1)}, bf16[512,256]{1,0:T(8,128)(2,1)S(1)}, u32[]{:S(2)}, u32[]{:S(2)}) collective-permute-start(bf16[512,256]{1,0:T(8,128)(2,1)S(1)} %constant_dynamic-update-slice_fusion.8.refs_1_), channel_id=1, source_target_pairs={{0,8},{8,0},{16,24},{24,16},{32,40},{40,32},{48,56},{56,48},{64,72... | collective-permute-start | bytes 786440 | tf_op jit(solution)/shard_map/ppermute | solution.py:502
  49.9 17.3 %copy-start = (f32[2048]{0:T(1024)S(1)}, f32[2048]{0:T(1024)}, u32[]{:S(2)}) copy-start(f32[2048]{0:T(1024)} %param.9) | copy-start | bytes 24580
  55.5 5.2 %collective-permute-start.12 = (f32[32,128]{1,0:T(8,128)S(1)}, f32[32,128]{1,0:T(8,128)S(1)}, u32[]{:S(2)}, u32[]{:S(2)}) collective-permute-start(f32[32,128]{1,0:T(8,128)S(1)} %get-tuple-element.109.own_ref), channel_id=1, source_target_pairs={{0,1},{1,0},{2,3},{3,2},{4,5},{5,4},{6,7},{7,6},{8,9},{9,8},{10,11... | collective-permute-start | bytes 49160 | tf_op jit(solution)/shard_map/ppermute | solution.py:502
  60.7 5.0 %collective-permute-start.15 = (f32[32,128]{1,0:T(8,128)S(1)}, f32[32,128]{1,0:T(8,128)S(1)}, u32[]{:S(2)}, u32[]{:S(2)}) collective-permute-start(f32[32,128]{1,0:T(8,128)S(1)} %join_stats.1.refs_6_), channel_id=1, source_target_pairs={{0,6},{1,7},{2,0},{3,1},{4,2},{5,3},{6,4},{7,5},{8,14},{9,15},{10,... | collective-permute-start | bytes 49160 | tf_op jit(solution)/shard_map/ppermute | solution.py:502
  61.1 5.2 %collective-permute-start.14 = (f32[32,128]{1,0:T(8,128)S(1)}, f32[32,128]{1,0:T(8,128)S(1)}, u32[]{:S(2)}, u32[]{:S(2)}) collective-permute-start(f32[32,128]{1,0:T(8,128)S(1)} %join_stats.1.refs_6_), channel_id=1, source_target_pairs={{0,4},{1,5},{2,6},{3,7},{4,0},{5,1},{6,2},{7,3},{8,12},{9,13},{10,... | collective-permute-start | bytes 49160 | tf_op jit(solution)/shard_map/ppermute | solution.py:502
  61.9 5.3 %collective-permute-start.13 = (f32[32,128]{1,0:T(8,128)S(1)}, f32[32,128]{1,0:T(8,128)S(1)}, u32[]{:S(2)}, u32[]{:S(2)}) collective-permute-start(f32[32,128]{1,0:T(8,128)S(1)} %join_stats.1.refs_6_), channel_id=1, source_target_pairs={{0,2},{1,3},{2,4},{3,5},{4,6},{5,7},{6,0},{7,1},{8,10},{9,11},{10,... | collective-permute-start | bytes 49160 | tf_op jit(solution)/shard_map/ppermute | solution.py:502
  69.4 7.2 %collective-permute-start.16 = (bf16[528,256]{1,0:T(8,128)(2,1)S(1)}, bf16[528,256]{1,0:T(8,128)(2,1)S(1)}, u32[]{:S(2)}, u32[]{:S(2)}) collective-permute-start(bf16[528,256]{1,0:T(8,128)(2,1)S(1)} %get-tuple-element.132), channel_id=1, source_target_pairs={{0,8},{8,0},{16,24},{24,16},{32,40},{40,32},{48,56},{56,48},{64,72... | collective-permute-start | bytes 811016 | tf_op jit(solution)/shard_map/ppermute | solution.py:502
  69.5 7.1 %collective-permute-start.17 = (bf16[256,256]{1,0:T(8,128)(2,1)S(1)}, bf16[256,256]{1,0:T(8,128)(2,1)S(1)}, u32[]{:S(2)}, u32[]{:S(2)}) collective-permute-start(bf16[256,256]{1,0:T(8,128)(2,1)S(1)} %get-tuple-element.133), channel_id=1, source_target_pairs={{0,2},{1,3},{2,4},{3,5},{4,6},{5,7},{6,0},{7,1},{8,10},{9,11},{10,... | collective-permute-start | bytes 393224 | tf_op jit(solution)/shard_map/ppermute | solution.py:502
  70.4 6.2 %collective-permute-start.18 = (bf16[256,256]{1,0:T(8,128)(2,1)S(1)}, bf16[256,256]{1,0:T(8,128)(2,1)S(1)}, u32[]{:S(2)}, u32[]{:S(2)}) collective-permute-start(bf16[256,256]{1,0:T(8,128)(2,1)S(1)} %get-tuple-element.134), channel_id=1, source_target_pairs={{0,6},{1,7},{2,0},{3,1},{4,2},{5,3},{6,4},{7,5},{8,14},{9,15},{10,... | collective-permute-start | bytes 393224 | tf_op jit(solution)/shard_map/ppermute | solution.py:502
  76.6 10.2 %collective-permute-start.23 = (bf16[1536,256]{1,0:T(8,128)(2,1)S(1)}, bf16[1536,256]{1,0:T(8,128)(2,1)S(1)}, u32[]{:S(2)}, u32[]{:S(2)}) collective-permute-start(bf16[1536,256]{1,0:T(8,128)(2,1)S(1)} %grads_far.1), channel_id=1, source_target_pairs={{0,8},{8,0},{16,24},{24,16},{32,40},{40,32},{48,56},{56,48},{64,72... | collective-permute-start | bytes 2359304 | tf_op jit(solution)/shard_map/ppermute | solution.py:502
  76.7 10.0 %collective-permute-start.21 = (bf16[512,256]{1,0:T(8,128)(2,1)S(1)}, bf16[512,256]{1,0:T(8,128)(2,1)S(1)}, u32[]{:S(2)}, u32[]{:S(2)}) collective-permute-start(bf16[512,256]{1,0:T(8,128)(2,1)S(1)} %get-tuple-element.149), channel_id=1, source_target_pairs={{0,2},{1,3},{2,4},{3,5},{4,6},{5,7},{6,0},{7,1},{8,10},{9,11},{10,... | collective-permute-start | bytes 786440 | tf_op jit(solution)/shard_map/ppermute | solution.py:502
  78.0 8.8 %collective-permute-start.22 = (bf16[512,256]{1,0:T(8,128)(2,1)S(1)}, bf16[512,256]{1,0:T(8,128)(2,1)S(1)}, u32[]{:S(2)}, u32[]{:S(2)}) collective-permute-start(bf16[512,256]{1,0:T(8,128)(2,1)S(1)} %get-tuple-element.150), channel_id=1, source_target_pairs={{0,6},{1,7},{2,0},{3,1},{4,2},{5,3},{6,4},{7,5},{8,14},{9,15},{10,... | collective-permute-start | bytes 786440 | tf_op jit(solution)/shard_map/ppermute | solution.py:502
  80.0 6.6 %collective-permute-start.19 = (bf16[272,256]{1,0:T(8,128)(2,1)S(1)}, bf16[272,256]{1,0:T(8,128)(2,1)S(1)}, u32[]{:S(2)}, u32[]{:S(2)}) collective-permute-start(bf16[272,256]{1,0:T(8,128)(2,1)S(1)} %get-tuple-element.147), channel_id=1, source_target_pairs={{0,48},{8,56},{16,0},{24,8},{32,16},{40,24},{48,32},{56,40},{64,11... | collective-permute-start | bytes 417800 | tf_op jit(solution)/shard_map/ppermute | solution.py:502
  80.3 6.4 %collective-permute-start.20 = (bf16[256,256]{1,0:T(8,128)(2,1)S(1)}, bf16[256,256]{1,0:T(8,128)(2,1)S(1)}, u32[]{:S(2)}, u32[]{:S(2)}) collective-permute-start(bf16[256,256]{1,0:T(8,128)(2,1)S(1)} %get-tuple-element.148), channel_id=1, source_target_pairs={{0,16},{8,24},{16,32},{24,40},{32,48},{40,56},{48,0},{56,8},{64,80... | collective-permute-start | bytes 393224 | tf_op jit(solution)/shard_map/ppermute | solution.py:502
  87.0 8.7 %collective-permute-start.24 = (bf16[528,256]{1,0:T(8,128)(2,1)S(1)}, bf16[528,256]{1,0:T(8,128)(2,1)S(1)}, u32[]{:S(2)}, u32[]{:S(2)}) collective-permute-start(bf16[528,256]{1,0:T(8,128)(2,1)S(1)} %get-tuple-element.159), channel_id=1, source_target_pairs={{0,48},{8,56},{16,0},{24,8},{32,16},{40,24},{48,32},{56,40},{64,11... | collective-permute-start | bytes 811016 | tf_op jit(solution)/shard_map/ppermute | solution.py:502
  87.4 9.0 %collective-permute-start.25 = (bf16[528,256]{1,0:T(8,128)(2,1)S(1)}, bf16[528,256]{1,0:T(8,128)(2,1)S(1)}, u32[]{:S(2)}, u32[]{:S(2)}) collective-permute-start(bf16[528,256]{1,0:T(8,128)(2,1)S(1)} %get-tuple-element.160), channel_id=1, source_target_pairs={{0,16},{8,24},{16,32},{24,40},{32,48},{40,56},{48,0},{56,8},{64,80... | collective-permute-start | bytes 811016 | tf_op jit(solution)/shard_map/ppermute | solution.py:502
  89.1 6.6 %collective-permute-start.26 = (bf16[256,256]{1,0:T(8,128)(2,1)S(1)}, bf16[256,256]{1,0:T(8,128)(2,1)S(1)}, u32[]{:S(2)}, u32[]{:S(2)}) collective-permute-start(bf16[256,256]{1,0:T(8,128)(2,1)S(1)} %get-tuple-element.161), channel_id=1, source_target_pairs={{0,1},{1,0},{2,3},{3,2},{4,5},{5,4},{6,7},{7,6},{8,9},{9,8},{10,11... | collective-permute-start | bytes 393224 | tf_op jit(solution)/shard_map/ppermute | solution.py:502
  96.5 5.1 %collective-permute-start.27 = (bf16[272,256]{1,0:T(8,128)(2,1)S(1)}, bf16[272,256]{1,0:T(8,128)(2,1)S(1)}, u32[]{:S(2)}, u32[]{:S(2)}) collective-permute-start(bf16[272,256]{1,0:T(8,128)(2,1)S(1)} %get-tuple-element.167), channel_id=1, source_target_pairs={{0,64},{8,72},{16,80},{24,88},{32,96},{40,104},{48,112},{56,120},{... | collective-permute-start | bytes 417800 | tf_op jit(solution)/shard_map/ppermute | solution.py:502

commit v5 on v4

--- a/solution.py
+++ b/solution.py
@@ -81,6 +81,7 @@
     n = NX * NZ
     steps = n // 2
     chunks = rows // T
+    deep = 2 * T
     first_call = group == "near"
     last_call = group == "mid"
     if first_call:
@@ -89,11 +90,15 @@
         (users_t,), refs = refs[:1], refs[1:]
     ads_refs, refs = refs[:n_ads], refs[n_ads:]
     (logc_ref, pos_ref), refs = refs[:2], refs[2:]
+    if first_call:
+        (ads_t,), refs = refs[:1], refs[1:]
     if not first_call:
         (acc_in, m_in, total_in, hit_in), refs = refs[:4], refs[4:]
-    (p_ref, top_ref, ads_t, acc_ref, m_ref, total_ref, hit_ref), refs = refs[:7], refs[7:]
+    (p_ref, top_ref, acc_ref, m_ref, total_ref, hit_ref), refs = refs[:6], refs[6:]
     if first_call:
         (staged, users_t), refs = refs[:2], refs[2:]
+    else:
+        (ads_t,), refs = refs[:1], refs[1:]
     if last_call:
         (stats_ref,), refs = refs[:1], refs[1:]
     ads_all, logc_all, s0, s1, *late = refs
@@ -108,7 +113,8 @@
         spot += r.shape[0]
     for c in range(chunks):
         part = slice(c * T, (c + 1) * T)
-        ads_t[:, part] = ads_all[part, :].T
+        if not first_call:
+            ads_t[:, part] = ads_all[part, :].T
         logc = logc_ref[:, pl.ds(first_row(group, c), T)]
         logc_all[part, :] = jnp.broadcast_to(logc, (LANES, T)).T
 
@@ -119,20 +125,21 @@
         def __init__(self, tile, dst):
             self.cols, self.dst = columns(tile), dst
             self.side = users_t[:, self.cols]
-            self.pos = pos_ref[:, self.cols] - lax.broadcasted_iota(jnp.int32, (8, T), 0)
-            self.best = jnp.full((8, T), -jnp.inf, F32)
-            self.found = jnp.zeros((8, T), F32)
+            self.pos = pos_ref[:, self.cols] - lax.broadcasted_iota(jnp.int32, (16, T), 0)
+            self.best = jnp.full((16, T), -jnp.inf, F32)
+            self.found = jnp.zeros((16, T), F32)
 
         def chunk(self, c):
-            ahead = self.pos - first_row(group, c)
-            prod = jnp.dot(ads_all[c * T : (c + 1) * T, :], self.side, preferred_element_type=F32)
-            for r in range(0, T, 8):
-                row = c * T + r
-                logc = logc_all[row : row + 8, :]
-                x = prod[r : r + 8, :] - jnp.concatenate([logc] * (T // LANES), axis=1)
-                self.dst[row : row + 8, :] = x
-                self.best = jnp.maximum(self.best, x)
-                self.found = jnp.where(ahead == r, x, self.found)
+            prod = jnp.dot(ads_all[c * deep : (c + 1) * deep, :], self.side, preferred_element_type=F32)
+            for half in range(2):
+                ahead = self.pos - first_row(group, 2 * c + half)
+                for r in range(0, T, 16):
+                    row = half * T + r
+                    at = slice(c * deep + row, c * deep + row + 16)
+                    x = prod[row : row + 16, :] - jnp.concatenate([logc_all[at, :]] * (T // LANES), axis=1)
+                    self.dst[at, :] = x
+                    self.best = jnp.maximum(self.best, x)
+                    self.found = jnp.where(ahead == r, x, self.found)
 
         def end(self):
             top_ref[:, self.cols] = jnp.max(self.best, axis=0, keepdims=True)
@@ -143,12 +150,12 @@
         def __init__(self, tile, src, extra):
             self.cols, self.src, self.extra = columns(tile), src, extra
             self.top = top_ref[:, self.cols]
-            self.total = jnp.zeros((8, T), F32)
+            self.total = jnp.zeros((16, T), F32)
 
         def chunk(self, c):
-            for r in range(c * T, (c + 1) * T, 16):
+            for r in range(c * deep, (c + 1) * deep, 16):
                 e = jnp.exp(self.src[r : r + 16, :] - self.top)
-                self.total += e[:8] + e[8:]
+                self.total += e
                 e = e.astype(BF16)
                 p_ref[r : r + 16, self.cols] = e
                 self.extra[r : r + 16, :] = e
@@ -176,14 +183,14 @@
     def turn(tile, src, dst, e_now, e_before):
         gather(jnp.maximum(tile - 1, 0), e_before)
         product, exps = Product(jnp.minimum(tile + 1, n - 1), dst), Exps(tile, src, e_now)
-        for c in range(chunks):
+        for c in range(chunks // 2):
             product.chunk(c)
             exps.chunk(c)
         product.end()
         exps.end()
 
     opening = Product(0, s0)
-    for c in range(chunks):
+    for c in range(chunks // 2):
         opening.chunk(c)
     opening.end()
     e0, e1 = late
@@ -218,7 +225,6 @@
     out_shape = [
         jax.ShapeDtypeStruct((count, total), BF16),
         row,
-        jax.ShapeDtypeStruct((width, count), BF16),
         jax.ShapeDtypeStruct((width, total), F32),
         row,
         row,
@@ -227,6 +233,8 @@
     if group == "near":
         out_shape.append(jax.ShapeDtypeStruct((total, width), BF16))
         out_shape.append(jax.ShapeDtypeStruct((width, total), BF16))
+    else:
+        out_shape.append(jax.ShapeDtypeStruct((width, count), BF16))
     if group == "mid":
         out_shape.append(jax.ShapeDtypeStruct((stats_rows, LANES), F32))
     scratch = [
@@ -247,18 +255,23 @@
     )
 
 
-GROUPS = ("near", "far", "mid")
-
-
-def rows_kernel(sizes, start, *refs):
-    ads_refs, (pos_ref, out_ref, h0, h1) = refs[: len(sizes)], refs[len(sizes) :]
+def rows_kernel(groups, sizes, start, *refs):
+    ads_refs, refs = refs[: len(sizes)], refs[len(sizes) :]
+    (pos_ref, out_ref), refs = refs[:2], refs[2:]
+    if groups == ("near",):
+        (ads_t, h0, h1) = refs
+        for spot in range(0, sizes[0], T):
+            ads_t[:, spot : spot + T] = ads_refs[0][spot : spot + T, :].T
+        ads_refs = (ads_t,)
+    else:
+        h0, h1 = refs
     tiles = out_ref.shape[1] // T
 
     def build(tile, dst):
         cols = pl.ds(pl.multiple_of(start + tile * T, T), T)
         pos = pos_ref[:, cols] - lax.broadcasted_iota(jnp.int32, (16, T), 0)
         spot = 0
-        for group, size in zip(GROUPS, sizes):
+        for group, size in zip(groups, sizes):
             for c in range(size // T):
                 ahead = pos - first_row(group, c)
                 for r in range(0, T, 16):
@@ -284,28 +297,32 @@
         build(jnp.minimum(2 * step + 2, tiles - 1), h0)
 
 
-def run_rows(ads_t, positives, start, total):
-    width = ads_t[0].shape[0]
-    sizes = [x.shape[1] for x in ads_t]
+def run_rows(groups, ads, positives, start, total):
+    near = groups == ("near",)
+    sizes = [x.shape[0] if near else x.shape[1] for x in ads]
+    width = ads[0].shape[1] if near else ads[0].shape[0]
+    out_shape = [jax.ShapeDtypeStruct((width, total), BF16)]
+    if near:
+        out_shape.append(jax.ShapeDtypeStruct((width, sizes[0]), BF16))
     return call(
-        lambda *refs: rows_kernel(sizes, start, *refs),
-        "positive_rows",
-        [jax.ShapeDtypeStruct((width, total), BF16)],
+        lambda *refs: rows_kernel(groups, sizes, start, *refs),
+        "positive_rows_" + groups[0],
+        out_shape,
         [pltpu.VMEM((sum(sizes), T), BF16)] * 2,
-        (*ads_t, positives),
+        (*ads, positives),
         cost(sum(sizes), total, width),
-    )[0]
-
-
-def users_kernel(inv, acc_ref, m_ref, rows_a, rows_b, hit_ref, weight_ref, *rest):
+    )
+
+
+def users_kernel(inv, acc_ref, m_ref, rows_n, rows_a, rows_b, hit_ref, weight_ref, *rest):
     stats_in, rest = rest[:NX], rest[NX:]
     du_refs, (lse_ref, coef_ref, loss_ref, stats_ref, rows_ref) = rest[:USER_PARTS], rest[USER_PARTS:]
     n = NX * NZ
     width = n * T // LANES
     for j in range(NX):
         stats_ref[pl.ds(lax.rem(lax.axis_index("aa") // NZ + NX - j, NX), 1)] = stats_in[j][...][None]
-    rows_ref[:, : n * T // 2] = rows_a[...]
-    rows_ref[:, n * T // 2 :] = rows_b[...]
+    rows_ref[:, : n * T // 2] = plus(rows_n[:, : n * T // 2], rows_a[...]).astype(BF16)
+    rows_ref[:, n * T // 2 :] = plus(rows_n[:, n * T // 2 :], rows_b[...]).astype(BF16)
     tops = stats_ref[:, :width, :]
     top = jnp.max(tops, axis=0)
     lse = top + jnp.log(jnp.sum(jnp.exp(tops - top[None]), axis=0))
@@ -331,7 +348,7 @@
     du_refs[4][...] = users_at(2, 1)
 
 
-def run_users(acc, m, rows_a, rows_b, hits, weights, stats, inv):
+def run_users(acc, m, rows_n, rows_a, rows_b, hits, weights, stats, inv):
     width, total = acc.shape
     row = jax.ShapeDtypeStruct((1, total), F32)
     shapes = [(NZ * width, T)] * 3 + [(width, T)] * 2
@@ -342,97 +359,94 @@
         "grad_users",
         out_shape,
         [pltpu.VMEM((NX, *stats[0].shape), F32), pltpu.VMEM((width, total), BF16)],
-        (acc, m, rows_a, rows_b, hits, weights, *stats),
-    )
-
-
-def grads_kernel(group, users_ref, p_ref, top_ref, lse_ref, coef_ref, weight_ref, pos_ref, loss_in, *refs):
-    outs, qs = refs[:-2], refs[-2:]
+        (acc, m, rows_n, rows_a, rows_b, hits, weights, *stats),
+    )
+
+
+def grads_kernel(
+    group, users_ref, p_ref, p_mid, top_ref, top_mid, lse_ref, coef_ref, weight_ref, pos_ref, loss_in, da_ref, *qs
+):
     deep = 2 * T
-    count, total = p_ref.shape
+    total = p_ref.shape[1]
+    mine = [(group, p_ref, top_ref, unit) for unit in range(p_ref.shape[0] // deep)]
+    units = mine + [("mid", p_mid, top_mid, 0 if group == "near" else 1)]
 
     def build(unit, dst):
+        name, p, tops, at = units[unit]
         for b in range(total // T):
             cols = slice(b * T, (b + 1) * T)
-            scale = weight_ref[:, cols] * jnp.exp(top_ref[:, cols] - lse_ref[:, cols])
+            scale = weight_ref[:, cols] * jnp.exp(tops[:, cols] - lse_ref[:, cols])
             coef = coef_ref[:, cols]
             pos = pos_ref[:, cols] - lax.broadcasted_iota(jnp.int32, (16, T), 0)
             for half in range(2):
-                ahead = pos - first_row(group, 2 * unit + half)
+                ahead = pos - first_row(name, 2 * at + half)
                 for r in range(0, T, 16):
                     row = half * T + r
-                    scaled = p_ref[unit * deep + row : unit * deep + row + 16, cols].astype(F32) * scale
+                    scaled = p[at * deep + row : at * deep + row + 16, cols].astype(F32) * scale
                     dst[row : row + 16, cols] = jnp.where(ahead == r, coef, scaled).astype(BF16)
 
-    def product(unit, src):
-        da = jnp.dot(src[...], users_ref[...], preferred_element_type=F32).astype(BF16)
-        if group == "mid":
-            outs[unit][:deep, :] = da
-        else:
-            outs[0][unit * deep : (unit + 1) * deep, :] = da
-
-    units = count // deep
     build(0, qs[0])
-    for unit in range(units):
-        product(unit, qs[unit % 2])
-        if unit + 1 < units:
+    for unit in range(len(units)):
+        da = jnp.dot(qs[unit % 2][...], users_ref[...], preferred_element_type=F32)
+        da_ref[unit * deep : (unit + 1) * deep, :] = da.astype(BF16)
+        if unit + 1 < len(units):
             build(unit + 1, qs[(unit + 1) % 2])
-    if group == "mid":
-        outs[1][deep:, :] = loss_in[...]
-
-
-def run_grads(group, users, p, top, lse, coefs, weights, positives, loss):
-    count, total = p.shape
-    width = users.shape[1]
-    deep = 2 * T
-    shapes = [(deep, width), (deep + EXTRA, width)] if group == "mid" else [(count, width)]
+    da_ref[len(units) * deep :, :] = loss_in[...]
+
+
+def run_grads(group, users, p, p_mid, top, top_mid, lse, coefs, weights, positives, loss):
+    total, width = users.shape
+    count = p.shape[0] + p_mid.shape[0] // 2
     return call(
         lambda *refs: grads_kernel(group, *refs),
         "grads_" + group,
-        [jax.ShapeDtypeStruct(x, BF16) for x in shapes],
-        [pltpu.VMEM((deep, total), BF16)] * 2,
-        (users, p, top, lse, coefs, weights, positives, loss),
+        [jax.ShapeDtypeStruct((count + EXTRA, width), BF16)],
+        [pltpu.VMEM((2 * T, total), BF16)] * 2,
+        (users, p, p_mid, top, top_mid, lse, coefs, weights, positives, loss),
         cost(count, total, width),
-    )
+    )[0]
 
 
 def simple_call(kernel, name, out_shape, *args):
     return call(kernel, name, out_shape, [], args)
 
 
-def add_mid(near, loss, back):
-    width = near.shape[1]
-
-    def kernel(near_ref, loss_ref, back_ref, first, second, both_ref):
-        both = plus(loss_ref[...], back_ref[NZ * T :, :]).astype(BF16)
-        first[:T, :] = plus(near_ref[:T, :], back_ref[:T, :]).astype(BF16)
-        first[T:, :] = both
-        second[...] = plus(near_ref[T:, :], back_ref[T : NZ * T, :]).astype(BF16)
-        both_ref[...] = both
-
-    shapes = [(T + EXTRA, width), (T, width), (EXTRA, width)]
-    shapes = [jax.ShapeDtypeStruct(x, BF16) for x in shapes]
-    return simple_call(kernel, "add_mid", shapes, near, loss, back)
-
-
-def add_near(near, back, both, first, second):
+def add_cores(near, back):
     width = near.shape[1]
     rows = NZ * T
 
-    def kernel(near_ref, back_ref, both_ref, first_ref, second_ref, keep, one, three):
-        total = plus(near_ref[...], back_ref[...])
-        keep[:rows, :] = total[:rows]
-        keep[rows:, :] = both_ref[...].astype(F32)
-        one[:T, :] = plus(total[rows : rows + T], first_ref[:T, :]).astype(BF16)
-        one[T:rows, :] = total[rows + T : 2 * rows].astype(BF16)
-        one[rows:, :] = plus(both_ref[...], first_ref[T:, :]).astype(BF16)
-        three[:T, :] = total[2 * rows : 2 * rows + T].astype(BF16)
-        three[T:rows, :] = plus(total[2 * rows + T :], second_ref[...]).astype(BF16)
-        three[rows:, :] = both_ref[...]
-
-    shape = jax.ShapeDtypeStruct((rows + EXTRA, width), BF16)
-    shapes = [jax.ShapeDtypeStruct((rows + EXTRA, width), F32), shape, shape]
-    return simple_call(kernel, "add_near", shapes, near, back, both, first, second)
+    def kernel(near_ref, back_ref, first, second, keep, one, three):
+        both = plus(near_ref[NY * rows :, :], back_ref[NY * rows :, :])
+
+        def place(i):
+            return plus(near_ref[i * rows : (i + 1) * rows, :], back_ref[i * rows : (i + 1) * rows, :])
+
+        two = place(3)
+        first[:T, :] = two[:T].astype(BF16)
+        first[T:, :] = both.astype(BF16)
+        second[...] = two[T:].astype(BF16)
+        for i, out in enumerate((keep, one, three)):
+            out[:rows, :] = place(i)
+            out[rows:, :] = both
+
+    shapes = [jax.ShapeDtypeStruct((T + EXTRA, width), BF16), jax.ShapeDtypeStruct((T, width), BF16)]
+    shapes += [jax.ShapeDtypeStruct((rows + EXTRA, width), F32)] * 3
+    return simple_call(kernel, "add_cores", shapes, near, back)
+
+
+def add_place_2(one, three, first, second):
+    rows = NZ * T
+
+    def kernel(one_ref, three_ref, first_ref, second_ref, out1, out3):
+        out1[:T, :] = plus(one_ref[:T, :], first_ref[:T, :]).astype(BF16)
+        out1[T:rows, :] = one_ref[T:rows, :].astype(BF16)
+        out1[rows:, :] = plus(one_ref[rows:, :], first_ref[T:, :]).astype(BF16)
+        out3[:T, :] = three_ref[:T, :].astype(BF16)
+        out3[T:rows, :] = plus(three_ref[T:rows, :], second_ref[...]).astype(BF16)
+        out3[rows:, :] = three_ref[rows:, :].astype(BF16)
+
+    shapes = [jax.ShapeDtypeStruct(one.shape, BF16)] * 2
+    return simple_call(kernel, "add_place_2", shapes, one, three, first, second)
 
 
 def add_rows(*parts):
@@ -539,43 +553,42 @@
     far = swap_core(near)
     parts = (user_pair, user_1, user_3, user_2a, user_2b)
 
-    p_near, top_near, at_near, acc, m, total, hits, staged, users_t = run_logits(
-        "near", parts, (near,), logc, pos_row, inv
+    rows_n, at_near = run_rows(("near",), (near,), pos_row, 0, positives.shape[0])
+    p_near, top_near, acc, m, total, hits, staged, users_t = run_logits(
+        "near", parts, (near,), logc, pos_row, inv, (at_near,)
     )
     ads_2a, ads_2b, hits = lax.optimization_barrier((ads_2a, ads_2b, hits))
     near_2 = jnp.concatenate([ads_2a, ads_2b], axis=0)
     far_2 = swap_core(near_2)
-    p_far, top_far, at_far, acc, m, total, hits = run_logits(
+    p_far, top_far, acc, m, total, hits, at_far = run_logits(
         "far", (users_t,), (far,), logc, pos_row, inv, (acc, m, total, hits)
     )
-    p_mid, top_mid, at_mid, acc, m, total, hits, stats = run_logits(
+    p_mid, top_mid, acc, m, total, hits, at_mid, stats = run_logits(
         "mid", (users_t,), (near_2, far_2), logc, pos_row, inv, (acc, m, total, hits)
     )
-    half = stats.shape[0] * LANES // 4
-    ads_t = (at_near, at_far, at_mid)
-    stats_z, rows_a = lax.optimization_barrier((swap_z_hi(stats), run_rows(ads_t, pos_row, 0, half)))
+    half = positives.shape[0] // 2
+    later = (("far", "mid"), (at_far, at_mid), pos_row)
+    stats_z, (rows_a,) = lax.optimization_barrier((swap_z_hi(stats), run_rows(*later, 0, half)))
     stats = join_stats(stats, stats_z)
     moved = tuple(shift_x(stats, j) for j in range(1, NX))
-    moved, rows_b = lax.optimization_barrier((moved, run_rows(ads_t, pos_row, half, half)))
+    moved, (rows_b,) = lax.optimization_barrier((moved, run_rows(*later, half, half)))
     du_0, du_1, du_3, du_2a, du_2b, lse, coefs, loss = run_users(
-        acc, m, rows_a, rows_b, hits, weight_row, (stats, *moved), inv
+        acc, m, rows_n, rows_a, rows_b, hits, weight_row, (stats, *moved), inv
     )
     tail = (lse, coefs, weight_row, pos_row, loss)
     du_2a, du_2b = shift_x(du_2a, 1), shift_x(du_2b, -1)
-    da_2, pay_2 = run_grads("mid", staged, p_mid, top_mid, *tail)
-    back_2 = swap_core(pay_2)
-    da_2, staged = lax.optimization_barrier((da_2, staged))
-    (da_far,) = run_grads("far", staged, p_far, top_far, *tail)
-    da_far, back_2, du_2a, du_2b = lax.optimization_barrier((da_far, back_2, du_2a, du_2b))
+    da_far = run_grads("far", staged, p_far, p_mid, top_far, top_mid, *tail)
+    da_far, du_2a, du_2b = lax.optimization_barrier((da_far, du_2a, du_2b))
+    back = swap_core(da_far)
     du_1, du_3 = add_halves(du_1, du_3, du_2a, du_2b)
-    back = swap_core(da_far)
-    first, second, both = add_mid(da_2, loss, back_2)
-    first, second, du_1, du_3, staged = lax.optimization_barrier((first, second, du_1, du_3, staged))
+    du_1, du_3, staged = lax.optimization_barrier((du_1, du_3, staged))
+    da_near = run_grads("near", staged, p_near, p_mid, top_near, top_mid, *tail)
+    first, second, kept, one, three = add_cores(da_near, back)
+    first, second, du_1, du_3 = lax.optimization_barrier((first, second, du_1, du_3))
     first, second = shift_y(first, -1), shift_y(second, 1)
     du_1, du_3 = shift_x(du_1, 1), shift_x(du_3, -1)
-    (da_near,) = run_grads("near", staged, p_near, top_near, *tail)
-    da_near, first, second, du_1, du_3 = lax.optimization_barrier((da_near, first, second, du_1, du_3))
-    kept, one, three = add_near(da_near, back, both, first, second)
+    first, second, du_1, du_3 = lax.optimization_barrier((first, second, du_1, du_3))
+    one, three = add_place_2(one, three, first, second)
     one, three = shift_y(one, -1), shift_y(three, 1)
     keep_u, send_u = add_users((du_0, du_1, du_3))
     one, three, received_u = lax.optimization_barrier((one, three, swap_z_hi(send_u)))

time: 103 us -> 105 us (1.019)
  waiting for transfers between devices: 32.3 us -> 33.6 us
  Pallas kernels: 33.2 us -> 34.4 us
    ppermute x28 -> x27, waiting for transfers between devices: 32.3 us -> 33.6 us  [move(): lax.ppermute(x, axis, [(i, target(i)) for i in range(lax.axis_size(axis))])]
    pallas_call x16, Pallas kernels: 33.2 us -> 34.4 us  [call(): pl.pallas_call(kernel, in_specs=[vmem] * len(args), out_specs=[vmem] * le...]
    ppermute x28 -> x27, starting transfers between devices: 32.8 us -> 32.9 us  [move(): lax.ppermute(x, axis, [(i, target(i)) for i in range(lax.axis_size(axis))])]
  transfers between devices with their start and end apart: 28 -> 27, of which waited for: 15 -> 13; matrix products, arithmetic and copies ran while one was open for 3% -> 3% of each run, Pallas kernels for 24% -> 25%
where the time goes in v5:
time: 105 us
  Pallas kernels  34.4 us (33%)
  waiting for transfers between devices  33.6 us (32%)
  starting transfers between devices  32.9 us (31%)
  local copies, waits for them, and re-layouts  1.97 us (2%)
  other arithmetic  1.43 us (1%)
    pallas_call x16, Pallas kernels, call(): pl.pallas_call(kernel, in_specs=[vmem] * len(args), out_specs=[vmem] * le...  34.4 us
    ppermute x27, waiting for transfers between devices, move(): lax.ppermute(x, axis, [(i, target(i)) for i in range(lax.axis_size(axis))])  33.6 us
    ppermute x27, starting transfers between devices, move(): lax.ppermute(x, axis, [(i, target(i)) for i in range(lax.axis_size(axis))])  32.9 us
  transfers between devices with their start and end apart: 27, of which 13 were waited for; matrix products, arithmetic and copies ran while one was open for 3% of the time, Pallas kernels for 25%

profile of v5, /device:TPU:0, one launch (start us, length us, event | category | flops | bytes accessed | tf_op | source)
XLA Modules:
  0.0 105.2 jit_solution(15315693251953616567)
XLA Ops:
  0.6 4.0 %collective-permute-start = (bf16[256,256]{1,0:T(8,128)(2,1)}, bf16[256,256]{1,0:T(8,128)(2,1)S(1)}, u32[]{:S(2)}, u32[]{:S(2)}) collective-permute-start(bf16[256,256]{1,0:T(8,128)(2,1)} %param.5), channel_id=1, source_target_pairs={{0,1},{1,0},{2,3},{3,2},{4,5},{5,4},{6,7},{7,6},{8,9},{9,8},{10,11... | collective-permute-start | bytes 393224 | tf_op jit(solution)/shard_map/ppermute | solution.py:516
  9.2 2.7 %collective-permute-done.1 = bf16[256,256]{1,0:T(8,128)(2,1)S(1)} collective-permute-done((bf16[256,256]{1,0:T(8,128)(2,1)}, bf16[256,256]{1,0:T(8,128)(2,1)S(1)}, u32[]{:S(2)}, u32[]{:S(2)}) %collective-permute-start.1) | collective-permute-done | bytes 131104 | tf_op jit(solution)/shard_map/ppermute | solution.py:516
  11.9 2.8 %collective-permute-start.3 = (bf16[512,256]{1,0:T(8,128)(2,1)S(1)}, bf16[512,256]{1,0:T(8,128)(2,1)S(1)}, u32[]{:S(2)}, u32[]{:S(2)}) collective-permute-start(bf16[512,256]{1,0:T(8,128)(2,1)S(1)} %constant_dynamic-update-slice_fusion.refs_0_), channel_id=1, source_target_pairs={{0,6},{1,7},{2,0},{3,1},{4,2},{5,3},{6,4},{7,5},{8,14},{9,15},{10,... | collective-permute-start | bytes 786440 | tf_op jit(solution)/shard_map/ppermute | solution.py:516
  14.8 3.1 %collective-permute-start.5 = (bf16[512,256]{1,0:T(8,128)(2,1)S(1)}, bf16[512,256]{1,0:T(8,128)(2,1)S(1)}, u32[]{:S(2)}, u32[]{:S(2)}) collective-permute-start(bf16[512,256]{1,0:T(8,128)(2,1)S(1)} %get-tuple-element.168), channel_id=1, source_target_pairs={{0,48},{8,56},{16,0},{24,8},{32,16},{40,24},{48,32},{56,40},{64,11... | collective-permute-start | bytes 786440 | tf_op jit(solution)/shard_map/ppermute | solution.py:516
  17.9 1.6 %collective-permute-done.3.refs_2_ = bf16[512,256]{1,0:T(8,128)(2,1)S(1)} collective-permute-done((bf16[512,256]{1,0:T(8,128)(2,1)S(1)}, bf16[512,256]{1,0:T(8,128)(2,1)S(1)}, u32[]{:S(2)}, u32[]{:S(2)}) %collective-permute-start.3) | collective-permute-done | bytes 262176 | tf_op jit(solution)/shard_map/ppermute | solution.py:516
  19.5 3.4 %collective-permute-done.2.refs_1_ = bf16[512,256]{1,0:T(8,128)(2,1)S(1)} collective-permute-done((bf16[512,256]{1,0:T(8,128)(2,1)S(1)}, bf16[512,256]{1,0:T(8,128)(2,1)S(1)}, u32[]{:S(2)}, u32[]{:S(2)}) %collective-permute-start.2) | collective-permute-done | bytes 262176 | tf_op jit(solution)/shard_map/ppermute | solution.py:516
  22.9 2.8 %collective-permute-done.4 = bf16[512,256]{1,0:T(8,128)(2,1)S(1)} collective-permute-done((bf16[512,256]{1,0:T(8,128)(2,1)S(1)}, bf16[512,256]{1,0:T(8,128)(2,1)S(1)}, u32[]{:S(2)}, u32[]{:S(2)}) %collective-permute-start.4) | collective-permute-done | bytes 262176 | tf_op jit(solution)/shard_map/ppermute | solution.py:516
  25.9 3.1 %collective-permute-start.7 = (bf16[256,256]{1,0:T(8,128)(2,1)S(1)}, bf16[256,256]{1,0:T(8,128)(2,1)S(1)}, u32[]{:S(2)}, u32[]{:S(2)}) collective-permute-start(bf16[256,256]{1,0:T(8,128)(2,1)S(1)} %slice.13), channel_id=1, source_target_pairs={{0,6},{1,7},{2,0},{3,1},{4,2},{5,3},{6,4},{7,5},{8,14},{9,15},{10,... | collective-permute-start | bytes 393224 | tf_op jit(solution)/shard_map/ppermute | solution.py:516
  29.3 1.8 %collective-permute-start.8 = (bf16[256,256]{1,0:T(8,128)(2,1)S(1)}, bf16[256,256]{1,0:T(8,128)(2,1)S(1)}, u32[]{:S(2)}, u32[]{:S(2)}) collective-permute-start(bf16[256,256]{1,0:T(8,128)(2,1)S(1)} %slice.14), channel_id=1, source_target_pairs={{0,16},{8,24},{16,32},{24,40},{32,48},{40,56},{48,0},{56,8},{64,80... | collective-permute-start | bytes 393224 | tf_op jit(solution)/shard_map/ppermute | solution.py:516
  31.1 2.7 %positive_rows_near.1 = (bf16[256,2048]{1,0:T(8,128)(2,1)S(1)}, bf16[256,1536]{1,0:T(8,128)(2,1)S(1)}) custom-call(bf16[1536,256]{1,0:T(8,128)(2,1)S(1)} %constant_dynamic-update-slice_fusion.4.refs_0_.refs_5_, s32[1,2048]{1,0:T(1,128)S(1)} %bitcast.4), custom_call_target="tpu_custom_call" | custom-call | flops 100663296 | bytes 393216 | tf_op jit(solution)/shard_map/positive_rows_near/pallas_call | solution.py:23
  33.8 2.0 %collective-permute-done.6.refs_3_ = bf16[256,256]{1,0:T(8,128)(2,1)S(1)} collective-permute-done((bf16[256,256]{1,0:T(8,128)(2,1)S(1)}, bf16[256,256]{1,0:T(8,128)(2,1)S(1)}, u32[]{:S(2)}, u32[]{:S(2)}) %collective-permute-start.6) | collective-permute-done | bytes 131104 | tf_op jit(solution)/shard_map/ppermute | solution.py:516
  35.8 7.1 %logits_near.1 = (bf16[1536,2048]{1,0:T(8,128)(2,1)S(1)}, f32[1,2048]{1,0:T(1,128)S(1)}, f32[256,2048]{1,0:T(8,128)S(1)}, f32[1,2048]{1,0:T(1,128)S(1)}, f32[1,2...) custom-call(bf16[512,256]{1,0:T(8,128)(2,1)S(1)} %constant_dynamic-update, ...), custom_call_target="tpu_custom_call" | custom-call | flops 100663296 | bytes 393216 | tf_op jit(solution)/shard_map/logits_near/pallas_call | solution.py:23
  43.1 7.0 %logits_far.1 = (bf16[1536,2048]{1,0:T(8,128)(2,1)S(1)}, f32[1,2048]{1,0:T(1,128)S(1)}, f32[256,2048]{1,0:T(8,128)S(1)}, f32[1,2048]{1,0:T(1,128)S(1)}, f32[1,20...) custom-call(bf16[256,2048]{1,0:T(8,128)(2,1)S(1)} %get-tuple-element.94.refs_0_, ...), custom_call_target="tpu_custom_call" | custom-call | flops 100663296 | bytes 393216 | tf_op jit(solution)/shard_map/logits_far/pallas_call | solution.py:23
  50.0 5.5 %logits_mid.1 = (bf16[1024,2048]{1,0:T(8,128)(2,1)S(1)}, f32[1,2048]{1,0:T(1,128)S(1)}, f32[256,2048]{1,0:T(8,128)S(1)}, f32[1,2048]{1,0:T(1,128)S(1)}, f32[1,20...) custom-call(bf16[256,2048]{1,0:T(8,128)(2,1)S(1)} %get-tuple-element.94.refs_0_, ...), custom_call_target="tpu_custom_call" | custom-call | flops 67108864 | bytes 262144 | tf_op jit(solution)/shard_map/logits_mid/pallas_call | solution.py:23
  55.5 1.2 %collective-permute-start.12 = (f32[32,128]{1,0:T(8,128)S(1)}, f32[32,128]{1,0:T(8,128)S(1)}, u32[]{:S(2)}, u32[]{:S(2)}) collective-permute-start(f32[32,128]{1,0:T(8,128)S(1)} %get-tuple-element.109.own_ref), channel_id=1, source_target_pairs={{0,1},{1,0},{2,3},{3,2},{4,5},{5,4},{6,7},{7,6},{8,9},{9,8},{10,11... | collective-permute-start | bytes 49160 | tf_op jit(solution)/shard_map/ppermute | solution.py:516
  56.7 1.9 %positive_rows_far.2.refs_3_ = bf16[256,1024]{1,0:T(8,128)(2,1)S(1)} custom-call(bf16[256,1536]{1,0:T(8,128)(2,1)S(1)} %get-tuple-element.110.refs_0_, bf16[256,1024]{1,0:T(8,128)(2,1)S(1)} %get-tuple-element.111.refs_1_, s32[1,2048]{1,0:T(1,128)S(1)} %bitcast.8), custom_call_target="tpu_custom_call" | custom-call | flops 83886080 | bytes 327680 | tf_op jit(solution)/shard_map/positive_rows_far/pallas_call | solution.py:23
  58.7 2.1 %collective-permute-done.12.other_ref = f32[32,128]{1,0:T(8,128)S(1)} collective-permute-done((f32[32,128]{1,0:T(8,128)S(1)}, f32[32,128]{1,0:T(8,128)S(1)}, u32[]{:S(2)}, u32[]{:S(2)}) %collective-permute-start.12) | collective-permute-done | bytes 16416 | tf_op jit(solution)/shard_map/ppermute | solution.py:516
  60.8 1.3 %collective-permute-start.15 = (f32[32,128]{1,0:T(8,128)S(1)}, f32[32,128]{1,0:T(8,128)S(1)}, u32[]{:S(2)}, u32[]{:S(2)}) collective-permute-start(f32[32,128]{1,0:T(8,128)S(1)} %join_stats.1.refs_7_), channel_id=1, source_target_pairs={{0,6},{1,7},{2,0},{3,1},{4,2},{5,3},{6,4},{7,5},{8,14},{9,15},{10,... | collective-permute-start | bytes 49160 | tf_op jit(solution)/shard_map/ppermute | solution.py:516
  63.1 1.9 %positive_rows_far.3.refs_4_ = bf16[256,1024]{1,0:T(8,128)(2,1)S(1)} custom-call(bf16[256,1536]{1,0:T(8,128)(2,1)S(1)} %get-tuple-element.110.refs_0_, bf16[256,1024]{1,0:T(8,128)(2,1)S(1)} %get-tuple-element.111.refs_1_, s32[1,2048]{1,0:T(1,128)S(1)} %bitcast.9), custom_call_target="tpu_custom_call" | custom-call | flops 83886080 | bytes 327680 | tf_op jit(solution)/shard_map/positive_rows_far/pallas_call | solution.py:23
  65.1 2.4 %collective-permute-done.14.refs_9_ = f32[32,128]{1,0:T(8,128)S(1)} collective-permute-done((f32[32,128]{1,0:T(8,128)S(1)}, f32[32,128]{1,0:T(8,128)S(1)}, u32[]{:S(2)}, u32[]{:S(2)}) %collective-permute-start.14) | collective-permute-done | bytes 16416 | tf_op jit(solution)/shard_map/ppermute | solution.py:516
  67.5 1.1 %grad_users.1 = (bf16[512,256]{1,0:T(8,128)(2,1)S(1)}, bf16[512,256]{1,0:T(8,128)(2,1)S(1)}, bf16[512,256]{1,0:T(8,128)(2,1)S(1)}, bf16[256,256]{1,0:T(8,128)(2,...) custom-call(f32[256,2048]{1,0:T(8,128)S(1)} %get-tuple-element.106.r, ...), custom_call_target="tpu_custom_call" | custom-call | tf_op jit(solution)/shard_map/grad_users/pallas_call | solution.py:23
  69.4 2.6 %collective-permute-start.17 = (bf16[256,256]{1,0:T(8,128)(2,1)S(1)}, bf16[256,256]{1,0:T(8,128)(2,1)S(1)}, u32[]{:S(2)}, u32[]{:S(2)}) collective-permute-start(bf16[256,256]{1,0:T(8,128)(2,1)S(1)} %get-tuple-element.131), channel_id=1, source_target_pairs={{0,6},{1,7},{2,0},{3,1},{4,2},{5,3},{6,4},{7,5},{8,14},{9,15},{10,... | collective-permute-start | bytes 393224 | tf_op jit(solution)/shard_map/ppermute | solution.py:516
  71.9 2.8 %grads_far.1 = bf16[2064,256]{1,0:T(8,128)(2,1)S(1)} custom-call(bf16[2048,256]{1,0:T(8,128)(2,1)S(1)} %get-tuple-element.136.refs_0_, bf16[1536,2048]{1,0:T(8,128)(2,1)S(1)} %get-tuple-element.123.refs_1_, bf16[1024,2048]{1,0:T(8,128)(2,1)S(1)} %get-tuple-element.124.refs_2_, f32[1,2048]{1,0:T(1,128)S(1)} %get-tuple-element.125.refs_3_, ...), custom_call_target="tpu_custom_call" | custom-call | flops 134217728 | bytes 524288 | tf_op jit(solution)/shard_map/grads_far/pallas_call | solution.py:23
  74.9 2.8 %grads_near.1.near_ref = bf16[2064,256]{1,0:T(8,128)(2,1)S(1)} custom-call(bf16[2048,256]{1,0:T(8,128)(2,1)S(1)} %get-tuple-element.136.refs_0_, bf16[1536,2048]{1,0:T(8,128)(2,1)S(1)} %get-tuple-element.137.refs_1_, bf16[1024,2048]{1,0:T(8,128)(2,1)S(1)} %get-tuple-element.124.refs_2_, f32[1,2048]{1,0:T(1,128)S(1)} %get-tuple-element.138.refs_3_, ...), custom_call_target="tpu_custom_call" | custom-call | flops 134217728 | bytes 524288 | tf_op jit(solution)/shard_map/grads_near/pallas_call | solution.py:23
  78.7 2.6 %collective-permute-start.22 = (bf16[512,256]{1,0:T(8,128)(2,1)S(1)}, bf16[512,256]{1,0:T(8,128)(2,1)S(1)}, u32[]{:S(2)}, u32[]{:S(2)}) collective-permute-start(bf16[512,256]{1,0:T(8,128)(2,1)S(1)} %get-tuple-element.147), channel_id=1, source_target_pairs={{0,6},{1,7},{2,0},{3,1},{4,2},{5,3},{6,4},{7,5},{8,14},{9,15},{10,... | collective-permute-start | bytes 786440 | tf_op jit(solution)/shard_map/ppermute | solution.py:516
  81.4 1.4 %collective-permute-start.19 = (bf16[272,256]{1,0:T(8,128)(2,1)S(1)}, bf16[272,256]{1,0:T(8,128)(2,1)S(1)}, u32[]{:S(2)}, u32[]{:S(2)}) collective-permute-start(bf16[272,256]{1,0:T(8,128)(2,1)S(1)} %get-tuple-element.144), channel_id=1, source_target_pairs={{0,48},{8,56},{16,0},{24,8},{32,16},{40,24},{48,32},{56,40},{64,11... | collective-permute-start | bytes 417800 | tf_op jit(solution)/shard_map/ppermute | solution.py:516
  83.4 5.9 %collective-permute-done.20.second_ref = bf16[256,256]{1,0:T(8,128)(2,1)S(1)} collective-permute-done((bf16[256,256]{1,0:T(8,128)(2,1)S(1)}, bf16[256,256]{1,0:T(8,128)(2,1)S(1)}, u32[]{:S(2)}, u32[]{:S(2)}) %collective-permute-start.20) | collective-permute-done | bytes 131104 | tf_op jit(solution)/shard_map/ppermute | solution.py:516
  89.9 1.6 %collective-permute-start.24 = (bf16[528,256]{1,0:T(8,128)(2,1)S(1)}, bf16[528,256]{1,0:T(8,128)(2,1)S(1)}, u32[]{:S(2)}, u32[]{:S(2)}) collective-permute-start(bf16[528,256]{1,0:T(8,128)(2,1)S(1)} %get-tuple-element.156), channel_id=1, source_target_pairs={{0,16},{8,24},{16,32},{24,40},{32,48},{40,56},{48,0},{56,8},{64,80... | collective-permute-start | bytes 811016 | tf_op jit(solution)/shard_map/ppermute | solution.py:516
  91.6 1.2 %collective-permute-start.25 = (bf16[256,256]{1,0:T(8,128)(2,1)S(1)}, bf16[256,256]{1,0:T(8,128)(2,1)S(1)}, u32[]{:S(2)}, u32[]{:S(2)}) collective-permute-start(bf16[256,256]{1,0:T(8,128)(2,1)S(1)} %get-tuple-element.157), channel_id=1, source_target_pairs={{0,1},{1,0},{2,3},{3,2},{4,5},{5,4},{6,7},{7,6},{8,9},{9,8},{10,11... | collective-permute-start | bytes 393224 | tf_op jit(solution)/shard_map/ppermute | solution.py:516
  92.8 5.3 %collective-permute-done.25.received_u_ref = bf16[256,256]{1,0:T(8,128)(2,1)S(1)} collective-permute-done((bf16[256,256]{1,0:T(8,128)(2,1)S(1)}, bf16[256,256]{1,0:T(8,128)(2,1)S(1)}, u32[]{:S(2)}, u32[]{:S(2)}) %collective-permute-start.25) | collective-permute-done | bytes 131104 | tf_op jit(solution)/shard_map/ppermute | solution.py:516
  99.1 1.1 %collective-permute-start.26 = (bf16[272,256]{1,0:T(8,128)(2,1)S(1)}, bf16[272,256]{1,0:T(8,128)(2,1)S(1)}, u32[]{:S(2)}, u32[]{:S(2)}) collective-permute-start(bf16[272,256]{1,0:T(8,128)(2,1)S(1)} %get-tuple-element.163), channel_id=1, source_target_pairs={{0,64},{8,72},{16,80},{24,88},{32,96},{40,104},{48,112},{56,120},{... | collective-permute-start | bytes 417800 | tf_op jit(solution)/shard_map/ppermute | solution.py:516
  100.2 4.0 %collective-permute-done.26.received_ref = bf16[272,256]{1,0:T(8,128)(2,1)S(1)} collective-permute-done((bf16[272,256]{1,0:T(8,128)(2,1)S(1)}, bf16[272,256]{1,0:T(8,128)(2,1)S(1)}, u32[]{:S(2)}, u32[]{:S(2)}) %collective-permute-start.26) | collective-permute-done | bytes 139296 | tf_op jit(solution)/shard_map/ppermute | solution.py:516
  (54 shorter events, 11.3 us)
Async XLA Ops:
  0.6 8.6 %collective-permute-start = (bf16[256,256]{1,0:T(8,128)(2,1)}, bf16[256,256]{1,0:T(8,128)(2,1)S(1)}, u32[]{:S(2)}, u32[]{:S(2)}) collective-permute-start(bf16[256,256]{1,0:T(8,128)(2,1)} %param.5), channel_id=1, source_target_pairs={{0,1},{1,0},{2,3},{3,2},{4,5},{5,4},{6,7},{7,6},{8,9},{9,8},{10,11... | collective-permute-start | bytes 393224 | tf_op jit(solution)/shard_map/ppermute | solution.py:516
  4.7 7.2 %collective-permute-start.1 = (bf16[256,256]{1,0:T(8,128)(2,1)}, bf16[256,256]{1,0:T(8,128)(2,1)S(1)}, u32[]{:S(2)}, u32[]{:S(2)}) collective-permute-start(bf16[256,256]{1,0:T(8,128)(2,1)} %param.6), channel_id=1, source_target_pairs={{0,64},{8,72},{16,80},{24,88},{32,96},{40,104},{48,112},{56,120},{... | collective-permute-start | bytes 393224 | tf_op jit(solution)/shard_map/ppermute | solution.py:516
  11.9 7.5 %collective-permute-start.3 = (bf16[512,256]{1,0:T(8,128)(2,1)S(1)}, bf16[512,256]{1,0:T(8,128)(2,1)S(1)}, u32[]{:S(2)}, u32[]{:S(2)}) collective-permute-start(bf16[512,256]{1,0:T(8,128)(2,1)S(1)} %constant_dynamic-update-slice_fusion.refs_0_), channel_id=1, source_target_pairs={{0,6},{1,7},{2,0},{3,1},{4,2},{5,3},{6,4},{7,5},{8,14},{9,15},{10,... | collective-permute-start | bytes 786440 | tf_op jit(solution)/shard_map/ppermute | solution.py:516
  14.8 8.1 %collective-permute-start.2 = (bf16[512,256]{1,0:T(8,128)(2,1)S(1)}, bf16[512,256]{1,0:T(8,128)(2,1)S(1)}, u32[]{:S(2)}, u32[]{:S(2)}) collective-permute-start(bf16[512,256]{1,0:T(8,128)(2,1)S(1)} %constant_dynamic-update-slice_fusion.refs_0_), channel_id=1, source_target_pairs={{0,2},{1,3},{2,4},{3,5},{4,6},{5,7},{6,0},{7,1},{8,10},{9,11},{10,... | collective-permute-start | bytes 786440 | tf_op jit(solution)/shard_map/ppermute | solution.py:516
  14.8 8.1 %collective-permute-start.5 = (bf16[512,256]{1,0:T(8,128)(2,1)S(1)}, bf16[512,256]{1,0:T(8,128)(2,1)S(1)}, u32[]{:S(2)}, u32[]{:S(2)}) collective-permute-start(bf16[512,256]{1,0:T(8,128)(2,1)S(1)} %get-tuple-element.168), channel_id=1, source_target_pairs={{0,48},{8,56},{16,0},{24,8},{32,16},{40,24},{48,32},{56,40},{64,11... | collective-permute-start | bytes 786440 | tf_op jit(solution)/shard_map/ppermute | solution.py:516
  17.9 7.8 %collective-permute-start.4 = (bf16[512,256]{1,0:T(8,128)(2,1)S(1)}, bf16[512,256]{1,0:T(8,128)(2,1)S(1)}, u32[]{:S(2)}, u32[]{:S(2)}) collective-permute-start(bf16[512,256]{1,0:T(8,128)(2,1)S(1)} %get-tuple-element.168), channel_id=1, source_target_pairs={{0,16},{8,24},{16,32},{24,40},{32,48},{40,56},{48,0},{56,8},{64,80... | collective-permute-start | bytes 786440 | tf_op jit(solution)/shard_map/ppermute | solution.py:516
  25.7 17.3 %collective-permute-start.11 = (bf16[1536,256]{1,0:T(8,128)(2,1)S(1)}, bf16[1536,256]{1,0:T(8,128)(2,1)S(1)}, u32[]{:S(2)}, u32[]{:S(2)}) collective-permute-start(bf16[1536,256]{1,0:T(8,128)(2,1)S(1)} %constant_dynamic-update-slice_fusion.4.refs_0_.refs_5_), channel_id=1, source_target_pairs={{0,8},{8,0},{16,24},{24,16},{32,40},{40,32},{48,56},{56,48},{64,72... | collective-permute-start | bytes 2359304 | tf_op jit(solution)/shard_map/ppermute | solution.py:516
  25.9 7.9 %collective-permute-start.7 = (bf16[256,256]{1,0:T(8,128)(2,1)S(1)}, bf16[256,256]{1,0:T(8,128)(2,1)S(1)}, u32[]{:S(2)}, u32[]{:S(2)}) collective-permute-start(bf16[256,256]{1,0:T(8,128)(2,1)S(1)} %slice.13), channel_id=1, source_target_pairs={{0,6},{1,7},{2,0},{3,1},{4,2},{5,3},{6,4},{7,5},{8,14},{9,15},{10,... | collective-permute-start | bytes 393224 | tf_op jit(solution)/shard_map/ppermute | solution.py:516
  28.9 6.8 %collective-permute-start.6 = (bf16[256,256]{1,0:T(8,128)(2,1)S(1)}, bf16[256,256]{1,0:T(8,128)(2,1)S(1)}, u32[]{:S(2)}, u32[]{:S(2)}) collective-permute-start(bf16[256,256]{1,0:T(8,128)(2,1)S(1)} %slice.12), channel_id=1, source_target_pairs={{0,2},{1,3},{2,4},{3,5},{4,6},{5,7},{6,0},{7,1},{8,10},{9,11},{10,... | collective-permute-start | bytes 393224 | tf_op jit(solution)/shard_map/ppermute | solution.py:516
  29.0 13.9 %collective-permute-start.9 = (bf16[256,256]{1,0:T(8,128)(2,1)S(1)}, bf16[256,256]{1,0:T(8,128)(2,1)S(1)}, u32[]{:S(2)}, u32[]{:S(2)}) collective-permute-start(bf16[256,256]{1,0:T(8,128)(2,1)S(1)} %slice.15), channel_id=1, source_target_pairs={{0,48},{8,56},{16,0},{24,8},{32,16},{40,24},{48,32},{56,40},{64,11... | collective-permute-start | bytes 393224 | tf_op jit(solution)/shard_map/ppermute | solution.py:516
  29.3 13.6 %collective-permute-start.8 = (bf16[256,256]{1,0:T(8,128)(2,1)S(1)}, bf16[256,256]{1,0:T(8,128)(2,1)S(1)}, u32[]{:S(2)}, u32[]{:S(2)}) collective-permute-start(bf16[256,256]{1,0:T(8,128)(2,1)S(1)} %slice.14), channel_id=1, source_target_pairs={{0,16},{8,24},{16,32},{24,40},{32,48},{40,56},{48,0},{56,8},{64,80... | collective-permute-start | bytes 393224 | tf_op jit(solution)/shard_map/ppermute | solution.py:516
  42.9 7.1 %collective-permute-start.10 = (bf16[512,256]{1,0:T(8,128)(2,1)S(1)}, bf16[512,256]{1,0:T(8,128)(2,1)S(1)}, u32[]{:S(2)}, u32[]{:S(2)}) collective-permute-start(bf16[512,256]{1,0:T(8,128)(2,1)S(1)} %constant_dynamic-update-slice_fusion.8.refs_1_), channel_id=1, source_target_pairs={{0,8},{8,0},{16,24},{24,16},{32,40},{40,32},{48,56},{56,48},{64,72... | collective-permute-start | bytes 786440 | tf_op jit(solution)/shard_map/ppermute | solution.py:516
  55.5 11.9 %copy-start = (f32[2048]{0:T(1024)S(1)}, f32[2048]{0:T(1024)}, u32[]{:S(2)}) copy-start(f32[2048]{0:T(1024)} %param.9) | copy-start | bytes 24580
  55.5 5.2 %collective-permute-start.12 = (f32[32,128]{1,0:T(8,128)S(1)}, f32[32,128]{1,0:T(8,128)S(1)}, u32[]{:S(2)}, u32[]{:S(2)}) collective-permute-start(f32[32,128]{1,0:T(8,128)S(1)} %get-tuple-element.109.own_ref), channel_id=1, source_target_pairs={{0,1},{1,0},{2,3},{3,2},{4,5},{5,4},{6,7},{7,6},{8,9},{9,8},{10,11... | collective-permute-start | bytes 49160 | tf_op jit(solution)/shard_map/ppermute | solution.py:516
  60.8 4.2 %collective-permute-start.15 = (f32[32,128]{1,0:T(8,128)S(1)}, f32[32,128]{1,0:T(8,128)S(1)}, u32[]{:S(2)}, u32[]{:S(2)}) collective-permute-start(f32[32,128]{1,0:T(8,128)S(1)} %join_stats.1.refs_7_), channel_id=1, source_target_pairs={{0,6},{1,7},{2,0},{3,1},{4,2},{5,3},{6,4},{7,5},{8,14},{9,15},{10,... | collective-permute-start | bytes 49160 | tf_op jit(solution)/shard_map/ppermute | solution.py:516
  62.1 5.3 %collective-permute-start.14 = (f32[32,128]{1,0:T(8,128)S(1)}, f32[32,128]{1,0:T(8,128)S(1)}, u32[]{:S(2)}, u32[]{:S(2)}) collective-permute-start(f32[32,128]{1,0:T(8,128)S(1)} %join_stats.1.refs_7_), channel_id=1, source_target_pairs={{0,4},{1,5},{2,6},{3,7},{4,0},{5,1},{6,2},{7,3},{8,12},{9,13},{10,... | collective-permute-start | bytes 49160 | tf_op jit(solution)/shard_map/ppermute | solution.py:516
  62.2 5.3 %collective-permute-start.13 = (f32[32,128]{1,0:T(8,128)S(1)}, f32[32,128]{1,0:T(8,128)S(1)}, u32[]{:S(2)}, u32[]{:S(2)}) collective-permute-start(f32[32,128]{1,0:T(8,128)S(1)} %join_stats.1.refs_7_), channel_id=1, source_target_pairs={{0,2},{1,3},{2,4},{3,5},{4,6},{5,7},{6,0},{7,1},{8,10},{9,11},{10,... | collective-permute-start | bytes 49160 | tf_op jit(solution)/shard_map/ppermute | solution.py:516
  68.6 6.2 %collective-permute-start.16 = (bf16[256,256]{1,0:T(8,128)(2,1)S(1)}, bf16[256,256]{1,0:T(8,128)(2,1)S(1)}, u32[]{:S(2)}, u32[]{:S(2)}) collective-permute-start(bf16[256,256]{1,0:T(8,128)(2,1)S(1)} %get-tuple-element.130), channel_id=1, source_target_pairs={{0,2},{1,3},{2,4},{3,5},{4,6},{5,7},{6,0},{7,1},{8,10},{9,11},{10,... | collective-permute-start | bytes 393224 | tf_op jit(solution)/shard_map/ppermute | solution.py:516
  69.4 5.5 %collective-permute-start.17 = (bf16[256,256]{1,0:T(8,128)(2,1)S(1)}, bf16[256,256]{1,0:T(8,128)(2,1)S(1)}, u32[]{:S(2)}, u32[]{:S(2)}) collective-permute-start(bf16[256,256]{1,0:T(8,128)(2,1)S(1)} %get-tuple-element.131), channel_id=1, source_target_pairs={{0,6},{1,7},{2,0},{3,1},{4,2},{5,3},{6,4},{7,5},{8,14},{9,15},{10,... | collective-permute-start | bytes 393224 | tf_op jit(solution)/shard_map/ppermute | solution.py:516
  74.9 2.9 %collective-permute-start.18 = (bf16[2064,256]{1,0:T(8,128)(2,1)S(1)}, bf16[2064,256]{1,0:T(8,128)(2,1)S(1)}, u32[]{:S(2)}, u32[]{:S(2)}) collective-permute-start(bf16[2064,256]{1,0:T(8,128)(2,1)S(1)} %grads_far.1), channel_id=1, source_target_pairs={{0,8},{8,0},{16,24},{24,16},{32,40},{40,32},{48,56},{56,48},{64,72... | collective-permute-start | bytes 3170312 | tf_op jit(solution)/shard_map/ppermute | solution.py:516
  78.0 11.3 %collective-permute-start.21 = (bf16[512,256]{1,0:T(8,128)(2,1)S(1)}, bf16[512,256]{1,0:T(8,128)(2,1)S(1)}, u32[]{:S(2)}, u32[]{:S(2)}) collective-permute-start(bf16[512,256]{1,0:T(8,128)(2,1)S(1)} %get-tuple-element.146), channel_id=1, source_target_pairs={{0,2},{1,3},{2,4},{3,5},{4,6},{5,7},{6,0},{7,1},{8,10},{9,11},{10,... | collective-permute-start | bytes 786440 | tf_op jit(solution)/shard_map/ppermute | solution.py:516
  78.7 10.6 %collective-permute-start.22 = (bf16[512,256]{1,0:T(8,128)(2,1)S(1)}, bf16[512,256]{1,0:T(8,128)(2,1)S(1)}, u32[]{:S(2)}, u32[]{:S(2)}) collective-permute-start(bf16[512,256]{1,0:T(8,128)(2,1)S(1)} %get-tuple-element.147), channel_id=1, source_target_pairs={{0,6},{1,7},{2,0},{3,1},{4,2},{5,3},{6,4},{7,5},{8,14},{9,15},{10,... | collective-permute-start | bytes 786440 | tf_op jit(solution)/shard_map/ppermute | solution.py:516
  81.4 7.9 %collective-permute-start.19 = (bf16[272,256]{1,0:T(8,128)(2,1)S(1)}, bf16[272,256]{1,0:T(8,128)(2,1)S(1)}, u32[]{:S(2)}, u32[]{:S(2)}) collective-permute-start(bf16[272,256]{1,0:T(8,128)(2,1)S(1)} %get-tuple-element.144), channel_id=1, source_target_pairs={{0,48},{8,56},{16,0},{24,8},{32,16},{40,24},{48,32},{56,40},{64,11... | collective-permute-start | bytes 417800 | tf_op jit(solution)/shard_map/ppermute | solution.py:516
  82.7 6.6 %collective-permute-start.20 = (bf16[256,256]{1,0:T(8,128)(2,1)S(1)}, bf16[256,256]{1,0:T(8,128)(2,1)S(1)}, u32[]{:S(2)}, u32[]{:S(2)}) collective-permute-start(bf16[256,256]{1,0:T(8,128)(2,1)S(1)} %get-tuple-element.145), channel_id=1, source_target_pairs={{0,16},{8,24},{16,32},{24,40},{32,48},{40,56},{48,0},{56,8},{64,80... | collective-permute-start | bytes 393224 | tf_op jit(solution)/shard_map/ppermute | solution.py:516
  89.4 8.7 %collective-permute-start.23 = (bf16[528,256]{1,0:T(8,128)(2,1)S(1)}, bf16[528,256]{1,0:T(8,128)(2,1)S(1)}, u32[]{:S(2)}, u32[]{:S(2)}) collective-permute-start(bf16[528,256]{1,0:T(8,128)(2,1)S(1)} %get-tuple-element.155), channel_id=1, source_target_pairs={{0,48},{8,56},{16,0},{24,8},{32,16},{40,24},{48,32},{56,40},{64,11... | collective-permute-start | bytes 811016 | tf_op jit(solution)/shard_map/ppermute | solution.py:516
  89.9 9.1 %collective-permute-start.24 = (bf16[528,256]{1,0:T(8,128)(2,1)S(1)}, bf16[528,256]{1,0:T(8,128)(2,1)S(1)}, u32[]{:S(2)}, u32[]{:S(2)}) collective-permute-start(bf16[528,256]{1,0:T(8,128)(2,1)S(1)} %get-tuple-element.156), channel_id=1, source_target_pairs={{0,16},{8,24},{16,32},{24,40},{32,48},{40,56},{48,0},{56,8},{64,80... | collective-permute-start | bytes 811016 | tf_op jit(solution)/shard_map/ppermute | solution.py:516
  91.6 6.6 %collective-permute-start.25 = (bf16[256,256]{1,0:T(8,128)(2,1)S(1)}, bf16[256,256]{1,0:T(8,128)(2,1)S(1)}, u32[]{:S(2)}, u32[]{:S(2)}) collective-permute-start(bf16[256,256]{1,0:T(8,128)(2,1)S(1)} %get-tuple-element.157), channel_id=1, source_target_pairs={{0,1},{1,0},{2,3},{3,2},{4,5},{5,4},{6,7},{7,6},{8,9},{9,8},{10,11... | collective-permute-start | bytes 393224 | tf_op jit(solution)/shard_map/ppermute | solution.py:516
  99.1 5.1 %collective-permute-start.26 = (bf16[272,256]{1,0:T(8,128)(2,1)S(1)}, bf16[272,256]{1,0:T(8,128)(2,1)S(1)}, u32[]{:S(2)}, u32[]{:S(2)}) collective-permute-start(bf16[272,256]{1,0:T(8,128)(2,1)S(1)} %get-tuple-element.163), channel_id=1, source_target_pairs={{0,64},{8,72},{16,80},{24,88},{32,96},{40,104},{48,112},{56,120},{... | collective-permute-start | bytes 417800 | tf_op jit(solution)/shard_map/ppermute | solution.py:516

commit v6 on v4

--- a/solution.py
+++ b/solution.py
@@ -10,6 +10,8 @@
 T = 256
 LANES = 128
 EXTRA = 16
+LOG2E = 1.4426950408889634
+LN2 = 0.6931471805599453
 NX, NZ, NY, NC = 4, 2, 4, 2
 VMEM_LIMIT = 24 * 2**20
 
@@ -40,21 +42,18 @@
 
 def ads_block(group, chunk):
     pair, zr = chunk // NZ, chunk % NZ
-    k, cr = {"near": (pair + pair // 2, 0), "far": (pair + pair // 2, 1), "mid": (2, pair)}[group]
+    k, cr = {"near": (pair ^ (pair >> 1), 0), "far": (pair ^ (pair >> 1), 1), "two": (2, 0)}[group]
     me = lax.axis_index("au")
     z, y, c = me // (NY * NC), (me // NC) % NY, me % NC
     return (z + zr - 2 * z * zr) * (NY * NC) + lax.rem(y + NY - k, NY) * NC + (c + cr - 2 * c * cr)
 
 
-USER_PARTS = 5
-
-
 def stage_users(user_refs, staged, inv):
-    places = [(0, 0, 0, 0), (0, 1, 0, 1), (1, 0, 1, 0), (1, 1, 1, 1), (3, 0, 2, 0), (3, 1, 2, 1), (2, 0, 3, 0), (2, 1, 4, 0)]
-    for j, zr, part, half in places:
-        spot = pl.multiple_of(user_block(j, zr) * T, T)
-        block = user_refs[part][half * T : (half + 1) * T, :].astype(F32) * inv
-        staged[pl.ds(spot, T), :] = block.astype(BF16)
+    for j in range(NX):
+        for zr in range(NZ):
+            spot = pl.multiple_of(user_block(j, zr) * T, T)
+            block = user_refs[j][zr * T : (zr + 1) * T, :].astype(F32) * inv
+            staged[pl.ds(spot, T), :] = block.astype(BF16)
 
 
 def first_row(group, chunk):
@@ -82,9 +81,9 @@
     steps = n // 2
     chunks = rows // T
     first_call = group == "near"
-    last_call = group == "mid"
+    last_call = group == "far"
     if first_call:
-        user_refs, refs = refs[:USER_PARTS], refs[USER_PARTS:]
+        user_refs, refs = refs[:NX], refs[NX:]
     else:
         (users_t,), refs = refs[:1], refs[1:]
     ads_refs, refs = refs[:n_ads], refs[n_ads:]
@@ -129,7 +128,7 @@
             for r in range(0, T, 8):
                 row = c * T + r
                 logc = logc_all[row : row + 8, :]
-                x = prod[r : r + 8, :] - jnp.concatenate([logc] * (T // LANES), axis=1)
+                x = prod[r : r + 8, :] * LOG2E - jnp.concatenate([logc] * (T // LANES), axis=1)
                 self.dst[row : row + 8, :] = x
                 self.best = jnp.maximum(self.best, x)
                 self.found = jnp.where(ahead == r, x, self.found)
@@ -147,7 +146,7 @@
 
         def chunk(self, c):
             for r in range(c * T, (c + 1) * T, 16):
-                e = jnp.exp(self.src[r : r + 16, :] - self.top)
+                e = jnp.exp2(self.src[r : r + 16, :] - self.top)
                 self.total += e[:8] + e[8:]
                 e = e.astype(BF16)
                 p_ref[r : r + 16, self.cols] = e
@@ -162,7 +161,7 @@
             else:
                 m = jnp.maximum(m_in[:, cols], top)
                 m_ref[:, cols] = m
-                total_ref[:, cols] = total_in[:, cols] * jnp.exp(m_in[:, cols] - m) + total * jnp.exp(top - m)
+                total_ref[:, cols] = total_in[:, cols] * jnp.exp2(m_in[:, cols] - m) + total * jnp.exp2(top - m)
 
     def gather(tile, e):
         cols = columns(tile)
@@ -171,7 +170,7 @@
             acc_ref[:, cols] = new
         else:
             m = m_ref[:, cols]
-            acc_ref[:, cols] = acc_in[:, cols] * jnp.exp(m_in[:, cols] - m) + new * jnp.exp(top_ref[:, cols] - m)
+            acc_ref[:, cols] = acc_in[:, cols] * jnp.exp2(m_in[:, cols] - m) + new * jnp.exp2(top_ref[:, cols] - m)
 
     def turn(tile, src, dst, e_now, e_before):
         gather(jnp.maximum(tile - 1, 0), e_before)
@@ -197,7 +196,7 @@
 
     gather(n - 1, e1)
     if last_call:
-        lse = m_ref[...] + jnp.log(total_ref[...])
+        lse = m_ref[...] + jnp.log2(total_ref[...])
         width = n * T // LANES
         for r in range(width):
             cols = slice(r * LANES, (r + 1) * LANES)
@@ -227,7 +226,7 @@
     if group == "near":
         out_shape.append(jax.ShapeDtypeStruct((total, width), BF16))
         out_shape.append(jax.ShapeDtypeStruct((width, total), BF16))
-    if group == "mid":
+    if group == "far":
         out_shape.append(jax.ShapeDtypeStruct((stats_rows, LANES), F32))
     scratch = [
         pltpu.VMEM((count, width), BF16),
@@ -247,7 +246,7 @@
     )
 
 
-GROUPS = ("near", "far", "mid")
+GROUPS = ("near", "two", "far")
 
 
 def rows_kernel(sizes, start, *refs):
@@ -299,7 +298,7 @@
 
 def users_kernel(inv, acc_ref, m_ref, rows_a, rows_b, hit_ref, weight_ref, *rest):
     stats_in, rest = rest[:NX], rest[NX:]
-    du_refs, (lse_ref, coef_ref, loss_ref, stats_ref, rows_ref) = rest[:USER_PARTS], rest[USER_PARTS:]
+    du_refs, (lse_ref, coef_ref, loss_ref, stats_ref, rows_ref) = rest[:-5], rest[-5:]
     n = NX * NZ
     width = n * T // LANES
     for j in range(NX):
@@ -308,20 +307,20 @@
     rows_ref[:, n * T // 2 :] = rows_b[...]
     tops = stats_ref[:, :width, :]
     top = jnp.max(tops, axis=0)
-    lse = top + jnp.log(jnp.sum(jnp.exp(tops - top[None]), axis=0))
-    diff = lse - jnp.sum(stats_ref[:, width:, :], axis=0)
+    lse = top + jnp.log2(jnp.sum(jnp.exp2(tops - top[None]), axis=0))
+    diff = (lse - jnp.sum(stats_ref[:, width:, :], axis=0)) * LN2
     loss = jnp.zeros((1, LANES), F32)
     for r in range(width):
         cols = slice(r * LANES, (r + 1) * LANES)
         lse_ref[:, cols] = lse[r : r + 1, :]
         loss += weight_ref[:, cols] * diff[r : r + 1, :]
     loss_ref[...] = loss_rows(jnp.sum(loss, axis=1, keepdims=True), loss_ref.shape[1])
-    coef_ref[...] = weight_ref[...] * (jnp.exp(hit_ref[...] - lse_ref[...]) - 1.0)
+    coef_ref[...] = weight_ref[...] * (jnp.exp2(hit_ref[...] - lse_ref[...]) - 1.0)
 
     def users_at(j, zr):
         cols = pl.ds(pl.multiple_of(user_block((NX - j) % NX, zr) * T, T), T)
         weight = weight_ref[:, cols] * inv
-        scale = weight * jnp.exp(m_ref[:, cols] - lse_ref[:, cols])
+        scale = weight * jnp.exp2(m_ref[:, cols] - lse_ref[:, cols])
         return (acc_ref[:, cols] * scale - rows_ref[:, cols].astype(F32) * weight).astype(BF16)
 
     for part, j in enumerate((0, 1, 3)):
@@ -346,53 +345,53 @@
     )
 
 
-def grads_kernel(group, users_ref, p_ref, top_ref, lse_ref, coef_ref, weight_ref, pos_ref, loss_in, *refs):
-    outs, qs = refs[:-2], refs[-2:]
+def grads_kernel(units, users_ref, lse_ref, coef_ref, weight_ref, pos_ref, loss_in, *refs):
+    ps, tops, outs, qs = refs[: len(units)], refs[len(units) : 2 * len(units)], refs[2 * len(units) : -2], refs[-2:]
     deep = 2 * T
-    count, total = p_ref.shape
-
-    def build(unit, dst):
+    total = users_ref.shape[0]
+
+    def build(i, dst):
+        group, at = units[i]
         for b in range(total // T):
             cols = slice(b * T, (b + 1) * T)
-            scale = weight_ref[:, cols] * jnp.exp(top_ref[:, cols] - lse_ref[:, cols])
+            scale = weight_ref[:, cols] * jnp.exp2(tops[i][:, cols] - lse_ref[:, cols])
             coef = coef_ref[:, cols]
             pos = pos_ref[:, cols] - lax.broadcasted_iota(jnp.int32, (16, T), 0)
             for half in range(2):
-                ahead = pos - first_row(group, 2 * unit + half)
+                ahead = pos - first_row(group, 2 * at + half)
                 for r in range(0, T, 16):
                     row = half * T + r
-                    scaled = p_ref[unit * deep + row : unit * deep + row + 16, cols].astype(F32) * scale
+                    scaled = ps[i][at * deep + row : at * deep + row + 16, cols].astype(F32) * scale
                     dst[row : row + 16, cols] = jnp.where(ahead == r, coef, scaled).astype(BF16)
 
-    def product(unit, src):
-        da = jnp.dot(src[...], users_ref[...], preferred_element_type=F32).astype(BF16)
-        if group == "mid":
-            outs[unit][:deep, :] = da
+    build(0, qs[0])
+    for i in range(len(units)):
+        da = jnp.dot(qs[i % 2][...], users_ref[...], preferred_element_type=F32)
+        if i + 1 < len(units):
+            build(i + 1, qs[(i + 1) % 2])
+        da = da.astype(BF16)
+        if len(outs) == 1:
+            outs[0][i * deep : (i + 1) * deep, :] = da
         else:
-            outs[0][unit * deep : (unit + 1) * deep, :] = da
-
-    units = count // deep
-    build(0, qs[0])
-    for unit in range(units):
-        product(unit, qs[unit % 2])
-        if unit + 1 < units:
-            build(unit + 1, qs[(unit + 1) % 2])
-    if group == "mid":
-        outs[1][deep:, :] = loss_in[...]
-
-
-def run_grads(group, users, p, top, lse, coefs, weights, positives, loss):
-    count, total = p.shape
-    width = users.shape[1]
+            outs[i][:deep, :] = da
+            outs[i][deep:, :] = loss_in[...]
+
+
+def run_grads(name, units, users, lse, coefs, weights, positives, loss):
+    total, width = users.shape
     deep = 2 * T
-    shapes = [(deep, width), (deep + EXTRA, width)] if group == "mid" else [(count, width)]
+    places = [u[:2] for u in units]
+    if name == "mid":
+        shapes = [(deep + EXTRA, width)] * 2
+    else:
+        shapes = [(len(units) * deep, width)]
     return call(
-        lambda *refs: grads_kernel(group, *refs),
-        "grads_" + group,
+        lambda *refs: grads_kernel(places, *refs),
+        "grads_" + name,
         [jax.ShapeDtypeStruct(x, BF16) for x in shapes],
         [pltpu.VMEM((deep, total), BF16)] * 2,
-        (users, p, top, lse, coefs, weights, positives, loss),
-        cost(count, total, width),
+        (users, lse, coefs, weights, positives, loss, *(u[2] for u in units), *(u[3] for u in units)),
+        cost(len(units) * deep, total, width),
     )
 
 
@@ -400,19 +399,18 @@
     return call(kernel, name, out_shape, [], args)
 
 
-def add_mid(near, loss, back):
+def add_mid(near, back):
     width = near.shape[1]
 
-    def kernel(near_ref, loss_ref, back_ref, first, second, both_ref):
-        both = plus(loss_ref[...], back_ref[NZ * T :, :]).astype(BF16)
-        first[:T, :] = plus(near_ref[:T, :], back_ref[:T, :]).astype(BF16)
-        first[T:, :] = both
-        second[...] = plus(near_ref[T:, :], back_ref[T : NZ * T, :]).astype(BF16)
-        both_ref[...] = both
+    def kernel(near_ref, back_ref, first, second, both):
+        total = plus(near_ref[...], back_ref[...]).astype(BF16)
+        first[:T, :] = total[:T, :]
+        first[T:, :] = total[NZ * T :, :]
+        second[...] = total[T : NZ * T, :]
+        both[...] = total[NZ * T :, :]
 
     shapes = [(T + EXTRA, width), (T, width), (EXTRA, width)]
-    shapes = [jax.ShapeDtypeStruct(x, BF16) for x in shapes]
-    return simple_call(kernel, "add_mid", shapes, near, loss, back)
+    return simple_call(kernel, "add_mid", [jax.ShapeDtypeStruct(x, BF16) for x in shapes], near, back)
 
 
 def add_near(near, back, both, first, second):
@@ -420,18 +418,20 @@
     rows = NZ * T
 
     def kernel(near_ref, back_ref, both_ref, first_ref, second_ref, keep, one, three):
-        total = plus(near_ref[...], back_ref[...])
-        keep[:rows, :] = total[:rows]
+        def term(i):
+            return plus(near_ref[i * T : (i + 1) * T, :], back_ref[i * T : (i + 1) * T, :])
+
+        keep[:T, :] = term(0)
+        keep[T:rows, :] = term(1)
         keep[rows:, :] = both_ref[...].astype(F32)
-        one[:T, :] = plus(total[rows : rows + T], first_ref[:T, :]).astype(BF16)
-        one[T:rows, :] = total[rows + T : 2 * rows].astype(BF16)
+        one[:T, :] = plus(term(2), first_ref[:T, :]).astype(BF16)
+        one[T:rows, :] = term(3).astype(BF16)
         one[rows:, :] = plus(both_ref[...], first_ref[T:, :]).astype(BF16)
-        three[:T, :] = total[2 * rows : 2 * rows + T].astype(BF16)
-        three[T:rows, :] = plus(total[2 * rows + T :], second_ref[...]).astype(BF16)
+        three[:T, :] = term(4).astype(BF16)
+        three[T:rows, :] = plus(term(5), second_ref[...]).astype(BF16)
         three[rows:, :] = both_ref[...]
 
-    shape = jax.ShapeDtypeStruct((rows + EXTRA, width), BF16)
-    shapes = [jax.ShapeDtypeStruct((rows + EXTRA, width), F32), shape, shape]
+    shapes = [jax.ShapeDtypeStruct((rows + EXTRA, width), t) for t in (F32, BF16, BF16)]
     return simple_call(kernel, "add_near", shapes, near, back, both, first, second)
 
 
@@ -439,7 +439,7 @@
     width = parts[0].shape[1]
 
     def kernel(*refs):
-        ins, (keep, send) = refs[:3], refs[3:]
+        ins, (keep, send) = refs[:-2], refs[-2:]
         loss = plus(*(r[NZ * T :, :] for r in ins))
         keep[:T, :] = plus(*(r[:T, :] for r in ins))
         keep[T:, :] = loss
@@ -492,7 +492,7 @@
     def kernel(own_ref, other_ref, out_ref):
         a, b = own_ref[:half, :], other_ref[:half, :]
         top = jnp.maximum(a, b)
-        out_ref[:half, :] = top + jnp.log(jnp.exp(a - top) + jnp.exp(b - top))
+        out_ref[:half, :] = top + jnp.log2(jnp.exp2(a - top) + jnp.exp2(b - top))
         out_ref[half:, :] = own_ref[half:, :] + other_ref[half:, :]
 
     return simple_call(kernel, "join_stats", [jax.ShapeDtypeStruct(own.shape, F32)], own, other)[0]
@@ -525,34 +525,31 @@
 def local(users, ads, counts, positives, weights):
     inv = users.shape[1] ** (-0.5)
     pos_row = (positives - lax.axis_index("aa") * counts.shape[0])[None, :]
-    logc = jnp.log(counts.astype(F32))[None, :]
+    logc = (jnp.log(counts.astype(F32)) * LOG2E)[None, :]
     weight_row = weights[None, :]
     users_z, ads_z, pos_row, logc = lax.optimization_barrier((swap_z_hi(users), swap_z_lo(ads), pos_row, logc))
     user_pair = jnp.concatenate([users, users_z], axis=0)
     ads_pair = jnp.concatenate([ads, ads_z], axis=0)
-    user_1, user_3, ads_1, ads_3 = lax.optimization_barrier(
-        (shift_x(user_pair, 1), shift_x(user_pair, -1), shift_y(ads_pair, 1), shift_y(ads_pair, -1))
-    )
-    user_2a, user_2b = shift_x(user_1[:T], 1), shift_x(user_3[T:], -1)
-    ads_2a, ads_2b = shift_y(ads_1[:T], 1), shift_y(ads_3[T:], -1)
-    near = jnp.concatenate([ads_pair, ads_1, ads_3], axis=0)
-    far = swap_core(near)
-    parts = (user_pair, user_1, user_3, user_2a, user_2b)
+    user_pair, ads_pair = lax.optimization_barrier((user_pair, ads_pair))
+    user_2 = shift_x(user_pair, 2)
+    user_1, user_3 = shift_x(user_pair, 1), shift_x(user_pair, -1)
+    ads_1, ads_3 = shift_y(ads_pair, 1), shift_y(ads_pair, -1)
+    ads_2 = shift_y(ads_pair, 2)
+    parts = lax.optimization_barrier((user_pair, user_1, user_2, user_3))
 
     p_near, top_near, at_near, acc, m, total, hits, staged, users_t = run_logits(
-        "near", parts, (near,), logc, pos_row, inv
-    )
-    ads_2a, ads_2b, hits = lax.optimization_barrier((ads_2a, ads_2b, hits))
-    near_2 = jnp.concatenate([ads_2a, ads_2b], axis=0)
-    far_2 = swap_core(near_2)
-    p_far, top_far, at_far, acc, m, total, hits = run_logits(
+        "near", parts, (ads_pair, ads_1, ads_3), logc, pos_row, inv
+    )
+    ads_2, ads_1, ads_3, hits = lax.optimization_barrier((ads_2, ads_1, ads_3, hits))
+    far = swap_core(jnp.concatenate([ads_pair, ads_1, ads_3, ads_2], axis=0))
+    p_two, top_two, at_two, acc, m, total, hits = run_logits(
+        "two", (users_t,), (ads_2,), logc, pos_row, inv, (acc, m, total, hits)
+    )
+    p_far, top_far, at_far, acc, m, total, hits, stats = run_logits(
         "far", (users_t,), (far,), logc, pos_row, inv, (acc, m, total, hits)
     )
-    p_mid, top_mid, at_mid, acc, m, total, hits, stats = run_logits(
-        "mid", (users_t,), (near_2, far_2), logc, pos_row, inv, (acc, m, total, hits)
-    )
     half = stats.shape[0] * LANES // 4
-    ads_t = (at_near, at_far, at_mid)
+    ads_t = (at_near, at_two, at_far)
     stats_z, rows_a = lax.optimization_barrier((swap_z_hi(stats), run_rows(ads_t, pos_row, 0, half)))
     stats = join_stats(stats, stats_z)
     moved = tuple(shift_x(stats, j) for j in range(1, NX))
@@ -561,20 +558,20 @@
         acc, m, rows_a, rows_b, hits, weight_row, (stats, *moved), inv
     )
     tail = (lse, coefs, weight_row, pos_row, loss)
-    du_2a, du_2b = shift_x(du_2a, 1), shift_x(du_2b, -1)
-    da_2, pay_2 = run_grads("mid", staged, p_mid, top_mid, *tail)
+    pay_2, da_2 = run_grads("mid", [("far", 3, p_far, top_far), ("two", 0, p_two, top_two)], staged, *tail)
     back_2 = swap_core(pay_2)
     da_2, staged = lax.optimization_barrier((da_2, staged))
-    (da_far,) = run_grads("far", staged, p_far, top_far, *tail)
-    da_far, back_2, du_2a, du_2b = lax.optimization_barrier((da_far, back_2, du_2a, du_2b))
+    (da_near,) = run_grads("near", [("near", i, p_near, top_near) for i in range(3)], staged, *tail)
+    da_near, back_2 = lax.optimization_barrier((da_near, back_2))
+    first, second, both = add_mid(da_2, back_2)
+    first, second, staged = lax.optimization_barrier((first, second, staged))
+    first, second = shift_y(first, -1), shift_y(second, 1)
+    du_2a, du_2b = shift_x(du_2a, 1), shift_x(du_2b, -1)
+    (da_far,) = run_grads("far", [("far", i, p_far, top_far) for i in range(3)], staged, *tail)
+    back = swap_core(da_far)
+    first, second, du_2a, du_2b = lax.optimization_barrier((first, second, du_2a, du_2b))
     du_1, du_3 = add_halves(du_1, du_3, du_2a, du_2b)
-    back = swap_core(da_far)
-    first, second, both = add_mid(da_2, loss, back_2)
-    first, second, du_1, du_3, staged = lax.optimization_barrier((first, second, du_1, du_3, staged))
-    first, second = shift_y(first, -1), shift_y(second, 1)
     du_1, du_3 = shift_x(du_1, 1), shift_x(du_3, -1)
-    (da_near,) = run_grads("near", staged, p_near, top_near, *tail)
-    da_near, first, second, du_1, du_3 = lax.optimization_barrier((da_near, first, second, du_1, du_3))
     kept, one, three = add_near(da_near, back, both, first, second)
     one, three = shift_y(one, -1), shift_y(three, 1)
     keep_u, send_u = add_users((du_0, du_1, du_3))

time: 103 us -> 106 us (1.029)
  starting transfers between devices: 32.8 us -> 38.3 us
  local copies, waits for them, and re-layouts: 1.97 us -> 0.01 us
  waiting for transfers between devices: 32.3 us -> 30.5 us
  other arithmetic: 1.43 us -> 2.5 us
    ppermute x28 -> x25, starting transfers between devices: 32.8 us -> 38.3 us  [move(): lax.ppermute(x, axis, [(i, target(i)) for i in range(lax.axis_size(axis))])]
    unnamed x7 -> x2, local copies, waits for them, and re-layouts: 1.89 us -> 0.01 us
    ppermute x28 -> x25, waiting for transfers between devices: 32.3 us -> 30.5 us  [move(): lax.ppermute(x, axis, [(i, target(i)) for i in range(lax.axis_size(axis))])]
    concatenate x0 -> x2, other arithmetic: none -> 1.07 us  [the longest x1 1 us: local(): user_pair = jnp.concatenate([users, users_z], axis=0)]
  transfers between devices with their start and end apart: 28 -> 25, of which waited for: 15 -> 12; matrix products, arithmetic and copies ran while one was open for 3% -> 1% of each run, Pallas kernels for 24% -> 17%
where the time goes in v6:
time: 106 us; the launch traced here: 105 us
  starting transfers between devices  38.3 us (36%)
  Pallas kernels  32.7 us (31%)
  waiting for transfers between devices  30.5 us (29%)
  other arithmetic  2.5 us (2%)
    ppermute x25, starting transfers between devices, move(): lax.ppermute(x, axis, [(i, target(i)) for i in range(lax.axis_size(axis))])  38.3 us
    pallas_call x16, Pallas kernels, call(): pl.pallas_call(kernel, in_specs=[vmem] * len(args), out_specs=[vmem] * le...  32.7 us
    ppermute x25, waiting for transfers between devices, move(): lax.ppermute(x, axis, [(i, target(i)) for i in range(lax.axis_size(axis))])  30.5 us
  transfers between devices with their start and end apart: 25, of which 12 were waited for; matrix products, arithmetic and copies ran while one was open for 1% of the time, Pallas kernels for 17%

profile of v6, /device:TPU:0, one launch (start us, length us, event | category | flops | bytes accessed | tf_op | source)
XLA Modules:
  0.0 104.9 jit_solution(17100716327237688655)
XLA Ops:
  0.6 4.0 %collective-permute-start = (bf16[256,256]{1,0:T(8,128)(2,1)}, bf16[256,256]{1,0:T(8,128)(2,1)S(1)}, u32[]{:S(2)}, u32[]{:S(2)}) collective-permute-start(bf16[256,256]{1,0:T(8,128)(2,1)} %param.5), channel_id=1, source_target_pairs={{0,1},{1,0},{2,3},{3,2},{4,5},{5,4},{6,7},{7,6},{8,9},{9,8},{10,11... | collective-permute-start | bytes 393224 | tf_op jit(solution)/shard_map/ppermute | solution.py:502
  4.7 1.0 collective-permute-start.1
  7.1 2.1 %collective-permute-done = bf16[256,256]{1,0:T(8,128)(2,1)S(1)} collective-permute-done((bf16[256,256]{1,0:T(8,128)(2,1)}, bf16[256,256]{1,0:T(8,128)(2,1)S(1)}, u32[]{:S(2)}, u32[]{:S(2)}) %collective-permute-start) | collective-permute-done | bytes 131104 | tf_op jit(solution)/shard_map/ppermute | solution.py:502
  9.2 2.7 %collective-permute-done.1 = bf16[256,256]{1,0:T(8,128)(2,1)S(1)} collective-permute-done((bf16[256,256]{1,0:T(8,128)(2,1)}, bf16[256,256]{1,0:T(8,128)(2,1)S(1)}, u32[]{:S(2)}, u32[]{:S(2)}) %collective-permute-start.1) | collective-permute-done | bytes 131104 | tf_op jit(solution)/shard_map/ppermute | solution.py:502
  12.9 2.8 %collective-permute-start.4 = (bf16[512,256]{1,0:T(8,128)(2,1)S(1)}, bf16[512,256]{1,0:T(8,128)(2,1)S(1)}, u32[]{:S(2)}, u32[]{:S(2)}) collective-permute-start(bf16[512,256]{1,0:T(8,128)(2,1)S(1)} %get-tuple-element.88.refs_0_), channel_id=1, source_target_pairs={{0,6},{1,7},{2,0},{3,1},{4,2},{5,3},{6,4},{7,5},{8,14},{9,15},{10,... | collective-permute-start | bytes 786440 | tf_op jit(solution)/shard_map/ppermute | solution.py:502
  17.4 3.0 %collective-permute-start.6 = (bf16[512,256]{1,0:T(8,128)(2,1)S(1)}, bf16[512,256]{1,0:T(8,128)(2,1)S(1)}, u32[]{:S(2)}, u32[]{:S(2)}) collective-permute-start(bf16[512,256]{1,0:T(8,128)(2,1)S(1)} %get-tuple-element.92.refs_4_), channel_id=1, source_target_pairs={{0,48},{8,56},{16,0},{24,8},{32,16},{40,24},{48,32},{56,40},{64,11... | collective-permute-start | bytes 786440 | tf_op jit(solution)/shard_map/ppermute | solution.py:502
  20.5 5.6 %collective-permute-done.4.refs_3_ = bf16[512,256]{1,0:T(8,128)(2,1)S(1)} collective-permute-done((bf16[512,256]{1,0:T(8,128)(2,1)S(1)}, bf16[512,256]{1,0:T(8,128)(2,1)S(1)}, u32[]{:S(2)}, u32[]{:S(2)}) %collective-permute-start.4) | collective-permute-done | bytes 262176 | tf_op jit(solution)/shard_map/ppermute | solution.py:502
  26.1 3.2 %collective-permute-start.7 = (bf16[512,256]{1,0:T(8,128)(2,1)S(1)}, bf16[512,256]{1,0:T(8,128)(2,1)S(1)}, u32[]{:S(2)}, u32[]{:S(2)}) collective-permute-start(bf16[512,256]{1,0:T(8,128)(2,1)S(1)} %get-tuple-element.92.refs_4_), channel_id=1, source_target_pairs={{0,32},{8,40},{16,48},{24,56},{32,0},{40,8},{48,16},{56,24},{64,96... | collective-permute-start | bytes 786440 | tf_op jit(solution)/shard_map/ppermute | solution.py:502
  30.5 7.1 %logits_near.1 = (bf16[1536,2048]{1,0:T(8,128)(2,1)S(1)}, f32[1,2048]{1,0:T(1,128)S(1)}, bf16[256,1536]{1,0:T(8,128)(2,1)S(1)}, f32[256,2048]{1,0:T(8,128)S(1)},...) custom-call(bf16[512,256]{1,0:T(8,128)(2,1)S(1)} %get-tuple-element., ...), custom_call_target="tpu_custom_call" | custom-call | flops 100663296 | bytes 393216 | tf_op jit(solution)/shard_map/logits_near/pallas_call | solution.py:25
  37.8 2.7 %logits_two.1 = (bf16[512,2048]{1,0:T(8,128)(2,1)S(1)}, f32[1,2048]{1,0:T(1,128)S(1)}, bf16[256,512]{1,0:T(8,128)(2,1)S(1)}, f32[256,2048]{1,0:T(8,128)S(1)}, f3...) custom-call(bf16[256,2048]{1,0:T(8,128)(2,1)S(1)} %get-tuple-element.95.refs_0_, ...), custom_call_target="tpu_custom_call" | custom-call | flops 33554432 | bytes 131072 | tf_op jit(solution)/shard_map/logits_two/pallas_call | solution.py:25
  40.5 9.3 %logits_far.1 = (bf16[2048,2048]{1,0:T(8,128)(2,1)S(1)}, f32[1,2048]{1,0:T(1,128)S(1)}, bf16[256,2048]{1,0:T(8,128)(2,1)S(1)}, f32[256,2048]{1,0:T(8,128)S(1)}, ...) custom-call(bf16[256,2048]{1,0:T(8,128)(2,1)S(1)} %get-tuple-element.95.refs_0_, ...), custom_call_target="tpu_custom_call" | custom-call | flops 134217728 | bytes 524288 | tf_op jit(solution)/shard_map/logits_far/pallas_call | solution.py:25
  49.8 1.2 %collective-permute-start.9 = (f32[32,128]{1,0:T(8,128)S(1)}, f32[32,128]{1,0:T(8,128)S(1)}, u32[]{:S(2)}, u32[]{:S(2)}) collective-permute-start(f32[32,128]{1,0:T(8,128)S(1)} %get-tuple-element.110.own_ref), channel_id=1, source_target_pairs={{0,1},{1,0},{2,3},{3,2},{4,5},{5,4},{6,7},{7,6},{8,9},{9,8},{10,11... | collective-permute-start | bytes 49160 | tf_op jit(solution)/shard_map/ppermute | solution.py:502
  51.0 2.9 %positive_rows.2.refs_2_ = bf16[256,1024]{1,0:T(8,128)(2,1)S(1)} custom-call(bf16[256,1536]{1,0:T(8,128)(2,1)S(1)} %get-tuple-element.111.refs_0_, bf16[256,512]{1,0:T(8,128)(2,1)S(1)} %get-tuple-element.112.refs_1_, bf16[256,2048]{1,0:T(8,128)(2,1)S(1)} %get-tuple-element.113.refs_2_, s32[1,2048]{1,0:T(1,128)S(1)} %bitcast.7), custom_call_target="tpu_custom_call" | custom-call | flops 134217728 | bytes 524288 | tf_op jit(solution)/shard_map/positive_rows/pallas_call | solution.py:25
  53.9 1.2 %collective-permute-done.9.other_ref = f32[32,128]{1,0:T(8,128)S(1)} collective-permute-done((f32[32,128]{1,0:T(8,128)S(1)}, f32[32,128]{1,0:T(8,128)S(1)}, u32[]{:S(2)}, u32[]{:S(2)}) %collective-permute-start.9) | collective-permute-done | bytes 16416 | tf_op jit(solution)/shard_map/ppermute | solution.py:502
  55.1 2.7 %collective-permute-start.12 = (f32[32,128]{1,0:T(8,128)S(1)}, f32[32,128]{1,0:T(8,128)S(1)}, u32[]{:S(2)}, u32[]{:S(2)}) collective-permute-start(f32[32,128]{1,0:T(8,128)S(1)} %join_stats.1.refs_6_), channel_id=1, source_target_pairs={{0,6},{1,7},{2,0},{3,1},{4,2},{5,3},{6,4},{7,5},{8,14},{9,15},{10,... | collective-permute-start | bytes 49160 | tf_op jit(solution)/shard_map/ppermute | solution.py:502
  57.9 4.0 %collective-permute-start.11 = (f32[32,128]{1,0:T(8,128)S(1)}, f32[32,128]{1,0:T(8,128)S(1)}, u32[]{:S(2)}, u32[]{:S(2)}) collective-permute-start(f32[32,128]{1,0:T(8,128)S(1)} %join_stats.1.refs_6_), channel_id=1, source_target_pairs={{0,4},{1,5},{2,6},{3,7},{4,0},{5,1},{6,2},{7,3},{8,12},{9,13},{10,... | collective-permute-start | bytes 49160 | tf_op jit(solution)/shard_map/ppermute | solution.py:502
  61.9 2.9 %positive_rows.3.refs_3_ = bf16[256,1024]{1,0:T(8,128)(2,1)S(1)} custom-call(bf16[256,1536]{1,0:T(8,128)(2,1)S(1)} %get-tuple-element.111.refs_0_, bf16[256,512]{1,0:T(8,128)(2,1)S(1)} %get-tuple-element.112.refs_1_, bf16[256,2048]{1,0:T(8,128)(2,1)S(1)} %get-tuple-element.113.refs_2_, s32[1,2048]{1,0:T(1,128)S(1)} %bitcast.8), custom_call_target="tpu_custom_call" | custom-call | flops 134217728 | bytes 524288 | tf_op jit(solution)/shard_map/positive_rows/pallas_call | solution.py:25
  64.8 2.0 %collective-permute-done.10.refs_7_ = f32[32,128]{1,0:T(8,128)S(1)} collective-permute-done((f32[32,128]{1,0:T(8,128)S(1)}, f32[32,128]{1,0:T(8,128)S(1)}, u32[]{:S(2)}, u32[]{:S(2)}) %collective-permute-start.10) | collective-permute-done | bytes 16416 | tf_op jit(solution)/shard_map/ppermute | solution.py:502
  67.5 1.4 %grads_mid.1 = (bf16[528,256]{1,0:T(8,128)(2,1)S(1)}, bf16[528,256]{1,0:T(8,128)(2,1)S(1)}) custom-call(bf16[2048,256]{1,0:T(8,128)(2,1)S(1)} %get-tuple-element.151.refs_0_, f32[1,2048]{1,0:T(1,128)S(1)} %get-tuple-element.125.refs_1_, f32[1,2048]{1,0:T(1,128)S(1)} %get-tuple-element.126.refs_2_, f32[1,2048]{1,0:T(1,128)S(1)} %bitcast.16, ...), custom_call_target="tpu_custom_call" | custom-call | flops 67108864 | bytes 262144 | tf_op jit(solution)/shard_map/grads_mid/pallas_call | solution.py:25
  69.0 2.1 %grads_near.1.near_ref = bf16[1536,256]{1,0:T(8,128)(2,1)S(1)} custom-call(bf16[2048,256]{1,0:T(8,128)(2,1)S(1)} %get-tuple-element.151.refs_0_, f32[1,2048]{1,0:T(1,128)S(1)} %get-tuple-element.125.refs_1_, f32[1,2048]{1,0:T(1,128)S(1)} %get-tuple-element.126.refs_2_, f32[1,2048]{1,0:T(1,128)S(1)} %bitcast.17, s32[1,2048]{1,0:T(1,128)S(1)} %bitcast.10, ...), custom_call_target="tpu_custom_call" | custom-call | flops 100663296 | bytes 393216 | tf_op jit(solution)/shard_map/grads_near/pallas_call | solution.py:25
  71.3 2.1 %grads_far.1 = bf16[1536,256]{1,0:T(8,128)(2,1)S(1)} custom-call(bf16[2048,256]{1,0:T(8,128)(2,1)S(1)} %get-tuple-element.151.refs_0_, f32[1,2048]{1,0:T(1,128)S(1)} %get-tuple-element.125.refs_1_, f32[1,2048]{1,0:T(1,128)S(1)} %get-tuple-element.126.refs_2_, f32[1,2048]{1,0:T(1,128)S(1)} %bitcast.18, s32[1,2048]{1,0:T(1,128)S(1)} %bitcast.11, ...), custom_call_target="tpu_custom_call" | custom-call | flops 100663296 | bytes 393216 | tf_op jit(solution)/shard_map/grads_far/pallas_call | solution.py:25
  74.3 3.2 %collective-permute-start.17 = (bf16[256,256]{1,0:T(8,128)(2,1)S(1)}, bf16[256,256]{1,0:T(8,128)(2,1)S(1)}, u32[]{:S(2)}, u32[]{:S(2)}) collective-permute-start(bf16[256,256]{1,0:T(8,128)(2,1)S(1)} %get-tuple-element.144), channel_id=1, source_target_pairs={{0,6},{1,7},{2,0},{3,1},{4,2},{5,3},{6,4},{7,5},{8,14},{9,15},{10,... | collective-permute-start | bytes 393224 | tf_op jit(solution)/shard_map/ppermute | solution.py:502
  77.5 1.7 %collective-permute-start.15 = (bf16[256,256]{1,0:T(8,128)(2,1)S(1)}, bf16[256,256]{1,0:T(8,128)(2,1)S(1)}, u32[]{:S(2)}, u32[]{:S(2)}) collective-permute-start(bf16[256,256]{1,0:T(8,128)(2,1)S(1)} %get-tuple-element.142), channel_id=1, source_target_pairs={{0,16},{8,24},{16,32},{24,40},{32,48},{40,56},{48,0},{56,8},{64,80... | collective-permute-start | bytes 393224 | tf_op jit(solution)/shard_map/ppermute | solution.py:502
  79.2 1.5 %collective-permute-done.16.first_ref = bf16[256,256]{1,0:T(8,128)(2,1)S(1)} collective-permute-done((bf16[256,256]{1,0:T(8,128)(2,1)S(1)}, bf16[256,256]{1,0:T(8,128)(2,1)S(1)}, u32[]{:S(2)}, u32[]{:S(2)}) %collective-permute-start.16) | collective-permute-done | bytes 131104 | tf_op jit(solution)/shard_map/ppermute | solution.py:502
  80.7 2.9 %collective-permute-done.15.second_ref = bf16[256,256]{1,0:T(8,128)(2,1)S(1)} collective-permute-done((bf16[256,256]{1,0:T(8,128)(2,1)S(1)}, bf16[256,256]{1,0:T(8,128)(2,1)S(1)}, u32[]{:S(2)}, u32[]{:S(2)}) %collective-permute-start.15) | collective-permute-done | bytes 131104 | tf_op jit(solution)/shard_map/ppermute | solution.py:502
  83.9 3.2 %collective-permute-start.19 = (bf16[512,256]{1,0:T(8,128)(2,1)S(1)}, bf16[512,256]{1,0:T(8,128)(2,1)S(1)}, u32[]{:S(2)}, u32[]{:S(2)}) collective-permute-start(bf16[512,256]{1,0:T(8,128)(2,1)S(1)} %get-tuple-element.148), channel_id=1, source_target_pairs={{0,6},{1,7},{2,0},{3,1},{4,2},{5,3},{6,4},{7,5},{8,14},{9,15},{10,... | collective-permute-start | bytes 786440 | tf_op jit(solution)/shard_map/ppermute | solution.py:502
  87.4 2.0 %collective-permute-start.22 = (bf16[528,256]{1,0:T(8,128)(2,1)S(1)}, bf16[528,256]{1,0:T(8,128)(2,1)S(1)}, u32[]{:S(2)}, u32[]{:S(2)}) collective-permute-start(bf16[528,256]{1,0:T(8,128)(2,1)S(1)} %get-tuple-element.156), channel_id=1, source_target_pairs={{0,16},{8,24},{16,32},{24,40},{32,48},{40,56},{48,0},{56,8},{64,80... | collective-permute-start | bytes 811016 | tf_op jit(solution)/shard_map/ppermute | solution.py:502
  89.4 2.0 %collective-permute-done.18.refs_1_ = bf16[512,256]{1,0:T(8,128)(2,1)S(1)} collective-permute-done((bf16[512,256]{1,0:T(8,128)(2,1)S(1)}, bf16[512,256]{1,0:T(8,128)(2,1)S(1)}, u32[]{:S(2)}, u32[]{:S(2)}) %collective-permute-start.18) | collective-permute-done | bytes 262176 | tf_op jit(solution)/shard_map/ppermute | solution.py:502
  91.5 1.3 %collective-permute-start.23 = (bf16[256,256]{1,0:T(8,128)(2,1)S(1)}, bf16[256,256]{1,0:T(8,128)(2,1)S(1)}, u32[]{:S(2)}, u32[]{:S(2)}) collective-permute-start(bf16[256,256]{1,0:T(8,128)(2,1)S(1)} %get-tuple-element.157), channel_id=1, source_target_pairs={{0,1},{1,0},{2,3},{3,2},{4,5},{5,4},{6,7},{7,6},{8,9},{9,8},{10,11... | collective-permute-start | bytes 393224 | tf_op jit(solution)/shard_map/ppermute | solution.py:502
  92.8 5.9 %collective-permute-done.23.received_u_ref = bf16[256,256]{1,0:T(8,128)(2,1)S(1)} collective-permute-done((bf16[256,256]{1,0:T(8,128)(2,1)S(1)}, bf16[256,256]{1,0:T(8,128)(2,1)S(1)}, u32[]{:S(2)}, u32[]{:S(2)}) %collective-permute-start.23) | collective-permute-done | bytes 131104 | tf_op jit(solution)/shard_map/ppermute | solution.py:502
  98.8 1.9 %collective-permute-start.24 = (bf16[272,256]{1,0:T(8,128)(2,1)S(1)}, bf16[272,256]{1,0:T(8,128)(2,1)S(1)}, u32[]{:S(2)}, u32[]{:S(2)}) collective-permute-start(bf16[272,256]{1,0:T(8,128)(2,1)S(1)} %get-tuple-element.163), channel_id=1, source_target_pairs={{0,64},{8,72},{16,80},{24,88},{32,96},{40,104},{48,112},{56,120},{... | collective-permute-start | bytes 417800 | tf_op jit(solution)/shard_map/ppermute | solution.py:502
  100.7 3.2 %collective-permute-done.24.received_ref = bf16[272,256]{1,0:T(8,128)(2,1)S(1)} collective-permute-done((bf16[272,256]{1,0:T(8,128)(2,1)S(1)}, bf16[272,256]{1,0:T(8,128)(2,1)S(1)}, u32[]{:S(2)}, u32[]{:S(2)}) %collective-permute-start.24) | collective-permute-done | bytes 139296 | tf_op jit(solution)/shard_map/ppermute | solution.py:502
  (40 shorter events, 8.8 us)
Async XLA Ops:
  0.6 8.6 %collective-permute-start = (bf16[256,256]{1,0:T(8,128)(2,1)}, bf16[256,256]{1,0:T(8,128)(2,1)S(1)}, u32[]{:S(2)}, u32[]{:S(2)}) collective-permute-start(bf16[256,256]{1,0:T(8,128)(2,1)} %param.5), channel_id=1, source_target_pairs={{0,1},{1,0},{2,3},{3,2},{4,5},{5,4},{6,7},{7,6},{8,9},{9,8},{10,11... | collective-permute-start | bytes 393224 | tf_op jit(solution)/shard_map/ppermute | solution.py:502
  4.7 7.2 %collective-permute-start.1 = (bf16[256,256]{1,0:T(8,128)(2,1)}, bf16[256,256]{1,0:T(8,128)(2,1)S(1)}, u32[]{:S(2)}, u32[]{:S(2)}) collective-permute-start(bf16[256,256]{1,0:T(8,128)(2,1)} %param.6), channel_id=1, source_target_pairs={{0,64},{8,72},{16,80},{24,88},{32,96},{40,104},{48,112},{56,120},{... | collective-permute-start | bytes 393224 | tf_op jit(solution)/shard_map/ppermute | solution.py:502
  12.9 13.2 %collective-permute-start.4 = (bf16[512,256]{1,0:T(8,128)(2,1)S(1)}, bf16[512,256]{1,0:T(8,128)(2,1)S(1)}, u32[]{:S(2)}, u32[]{:S(2)}) collective-permute-start(bf16[512,256]{1,0:T(8,128)(2,1)S(1)} %get-tuple-element.88.refs_0_), channel_id=1, source_target_pairs={{0,6},{1,7},{2,0},{3,1},{4,2},{5,3},{6,4},{7,5},{8,14},{9,15},{10,... | collective-permute-start | bytes 786440 | tf_op jit(solution)/shard_map/ppermute | solution.py:502
  15.8 13.5 %collective-permute-start.3 = (bf16[512,256]{1,0:T(8,128)(2,1)S(1)}, bf16[512,256]{1,0:T(8,128)(2,1)S(1)}, u32[]{:S(2)}, u32[]{:S(2)}) collective-permute-start(bf16[512,256]{1,0:T(8,128)(2,1)S(1)} %get-tuple-element.88.refs_0_), channel_id=1, source_target_pairs={{0,4},{1,5},{2,6},{3,7},{4,0},{5,1},{6,2},{7,3},{8,12},{9,13},{10,... | collective-permute-start | bytes 786440 | tf_op jit(solution)/shard_map/ppermute | solution.py:502
  16.6 13.2 %collective-permute-start.2 = (bf16[512,256]{1,0:T(8,128)(2,1)S(1)}, bf16[512,256]{1,0:T(8,128)(2,1)S(1)}, u32[]{:S(2)}, u32[]{:S(2)}) collective-permute-start(bf16[512,256]{1,0:T(8,128)(2,1)S(1)} %get-tuple-element.88.refs_0_), channel_id=1, source_target_pairs={{0,2},{1,3},{2,4},{3,5},{4,6},{5,7},{6,0},{7,1},{8,10},{9,11},{10,... | collective-permute-start | bytes 786440 | tf_op jit(solution)/shard_map/ppermute | solution.py:502
  17.4 12.3 %collective-permute-start.6 = (bf16[512,256]{1,0:T(8,128)(2,1)S(1)}, bf16[512,256]{1,0:T(8,128)(2,1)S(1)}, u32[]{:S(2)}, u32[]{:S(2)}) collective-permute-start(bf16[512,256]{1,0:T(8,128)(2,1)S(1)} %get-tuple-element.92.refs_4_), channel_id=1, source_target_pairs={{0,48},{8,56},{16,0},{24,8},{32,16},{40,24},{48,32},{56,40},{64,11... | collective-permute-start | bytes 786440 | tf_op jit(solution)/shard_map/ppermute | solution.py:502
  20.5 10.1 %collective-permute-start.5 = (bf16[512,256]{1,0:T(8,128)(2,1)S(1)}, bf16[512,256]{1,0:T(8,128)(2,1)S(1)}, u32[]{:S(2)}, u32[]{:S(2)}) collective-permute-start(bf16[512,256]{1,0:T(8,128)(2,1)S(1)} %get-tuple-element.92.refs_4_), channel_id=1, source_target_pairs={{0,16},{8,24},{16,32},{24,40},{32,48},{40,56},{48,0},{56,8},{64,80... | collective-permute-start | bytes 786440 | tf_op jit(solution)/shard_map/ppermute | solution.py:502
  26.1 11.5 %collective-permute-start.7 = (bf16[512,256]{1,0:T(8,128)(2,1)S(1)}, bf16[512,256]{1,0:T(8,128)(2,1)S(1)}, u32[]{:S(2)}, u32[]{:S(2)}) collective-permute-start(bf16[512,256]{1,0:T(8,128)(2,1)S(1)} %get-tuple-element.92.refs_4_), channel_id=1, source_target_pairs={{0,32},{8,40},{16,48},{24,56},{32,0},{40,8},{48,16},{56,24},{64,96... | collective-permute-start | bytes 786440 | tf_op jit(solution)/shard_map/ppermute | solution.py:502
  37.7 2.8 %collective-permute-start.8 = (bf16[2048,256]{1,0:T(8,128)(2,1)S(1)}, bf16[2048,256]{1,0:T(8,128)(2,1)S(1)}, u32[]{:S(2)}, u32[]{:S(2)}) collective-permute-start(bf16[2048,256]{1,0:T(8,128)(2,1)S(1)} %pad_maximum_fusion), channel_id=1, source_target_pairs={{0,8},{8,0},{16,24},{24,16},{32,40},{40,32},{48,56},{56,48},{64,72... | collective-permute-start | bytes 3145736 | tf_op jit(solution)/shard_map/ppermute | solution.py:502
  49.8 5.3 %collective-permute-start.9 = (f32[32,128]{1,0:T(8,128)S(1)}, f32[32,128]{1,0:T(8,128)S(1)}, u32[]{:S(2)}, u32[]{:S(2)}) collective-permute-start(f32[32,128]{1,0:T(8,128)S(1)} %get-tuple-element.110.own_ref), channel_id=1, source_target_pairs={{0,1},{1,0},{2,3},{3,2},{4,5},{5,4},{6,7},{7,6},{8,9},{9,8},{10,11... | collective-permute-start | bytes 49160 | tf_op jit(solution)/shard_map/ppermute | solution.py:502
  51.0 15.8 %copy-start = (f32[2048]{0:T(1024)S(1)}, f32[2048]{0:T(1024)}, u32[]{:S(2)}) copy-start(f32[2048]{0:T(1024)} %param.9) | copy-start | bytes 24580
  55.1 9.7 %collective-permute-start.12 = (f32[32,128]{1,0:T(8,128)S(1)}, f32[32,128]{1,0:T(8,128)S(1)}, u32[]{:S(2)}, u32[]{:S(2)}) collective-permute-start(f32[32,128]{1,0:T(8,128)S(1)} %join_stats.1.refs_6_), channel_id=1, source_target_pairs={{0,6},{1,7},{2,0},{3,1},{4,2},{5,3},{6,4},{7,5},{8,14},{9,15},{10,... | collective-permute-start | bytes 49160 | tf_op jit(solution)/shard_map/ppermute | solution.py:502
  57.9 6.9 %collective-permute-start.11 = (f32[32,128]{1,0:T(8,128)S(1)}, f32[32,128]{1,0:T(8,128)S(1)}, u32[]{:S(2)}, u32[]{:S(2)}) collective-permute-start(f32[32,128]{1,0:T(8,128)S(1)} %join_stats.1.refs_6_), channel_id=1, source_target_pairs={{0,4},{1,5},{2,6},{3,7},{4,0},{5,1},{6,2},{7,3},{8,12},{9,13},{10,... | collective-permute-start | bytes 49160 | tf_op jit(solution)/shard_map/ppermute | solution.py:502
  61.9 4.9 %collective-permute-start.10 = (f32[32,128]{1,0:T(8,128)S(1)}, f32[32,128]{1,0:T(8,128)S(1)}, u32[]{:S(2)}, u32[]{:S(2)}) collective-permute-start(f32[32,128]{1,0:T(8,128)S(1)} %join_stats.1.refs_6_), channel_id=1, source_target_pairs={{0,2},{1,3},{2,4},{3,5},{4,6},{5,7},{6,0},{7,1},{8,10},{9,11},{10,... | collective-permute-start | bytes 49160 | tf_op jit(solution)/shard_map/ppermute | solution.py:502
  68.9 2.2 %collective-permute-start.13 = (bf16[528,256]{1,0:T(8,128)(2,1)S(1)}, bf16[528,256]{1,0:T(8,128)(2,1)S(1)}, u32[]{:S(2)}, u32[]{:S(2)}) collective-permute-start(bf16[528,256]{1,0:T(8,128)(2,1)S(1)} %get-tuple-element.137), channel_id=1, source_target_pairs={{0,8},{8,0},{16,24},{24,16},{32,40},{40,32},{48,56},{56,48},{64,72... | collective-permute-start | bytes 811016 | tf_op jit(solution)/shard_map/ppermute | solution.py:502
  73.4 13.7 %collective-permute-start.20 = (bf16[1536,256]{1,0:T(8,128)(2,1)S(1)}, bf16[1536,256]{1,0:T(8,128)(2,1)S(1)}, u32[]{:S(2)}, u32[]{:S(2)}) collective-permute-start(bf16[1536,256]{1,0:T(8,128)(2,1)S(1)} %grads_far.1), channel_id=1, source_target_pairs={{0,8},{8,0},{16,24},{24,16},{32,40},{40,32},{48,56},{56,48},{64,72... | collective-permute-start | bytes 2359304 | tf_op jit(solution)/shard_map/ppermute | solution.py:502
  74.0 9.7 %collective-permute-start.14 = (bf16[272,256]{1,0:T(8,128)(2,1)S(1)}, bf16[272,256]{1,0:T(8,128)(2,1)S(1)}, u32[]{:S(2)}, u32[]{:S(2)}) collective-permute-start(bf16[272,256]{1,0:T(8,128)(2,1)S(1)} %get-tuple-element.141), channel_id=1, source_target_pairs={{0,48},{8,56},{16,0},{24,8},{32,16},{40,24},{48,32},{56,40},{64,11... | collective-permute-start | bytes 417800 | tf_op jit(solution)/shard_map/ppermute | solution.py:502
  74.3 6.5 %collective-permute-start.16 = (bf16[256,256]{1,0:T(8,128)(2,1)S(1)}, bf16[256,256]{1,0:T(8,128)(2,1)S(1)}, u32[]{:S(2)}, u32[]{:S(2)}) collective-permute-start(bf16[256,256]{1,0:T(8,128)(2,1)S(1)} %get-tuple-element.143), channel_id=1, source_target_pairs={{0,2},{1,3},{2,4},{3,5},{4,6},{5,7},{6,0},{7,1},{8,10},{9,11},{10,... | collective-permute-start | bytes 393224 | tf_op jit(solution)/shard_map/ppermute | solution.py:502
  74.3 6.5 %collective-permute-start.17 = (bf16[256,256]{1,0:T(8,128)(2,1)S(1)}, bf16[256,256]{1,0:T(8,128)(2,1)S(1)}, u32[]{:S(2)}, u32[]{:S(2)}) collective-permute-start(bf16[256,256]{1,0:T(8,128)(2,1)S(1)} %get-tuple-element.144), channel_id=1, source_target_pairs={{0,6},{1,7},{2,0},{3,1},{4,2},{5,3},{6,4},{7,5},{8,14},{9,15},{10,... | collective-permute-start | bytes 393224 | tf_op jit(solution)/shard_map/ppermute | solution.py:502
  77.5 6.2 %collective-permute-start.15 = (bf16[256,256]{1,0:T(8,128)(2,1)S(1)}, bf16[256,256]{1,0:T(8,128)(2,1)S(1)}, u32[]{:S(2)}, u32[]{:S(2)}) collective-permute-start(bf16[256,256]{1,0:T(8,128)(2,1)S(1)} %get-tuple-element.142), channel_id=1, source_target_pairs={{0,16},{8,24},{16,32},{24,40},{32,48},{40,56},{48,0},{56,8},{64,80... | collective-permute-start | bytes 393224 | tf_op jit(solution)/shard_map/ppermute | solution.py:502
  83.8 7.7 %collective-permute-start.18 = (bf16[512,256]{1,0:T(8,128)(2,1)S(1)}, bf16[512,256]{1,0:T(8,128)(2,1)S(1)}, u32[]{:S(2)}, u32[]{:S(2)}) collective-permute-start(bf16[512,256]{1,0:T(8,128)(2,1)S(1)} %get-tuple-element.147), channel_id=1, source_target_pairs={{0,2},{1,3},{2,4},{3,5},{4,6},{5,7},{6,0},{7,1},{8,10},{9,11},{10,... | collective-permute-start | bytes 786440 | tf_op jit(solution)/shard_map/ppermute | solution.py:502
  83.9 7.6 %collective-permute-start.19 = (bf16[512,256]{1,0:T(8,128)(2,1)S(1)}, bf16[512,256]{1,0:T(8,128)(2,1)S(1)}, u32[]{:S(2)}, u32[]{:S(2)}) collective-permute-start(bf16[512,256]{1,0:T(8,128)(2,1)S(1)} %get-tuple-element.148), channel_id=1, source_target_pairs={{0,6},{1,7},{2,0},{3,1},{4,2},{5,3},{6,4},{7,5},{8,14},{9,15},{10,... | collective-permute-start | bytes 786440 | tf_op jit(solution)/shard_map/ppermute | solution.py:502
  87.3 11.4 %collective-permute-start.21 = (bf16[528,256]{1,0:T(8,128)(2,1)S(1)}, bf16[528,256]{1,0:T(8,128)(2,1)S(1)}, u32[]{:S(2)}, u32[]{:S(2)}) collective-permute-start(bf16[528,256]{1,0:T(8,128)(2,1)S(1)} %get-tuple-element.155), channel_id=1, source_target_pairs={{0,48},{8,56},{16,0},{24,8},{32,16},{40,24},{48,32},{56,40},{64,11... | collective-permute-start | bytes 811016 | tf_op jit(solution)/shard_map/ppermute | solution.py:502
  87.4 11.3 %collective-permute-start.22 = (bf16[528,256]{1,0:T(8,128)(2,1)S(1)}, bf16[528,256]{1,0:T(8,128)(2,1)S(1)}, u32[]{:S(2)}, u32[]{:S(2)}) collective-permute-start(bf16[528,256]{1,0:T(8,128)(2,1)S(1)} %get-tuple-element.156), channel_id=1, source_target_pairs={{0,16},{8,24},{16,32},{24,40},{32,48},{40,56},{48,0},{56,8},{64,80... | collective-permute-start | bytes 811016 | tf_op jit(solution)/shard_map/ppermute | solution.py:502
  91.5 7.2 %collective-permute-start.23 = (bf16[256,256]{1,0:T(8,128)(2,1)S(1)}, bf16[256,256]{1,0:T(8,128)(2,1)S(1)}, u32[]{:S(2)}, u32[]{:S(2)}) collective-permute-start(bf16[256,256]{1,0:T(8,128)(2,1)S(1)} %get-tuple-element.157), channel_id=1, source_target_pairs={{0,1},{1,0},{2,3},{3,2},{4,5},{5,4},{6,7},{7,6},{8,9},{9,8},{10,11... | collective-permute-start | bytes 393224 | tf_op jit(solution)/shard_map/ppermute | solution.py:502
  98.8 5.1 %collective-permute-start.24 = (bf16[272,256]{1,0:T(8,128)(2,1)S(1)}, bf16[272,256]{1,0:T(8,128)(2,1)S(1)}, u32[]{:S(2)}, u32[]{:S(2)}) collective-permute-start(bf16[272,256]{1,0:T(8,128)(2,1)S(1)} %get-tuple-element.163), channel_id=1, source_target_pairs={{0,64},{8,72},{16,80},{24,88},{32,96},{40,104},{48,112},{56,120},{... | collective-permute-start | bytes 417800 | tf_op jit(solution)/shard_map/ppermute | solution.py:502

commit v7 on v6

--- a/solution.py
+++ b/solution.py
@@ -80,6 +80,7 @@
     n = NX * NZ
     steps = n // 2
     chunks = rows // T
+    deep = 2 * T
     first_call = group == "near"
     last_call = group == "far"
     if first_call:
@@ -114,54 +115,43 @@
     def columns(tile):
         return pl.ds(pl.multiple_of(tile * T, T), T)
 
-    class Product:
-        def __init__(self, tile, dst):
-            self.cols, self.dst = columns(tile), dst
-            self.side = users_t[:, self.cols]
-            self.pos = pos_ref[:, self.cols] - lax.broadcasted_iota(jnp.int32, (8, T), 0)
-            self.best = jnp.full((8, T), -jnp.inf, F32)
-            self.found = jnp.zeros((8, T), F32)
-
-        def chunk(self, c):
-            ahead = self.pos - first_row(group, c)
-            prod = jnp.dot(ads_all[c * T : (c + 1) * T, :], self.side, preferred_element_type=F32)
+    def product(tile, dst):
+        side = users_t[:, columns(tile)]
+        for c in range(0, rows, deep):
+            dst[c : c + deep, :] = jnp.dot(ads_all[c : c + deep, :], side, preferred_element_type=F32)
+
+    def exps(tile, src, extra):
+        cols = columns(tile)
+        pos = pos_ref[:, cols] - lax.broadcasted_iota(jnp.int32, (8, T), 0)
+        best = jnp.full((8, T), -jnp.inf, F32)
+        found = jnp.zeros((8, T), F32)
+        for c in range(chunks):
+            ahead = pos - first_row(group, c)
             for r in range(0, T, 8):
-                row = c * T + r
-                logc = logc_all[row : row + 8, :]
-                x = prod[r : r + 8, :] * LOG2E - jnp.concatenate([logc] * (T // LANES), axis=1)
-                self.dst[row : row + 8, :] = x
-                self.best = jnp.maximum(self.best, x)
-                self.found = jnp.where(ahead == r, x, self.found)
-
-        def end(self):
-            top_ref[:, self.cols] = jnp.max(self.best, axis=0, keepdims=True)
-            hit = jnp.sum(self.found, axis=0, keepdims=True)
-            hit_ref[:, self.cols] = hit if first_call else hit + hit_in[:, self.cols]
-
-    class Exps:
-        def __init__(self, tile, src, extra):
-            self.cols, self.src, self.extra = columns(tile), src, extra
-            self.top = top_ref[:, self.cols]
-            self.total = jnp.zeros((8, T), F32)
-
-        def chunk(self, c):
-            for r in range(c * T, (c + 1) * T, 16):
-                e = jnp.exp2(self.src[r : r + 16, :] - self.top)
-                self.total += e[:8] + e[8:]
-                e = e.astype(BF16)
-                p_ref[r : r + 16, self.cols] = e
-                self.extra[r : r + 16, :] = e
-
-        def end(self):
-            cols, top = self.cols, self.top
-            total = jnp.sum(self.total, axis=0, keepdims=True)
-            if first_call:
-                m_ref[:, cols] = top
-                total_ref[:, cols] = total
-            else:
-                m = jnp.maximum(m_in[:, cols], top)
-                m_ref[:, cols] = m
-                total_ref[:, cols] = total_in[:, cols] * jnp.exp2(m_in[:, cols] - m) + total * jnp.exp2(top - m)
+                at = slice(c * T + r, c * T + r + 8)
+                x = src[at, :] * LOG2E - jnp.concatenate([logc_all[at, :]] * (T // LANES), axis=1)
+                src[at, :] = x
+                best = jnp.maximum(best, x)
+                found = jnp.where(ahead == r, x, found)
+        top = jnp.max(best, axis=0, keepdims=True)
+        top_ref[:, cols] = top
+        hit = jnp.sum(found, axis=0, keepdims=True)
+        hit_ref[:, cols] = hit if first_call else hit + hit_in[:, cols]
+        total = jnp.zeros((8, T), F32)
+        for r in range(0, rows, 16):
+            e = jnp.exp2(src[r : r + 16, :] - top)
+            total += e[:8] + e[8:]
+            e = e.astype(BF16)
+            p_ref[r : r + 16, cols] = e
+            extra[r : r + 16, :] = e
+        total = jnp.sum(total, axis=0, keepdims=True)
+        if first_call:
+            m_ref[:, cols] = top
+            total_ref[:, cols] = total
+        else:
+            m = jnp.maximum(m_in[:, cols], top)
+            m_ref[:, cols] = m
+            total_ref[:, cols] = total_in[:, cols] * jnp.exp2(m_in[:, cols] - m) + total * jnp.exp2(top - m)
 
     def gather(tile, e):
         cols = columns(tile)
@@ -174,17 +164,10 @@
 
     def turn(tile, src, dst, e_now, e_before):
         gather(jnp.maximum(tile - 1, 0), e_before)
-        product, exps = Product(jnp.minimum(tile + 1, n - 1), dst), Exps(tile, src, e_now)
-        for c in range(chunks):
-            product.chunk(c)
-            exps.chunk(c)
-        product.end()
-        exps.end()
-
-    opening = Product(0, s0)
-    for c in range(chunks):
-        opening.chunk(c)
-    opening.end()
+        product(jnp.minimum(tile + 1, n - 1), dst)
+        exps(tile, src, e_now)
+
+    product(0, s0)
     e0, e1 = late
     e1[...] = jnp.zeros_like(e1)
     m_ref[...] = jnp.zeros_like(m_ref) if first_call else m_in[...]
@@ -558,20 +541,20 @@
         acc, m, rows_a, rows_b, hits, weight_row, (stats, *moved), inv
     )
     tail = (lse, coefs, weight_row, pos_row, loss)
+    du_2a, du_2b = shift_x(du_2a, 1), shift_x(du_2b, -1)
     pay_2, da_2 = run_grads("mid", [("far", 3, p_far, top_far), ("two", 0, p_two, top_two)], staged, *tail)
     back_2 = swap_core(pay_2)
     da_2, staged = lax.optimization_barrier((da_2, staged))
+    (da_far,) = run_grads("far", [("far", i, p_far, top_far) for i in range(3)], staged, *tail)
+    da_far, back_2, du_2a, du_2b = lax.optimization_barrier((da_far, back_2, du_2a, du_2b))
+    du_1, du_3 = add_halves(du_1, du_3, du_2a, du_2b)
+    back = swap_core(da_far)
+    first, second, both = add_mid(da_2, back_2)
+    first, second, du_1, du_3, staged = lax.optimization_barrier((first, second, du_1, du_3, staged))
+    first, second = shift_y(first, -1), shift_y(second, 1)
+    du_1, du_3 = shift_x(du_1, 1), shift_x(du_3, -1)
     (da_near,) = run_grads("near", [("near", i, p_near, top_near) for i in range(3)], staged, *tail)
-    da_near, back_2 = lax.optimization_barrier((da_near, back_2))
-    first, second, both = add_mid(da_2, back_2)
-    first, second, staged = lax.optimization_barrier((first, second, staged))
-    first, second = shift_y(first, -1), shift_y(second, 1)
-    du_2a, du_2b = shift_x(du_2a, 1), shift_x(du_2b, -1)
-    (da_far,) = run_grads("far", [("far", i, p_far, top_far) for i in range(3)], staged, *tail)
-    back = swap_core(da_far)
-    first, second, du_2a, du_2b = lax.optimization_barrier((first, second, du_2a, du_2b))
-    du_1, du_3 = add_halves(du_1, du_3, du_2a, du_2b)
-    du_1, du_3 = shift_x(du_1, 1), shift_x(du_3, -1)
+    da_near, first, second, du_1, du_3 = lax.optimization_barrier((da_near, first, second, du_1, du_3))
     kept, one, three = add_near(da_near, back, both, first, second)
     one, three = shift_y(one, -1), shift_y(three, 1)
     keep_u, send_u = add_users((du_0, du_1, du_3))

time: 106 us -> 105 us (level)
  Pallas kernels: 32.7 us -> 34.8 us
  waiting for transfers between devices: 30.5 us -> 29.2 us
  starting transfers between devices: 38.3 us -> 37 us
    pallas_call x16, Pallas kernels: 32.7 us -> 34.8 us  [call(): pl.pallas_call(kernel, in_specs=[vmem] * len(args), out_specs=[vmem] * le...]
    ppermute x25, starting transfers between devices: 38.3 us -> 37 us  [move(): lax.ppermute(x, axis, [(i, target(i)) for i in range(lax.axis_size(axis))])]
    ppermute x25, waiting for transfers between devices: 30.5 us -> 29.2 us  [move(): lax.ppermute(x, axis, [(i, target(i)) for i in range(lax.axis_size(axis))])]
  transfers between devices with their start and end apart: 25 -> 25, of which waited for: 12 -> 13; matrix products, arithmetic and copies ran while one was open for 1% -> 1% of each run, Pallas kernels for 17% -> 20%
where the time goes in v7:
time: 105 us; the launch traced here: 104 us
  starting transfers between devices  37 us (35%)
  Pallas kernels  34.8 us (33%)
  waiting for transfers between devices  29.2 us (28%)
  other arithmetic  2.5 us (2%)
    ppermute x25, starting transfers between devices, move(): lax.ppermute(x, axis, [(i, target(i)) for i in range(lax.axis_size(axis))])  37 us
    pallas_call x16, Pallas kernels, call(): pl.pallas_call(kernel, in_specs=[vmem] * len(args), out_specs=[vmem] * le...  34.8 us
    ppermute x25, waiting for transfers between devices, move(): lax.ppermute(x, axis, [(i, target(i)) for i in range(lax.axis_size(axis))])  29.2 us
  transfers between devices with their start and end apart: 25, of which 13 were waited for; matrix products, arithmetic and copies ran while one was open for 1% of the time, Pallas kernels for 20%

profile of v7, /device:TPU:0, one launch (start us, length us, event | category | flops | bytes accessed | tf_op | source)
XLA Modules:
  0.0 104.3 jit_solution(12687767405488735892)
XLA Ops:
  0.6 4.0 %collective-permute-start = (bf16[256,256]{1,0:T(8,128)(2,1)}, bf16[256,256]{1,0:T(8,128)(2,1)S(1)}, u32[]{:S(2)}, u32[]{:S(2)}) collective-permute-start(bf16[256,256]{1,0:T(8,128)(2,1)} %param.5), channel_id=1, source_target_pairs={{0,1},{1,0},{2,3},{3,2},{4,5},{5,4},{6,7},{7,6},{8,9},{9,8},{10,11... | collective-permute-start | bytes 393224 | tf_op jit(solution)/shard_map/ppermute | solution.py:485
  4.7 1.0 collective-permute-start.1
  7.1 2.1 %collective-permute-done = bf16[256,256]{1,0:T(8,128)(2,1)S(1)} collective-permute-done((bf16[256,256]{1,0:T(8,128)(2,1)}, bf16[256,256]{1,0:T(8,128)(2,1)S(1)}, u32[]{:S(2)}, u32[]{:S(2)}) %collective-permute-start) | collective-permute-done | bytes 131104 | tf_op jit(solution)/shard_map/ppermute | solution.py:485
  9.2 2.7 %collective-permute-done.1 = bf16[256,256]{1,0:T(8,128)(2,1)S(1)} collective-permute-done((bf16[256,256]{1,0:T(8,128)(2,1)}, bf16[256,256]{1,0:T(8,128)(2,1)S(1)}, u32[]{:S(2)}, u32[]{:S(2)}) %collective-permute-start.1) | collective-permute-done | bytes 131104 | tf_op jit(solution)/shard_map/ppermute | solution.py:485
  11.9 1.0 pad_maximum_fusion.1
  12.9 2.8 %collective-permute-start.4 = (bf16[512,256]{1,0:T(8,128)(2,1)S(1)}, bf16[512,256]{1,0:T(8,128)(2,1)S(1)}, u32[]{:S(2)}, u32[]{:S(2)}) collective-permute-start(bf16[512,256]{1,0:T(8,128)(2,1)S(1)} %get-tuple-element.93.refs_0_), channel_id=1, source_target_pairs={{0,6},{1,7},{2,0},{3,1},{4,2},{5,3},{6,4},{7,5},{8,14},{9,15},{10,... | collective-permute-start | bytes 786440 | tf_op jit(solution)/shard_map/ppermute | solution.py:485
  17.4 3.0 %collective-permute-start.6 = (bf16[512,256]{1,0:T(8,128)(2,1)S(1)}, bf16[512,256]{1,0:T(8,128)(2,1)S(1)}, u32[]{:S(2)}, u32[]{:S(2)}) collective-permute-start(bf16[512,256]{1,0:T(8,128)(2,1)S(1)} %get-tuple-element.97.refs_4_), channel_id=1, source_target_pairs={{0,48},{8,56},{16,0},{24,8},{32,16},{40,24},{48,32},{56,40},{64,11... | collective-permute-start | bytes 786440 | tf_op jit(solution)/shard_map/ppermute | solution.py:485
  20.5 5.6 %collective-permute-done.4.refs_3_ = bf16[512,256]{1,0:T(8,128)(2,1)S(1)} collective-permute-done((bf16[512,256]{1,0:T(8,128)(2,1)S(1)}, bf16[512,256]{1,0:T(8,128)(2,1)S(1)}, u32[]{:S(2)}, u32[]{:S(2)}) %collective-permute-start.4) | collective-permute-done | bytes 262176 | tf_op jit(solution)/shard_map/ppermute | solution.py:485
  26.1 3.2 %collective-permute-start.7 = (bf16[512,256]{1,0:T(8,128)(2,1)S(1)}, bf16[512,256]{1,0:T(8,128)(2,1)S(1)}, u32[]{:S(2)}, u32[]{:S(2)}) collective-permute-start(bf16[512,256]{1,0:T(8,128)(2,1)S(1)} %get-tuple-element.97.refs_4_), channel_id=1, source_target_pairs={{0,32},{8,40},{16,48},{24,56},{32,0},{40,8},{48,16},{56,24},{64,96... | collective-permute-start | bytes 786440 | tf_op jit(solution)/shard_map/ppermute | solution.py:485
  30.5 8.1 %logits_near.1 = (bf16[1536,2048]{1,0:T(8,128)(2,1)S(1)}, f32[1,2048]{1,0:T(1,128)S(1)}, bf16[256,1536]{1,0:T(8,128)(2,1)S(1)}, f32[256,2048]{1,0:T(8,128)S(1)},...) custom-call(bf16[512,256]{1,0:T(8,128)(2,1)S(1)} %get-tuple-element., ...), custom_call_target="tpu_custom_call" | custom-call | flops 100663296 | bytes 393216 | tf_op jit(solution)/shard_map/logits_near/pallas_call | solution.py:25
  38.8 2.5 %logits_two.1 = (bf16[512,2048]{1,0:T(8,128)(2,1)S(1)}, f32[1,2048]{1,0:T(1,128)S(1)}, bf16[256,512]{1,0:T(8,128)(2,1)S(1)}, f32[256,2048]{1,0:T(8,128)S(1)}, f3...) custom-call(bf16[256,2048]{1,0:T(8,128)(2,1)S(1)} %get-tuple-element.100.refs_0_, ...), custom_call_target="tpu_custom_call" | custom-call | flops 33554432 | bytes 131072 | tf_op jit(solution)/shard_map/logits_two/pallas_call | solution.py:25
  41.5 10.5 %logits_far.1 = (bf16[2048,2048]{1,0:T(8,128)(2,1)S(1)}, f32[1,2048]{1,0:T(1,128)S(1)}, bf16[256,2048]{1,0:T(8,128)(2,1)S(1)}, f32[256,2048]{1,0:T(8,128)S(1)}, ...) custom-call(bf16[256,2048]{1,0:T(8,128)(2,1)S(1)} %get-tuple-element.100.refs_0_, ...), custom_call_target="tpu_custom_call" | custom-call | flops 134217728 | bytes 524288 | tf_op jit(solution)/shard_map/logits_far/pallas_call | solution.py:25
  52.0 1.2 %collective-permute-start.9 = (f32[32,128]{1,0:T(8,128)S(1)}, f32[32,128]{1,0:T(8,128)S(1)}, u32[]{:S(2)}, u32[]{:S(2)}) collective-permute-start(f32[32,128]{1,0:T(8,128)S(1)} %get-tuple-element.115.own_ref), channel_id=1, source_target_pairs={{0,1},{1,0},{2,3},{3,2},{4,5},{5,4},{6,7},{7,6},{8,9},{9,8},{10,11... | collective-permute-start | bytes 49160 | tf_op jit(solution)/shard_map/ppermute | solution.py:485
  53.2 2.9 %positive_rows.2.refs_2_ = bf16[256,1024]{1,0:T(8,128)(2,1)S(1)} custom-call(bf16[256,1536]{1,0:T(8,128)(2,1)S(1)} %get-tuple-element.116.refs_0_, bf16[256,512]{1,0:T(8,128)(2,1)S(1)} %get-tuple-element.117.refs_1_, bf16[256,2048]{1,0:T(8,128)(2,1)S(1)} %get-tuple-element.118.refs_2_, s32[1,2048]{1,0:T(1,128)S(1)} %bitcast.7), custom_call_target="tpu_custom_call" | custom-call | flops 134217728 | bytes 524288 | tf_op jit(solution)/shard_map/positive_rows/pallas_call | solution.py:25
  56.1 1.2 %collective-permute-done.9.other_ref = f32[32,128]{1,0:T(8,128)S(1)} collective-permute-done((f32[32,128]{1,0:T(8,128)S(1)}, f32[32,128]{1,0:T(8,128)S(1)}, u32[]{:S(2)}, u32[]{:S(2)}) %collective-permute-start.9) | collective-permute-done | bytes 16416 | tf_op jit(solution)/shard_map/ppermute | solution.py:485
  57.3 2.7 %collective-permute-start.12 = (f32[32,128]{1,0:T(8,128)S(1)}, f32[32,128]{1,0:T(8,128)S(1)}, u32[]{:S(2)}, u32[]{:S(2)}) collective-permute-start(f32[32,128]{1,0:T(8,128)S(1)} %join_stats.1.refs_6_), channel_id=1, source_target_pairs={{0,6},{1,7},{2,0},{3,1},{4,2},{5,3},{6,4},{7,5},{8,14},{9,15},{10,... | collective-permute-start | bytes 49160 | tf_op jit(solution)/shard_map/ppermute | solution.py:485
  60.0 4.0 %collective-permute-start.11 = (f32[32,128]{1,0:T(8,128)S(1)}, f32[32,128]{1,0:T(8,128)S(1)}, u32[]{:S(2)}, u32[]{:S(2)}) collective-permute-start(f32[32,128]{1,0:T(8,128)S(1)} %join_stats.1.refs_6_), channel_id=1, source_target_pairs={{0,4},{1,5},{2,6},{3,7},{4,0},{5,1},{6,2},{7,3},{8,12},{9,13},{10,... | collective-permute-start | bytes 49160 | tf_op jit(solution)/shard_map/ppermute | solution.py:485
  64.0 2.9 %positive_rows.3.refs_3_ = bf16[256,1024]{1,0:T(8,128)(2,1)S(1)} custom-call(bf16[256,1536]{1,0:T(8,128)(2,1)S(1)} %get-tuple-element.116.refs_0_, bf16[256,512]{1,0:T(8,128)(2,1)S(1)} %get-tuple-element.117.refs_1_, bf16[256,2048]{1,0:T(8,128)(2,1)S(1)} %get-tuple-element.118.refs_2_, s32[1,2048]{1,0:T(1,128)S(1)} %bitcast.8), custom_call_target="tpu_custom_call" | custom-call | flops 134217728 | bytes 524288 | tf_op jit(solution)/shard_map/positive_rows/pallas_call | solution.py:25
  67.0 2.0 %collective-permute-done.10.refs_7_ = f32[32,128]{1,0:T(8,128)S(1)} collective-permute-done((f32[32,128]{1,0:T(8,128)S(1)}, f32[32,128]{1,0:T(8,128)S(1)}, u32[]{:S(2)}, u32[]{:S(2)}) %collective-permute-start.10) | collective-permute-done | bytes 16416 | tf_op jit(solution)/shard_map/ppermute | solution.py:485
  69.6 1.4 %grads_mid.1 = (bf16[528,256]{1,0:T(8,128)(2,1)S(1)}, bf16[528,256]{1,0:T(8,128)(2,1)S(1)}) custom-call(bf16[2048,256]{1,0:T(8,128)(2,1)S(1)} %get-tuple-element.150.refs_0_, f32[1,2048]{1,0:T(1,128)S(1)} %get-tuple-element.128.refs_1_, f32[1,2048]{1,0:T(1,128)S(1)} %get-tuple-element.129.refs_2_, f32[1,2048]{1,0:T(1,128)S(1)} %bitcast.16, ...), custom_call_target="tpu_custom_call" | custom-call | flops 67108864 | bytes 262144 | tf_op jit(solution)/shard_map/grads_mid/pallas_call | solution.py:25
  71.3 3.2 %collective-permute-start.15 = (bf16[256,256]{1,0:T(8,128)(2,1)S(1)}, bf16[256,256]{1,0:T(8,128)(2,1)S(1)}, u32[]{:S(2)}, u32[]{:S(2)}) collective-permute-start(bf16[256,256]{1,0:T(8,128)(2,1)S(1)} %get-tuple-element.140), channel_id=1, source_target_pairs={{0,6},{1,7},{2,0},{3,1},{4,2},{5,3},{6,4},{7,5},{8,14},{9,15},{10,... | collective-permute-start | bytes 393224 | tf_op jit(solution)/shard_map/ppermute | solution.py:485
  74.5 2.1 %grads_far.1 = bf16[1536,256]{1,0:T(8,128)(2,1)S(1)} custom-call(bf16[2048,256]{1,0:T(8,128)(2,1)S(1)} %get-tuple-element.150.refs_0_, f32[1,2048]{1,0:T(1,128)S(1)} %get-tuple-element.128.refs_1_, f32[1,2048]{1,0:T(1,128)S(1)} %get-tuple-element.129.refs_2_, f32[1,2048]{1,0:T(1,128)S(1)} %bitcast.17, s32[1,2048]{1,0:T(1,128)S(1)} %bitcast.10, ...), custom_call_target="tpu_custom_call" | custom-call | flops 100663296 | bytes 393216 | tf_op jit(solution)/shard_map/grads_far/pallas_call | solution.py:25
  76.6 1.7 %collective-permute-done.14.first_ref = bf16[256,256]{1,0:T(8,128)(2,1)S(1)} collective-permute-done((bf16[256,256]{1,0:T(8,128)(2,1)S(1)}, bf16[256,256]{1,0:T(8,128)(2,1)S(1)}, u32[]{:S(2)}, u32[]{:S(2)}) %collective-permute-start.14) | collective-permute-done | bytes 131104 | tf_op jit(solution)/shard_map/ppermute | solution.py:485
  78.6 3.2 %collective-permute-start.19 = (bf16[512,256]{1,0:T(8,128)(2,1)S(1)}, bf16[512,256]{1,0:T(8,128)(2,1)S(1)}, u32[]{:S(2)}, u32[]{:S(2)}) collective-permute-start(bf16[512,256]{1,0:T(8,128)(2,1)S(1)} %get-tuple-element.156), channel_id=1, source_target_pairs={{0,6},{1,7},{2,0},{3,1},{4,2},{5,3},{6,4},{7,5},{8,14},{9,15},{10,... | collective-permute-start | bytes 786440 | tf_op jit(solution)/shard_map/ppermute | solution.py:485
  82.1 1.7 %collective-permute-start.17 = (bf16[256,256]{1,0:T(8,128)(2,1)S(1)}, bf16[256,256]{1,0:T(8,128)(2,1)S(1)}, u32[]{:S(2)}, u32[]{:S(2)}) collective-permute-start(bf16[256,256]{1,0:T(8,128)(2,1)S(1)} %get-tuple-element.154), channel_id=1, source_target_pairs={{0,16},{8,24},{16,32},{24,40},{32,48},{40,56},{48,0},{56,8},{64,80... | collective-permute-start | bytes 393224 | tf_op jit(solution)/shard_map/ppermute | solution.py:485
  83.8 2.1 %grads_near.1.near_ref = bf16[1536,256]{1,0:T(8,128)(2,1)S(1)} custom-call(bf16[2048,256]{1,0:T(8,128)(2,1)S(1)} %get-tuple-element.150.refs_0_, f32[1,2048]{1,0:T(1,128)S(1)} %get-tuple-element.128.refs_1_, f32[1,2048]{1,0:T(1,128)S(1)} %get-tuple-element.129.refs_2_, f32[1,2048]{1,0:T(1,128)S(1)} %bitcast.18, s32[1,2048]{1,0:T(1,128)S(1)} %bitcast.11, ...), custom_call_target="tpu_custom_call" | custom-call | flops 100663296 | bytes 393216 | tf_op jit(solution)/shard_map/grads_near/pallas_call | solution.py:25
  85.9 2.5 %collective-permute-done.17.second_ref = bf16[256,256]{1,0:T(8,128)(2,1)S(1)} collective-permute-done((bf16[256,256]{1,0:T(8,128)(2,1)S(1)}, bf16[256,256]{1,0:T(8,128)(2,1)S(1)}, u32[]{:S(2)}, u32[]{:S(2)}) %collective-permute-start.17) | collective-permute-done | bytes 131104 | tf_op jit(solution)/shard_map/ppermute | solution.py:485
  89.2 1.6 %collective-permute-start.22 = (bf16[528,256]{1,0:T(8,128)(2,1)S(1)}, bf16[528,256]{1,0:T(8,128)(2,1)S(1)}, u32[]{:S(2)}, u32[]{:S(2)}) collective-permute-start(bf16[528,256]{1,0:T(8,128)(2,1)S(1)} %get-tuple-element.166), channel_id=1, source_target_pairs={{0,16},{8,24},{16,32},{24,40},{32,48},{40,56},{48,0},{56,8},{64,80... | collective-permute-start | bytes 811016 | tf_op jit(solution)/shard_map/ppermute | solution.py:485
  90.9 1.3 %collective-permute-start.23 = (bf16[256,256]{1,0:T(8,128)(2,1)S(1)}, bf16[256,256]{1,0:T(8,128)(2,1)S(1)}, u32[]{:S(2)}, u32[]{:S(2)}) collective-permute-start(bf16[256,256]{1,0:T(8,128)(2,1)S(1)} %get-tuple-element.167), channel_id=1, source_target_pairs={{0,1},{1,0},{2,3},{3,2},{4,5},{5,4},{6,7},{7,6},{8,9},{9,8},{10,11... | collective-permute-start | bytes 393224 | tf_op jit(solution)/shard_map/ppermute | solution.py:485
  92.2 5.3 %collective-permute-done.23.received_u_ref = bf16[256,256]{1,0:T(8,128)(2,1)S(1)} collective-permute-done((bf16[256,256]{1,0:T(8,128)(2,1)S(1)}, bf16[256,256]{1,0:T(8,128)(2,1)S(1)}, u32[]{:S(2)}, u32[]{:S(2)}) %collective-permute-start.23) | collective-permute-done | bytes 131104 | tf_op jit(solution)/shard_map/ppermute | solution.py:485
  98.2 1.1 %collective-permute-start.24 = (bf16[272,256]{1,0:T(8,128)(2,1)S(1)}, bf16[272,256]{1,0:T(8,128)(2,1)S(1)}, u32[]{:S(2)}, u32[]{:S(2)}) collective-permute-start(bf16[272,256]{1,0:T(8,128)(2,1)S(1)} %get-tuple-element.173), channel_id=1, source_target_pairs={{0,64},{8,72},{16,80},{24,88},{32,96},{40,104},{48,112},{56,120},{... | collective-permute-start | bytes 417800 | tf_op jit(solution)/shard_map/ppermute | solution.py:485
  99.3 4.0 %collective-permute-done.24.received_ref = bf16[272,256]{1,0:T(8,128)(2,1)S(1)} collective-permute-done((bf16[272,256]{1,0:T(8,128)(2,1)S(1)}, bf16[272,256]{1,0:T(8,128)(2,1)S(1)}, u32[]{:S(2)}, u32[]{:S(2)}) %collective-permute-start.24) | collective-permute-done | bytes 139296 | tf_op jit(solution)/shard_map/ppermute | solution.py:485
  (40 shorter events, 8.5 us)
Async XLA Ops:
  0.6 8.6 %collective-permute-start = (bf16[256,256]{1,0:T(8,128)(2,1)}, bf16[256,256]{1,0:T(8,128)(2,1)S(1)}, u32[]{:S(2)}, u32[]{:S(2)}) collective-permute-start(bf16[256,256]{1,0:T(8,128)(2,1)} %param.5), channel_id=1, source_target_pairs={{0,1},{1,0},{2,3},{3,2},{4,5},{5,4},{6,7},{7,6},{8,9},{9,8},{10,11... | collective-permute-start | bytes 393224 | tf_op jit(solution)/shard_map/ppermute | solution.py:485
  4.7 7.2 %collective-permute-start.1 = (bf16[256,256]{1,0:T(8,128)(2,1)}, bf16[256,256]{1,0:T(8,128)(2,1)S(1)}, u32[]{:S(2)}, u32[]{:S(2)}) collective-permute-start(bf16[256,256]{1,0:T(8,128)(2,1)} %param.6), channel_id=1, source_target_pairs={{0,64},{8,72},{16,80},{24,88},{32,96},{40,104},{48,112},{56,120},{... | collective-permute-start | bytes 393224 | tf_op jit(solution)/shard_map/ppermute | solution.py:485
  12.9 13.2 %collective-permute-start.4 = (bf16[512,256]{1,0:T(8,128)(2,1)S(1)}, bf16[512,256]{1,0:T(8,128)(2,1)S(1)}, u32[]{:S(2)}, u32[]{:S(2)}) collective-permute-start(bf16[512,256]{1,0:T(8,128)(2,1)S(1)} %get-tuple-element.93.refs_0_), channel_id=1, source_target_pairs={{0,6},{1,7},{2,0},{3,1},{4,2},{5,3},{6,4},{7,5},{8,14},{9,15},{10,... | collective-permute-start | bytes 786440 | tf_op jit(solution)/shard_map/ppermute | solution.py:485
  15.8 13.5 %collective-permute-start.3 = (bf16[512,256]{1,0:T(8,128)(2,1)S(1)}, bf16[512,256]{1,0:T(8,128)(2,1)S(1)}, u32[]{:S(2)}, u32[]{:S(2)}) collective-permute-start(bf16[512,256]{1,0:T(8,128)(2,1)S(1)} %get-tuple-element.93.refs_0_), channel_id=1, source_target_pairs={{0,4},{1,5},{2,6},{3,7},{4,0},{5,1},{6,2},{7,3},{8,12},{9,13},{10,... | collective-permute-start | bytes 786440 | tf_op jit(solution)/shard_map/ppermute | solution.py:485
  16.6 13.2 %collective-permute-start.2 = (bf16[512,256]{1,0:T(8,128)(2,1)S(1)}, bf16[512,256]{1,0:T(8,128)(2,1)S(1)}, u32[]{:S(2)}, u32[]{:S(2)}) collective-permute-start(bf16[512,256]{1,0:T(8,128)(2,1)S(1)} %get-tuple-element.93.refs_0_), channel_id=1, source_target_pairs={{0,2},{1,3},{2,4},{3,5},{4,6},{5,7},{6,0},{7,1},{8,10},{9,11},{10,... | collective-permute-start | bytes 786440 | tf_op jit(solution)/shard_map/ppermute | solution.py:485
  17.4 12.3 %collective-permute-start.6 = (bf16[512,256]{1,0:T(8,128)(2,1)S(1)}, bf16[512,256]{1,0:T(8,128)(2,1)S(1)}, u32[]{:S(2)}, u32[]{:S(2)}) collective-permute-start(bf16[512,256]{1,0:T(8,128)(2,1)S(1)} %get-tuple-element.97.refs_4_), channel_id=1, source_target_pairs={{0,48},{8,56},{16,0},{24,8},{32,16},{40,24},{48,32},{56,40},{64,11... | collective-permute-start | bytes 786440 | tf_op jit(solution)/shard_map/ppermute | solution.py:485
  20.5 10.1 %collective-permute-start.5 = (bf16[512,256]{1,0:T(8,128)(2,1)S(1)}, bf16[512,256]{1,0:T(8,128)(2,1)S(1)}, u32[]{:S(2)}, u32[]{:S(2)}) collective-permute-start(bf16[512,256]{1,0:T(8,128)(2,1)S(1)} %get-tuple-element.97.refs_4_), channel_id=1, source_target_pairs={{0,16},{8,24},{16,32},{24,40},{32,48},{40,56},{48,0},{56,8},{64,80... | collective-permute-start | bytes 786440 | tf_op jit(solution)/shard_map/ppermute | solution.py:485
  26.1 12.5 %collective-permute-start.7 = (bf16[512,256]{1,0:T(8,128)(2,1)S(1)}, bf16[512,256]{1,0:T(8,128)(2,1)S(1)}, u32[]{:S(2)}, u32[]{:S(2)}) collective-permute-start(bf16[512,256]{1,0:T(8,128)(2,1)S(1)} %get-tuple-element.97.refs_4_), channel_id=1, source_target_pairs={{0,32},{8,40},{16,48},{24,56},{32,0},{40,8},{48,16},{56,24},{64,96... | collective-permute-start | bytes 786440 | tf_op jit(solution)/shard_map/ppermute | solution.py:485
  38.7 2.7 %collective-permute-start.8 = (bf16[2048,256]{1,0:T(8,128)(2,1)S(1)}, bf16[2048,256]{1,0:T(8,128)(2,1)S(1)}, u32[]{:S(2)}, u32[]{:S(2)}) collective-permute-start(bf16[2048,256]{1,0:T(8,128)(2,1)S(1)} %pad_maximum_fusion), channel_id=1, source_target_pairs={{0,8},{8,0},{16,24},{24,16},{32,40},{40,32},{48,56},{56,48},{64,72... | collective-permute-start | bytes 3145736 | tf_op jit(solution)/shard_map/ppermute | solution.py:485
  52.0 5.2 %collective-permute-start.9 = (f32[32,128]{1,0:T(8,128)S(1)}, f32[32,128]{1,0:T(8,128)S(1)}, u32[]{:S(2)}, u32[]{:S(2)}) collective-permute-start(f32[32,128]{1,0:T(8,128)S(1)} %get-tuple-element.115.own_ref), channel_id=1, source_target_pairs={{0,1},{1,0},{2,3},{3,2},{4,5},{5,4},{6,7},{7,6},{8,9},{9,8},{10,11... | collective-permute-start | bytes 49160 | tf_op jit(solution)/shard_map/ppermute | solution.py:485
  53.2 15.8 %copy-start = (f32[2048]{0:T(1024)S(1)}, f32[2048]{0:T(1024)}, u32[]{:S(2)}) copy-start(f32[2048]{0:T(1024)} %param.9) | copy-start | bytes 24580
  57.3 9.7 %collective-permute-start.12 = (f32[32,128]{1,0:T(8,128)S(1)}, f32[32,128]{1,0:T(8,128)S(1)}, u32[]{:S(2)}, u32[]{:S(2)}) collective-permute-start(f32[32,128]{1,0:T(8,128)S(1)} %join_stats.1.refs_6_), channel_id=1, source_target_pairs={{0,6},{1,7},{2,0},{3,1},{4,2},{5,3},{6,4},{7,5},{8,14},{9,15},{10,... | collective-permute-start | bytes 49160 | tf_op jit(solution)/shard_map/ppermute | solution.py:485
  60.0 6.9 %collective-permute-start.11 = (f32[32,128]{1,0:T(8,128)S(1)}, f32[32,128]{1,0:T(8,128)S(1)}, u32[]{:S(2)}, u32[]{:S(2)}) collective-permute-start(f32[32,128]{1,0:T(8,128)S(1)} %join_stats.1.refs_6_), channel_id=1, source_target_pairs={{0,4},{1,5},{2,6},{3,7},{4,0},{5,1},{6,2},{7,3},{8,12},{9,13},{10,... | collective-permute-start | bytes 49160 | tf_op jit(solution)/shard_map/ppermute | solution.py:485
  64.0 4.9 %collective-permute-start.10 = (f32[32,128]{1,0:T(8,128)S(1)}, f32[32,128]{1,0:T(8,128)S(1)}, u32[]{:S(2)}, u32[]{:S(2)}) collective-permute-start(f32[32,128]{1,0:T(8,128)S(1)} %join_stats.1.refs_6_), channel_id=1, source_target_pairs={{0,2},{1,3},{2,4},{3,5},{4,6},{5,7},{6,0},{7,1},{8,10},{9,11},{10,... | collective-permute-start | bytes 49160 | tf_op jit(solution)/shard_map/ppermute | solution.py:485
  71.1 7.2 %collective-permute-start.13 = (bf16[528,256]{1,0:T(8,128)(2,1)S(1)}, bf16[528,256]{1,0:T(8,128)(2,1)S(1)}, u32[]{:S(2)}, u32[]{:S(2)}) collective-permute-start(bf16[528,256]{1,0:T(8,128)(2,1)S(1)} %get-tuple-element.138), channel_id=1, source_target_pairs={{0,8},{8,0},{16,24},{24,16},{32,40},{40,32},{48,56},{56,48},{64,72... | collective-permute-start | bytes 811016 | tf_op jit(solution)/shard_map/ppermute | solution.py:485
  71.2 7.1 %collective-permute-start.14 = (bf16[256,256]{1,0:T(8,128)(2,1)S(1)}, bf16[256,256]{1,0:T(8,128)(2,1)S(1)}, u32[]{:S(2)}, u32[]{:S(2)}) collective-permute-start(bf16[256,256]{1,0:T(8,128)(2,1)S(1)} %get-tuple-element.139), channel_id=1, source_target_pairs={{0,2},{1,3},{2,4},{3,5},{4,6},{5,7},{6,0},{7,1},{8,10},{9,11},{10,... | collective-permute-start | bytes 393224 | tf_op jit(solution)/shard_map/ppermute | solution.py:485
  71.3 7.0 %collective-permute-start.15 = (bf16[256,256]{1,0:T(8,128)(2,1)S(1)}, bf16[256,256]{1,0:T(8,128)(2,1)S(1)}, u32[]{:S(2)}, u32[]{:S(2)}) collective-permute-start(bf16[256,256]{1,0:T(8,128)(2,1)S(1)} %get-tuple-element.140), channel_id=1, source_target_pairs={{0,6},{1,7},{2,0},{3,1},{4,2},{5,3},{6,4},{7,5},{8,14},{9,15},{10,... | collective-permute-start | bytes 393224 | tf_op jit(solution)/shard_map/ppermute | solution.py:485
  78.3 10.2 %collective-permute-start.20 = (bf16[1536,256]{1,0:T(8,128)(2,1)S(1)}, bf16[1536,256]{1,0:T(8,128)(2,1)S(1)}, u32[]{:S(2)}, u32[]{:S(2)}) collective-permute-start(bf16[1536,256]{1,0:T(8,128)(2,1)S(1)} %grads_far.1), channel_id=1, source_target_pairs={{0,8},{8,0},{16,24},{24,16},{32,40},{40,32},{48,56},{56,48},{64,72... | collective-permute-start | bytes 2359304 | tf_op jit(solution)/shard_map/ppermute | solution.py:485
  78.5 10.0 %collective-permute-start.18 = (bf16[512,256]{1,0:T(8,128)(2,1)S(1)}, bf16[512,256]{1,0:T(8,128)(2,1)S(1)}, u32[]{:S(2)}, u32[]{:S(2)}) collective-permute-start(bf16[512,256]{1,0:T(8,128)(2,1)S(1)} %get-tuple-element.155), channel_id=1, source_target_pairs={{0,2},{1,3},{2,4},{3,5},{4,6},{5,7},{6,0},{7,1},{8,10},{9,11},{10,... | collective-permute-start | bytes 786440 | tf_op jit(solution)/shard_map/ppermute | solution.py:485
  78.6 9.9 %collective-permute-start.19 = (bf16[512,256]{1,0:T(8,128)(2,1)S(1)}, bf16[512,256]{1,0:T(8,128)(2,1)S(1)}, u32[]{:S(2)}, u32[]{:S(2)}) collective-permute-start(bf16[512,256]{1,0:T(8,128)(2,1)S(1)} %get-tuple-element.156), channel_id=1, source_target_pairs={{0,6},{1,7},{2,0},{3,1},{4,2},{5,3},{6,4},{7,5},{8,14},{9,15},{10,... | collective-permute-start | bytes 786440 | tf_op jit(solution)/shard_map/ppermute | solution.py:485
  81.8 6.7 %collective-permute-start.16 = (bf16[272,256]{1,0:T(8,128)(2,1)S(1)}, bf16[272,256]{1,0:T(8,128)(2,1)S(1)}, u32[]{:S(2)}, u32[]{:S(2)}) collective-permute-start(bf16[272,256]{1,0:T(8,128)(2,1)S(1)} %get-tuple-element.153), channel_id=1, source_target_pairs={{0,48},{8,56},{16,0},{24,8},{32,16},{40,24},{48,32},{56,40},{64,11... | collective-permute-start | bytes 417800 | tf_op jit(solution)/shard_map/ppermute | solution.py:485
  82.1 6.3 %collective-permute-start.17 = (bf16[256,256]{1,0:T(8,128)(2,1)S(1)}, bf16[256,256]{1,0:T(8,128)(2,1)S(1)}, u32[]{:S(2)}, u32[]{:S(2)}) collective-permute-start(bf16[256,256]{1,0:T(8,128)(2,1)S(1)} %get-tuple-element.154), channel_id=1, source_target_pairs={{0,16},{8,24},{16,32},{24,40},{32,48},{40,56},{48,0},{56,8},{64,80... | collective-permute-start | bytes 393224 | tf_op jit(solution)/shard_map/ppermute | solution.py:485
  88.7 8.7 %collective-permute-start.21 = (bf16[528,256]{1,0:T(8,128)(2,1)S(1)}, bf16[528,256]{1,0:T(8,128)(2,1)S(1)}, u32[]{:S(2)}, u32[]{:S(2)}) collective-permute-start(bf16[528,256]{1,0:T(8,128)(2,1)S(1)} %get-tuple-element.165), channel_id=1, source_target_pairs={{0,48},{8,56},{16,0},{24,8},{32,16},{40,24},{48,32},{56,40},{64,11... | collective-permute-start | bytes 811016 | tf_op jit(solution)/shard_map/ppermute | solution.py:485
  89.2 8.9 %collective-permute-start.22 = (bf16[528,256]{1,0:T(8,128)(2,1)S(1)}, bf16[528,256]{1,0:T(8,128)(2,1)S(1)}, u32[]{:S(2)}, u32[]{:S(2)}) collective-permute-start(bf16[528,256]{1,0:T(8,128)(2,1)S(1)} %get-tuple-element.166), channel_id=1, source_target_pairs={{0,16},{8,24},{16,32},{24,40},{32,48},{40,56},{48,0},{56,8},{64,80... | collective-permute-start | bytes 811016 | tf_op jit(solution)/shard_map/ppermute | solution.py:485
  90.9 6.6 %collective-permute-start.23 = (bf16[256,256]{1,0:T(8,128)(2,1)S(1)}, bf16[256,256]{1,0:T(8,128)(2,1)S(1)}, u32[]{:S(2)}, u32[]{:S(2)}) collective-permute-start(bf16[256,256]{1,0:T(8,128)(2,1)S(1)} %get-tuple-element.167), channel_id=1, source_target_pairs={{0,1},{1,0},{2,3},{3,2},{4,5},{5,4},{6,7},{7,6},{8,9},{9,8},{10,11... | collective-permute-start | bytes 393224 | tf_op jit(solution)/shard_map/ppermute | solution.py:485
  98.2 5.1 %collective-permute-start.24 = (bf16[272,256]{1,0:T(8,128)(2,1)S(1)}, bf16[272,256]{1,0:T(8,128)(2,1)S(1)}, u32[]{:S(2)}, u32[]{:S(2)}) collective-permute-start(bf16[272,256]{1,0:T(8,128)(2,1)S(1)} %get-tuple-element.173), channel_id=1, source_target_pairs={{0,64},{8,72},{16,80},{24,88},{32,96},{40,104},{48,112},{56,120},{... | collective-permute-start | bytes 417800 | tf_op jit(solution)/shard_map/ppermute | solution.py:485

commit v8 on v6

--- a/solution.py
+++ b/solution.py
@@ -78,7 +78,6 @@
 
 def logits_kernel(group, n_ads, rows, inv, *refs):
     n = NX * NZ
-    steps = n // 2
     chunks = rows // T
     first_call = group == "near"
     last_call = group == "far"
@@ -112,7 +111,7 @@
         logc_all[part, :] = jnp.broadcast_to(logc, (LANES, T)).T
 
     def columns(tile):
-        return pl.ds(pl.multiple_of(tile * T, T), T)
+        return slice(tile * T, (tile + 1) * T)
 
     class Product:
         def __init__(self, tile, dst):
@@ -173,28 +172,28 @@
             acc_ref[:, cols] = acc_in[:, cols] * jnp.exp2(m_in[:, cols] - m) + new * jnp.exp2(top_ref[:, cols] - m)
 
     def turn(tile, src, dst, e_now, e_before):
-        gather(jnp.maximum(tile - 1, 0), e_before)
-        product, exps = Product(jnp.minimum(tile + 1, n - 1), dst), Exps(tile, src, e_now)
+        if tile:
+            gather(tile - 1, e_before)
+        product = Product(tile + 1, dst) if tile + 1 < n else None
+        exps = Exps(tile, src, e_now)
         for c in range(chunks):
-            product.chunk(c)
+            if product:
+                product.chunk(c)
             exps.chunk(c)
-        product.end()
+        if product:
+            product.end()
         exps.end()
 
     opening = Product(0, s0)
     for c in range(chunks):
         opening.chunk(c)
     opening.end()
-    e0, e1 = late
-    e1[...] = jnp.zeros_like(e1)
-    m_ref[...] = jnp.zeros_like(m_ref) if first_call else m_in[...]
-
-    @pl.loop(0, steps)
-    def _(step):
-        turn(2 * step, s0, s1, e0, e1)
-        turn(2 * step + 1, s1, s0, e1, e0)
-
-    gather(n - 1, e1)
+    for tile in range(n):
+        if tile % 2:
+            turn(tile, s1, s0, late[1], late[0])
+        else:
+            turn(tile, s0, s1, late[0], late[1])
+    gather(n - 1, late[(n - 1) % 2])
     if last_call:
         lse = m_ref[...] + jnp.log2(total_ref[...])
         width = n * T // LANES
@@ -254,7 +253,7 @@
     tiles = out_ref.shape[1] // T
 
     def build(tile, dst):
-        cols = pl.ds(pl.multiple_of(start + tile * T, T), T)
+        cols = slice(start + tile * T, start + (tile + 1) * T)
         pos = pos_ref[:, cols] - lax.broadcasted_iota(jnp.int32, (16, T), 0)
         spot = 0
         for group, size in zip(GROUPS, sizes):
@@ -265,7 +264,7 @@
                 spot += T
 
     def product(tile, src):
-        cols = pl.ds(pl.multiple_of(tile * T, T), T)
+        cols = slice(tile * T, (tile + 1) * T)
         out = jnp.zeros((out_ref.shape[0], T), F32)
         spot = 0
         for ads, size in zip(ads_refs, sizes):
@@ -274,13 +273,11 @@
         out_ref[:, cols] = out.astype(BF16)
 
     build(0, h0)
-
-    @pl.loop(0, tiles // 2)
-    def _(step):
-        product(2 * step, h0)
-        build(2 * step + 1, h1)
-        product(2 * step + 1, h1)
-        build(jnp.minimum(2 * step + 2, tiles - 1), h0)
+    for tile in range(tiles):
+        now, then = (h1, h0) if tile % 2 else (h0, h1)
+        product(tile, now)
+        if tile + 1 < tiles:
+            build(tile + 1, then)
 
 
 def run_rows(ads_t, positives, start, total):
@@ -558,20 +555,20 @@
         acc, m, rows_a, rows_b, hits, weight_row, (stats, *moved), inv
     )
     tail = (lse, coefs, weight_row, pos_row, loss)
+    du_2a, du_2b = shift_x(du_2a, 1), shift_x(du_2b, -1)
     pay_2, da_2 = run_grads("mid", [("far", 3, p_far, top_far), ("two", 0, p_two, top_two)], staged, *tail)
     back_2 = swap_core(pay_2)
     da_2, staged = lax.optimization_barrier((da_2, staged))
+    (da_far,) = run_grads("far", [("far", i, p_far, top_far) for i in range(3)], staged, *tail)
+    da_far, back_2, du_2a, du_2b = lax.optimization_barrier((da_far, back_2, du_2a, du_2b))
+    du_1, du_3 = add_halves(du_1, du_3, du_2a, du_2b)
+    back = swap_core(da_far)
+    first, second, both = add_mid(da_2, back_2)
+    first, second, du_1, du_3, staged = lax.optimization_barrier((first, second, du_1, du_3, staged))
+    first, second = shift_y(first, -1), shift_y(second, 1)
+    du_1, du_3 = shift_x(du_1, 1), shift_x(du_3, -1)
     (da_near,) = run_grads("near", [("near", i, p_near, top_near) for i in range(3)], staged, *tail)
-    da_near, back_2 = lax.optimization_barrier((da_near, back_2))
-    first, second, both = add_mid(da_2, back_2)
-    first, second, staged = lax.optimization_barrier((first, second, staged))
-    first, second = shift_y(first, -1), shift_y(second, 1)
-    du_2a, du_2b = shift_x(du_2a, 1), shift_x(du_2b, -1)
-    (da_far,) = run_grads("far", [("far", i, p_far, top_far) for i in range(3)], staged, *tail)
-    back = swap_core(da_far)
-    first, second, du_2a, du_2b = lax.optimization_barrier((first, second, du_2a, du_2b))
-    du_1, du_3 = add_halves(du_1, du_3, du_2a, du_2b)
-    du_1, du_3 = shift_x(du_1, 1), shift_x(du_3, -1)
+    da_near, first, second, du_1, du_3 = lax.optimization_barrier((da_near, first, second, du_1, du_3))
     kept, one, three = add_near(da_near, back, both, first, second)
     one, three = shift_y(one, -1), shift_y(three, 1)
     keep_u, send_u = add_users((du_0, du_1, du_3))

time: 106 us -> 102 us (0.962)
  Pallas kernels: 32.7 us -> 30.7 us
  starting transfers between devices: 38.3 us -> 37.1 us
    pallas_call x16, Pallas kernels: 32.7 us -> 30.7 us  [call(): pl.pallas_call(kernel, in_specs=[vmem] * len(args), out_specs=[vmem] * le...]
    ppermute x25, starting transfers between devices: 38.3 us -> 37.1 us  [move(): lax.ppermute(x, axis, [(i, target(i)) for i in range(lax.axis_size(axis))])]
  transfers between devices with their start and end apart: 25 -> 25, of which waited for: 12 -> 13; matrix products, arithmetic and copies ran while one was open for 1% -> 1% of each run, Pallas kernels for 17% -> 18%
where the time goes in v8:
time: 102 us
  starting transfers between devices  37.1 us (36%)
  Pallas kernels  30.7 us (30%)
  waiting for transfers between devices  30.5 us (30%)
  other arithmetic  2.5 us (2%)
    ppermute x25, starting transfers between devices, move(): lax.ppermute(x, axis, [(i, target(i)) for i in range(lax.axis_size(axis))])  37.1 us
    pallas_call x16, Pallas kernels, call(): pl.pallas_call(kernel, in_specs=[vmem] * len(args), out_specs=[vmem] * le...  30.7 us
    ppermute x25, waiting for transfers between devices, move(): lax.ppermute(x, axis, [(i, target(i)) for i in range(lax.axis_size(axis))])  30.5 us
  transfers between devices with their start and end apart: 25, of which 13 were waited for; matrix products, arithmetic and copies ran while one was open for 1% of the time, Pallas kernels for 18%

profile of v8, /device:TPU:0, one launch (start us, length us, event | category | flops | bytes accessed | tf_op | source)
XLA Modules:
  0.0 101.6 jit_solution(7582276976988039111)
XLA Ops:
  0.6 4.0 %collective-permute-start = (bf16[256,256]{1,0:T(8,128)(2,1)}, bf16[256,256]{1,0:T(8,128)(2,1)S(1)}, u32[]{:S(2)}, u32[]{:S(2)}) collective-permute-start(bf16[256,256]{1,0:T(8,128)(2,1)} %param.5), channel_id=1, source_target_pairs={{0,1},{1,0},{2,3},{3,2},{4,5},{5,4},{6,7},{7,6},{8,9},{9,8},{10,11... | collective-permute-start | bytes 393224 | tf_op jit(solution)/shard_map/ppermute | solution.py:499
  4.7 1.0 %collective-permute-start.1 = (bf16[256,256]{1,0:T(8,128)(2,1)}, bf16[256,256]{1,0:T(8,128)(2,1)S(1)}, u32[]{:S(2)}, u32[]{:S(2)}) collective-permute-start(bf16[256,256]{1,0:T(8,128)(2,1)} %param.6), channel_id=1, source_target_pairs={{0,64},{8,72},{16,80},{24,88},{32,96},{40,104},{48,112},{56,120},{... | collective-permute-start | bytes 393224 | tf_op jit(solution)/shard_map/ppermute | solution.py:499
  7.1 2.1 %collective-permute-done = bf16[256,256]{1,0:T(8,128)(2,1)S(1)} collective-permute-done((bf16[256,256]{1,0:T(8,128)(2,1)}, bf16[256,256]{1,0:T(8,128)(2,1)S(1)}, u32[]{:S(2)}, u32[]{:S(2)}) %collective-permute-start) | collective-permute-done | bytes 131104 | tf_op jit(solution)/shard_map/ppermute | solution.py:499
  9.2 2.7 %collective-permute-done.1 = bf16[256,256]{1,0:T(8,128)(2,1)S(1)} collective-permute-done((bf16[256,256]{1,0:T(8,128)(2,1)}, bf16[256,256]{1,0:T(8,128)(2,1)S(1)}, u32[]{:S(2)}, u32[]{:S(2)}) %collective-permute-start.1) | collective-permute-done | bytes 131104 | tf_op jit(solution)/shard_map/ppermute | solution.py:499
  11.9 1.0 pad_maximum_fusion.1
  12.9 2.8 %collective-permute-start.4 = (bf16[512,256]{1,0:T(8,128)(2,1)S(1)}, bf16[512,256]{1,0:T(8,128)(2,1)S(1)}, u32[]{:S(2)}, u32[]{:S(2)}) collective-permute-start(bf16[512,256]{1,0:T(8,128)(2,1)S(1)} %get-tuple-element.93.refs_0_), channel_id=1, source_target_pairs={{0,6},{1,7},{2,0},{3,1},{4,2},{5,3},{6,4},{7,5},{8,14},{9,15},{10,... | collective-permute-start | bytes 786440 | tf_op jit(solution)/shard_map/ppermute | solution.py:499
  17.4 3.0 %collective-permute-start.6 = (bf16[512,256]{1,0:T(8,128)(2,1)S(1)}, bf16[512,256]{1,0:T(8,128)(2,1)S(1)}, u32[]{:S(2)}, u32[]{:S(2)}) collective-permute-start(bf16[512,256]{1,0:T(8,128)(2,1)S(1)} %get-tuple-element.97.refs_4_), channel_id=1, source_target_pairs={{0,48},{8,56},{16,0},{24,8},{32,16},{40,24},{48,32},{56,40},{64,11... | collective-permute-start | bytes 786440 | tf_op jit(solution)/shard_map/ppermute | solution.py:499
  20.5 5.6 %collective-permute-done.4.refs_3_ = bf16[512,256]{1,0:T(8,128)(2,1)S(1)} collective-permute-done((bf16[512,256]{1,0:T(8,128)(2,1)S(1)}, bf16[512,256]{1,0:T(8,128)(2,1)S(1)}, u32[]{:S(2)}, u32[]{:S(2)}) %collective-permute-start.4) | collective-permute-done | bytes 262176 | tf_op jit(solution)/shard_map/ppermute | solution.py:499
  26.1 3.2 %collective-permute-start.7 = (bf16[512,256]{1,0:T(8,128)(2,1)S(1)}, bf16[512,256]{1,0:T(8,128)(2,1)S(1)}, u32[]{:S(2)}, u32[]{:S(2)}) collective-permute-start(bf16[512,256]{1,0:T(8,128)(2,1)S(1)} %get-tuple-element.97.refs_4_), channel_id=1, source_target_pairs={{0,32},{8,40},{16,48},{24,56},{32,0},{40,8},{48,16},{56,24},{64,96... | collective-permute-start | bytes 786440 | tf_op jit(solution)/shard_map/ppermute | solution.py:499
  30.5 6.4 %logits_near.1 = (bf16[1536,2048]{1,0:T(8,128)(2,1)S(1)}, f32[1,2048]{1,0:T(1,128)S(1)}, bf16[256,1536]{1,0:T(8,128)(2,1)S(1)}, f32[256,2048]{1,0:T(8,128)S(1)},...) custom-call(bf16[512,256]{1,0:T(8,128)(2,1)S(1)} %get-tuple-element., ...), custom_call_target="tpu_custom_call" | custom-call | flops 100663296 | bytes 393216 | tf_op jit(solution)/shard_map/logits_near/pallas_call | solution.py:25
  37.3 2.4 %logits_two.1 = (bf16[512,2048]{1,0:T(8,128)(2,1)S(1)}, f32[1,2048]{1,0:T(1,128)S(1)}, bf16[256,512]{1,0:T(8,128)(2,1)S(1)}, f32[256,2048]{1,0:T(8,128)S(1)}, f3...) custom-call(bf16[256,2048]{1,0:T(8,128)(2,1)S(1)} %get-tuple-element.100.refs_0_, ...), custom_call_target="tpu_custom_call" | custom-call | flops 33554432 | bytes 131072 | tf_op jit(solution)/shard_map/logits_two/pallas_call | solution.py:25
  39.9 9.4 %logits_far.1 = (bf16[2048,2048]{1,0:T(8,128)(2,1)S(1)}, f32[1,2048]{1,0:T(1,128)S(1)}, bf16[256,2048]{1,0:T(8,128)(2,1)S(1)}, f32[256,2048]{1,0:T(8,128)S(1)}, ...) custom-call(bf16[256,2048]{1,0:T(8,128)(2,1)S(1)} %get-tuple-element.100.refs_0_, ...), custom_call_target="tpu_custom_call" | custom-call | flops 134217728 | bytes 524288 | tf_op jit(solution)/shard_map/logits_far/pallas_call | solution.py:25
  49.3 1.2 %collective-permute-start.9 = (f32[32,128]{1,0:T(8,128)S(1)}, f32[32,128]{1,0:T(8,128)S(1)}, u32[]{:S(2)}, u32[]{:S(2)}) collective-permute-start(f32[32,128]{1,0:T(8,128)S(1)} %get-tuple-element.115.own_ref), channel_id=1, source_target_pairs={{0,1},{1,0},{2,3},{3,2},{4,5},{5,4},{6,7},{7,6},{8,9},{9,8},{10,11... | collective-permute-start | bytes 49160 | tf_op jit(solution)/shard_map/ppermute | solution.py:499
  50.5 2.3 %positive_rows.2.refs_2_ = bf16[256,1024]{1,0:T(8,128)(2,1)S(1)} custom-call(bf16[256,1536]{1,0:T(8,128)(2,1)S(1)} %get-tuple-element.116.refs_0_, bf16[256,512]{1,0:T(8,128)(2,1)S(1)} %get-tuple-element.117.refs_1_, bf16[256,2048]{1,0:T(8,128)(2,1)S(1)} %get-tuple-element.118.refs_2_, s32[1,2048]{1,0:T(1,128)S(1)} %bitcast.7), custom_call_target="tpu_custom_call" | custom-call | flops 134217728 | bytes 524288 | tf_op jit(solution)/shard_map/positive_rows/pallas_call | solution.py:25
  52.8 1.7 %collective-permute-done.9.other_ref = f32[32,128]{1,0:T(8,128)S(1)} collective-permute-done((f32[32,128]{1,0:T(8,128)S(1)}, f32[32,128]{1,0:T(8,128)S(1)}, u32[]{:S(2)}, u32[]{:S(2)}) %collective-permute-start.9) | collective-permute-done | bytes 16416 | tf_op jit(solution)/shard_map/ppermute | solution.py:499
  54.6 2.7 %collective-permute-start.12 = (f32[32,128]{1,0:T(8,128)S(1)}, f32[32,128]{1,0:T(8,128)S(1)}, u32[]{:S(2)}, u32[]{:S(2)}) collective-permute-start(f32[32,128]{1,0:T(8,128)S(1)} %join_stats.1.refs_6_), channel_id=1, source_target_pairs={{0,6},{1,7},{2,0},{3,1},{4,2},{5,3},{6,4},{7,5},{8,14},{9,15},{10,... | collective-permute-start | bytes 49160 | tf_op jit(solution)/shard_map/ppermute | solution.py:499
  57.3 4.0 %collective-permute-start.11 = (f32[32,128]{1,0:T(8,128)S(1)}, f32[32,128]{1,0:T(8,128)S(1)}, u32[]{:S(2)}, u32[]{:S(2)}) collective-permute-start(f32[32,128]{1,0:T(8,128)S(1)} %join_stats.1.refs_6_), channel_id=1, source_target_pairs={{0,4},{1,5},{2,6},{3,7},{4,0},{5,1},{6,2},{7,3},{8,12},{9,13},{10,... | collective-permute-start | bytes 49160 | tf_op jit(solution)/shard_map/ppermute | solution.py:499
  61.3 2.3 %positive_rows.3.refs_3_ = bf16[256,1024]{1,0:T(8,128)(2,1)S(1)} custom-call(bf16[256,1536]{1,0:T(8,128)(2,1)S(1)} %get-tuple-element.116.refs_0_, bf16[256,512]{1,0:T(8,128)(2,1)S(1)} %get-tuple-element.117.refs_1_, bf16[256,2048]{1,0:T(8,128)(2,1)S(1)} %get-tuple-element.118.refs_2_, s32[1,2048]{1,0:T(1,128)S(1)} %bitcast.8), custom_call_target="tpu_custom_call" | custom-call | flops 134217728 | bytes 524288 | tf_op jit(solution)/shard_map/positive_rows/pallas_call | solution.py:25
  63.7 2.6 %collective-permute-done.10.refs_7_ = f32[32,128]{1,0:T(8,128)S(1)} collective-permute-done((f32[32,128]{1,0:T(8,128)S(1)}, f32[32,128]{1,0:T(8,128)S(1)}, u32[]{:S(2)}, u32[]{:S(2)}) %collective-permute-start.10) | collective-permute-done | bytes 16416 | tf_op jit(solution)/shard_map/ppermute | solution.py:499
  66.9 1.4 %grads_mid.1 = (bf16[528,256]{1,0:T(8,128)(2,1)S(1)}, bf16[528,256]{1,0:T(8,128)(2,1)S(1)}) custom-call(bf16[2048,256]{1,0:T(8,128)(2,1)S(1)} %get-tuple-element.150.refs_0_, f32[1,2048]{1,0:T(1,128)S(1)} %get-tuple-element.128.refs_1_, f32[1,2048]{1,0:T(1,128)S(1)} %get-tuple-element.129.refs_2_, f32[1,2048]{1,0:T(1,128)S(1)} %bitcast.16, ...), custom_call_target="tpu_custom_call" | custom-call | flops 67108864 | bytes 262144 | tf_op jit(solution)/shard_map/grads_mid/pallas_call | solution.py:25
  68.6 3.2 %collective-permute-start.15 = (bf16[256,256]{1,0:T(8,128)(2,1)S(1)}, bf16[256,256]{1,0:T(8,128)(2,1)S(1)}, u32[]{:S(2)}, u32[]{:S(2)}) collective-permute-start(bf16[256,256]{1,0:T(8,128)(2,1)S(1)} %get-tuple-element.140), channel_id=1, source_target_pairs={{0,6},{1,7},{2,0},{3,1},{4,2},{5,3},{6,4},{7,5},{8,14},{9,15},{10,... | collective-permute-start | bytes 393224 | tf_op jit(solution)/shard_map/ppermute | solution.py:499
  71.8 2.1 %grads_far.1 = bf16[1536,256]{1,0:T(8,128)(2,1)S(1)} custom-call(bf16[2048,256]{1,0:T(8,128)(2,1)S(1)} %get-tuple-element.150.refs_0_, f32[1,2048]{1,0:T(1,128)S(1)} %get-tuple-element.128.refs_1_, f32[1,2048]{1,0:T(1,128)S(1)} %get-tuple-element.129.refs_2_, f32[1,2048]{1,0:T(1,128)S(1)} %bitcast.17, s32[1,2048]{1,0:T(1,128)S(1)} %bitcast.10, ...), custom_call_target="tpu_custom_call" | custom-call | flops 100663296 | bytes 393216 | tf_op jit(solution)/shard_map/grads_far/pallas_call | solution.py:25
  73.9 1.7 %collective-permute-done.14.first_ref = bf16[256,256]{1,0:T(8,128)(2,1)S(1)} collective-permute-done((bf16[256,256]{1,0:T(8,128)(2,1)S(1)}, bf16[256,256]{1,0:T(8,128)(2,1)S(1)}, u32[]{:S(2)}, u32[]{:S(2)}) %collective-permute-start.14) | collective-permute-done | bytes 131104 | tf_op jit(solution)/shard_map/ppermute | solution.py:499
  75.9 3.2 %collective-permute-start.19 = (bf16[512,256]{1,0:T(8,128)(2,1)S(1)}, bf16[512,256]{1,0:T(8,128)(2,1)S(1)}, u32[]{:S(2)}, u32[]{:S(2)}) collective-permute-start(bf16[512,256]{1,0:T(8,128)(2,1)S(1)} %get-tuple-element.156), channel_id=1, source_target_pairs={{0,6},{1,7},{2,0},{3,1},{4,2},{5,3},{6,4},{7,5},{8,14},{9,15},{10,... | collective-permute-start | bytes 786440 | tf_op jit(solution)/shard_map/ppermute | solution.py:499
  79.4 1.7 %collective-permute-start.17 = (bf16[256,256]{1,0:T(8,128)(2,1)S(1)}, bf16[256,256]{1,0:T(8,128)(2,1)S(1)}, u32[]{:S(2)}, u32[]{:S(2)}) collective-permute-start(bf16[256,256]{1,0:T(8,128)(2,1)S(1)} %get-tuple-element.154), channel_id=1, source_target_pairs={{0,16},{8,24},{16,32},{24,40},{32,48},{40,56},{48,0},{56,8},{64,80... | collective-permute-start | bytes 393224 | tf_op jit(solution)/shard_map/ppermute | solution.py:499
  81.1 2.1 %grads_near.1.near_ref = bf16[1536,256]{1,0:T(8,128)(2,1)S(1)} custom-call(bf16[2048,256]{1,0:T(8,128)(2,1)S(1)} %get-tuple-element.150.refs_0_, f32[1,2048]{1,0:T(1,128)S(1)} %get-tuple-element.128.refs_1_, f32[1,2048]{1,0:T(1,128)S(1)} %get-tuple-element.129.refs_2_, f32[1,2048]{1,0:T(1,128)S(1)} %bitcast.18, s32[1,2048]{1,0:T(1,128)S(1)} %bitcast.11, ...), custom_call_target="tpu_custom_call" | custom-call | flops 100663296 | bytes 393216 | tf_op jit(solution)/shard_map/grads_near/pallas_call | solution.py:25
  83.2 2.5 %collective-permute-done.17.second_ref = bf16[256,256]{1,0:T(8,128)(2,1)S(1)} collective-permute-done((bf16[256,256]{1,0:T(8,128)(2,1)S(1)}, bf16[256,256]{1,0:T(8,128)(2,1)S(1)}, u32[]{:S(2)}, u32[]{:S(2)}) %collective-permute-start.17) | collective-permute-done | bytes 131104 | tf_op jit(solution)/shard_map/ppermute | solution.py:499
  86.5 1.6 %collective-permute-start.22 = (bf16[528,256]{1,0:T(8,128)(2,1)S(1)}, bf16[528,256]{1,0:T(8,128)(2,1)S(1)}, u32[]{:S(2)}, u32[]{:S(2)}) collective-permute-start(bf16[528,256]{1,0:T(8,128)(2,1)S(1)} %get-tuple-element.166), channel_id=1, source_target_pairs={{0,16},{8,24},{16,32},{24,40},{32,48},{40,56},{48,0},{56,8},{64,80... | collective-permute-start | bytes 811016 | tf_op jit(solution)/shard_map/ppermute | solution.py:499
  88.2 1.3 %collective-permute-start.23 = (bf16[256,256]{1,0:T(8,128)(2,1)S(1)}, bf16[256,256]{1,0:T(8,128)(2,1)S(1)}, u32[]{:S(2)}, u32[]{:S(2)}) collective-permute-start(bf16[256,256]{1,0:T(8,128)(2,1)S(1)} %get-tuple-element.167), channel_id=1, source_target_pairs={{0,1},{1,0},{2,3},{3,2},{4,5},{5,4},{6,7},{7,6},{8,9},{9,8},{10,11... | collective-permute-start | bytes 393224 | tf_op jit(solution)/shard_map/ppermute | solution.py:499
  89.4 5.3 %collective-permute-done.23.received_u_ref = bf16[256,256]{1,0:T(8,128)(2,1)S(1)} collective-permute-done((bf16[256,256]{1,0:T(8,128)(2,1)S(1)}, bf16[256,256]{1,0:T(8,128)(2,1)S(1)}, u32[]{:S(2)}, u32[]{:S(2)}) %collective-permute-start.23) | collective-permute-done | bytes 131104 | tf_op jit(solution)/shard_map/ppermute | solution.py:499
  95.5 1.1 %collective-permute-start.24 = (bf16[272,256]{1,0:T(8,128)(2,1)S(1)}, bf16[272,256]{1,0:T(8,128)(2,1)S(1)}, u32[]{:S(2)}, u32[]{:S(2)}) collective-permute-start(bf16[272,256]{1,0:T(8,128)(2,1)S(1)} %get-tuple-element.173), channel_id=1, source_target_pairs={{0,64},{8,72},{16,80},{24,88},{32,96},{40,104},{48,112},{56,120},{... | collective-permute-start | bytes 417800 | tf_op jit(solution)/shard_map/ppermute | solution.py:499
  96.6 4.0 %collective-permute-done.24.received_ref = bf16[272,256]{1,0:T(8,128)(2,1)S(1)} collective-permute-done((bf16[272,256]{1,0:T(8,128)(2,1)S(1)}, bf16[272,256]{1,0:T(8,128)(2,1)S(1)}, u32[]{:S(2)}, u32[]{:S(2)}) %collective-permute-start.24) | collective-permute-done | bytes 139296 | tf_op jit(solution)/shard_map/ppermute | solution.py:499
  (40 shorter events, 8.9 us)
Async XLA Ops:
  0.6 8.6 %collective-permute-start = (bf16[256,256]{1,0:T(8,128)(2,1)}, bf16[256,256]{1,0:T(8,128)(2,1)S(1)}, u32[]{:S(2)}, u32[]{:S(2)}) collective-permute-start(bf16[256,256]{1,0:T(8,128)(2,1)} %param.5), channel_id=1, source_target_pairs={{0,1},{1,0},{2,3},{3,2},{4,5},{5,4},{6,7},{7,6},{8,9},{9,8},{10,11... | collective-permute-start | bytes 393224 | tf_op jit(solution)/shard_map/ppermute | solution.py:499
  4.7 7.2 %collective-permute-start.1 = (bf16[256,256]{1,0:T(8,128)(2,1)}, bf16[256,256]{1,0:T(8,128)(2,1)S(1)}, u32[]{:S(2)}, u32[]{:S(2)}) collective-permute-start(bf16[256,256]{1,0:T(8,128)(2,1)} %param.6), channel_id=1, source_target_pairs={{0,64},{8,72},{16,80},{24,88},{32,96},{40,104},{48,112},{56,120},{... | collective-permute-start | bytes 393224 | tf_op jit(solution)/shard_map/ppermute | solution.py:499
  12.9 13.2 %collective-permute-start.4 = (bf16[512,256]{1,0:T(8,128)(2,1)S(1)}, bf16[512,256]{1,0:T(8,128)(2,1)S(1)}, u32[]{:S(2)}, u32[]{:S(2)}) collective-permute-start(bf16[512,256]{1,0:T(8,128)(2,1)S(1)} %get-tuple-element.93.refs_0_), channel_id=1, source_target_pairs={{0,6},{1,7},{2,0},{3,1},{4,2},{5,3},{6,4},{7,5},{8,14},{9,15},{10,... | collective-permute-start | bytes 786440 | tf_op jit(solution)/shard_map/ppermute | solution.py:499
  15.8 13.5 %collective-permute-start.3 = (bf16[512,256]{1,0:T(8,128)(2,1)S(1)}, bf16[512,256]{1,0:T(8,128)(2,1)S(1)}, u32[]{:S(2)}, u32[]{:S(2)}) collective-permute-start(bf16[512,256]{1,0:T(8,128)(2,1)S(1)} %get-tuple-element.93.refs_0_), channel_id=1, source_target_pairs={{0,4},{1,5},{2,6},{3,7},{4,0},{5,1},{6,2},{7,3},{8,12},{9,13},{10,... | collective-permute-start | bytes 786440 | tf_op jit(solution)/shard_map/ppermute | solution.py:499
  16.6 13.2 %collective-permute-start.2 = (bf16[512,256]{1,0:T(8,128)(2,1)S(1)}, bf16[512,256]{1,0:T(8,128)(2,1)S(1)}, u32[]{:S(2)}, u32[]{:S(2)}) collective-permute-start(bf16[512,256]{1,0:T(8,128)(2,1)S(1)} %get-tuple-element.93.refs_0_), channel_id=1, source_target_pairs={{0,2},{1,3},{2,4},{3,5},{4,6},{5,7},{6,0},{7,1},{8,10},{9,11},{10,... | collective-permute-start | bytes 786440 | tf_op jit(solution)/shard_map/ppermute | solution.py:499
  17.4 12.3 %collective-permute-start.6 = (bf16[512,256]{1,0:T(8,128)(2,1)S(1)}, bf16[512,256]{1,0:T(8,128)(2,1)S(1)}, u32[]{:S(2)}, u32[]{:S(2)}) collective-permute-start(bf16[512,256]{1,0:T(8,128)(2,1)S(1)} %get-tuple-element.97.refs_4_), channel_id=1, source_target_pairs={{0,48},{8,56},{16,0},{24,8},{32,16},{40,24},{48,32},{56,40},{64,11... | collective-permute-start | bytes 786440 | tf_op jit(solution)/shard_map/ppermute | solution.py:499
  20.5 10.1 %collective-permute-start.5 = (bf16[512,256]{1,0:T(8,128)(2,1)S(1)}, bf16[512,256]{1,0:T(8,128)(2,1)S(1)}, u32[]{:S(2)}, u32[]{:S(2)}) collective-permute-start(bf16[512,256]{1,0:T(8,128)(2,1)S(1)} %get-tuple-element.97.refs_4_), channel_id=1, source_target_pairs={{0,16},{8,24},{16,32},{24,40},{32,48},{40,56},{48,0},{56,8},{64,80... | collective-permute-start | bytes 786440 | tf_op jit(solution)/shard_map/ppermute | solution.py:499
  26.1 10.8 %collective-permute-start.7 = (bf16[512,256]{1,0:T(8,128)(2,1)S(1)}, bf16[512,256]{1,0:T(8,128)(2,1)S(1)}, u32[]{:S(2)}, u32[]{:S(2)}) collective-permute-start(bf16[512,256]{1,0:T(8,128)(2,1)S(1)} %get-tuple-element.97.refs_4_), channel_id=1, source_target_pairs={{0,32},{8,40},{16,48},{24,56},{32,0},{40,8},{48,16},{56,24},{64,96... | collective-permute-start | bytes 786440 | tf_op jit(solution)/shard_map/ppermute | solution.py:499
  37.0 2.9 %collective-permute-start.8 = (bf16[2048,256]{1,0:T(8,128)(2,1)S(1)}, bf16[2048,256]{1,0:T(8,128)(2,1)S(1)}, u32[]{:S(2)}, u32[]{:S(2)}) collective-permute-start(bf16[2048,256]{1,0:T(8,128)(2,1)S(1)} %pad_maximum_fusion), channel_id=1, source_target_pairs={{0,8},{8,0},{16,24},{24,16},{32,40},{40,32},{48,56},{56,48},{64,72... | collective-permute-start | bytes 3145736 | tf_op jit(solution)/shard_map/ppermute | solution.py:499
  49.3 5.2 %collective-permute-start.9 = (f32[32,128]{1,0:T(8,128)S(1)}, f32[32,128]{1,0:T(8,128)S(1)}, u32[]{:S(2)}, u32[]{:S(2)}) collective-permute-start(f32[32,128]{1,0:T(8,128)S(1)} %get-tuple-element.115.own_ref), channel_id=1, source_target_pairs={{0,1},{1,0},{2,3},{3,2},{4,5},{5,4},{6,7},{7,6},{8,9},{9,8},{10,11... | collective-permute-start | bytes 49160 | tf_op jit(solution)/shard_map/ppermute | solution.py:499
  50.5 15.8 %copy-start = (f32[2048]{0:T(1024)S(1)}, f32[2048]{0:T(1024)}, u32[]{:S(2)}) copy-start(f32[2048]{0:T(1024)} %param.9) | copy-start | bytes 24580
  54.6 9.1 %collective-permute-start.12 = (f32[32,128]{1,0:T(8,128)S(1)}, f32[32,128]{1,0:T(8,128)S(1)}, u32[]{:S(2)}, u32[]{:S(2)}) collective-permute-start(f32[32,128]{1,0:T(8,128)S(1)} %join_stats.1.refs_6_), channel_id=1, source_target_pairs={{0,6},{1,7},{2,0},{3,1},{4,2},{5,3},{6,4},{7,5},{8,14},{9,15},{10,... | collective-permute-start | bytes 49160 | tf_op jit(solution)/shard_map/ppermute | solution.py:499
  57.3 6.4 %collective-permute-start.11 = (f32[32,128]{1,0:T(8,128)S(1)}, f32[32,128]{1,0:T(8,128)S(1)}, u32[]{:S(2)}, u32[]{:S(2)}) collective-permute-start(f32[32,128]{1,0:T(8,128)S(1)} %join_stats.1.refs_6_), channel_id=1, source_target_pairs={{0,4},{1,5},{2,6},{3,7},{4,0},{5,1},{6,2},{7,3},{8,12},{9,13},{10,... | collective-permute-start | bytes 49160 | tf_op jit(solution)/shard_map/ppermute | solution.py:499
  61.3 4.9 %collective-permute-start.10 = (f32[32,128]{1,0:T(8,128)S(1)}, f32[32,128]{1,0:T(8,128)S(1)}, u32[]{:S(2)}, u32[]{:S(2)}) collective-permute-start(f32[32,128]{1,0:T(8,128)S(1)} %join_stats.1.refs_6_), channel_id=1, source_target_pairs={{0,2},{1,3},{2,4},{3,5},{4,6},{5,7},{6,0},{7,1},{8,10},{9,11},{10,... | collective-permute-start | bytes 49160 | tf_op jit(solution)/shard_map/ppermute | solution.py:499
  68.4 7.2 %collective-permute-start.13 = (bf16[528,256]{1,0:T(8,128)(2,1)S(1)}, bf16[528,256]{1,0:T(8,128)(2,1)S(1)}, u32[]{:S(2)}, u32[]{:S(2)}) collective-permute-start(bf16[528,256]{1,0:T(8,128)(2,1)S(1)} %get-tuple-element.138), channel_id=1, source_target_pairs={{0,8},{8,0},{16,24},{24,16},{32,40},{40,32},{48,56},{56,48},{64,72... | collective-permute-start | bytes 811016 | tf_op jit(solution)/shard_map/ppermute | solution.py:499
  68.5 7.1 %collective-permute-start.14 = (bf16[256,256]{1,0:T(8,128)(2,1)S(1)}, bf16[256,256]{1,0:T(8,128)(2,1)S(1)}, u32[]{:S(2)}, u32[]{:S(2)}) collective-permute-start(bf16[256,256]{1,0:T(8,128)(2,1)S(1)} %get-tuple-element.139), channel_id=1, source_target_pairs={{0,2},{1,3},{2,4},{3,5},{4,6},{5,7},{6,0},{7,1},{8,10},{9,11},{10,... | collective-permute-start | bytes 393224 | tf_op jit(solution)/shard_map/ppermute | solution.py:499
  68.6 7.0 %collective-permute-start.15 = (bf16[256,256]{1,0:T(8,128)(2,1)S(1)}, bf16[256,256]{1,0:T(8,128)(2,1)S(1)}, u32[]{:S(2)}, u32[]{:S(2)}) collective-permute-start(bf16[256,256]{1,0:T(8,128)(2,1)S(1)} %get-tuple-element.140), channel_id=1, source_target_pairs={{0,6},{1,7},{2,0},{3,1},{4,2},{5,3},{6,4},{7,5},{8,14},{9,15},{10,... | collective-permute-start | bytes 393224 | tf_op jit(solution)/shard_map/ppermute | solution.py:499
  75.6 10.2 %collective-permute-start.20 = (bf16[1536,256]{1,0:T(8,128)(2,1)S(1)}, bf16[1536,256]{1,0:T(8,128)(2,1)S(1)}, u32[]{:S(2)}, u32[]{:S(2)}) collective-permute-start(bf16[1536,256]{1,0:T(8,128)(2,1)S(1)} %grads_far.1), channel_id=1, source_target_pairs={{0,8},{8,0},{16,24},{24,16},{32,40},{40,32},{48,56},{56,48},{64,72... | collective-permute-start | bytes 2359304 | tf_op jit(solution)/shard_map/ppermute | solution.py:499
  75.8 10.0 %collective-permute-start.18 = (bf16[512,256]{1,0:T(8,128)(2,1)S(1)}, bf16[512,256]{1,0:T(8,128)(2,1)S(1)}, u32[]{:S(2)}, u32[]{:S(2)}) collective-permute-start(bf16[512,256]{1,0:T(8,128)(2,1)S(1)} %get-tuple-element.155), channel_id=1, source_target_pairs={{0,2},{1,3},{2,4},{3,5},{4,6},{5,7},{6,0},{7,1},{8,10},{9,11},{10,... | collective-permute-start | bytes 786440 | tf_op jit(solution)/shard_map/ppermute | solution.py:499
  75.9 9.9 %collective-permute-start.19 = (bf16[512,256]{1,0:T(8,128)(2,1)S(1)}, bf16[512,256]{1,0:T(8,128)(2,1)S(1)}, u32[]{:S(2)}, u32[]{:S(2)}) collective-permute-start(bf16[512,256]{1,0:T(8,128)(2,1)S(1)} %get-tuple-element.156), channel_id=1, source_target_pairs={{0,6},{1,7},{2,0},{3,1},{4,2},{5,3},{6,4},{7,5},{8,14},{9,15},{10,... | collective-permute-start | bytes 786440 | tf_op jit(solution)/shard_map/ppermute | solution.py:499
  79.1 6.7 %collective-permute-start.16 = (bf16[272,256]{1,0:T(8,128)(2,1)S(1)}, bf16[272,256]{1,0:T(8,128)(2,1)S(1)}, u32[]{:S(2)}, u32[]{:S(2)}) collective-permute-start(bf16[272,256]{1,0:T(8,128)(2,1)S(1)} %get-tuple-element.153), channel_id=1, source_target_pairs={{0,48},{8,56},{16,0},{24,8},{32,16},{40,24},{48,32},{56,40},{64,11... | collective-permute-start | bytes 417800 | tf_op jit(solution)/shard_map/ppermute | solution.py:499
  79.4 6.3 %collective-permute-start.17 = (bf16[256,256]{1,0:T(8,128)(2,1)S(1)}, bf16[256,256]{1,0:T(8,128)(2,1)S(1)}, u32[]{:S(2)}, u32[]{:S(2)}) collective-permute-start(bf16[256,256]{1,0:T(8,128)(2,1)S(1)} %get-tuple-element.154), channel_id=1, source_target_pairs={{0,16},{8,24},{16,32},{24,40},{32,48},{40,56},{48,0},{56,8},{64,80... | collective-permute-start | bytes 393224 | tf_op jit(solution)/shard_map/ppermute | solution.py:499
  86.0 8.7 %collective-permute-start.21 = (bf16[528,256]{1,0:T(8,128)(2,1)S(1)}, bf16[528,256]{1,0:T(8,128)(2,1)S(1)}, u32[]{:S(2)}, u32[]{:S(2)}) collective-permute-start(bf16[528,256]{1,0:T(8,128)(2,1)S(1)} %get-tuple-element.165), channel_id=1, source_target_pairs={{0,48},{8,56},{16,0},{24,8},{32,16},{40,24},{48,32},{56,40},{64,11... | collective-permute-start | bytes 811016 | tf_op jit(solution)/shard_map/ppermute | solution.py:499
  86.5 8.9 %collective-permute-start.22 = (bf16[528,256]{1,0:T(8,128)(2,1)S(1)}, bf16[528,256]{1,0:T(8,128)(2,1)S(1)}, u32[]{:S(2)}, u32[]{:S(2)}) collective-permute-start(bf16[528,256]{1,0:T(8,128)(2,1)S(1)} %get-tuple-element.166), channel_id=1, source_target_pairs={{0,16},{8,24},{16,32},{24,40},{32,48},{40,56},{48,0},{56,8},{64,80... | collective-permute-start | bytes 811016 | tf_op jit(solution)/shard_map/ppermute | solution.py:499
  88.2 6.6 %collective-permute-start.23 = (bf16[256,256]{1,0:T(8,128)(2,1)S(1)}, bf16[256,256]{1,0:T(8,128)(2,1)S(1)}, u32[]{:S(2)}, u32[]{:S(2)}) collective-permute-start(bf16[256,256]{1,0:T(8,128)(2,1)S(1)} %get-tuple-element.167), channel_id=1, source_target_pairs={{0,1},{1,0},{2,3},{3,2},{4,5},{5,4},{6,7},{7,6},{8,9},{9,8},{10,11... | collective-permute-start | bytes 393224 | tf_op jit(solution)/shard_map/ppermute | solution.py:499
  95.5 5.1 %collective-permute-start.24 = (bf16[272,256]{1,0:T(8,128)(2,1)S(1)}, bf16[272,256]{1,0:T(8,128)(2,1)S(1)}, u32[]{:S(2)}, u32[]{:S(2)}) collective-permute-start(bf16[272,256]{1,0:T(8,128)(2,1)S(1)} %get-tuple-element.173), channel_id=1, source_target_pairs={{0,64},{8,72},{16,80},{24,88},{32,96},{40,104},{48,112},{56,120},{... | collective-permute-start | bytes 417800 | tf_op jit(solution)/shard_map/ppermute | solution.py:499

commit v9 on v8

--- a/solution.py
+++ b/solution.py
@@ -295,7 +295,7 @@
 
 def users_kernel(inv, acc_ref, m_ref, rows_a, rows_b, hit_ref, weight_ref, *rest):
     stats_in, rest = rest[:NX], rest[NX:]
-    du_refs, (lse_ref, coef_ref, loss_ref, stats_ref, rows_ref) = rest[:-5], rest[-5:]
+    du_ref, lse_ref, coef_ref, loss_ref, stats_ref, rows_ref = rest
     n = NX * NZ
     width = n * T // LANES
     for j in range(NX):
@@ -314,24 +314,18 @@
     loss_ref[...] = loss_rows(jnp.sum(loss, axis=1, keepdims=True), loss_ref.shape[1])
     coef_ref[...] = weight_ref[...] * (jnp.exp2(hit_ref[...] - lse_ref[...]) - 1.0)
 
-    def users_at(j, zr):
-        cols = pl.ds(pl.multiple_of(user_block((NX - j) % NX, zr) * T, T), T)
+    for b in range(n):
+        cols = slice(b * T, (b + 1) * T)
         weight = weight_ref[:, cols] * inv
         scale = weight * jnp.exp2(m_ref[:, cols] - lse_ref[:, cols])
-        return (acc_ref[:, cols] * scale - rows_ref[:, cols].astype(F32) * weight).astype(BF16)
-
-    for part, j in enumerate((0, 1, 3)):
-        for zr in range(NZ):
-            du_refs[part][zr * T : (zr + 1) * T, :] = users_at(j, zr)
-    du_refs[3][...] = users_at(2, 0)
-    du_refs[4][...] = users_at(2, 1)
+        du = acc_ref[:, cols] * scale - rows_ref[:, cols].astype(F32) * weight
+        du_ref[cols, :] = du.astype(BF16)
 
 
 def run_users(acc, m, rows_a, rows_b, hits, weights, stats, inv):
     width, total = acc.shape
     row = jax.ShapeDtypeStruct((1, total), F32)
-    shapes = [(NZ * width, T)] * 3 + [(width, T)] * 2
-    out_shape = [jax.ShapeDtypeStruct(x, BF16) for x in shapes]
+    out_shape = [jax.ShapeDtypeStruct((total // T * width, T), BF16)]
     out_shape += [row, row, jax.ShapeDtypeStruct((EXTRA, width), BF16)]
     return call(
         lambda *refs: users_kernel(inv, *refs),
@@ -447,40 +441,16 @@
     return simple_call(kernel, "add_rows", shapes, *parts)
 
 
-def add_halves(one, three, first, second):
-    half = one.shape[0] // NZ
-
-    def kernel(one_ref, three_ref, first_ref, second_ref, out1, out3):
-        out1[:half, :] = (one_ref[:half, :].astype(F32) + first_ref[...].astype(F32)).astype(BF16)
-        out1[half:, :] = one_ref[half:, :]
-        out3[:half, :] = three_ref[:half, :]
-        out3[half:, :] = (three_ref[half:, :].astype(F32) + second_ref[...].astype(F32)).astype(BF16)
-
-    shapes = [jax.ShapeDtypeStruct(one.shape, BF16)] * 2
-    return simple_call(kernel, "add_halves", shapes, one, three, first, second)
-
-
-def add_users(parts):
-    width = parts[0].shape[0] // NZ
-
-    def kernel(*refs):
-        ins, (keep, send) = refs[:-2], refs[-2:]
-        keep[...] = sum(r[:width, :].astype(F32) for r in ins)
-        send[...] = sum(r[width:, :].astype(F32) for r in ins).astype(BF16)
-
-    shapes = [jax.ShapeDtypeStruct((width, T), F32), jax.ShapeDtypeStruct((width, T), BF16)]
-    return simple_call(kernel, "add_users", shapes, *parts)
-
-
-def finish(keep_u, received_u, keep, received):
-    def kernel(keep_u_ref, received_u_ref, keep_ref, received_ref, grad_u, grad, loss):
-        grad_u[...] = plus(keep_u_ref[...], received_u_ref[...]).T
+def finish(parts_u, keep, received):
+    def kernel(parts_ref, keep_ref, received_ref, grad_u, grad, loss):
+        width = parts_ref.shape[0] // (NX * NZ)
+        grad_u[...] = plus(*(parts_ref[b * width : (b + 1) * width, :] for b in range(NX * NZ))).T
         grad[...] = plus(keep_ref[:T, :], received_ref[:T, :])
         loss[...] = jnp.sum(plus(keep_ref[T : T + 1, :], received_ref[T : T + 1, :]), axis=1, keepdims=True)
 
-    shapes = [(T, keep_u.shape[0]), (T, keep.shape[1]), (1, 1)]
+    shapes = [(T, parts_u.shape[0] // (NX * NZ)), (T, keep.shape[1]), (1, 1)]
     shapes = [jax.ShapeDtypeStruct(x, F32) for x in shapes]
-    return simple_call(kernel, "finish", shapes, keep_u, received_u, keep, received)
+    return simple_call(kernel, "finish", shapes, parts_u, keep, received)
 
 
 def join_stats(own, other):
@@ -551,30 +521,25 @@
     stats = join_stats(stats, stats_z)
     moved = tuple(shift_x(stats, j) for j in range(1, NX))
     moved, rows_b = lax.optimization_barrier((moved, run_rows(ads_t, pos_row, half, half)))
-    du_0, du_1, du_3, du_2a, du_2b, lse, coefs, loss = run_users(
-        acc, m, rows_a, rows_b, hits, weight_row, (stats, *moved), inv
-    )
+    du, lse, coefs, loss = run_users(acc, m, rows_a, rows_b, hits, weight_row, (stats, *moved), inv)
     tail = (lse, coefs, weight_row, pos_row, loss)
-    du_2a, du_2b = shift_x(du_2a, 1), shift_x(du_2b, -1)
+    du = lax.all_to_all(du, "aa", split_axis=0, concat_axis=0, tiled=True)
     pay_2, da_2 = run_grads("mid", [("far", 3, p_far, top_far), ("two", 0, p_two, top_two)], staged, *tail)
     back_2 = swap_core(pay_2)
     da_2, staged = lax.optimization_barrier((da_2, staged))
     (da_far,) = run_grads("far", [("far", i, p_far, top_far) for i in range(3)], staged, *tail)
-    da_far, back_2, du_2a, du_2b = lax.optimization_barrier((da_far, back_2, du_2a, du_2b))
-    du_1, du_3 = add_halves(du_1, du_3, du_2a, du_2b)
+    da_far, back_2 = lax.optimization_barrier((da_far, back_2))
     back = swap_core(da_far)
     first, second, both = add_mid(da_2, back_2)
-    first, second, du_1, du_3, staged = lax.optimization_barrier((first, second, du_1, du_3, staged))
+    first, second, staged = lax.optimization_barrier((first, second, staged))
     first, second = shift_y(first, -1), shift_y(second, 1)
-    du_1, du_3 = shift_x(du_1, 1), shift_x(du_3, -1)
     (da_near,) = run_grads("near", [("near", i, p_near, top_near) for i in range(3)], staged, *tail)
-    da_near, first, second, du_1, du_3 = lax.optimization_barrier((da_near, first, second, du_1, du_3))
+    da_near, first, second = lax.optimization_barrier((da_near, first, second))
     kept, one, three = add_near(da_near, back, both, first, second)
     one, three = shift_y(one, -1), shift_y(three, 1)
-    keep_u, send_u = add_users((du_0, du_1, du_3))
-    one, three, received_u = lax.optimization_barrier((one, three, swap_z_hi(send_u)))
+    one, three, du = lax.optimization_barrier((one, three, du))
     keep, send = add_rows(kept, one, three)
-    grad_users, grad_ads, loss = finish(keep_u, received_u, keep, swap_z_lo(send))
+    grad_users, grad_ads, loss = finish(du, keep, swap_z_lo(send))
     return grad_users, grad_ads, loss.reshape(())
 
 

time: 102 us -> 104 us (1.020)
  local copies, waits for them, and re-layouts: 0.01 us -> 5.41 us
  starting transfers between devices: 37.1 us -> 33.5 us
  waiting for transfers between devices: 30.5 us -> 28.8 us
  Pallas kernels: 30.7 us -> 32.3 us
    ppermute x25 -> x20, waiting for transfers between devices: 30.5 us -> 22.6 us  [move(): lax.ppermute(x, axis, [(i, target(i)) for i in range(lax.axis_size(axis))])]
    ppermute x25 -> x20, starting transfers between devices: 37.1 us -> 29.9 us  [move(): lax.ppermute(x, axis, [(i, target(i)) for i in range(lax.axis_size(axis))])]
    all_to_all x0 -> x1, waiting for transfers between devices: none -> 6.22 us  [local(): du = lax.all_to_all(du, 'aa', split_axis=0, concat_axis=0, tiled=True)]
    unnamed x2 -> x6, local copies, waits for them, and re-layouts: 0.01 us -> 5.41 us
    all_to_all x0 -> x1, starting transfers between devices: none -> 3.56 us  [local(): du = lax.all_to_all(du, 'aa', split_axis=0, concat_axis=0, tiled=True)]
    pallas_call x16 -> x14, Pallas kernels: 30.7 us -> 32.3 us  [call(): pl.pallas_call(kernel, in_specs=[vmem] * len(args), out_specs=[vmem] * le...]
  transfers between devices with their start and end apart: 25 -> 21, of which waited for: 13 -> 11; matrix products, arithmetic and copies ran while one was open for 1% -> 1% of each run, Pallas kernels for 18% -> 19%
where the time goes in v9:
time: 104 us; the launch traced here: 103 us
  starting transfers between devices  33.5 us (32%)
  Pallas kernels  32.3 us (31%)
  waiting for transfers between devices  28.8 us (28%)
  local copies, waits for them, and re-layouts  5.41 us (5%)
  other arithmetic  2.5 us (2%)
    pallas_call x14, Pallas kernels, call(): pl.pallas_call(kernel, in_specs=[vmem] * len(args), out_specs=[vmem] * le...  32.3 us
    ppermute x20, starting transfers between devices, move(): lax.ppermute(x, axis, [(i, target(i)) for i in range(lax.axis_size(axis))])  29.9 us
    ppermute x20, waiting for transfers between devices, move(): lax.ppermute(x, axis, [(i, target(i)) for i in range(lax.axis_size(axis))])  22.6 us
    all_to_all x1, waiting for transfers between devices, local(): du = lax.all_to_all(du, 'aa', split_axis=0, concat_axis=0, tiled=True)  6.22 us
    unnamed x6, local copies, waits for them, and re-layouts  5.41 us
    all_to_all x1, starting transfers between devices, local(): du = lax.all_to_all(du, 'aa', split_axis=0, concat_axis=0, tiled=True)  3.56 us
  transfers between devices with their start and end apart: 21, of which 11 were waited for; matrix products, arithmetic and copies ran while one was open for 1% of the time, Pallas kernels for 19%

profile of v9, /device:TPU:0, one launch (start us, length us, event | category | flops | bytes accessed | tf_op | source)
XLA Modules:
  0.0 103.3 jit_solution(16441405219043522826)
XLA Ops:
  0.6 4.0 %collective-permute-start = (bf16[256,256]{1,0:T(8,128)(2,1)}, bf16[256,256]{1,0:T(8,128)(2,1)S(1)}, u32[]{:S(2)}, u32[]{:S(2)}) collective-permute-start(bf16[256,256]{1,0:T(8,128)(2,1)} %param.5), channel_id=1, source_target_pairs={{0,1},{1,0},{2,3},{3,2},{4,5},{5,4},{6,7},{7,6},{8,9},{9,8},{10,11... | collective-permute-start | bytes 393224 | tf_op jit(solution)/shard_map/ppermute | solution.py:469
  4.7 1.0 collective-permute-start.1
  7.1 2.1 %collective-permute-done = bf16[256,256]{1,0:T(8,128)(2,1)S(1)} collective-permute-done((bf16[256,256]{1,0:T(8,128)(2,1)}, bf16[256,256]{1,0:T(8,128)(2,1)S(1)}, u32[]{:S(2)}, u32[]{:S(2)}) %collective-permute-start) | collective-permute-done | bytes 131104 | tf_op jit(solution)/shard_map/ppermute | solution.py:469
  9.2 2.7 %collective-permute-done.1 = bf16[256,256]{1,0:T(8,128)(2,1)S(1)} collective-permute-done((bf16[256,256]{1,0:T(8,128)(2,1)}, bf16[256,256]{1,0:T(8,128)(2,1)S(1)}, u32[]{:S(2)}, u32[]{:S(2)}) %collective-permute-start.1) | collective-permute-done | bytes 131104 | tf_op jit(solution)/shard_map/ppermute | solution.py:469
  12.9 2.8 %collective-permute-start.4 = (bf16[512,256]{1,0:T(8,128)(2,1)S(1)}, bf16[512,256]{1,0:T(8,128)(2,1)S(1)}, u32[]{:S(2)}, u32[]{:S(2)}) collective-permute-start(bf16[512,256]{1,0:T(8,128)(2,1)S(1)} %get-tuple-element.79.refs_0_), channel_id=1, source_target_pairs={{0,6},{1,7},{2,0},{3,1},{4,2},{5,3},{6,4},{7,5},{8,14},{9,15},{10,... | collective-permute-start | bytes 786440 | tf_op jit(solution)/shard_map/ppermute | solution.py:469
  17.4 3.0 %collective-permute-start.6 = (bf16[512,256]{1,0:T(8,128)(2,1)S(1)}, bf16[512,256]{1,0:T(8,128)(2,1)S(1)}, u32[]{:S(2)}, u32[]{:S(2)}) collective-permute-start(bf16[512,256]{1,0:T(8,128)(2,1)S(1)} %get-tuple-element.83.refs_4_), channel_id=1, source_target_pairs={{0,48},{8,56},{16,0},{24,8},{32,16},{40,24},{48,32},{56,40},{64,11... | collective-permute-start | bytes 786440 | tf_op jit(solution)/shard_map/ppermute | solution.py:469
  20.5 5.6 %collective-permute-done.4.refs_3_ = bf16[512,256]{1,0:T(8,128)(2,1)S(1)} collective-permute-done((bf16[512,256]{1,0:T(8,128)(2,1)S(1)}, bf16[512,256]{1,0:T(8,128)(2,1)S(1)}, u32[]{:S(2)}, u32[]{:S(2)}) %collective-permute-start.4) | collective-permute-done | bytes 262176 | tf_op jit(solution)/shard_map/ppermute | solution.py:469
  26.1 3.2 %collective-permute-start.7 = (bf16[512,256]{1,0:T(8,128)(2,1)S(1)}, bf16[512,256]{1,0:T(8,128)(2,1)S(1)}, u32[]{:S(2)}, u32[]{:S(2)}) collective-permute-start(bf16[512,256]{1,0:T(8,128)(2,1)S(1)} %get-tuple-element.83.refs_4_), channel_id=1, source_target_pairs={{0,32},{8,40},{16,48},{24,56},{32,0},{40,8},{48,16},{56,24},{64,96... | collective-permute-start | bytes 786440 | tf_op jit(solution)/shard_map/ppermute | solution.py:469
  30.5 6.4 %logits_near.1 = (bf16[1536,2048]{1,0:T(8,128)(2,1)S(1)}, f32[1,2048]{1,0:T(1,128)S(1)}, bf16[256,1536]{1,0:T(8,128)(2,1)S(1)}, f32[256,2048]{1,0:T(8,128)S(1)},...) custom-call(bf16[512,256]{1,0:T(8,128)(2,1)S(1)} %get-tuple-element., ...), custom_call_target="tpu_custom_call" | custom-call | flops 100663296 | bytes 393216 | tf_op jit(solution)/shard_map/logits_near/pallas_call | solution.py:25
  36.9 2.6 %copy-done = bf16[1536,2048]{1,0:T(8,128)(2,1)} copy-done((bf16[1536,2048]{1,0:T(8,128)(2,1)}, bf16[1536,2048]{1,0:T(8,128)(2,1)S(1)}, u32[]{:S(2)}) %copy-start) | copy-done | bytes 6291480
  39.9 2.5 %logits_two.1 = (bf16[512,2048]{1,0:T(8,128)(2,1)S(1)}, f32[1,2048]{1,0:T(1,128)S(1)}, bf16[256,512]{1,0:T(8,128)(2,1)S(1)}, f32[256,2048]{1,0:T(8,128)S(1)}, f3...) custom-call(bf16[256,2048]{1,0:T(8,128)(2,1)S(1)} %get-tuple-element.87.refs_0_, ...), custom_call_target="tpu_custom_call" | custom-call | flops 33554432 | bytes 131072 | tf_op jit(solution)/shard_map/logits_two/pallas_call | solution.py:25
  42.5 9.0 %logits_far.1 = (bf16[2048,2048]{1,0:T(8,128)(2,1)S(1)}, f32[1,2048]{1,0:T(1,128)S(1)}, bf16[256,2048]{1,0:T(8,128)(2,1)S(1)}, f32[256,2048]{1,0:T(8,128)S(1)}, ...) custom-call(bf16[256,2048]{1,0:T(8,128)(2,1)S(1)} %get-tuple-element.87.refs_0_, ...), custom_call_target="tpu_custom_call" | custom-call | flops 134217728 | bytes 524288 | tf_op jit(solution)/shard_map/logits_far/pallas_call | solution.py:25
  51.6 1.2 %collective-permute-start.9 = (f32[32,128]{1,0:T(8,128)S(1)}, f32[32,128]{1,0:T(8,128)S(1)}, u32[]{:S(2)}, u32[]{:S(2)}) collective-permute-start(f32[32,128]{1,0:T(8,128)S(1)} %get-tuple-element.102.own_ref), channel_id=1, source_target_pairs={{0,1},{1,0},{2,3},{3,2},{4,5},{5,4},{6,7},{7,6},{8,9},{9,8},{10,11... | collective-permute-start | bytes 49160 | tf_op jit(solution)/shard_map/ppermute | solution.py:469
  52.7 2.3 %positive_rows.2.refs_2_ = bf16[256,1024]{1,0:T(8,128)(2,1)S(1)} custom-call(bf16[256,1536]{1,0:T(8,128)(2,1)S(1)} %get-tuple-element.103.refs_0_, bf16[256,512]{1,0:T(8,128)(2,1)S(1)} %get-tuple-element.104.refs_1_, bf16[256,2048]{1,0:T(8,128)(2,1)S(1)} %get-tuple-element.105.refs_2_, s32[1,2048]{1,0:T(1,128)S(1)} %bitcast.10), custom_call_target="tpu_custom_call" | custom-call | flops 134217728 | bytes 524288 | tf_op jit(solution)/shard_map/positive_rows/pallas_call | solution.py:25
  55.1 1.7 %collective-permute-done.9.other_ref = f32[32,128]{1,0:T(8,128)S(1)} collective-permute-done((f32[32,128]{1,0:T(8,128)S(1)}, f32[32,128]{1,0:T(8,128)S(1)}, u32[]{:S(2)}, u32[]{:S(2)}) %collective-permute-start.9) | collective-permute-done | bytes 16416 | tf_op jit(solution)/shard_map/ppermute | solution.py:469
  56.8 2.7 %collective-permute-start.12 = (f32[32,128]{1,0:T(8,128)S(1)}, f32[32,128]{1,0:T(8,128)S(1)}, u32[]{:S(2)}, u32[]{:S(2)}) collective-permute-start(f32[32,128]{1,0:T(8,128)S(1)} %join_stats.1.refs_6_), channel_id=1, source_target_pairs={{0,6},{1,7},{2,0},{3,1},{4,2},{5,3},{6,4},{7,5},{8,14},{9,15},{10,... | collective-permute-start | bytes 49160 | tf_op jit(solution)/shard_map/ppermute | solution.py:469
  59.6 4.0 %collective-permute-start.11 = (f32[32,128]{1,0:T(8,128)S(1)}, f32[32,128]{1,0:T(8,128)S(1)}, u32[]{:S(2)}, u32[]{:S(2)}) collective-permute-start(f32[32,128]{1,0:T(8,128)S(1)} %join_stats.1.refs_6_), channel_id=1, source_target_pairs={{0,4},{1,5},{2,6},{3,7},{4,0},{5,1},{6,2},{7,3},{8,12},{9,13},{10,... | collective-permute-start | bytes 49160 | tf_op jit(solution)/shard_map/ppermute | solution.py:469
  63.6 2.3 %positive_rows.3.refs_3_ = bf16[256,1024]{1,0:T(8,128)(2,1)S(1)} custom-call(bf16[256,1536]{1,0:T(8,128)(2,1)S(1)} %get-tuple-element.103.refs_0_, bf16[256,512]{1,0:T(8,128)(2,1)S(1)} %get-tuple-element.104.refs_1_, bf16[256,2048]{1,0:T(8,128)(2,1)S(1)} %get-tuple-element.105.refs_2_, s32[1,2048]{1,0:T(1,128)S(1)} %bitcast.11), custom_call_target="tpu_custom_call" | custom-call | flops 134217728 | bytes 524288 | tf_op jit(solution)/shard_map/positive_rows/pallas_call | solution.py:25
  66.0 2.6 %collective-permute-done.10.refs_7_ = f32[32,128]{1,0:T(8,128)S(1)} collective-permute-done((f32[32,128]{1,0:T(8,128)S(1)}, f32[32,128]{1,0:T(8,128)S(1)}, u32[]{:S(2)}, u32[]{:S(2)}) %collective-permute-start.10) | collective-permute-done | bytes 16416 | tf_op jit(solution)/shard_map/ppermute | solution.py:469
  68.5 1.6 %grad_users.1 = (bf16[2048,256]{1,0:T(8,128)(2,1)}, f32[1,2048]{1,0:T(1,128)S(1)}, f32[1,2048]{1,0:T(1,128)S(1)}, bf16[16,256]{1,0:T(8,128)(2,1)S(1)}) custom-call(f32[256,2048]{1,0:T(8,128)S(1)} %get-tuple-element.100.refs_0_, f32[1,2048]{1,0:T(1,128)S(1)} %get-tuple-element.101.refs_1_, bf16[256,1024]{1,0:T(8,128)(2,1)S(1)} %positive_rows.2.refs_2_, ...), custom_call_target="tpu_custom_call" | custom-call | tf_op jit(solution)/shard_map/grad_users/pallas_call | solution.py:25
  70.1 1.4 %grads_mid.1 = (bf16[528,256]{1,0:T(8,128)(2,1)S(1)}, bf16[528,256]{1,0:T(8,128)(2,1)S(1)}) custom-call(bf16[2048,256]{1,0:T(8,128)(2,1)S(1)} %get-tuple-element.127.refs_0_, f32[1,2048]{1,0:T(1,128)S(1)} %get-tuple-element.113.refs_1_, f32[1,2048]{1,0:T(1,128)S(1)} %get-tuple-element.114.refs_2_, f32[1,2048]{1,0:T(1,128)S(1)} %bitcast.19, ...), custom_call_target="tpu_custom_call" | custom-call | flops 67108864 | bytes 262144 | tf_op jit(solution)/shard_map/grads_mid/pallas_call | solution.py:25
  71.6 2.1 %grads_far.1 = bf16[1536,256]{1,0:T(8,128)(2,1)S(1)} custom-call(bf16[2048,256]{1,0:T(8,128)(2,1)S(1)} %get-tuple-element.127.refs_0_, f32[1,2048]{1,0:T(1,128)S(1)} %get-tuple-element.113.refs_1_, f32[1,2048]{1,0:T(1,128)S(1)} %get-tuple-element.114.refs_2_, f32[1,2048]{1,0:T(1,128)S(1)} %bitcast.20, s32[1,2048]{1,0:T(1,128)S(1)} %bitcast.13, ...), custom_call_target="tpu_custom_call" | custom-call | flops 100663296 | bytes 393216 | tf_op jit(solution)/shard_map/grads_far/pallas_call | solution.py:25
  74.4 3.6 %all-to-all-start = ((bf16[8,256,256]{2,1,0:T(8,128)(2,1)}), bf16[8,256,256]{2,1,0:T(8,128)(2,1)S(1)}, u32[]{:S(2)}, u32[]{:S(2)}) async-start(bf16[8,256,256]{2,1,0:T(8,128)(2,1)} %bitcast.3), calls=%async_computation | async-start | bytes 2097152 | tf_op jit(solution)/shard_map/all_to_all | solution.py:526
  78.4 1.7 %collective-permute-start.15 = (bf16[256,256]{1,0:T(8,128)(2,1)S(1)}, bf16[256,256]{1,0:T(8,128)(2,1)S(1)}, u32[]{:S(2)}, u32[]{:S(2)}) collective-permute-start(bf16[256,256]{1,0:T(8,128)(2,1)S(1)} %get-tuple-element.131), channel_id=1, source_target_pairs={{0,16},{8,24},{16,32},{24,40},{32,48},{40,56},{48,0},{56,8},{64,80... | collective-permute-start | bytes 393224 | tf_op jit(solution)/shard_map/ppermute | solution.py:469
  80.1 2.8 %copy-done.1 = bf16[1536,2048]{1,0:T(8,128)(2,1)S(1)} copy-done((bf16[1536,2048]{1,0:T(8,128)(2,1)S(1)}, bf16[1536,2048]{1,0:T(8,128)(2,1)}, u32[]{:S(2)}) %copy-start.1) | copy-done | bytes 6291480
  82.9 2.2 %grads_near.1.near_ref = bf16[1536,256]{1,0:T(8,128)(2,1)S(1)} custom-call(bf16[2048,256]{1,0:T(8,128)(2,1)S(1)} %get-tuple-element.127.refs_0_, f32[1,2048]{1,0:T(1,128)S(1)} %get-tuple-element.113.refs_1_, f32[1,2048]{1,0:T(1,128)S(1)} %get-tuple-element.114.refs_2_, f32[1,2048]{1,0:T(1,128)S(1)} %bitcast.21, s32[1,2048]{1,0:T(1,128)S(1)} %bitcast.14, ...), custom_call_target="tpu_custom_call" | custom-call | flops 100663296 | bytes 393216 | tf_op jit(solution)/shard_map/grads_near/pallas_call | solution.py:25
  85.1 1.3 %add_near.1 = (f32[528,256]{1,0:T(8,128)S(1)}, bf16[528,256]{1,0:T(8,128)(2,1)S(1)}, bf16[528,256]{1,0:T(8,128)(2,1)S(1)}) custom-call(bf16[1536,256]{1,0:T(8,128)(2,1)S(1)} %grads_near.1.near_ref, bf16[1536,256]{1,0:T(8,128)(2,1)} %collective-permute-done.16.back_ref, bf16[16,256]{1,0:T(8,128)(2,1)S(1)} %get-tuple-element.134.both_ref, ...), custom_call_target="tpu_custom_call" | custom-call | tf_op jit(solution)/shard_map/add_near/pallas_call | solution.py:25
  86.4 1.6 %collective-permute-start.17 = (bf16[528,256]{1,0:T(8,128)(2,1)S(1)}, bf16[528,256]{1,0:T(8,128)(2,1)S(1)}, u32[]{:S(2)}, u32[]{:S(2)}) collective-permute-start(bf16[528,256]{1,0:T(8,128)(2,1)S(1)} %get-tuple-element.137), channel_id=1, source_target_pairs={{0,48},{8,56},{16,0},{24,8},{32,16},{40,24},{48,32},{56,40},{64,11... | collective-permute-start | bytes 811016 | tf_op jit(solution)/shard_map/ppermute | solution.py:469
  88.5 6.2 %all-to-all-done = bf16[8,256,256]{2,1,0:T(8,128)(2,1)S(1)} async-done(((bf16[8,256,256]{2,1,0:T(8,128)(2,1)}), bf16[8,256,256]{2,1,0:T(8,128)(2,1)S(1)}, u32[]{:S(2)}, u32[]{:S(2)}) %all-to-all-start) | async-done | bytes 1048608 | tf_op jit(solution)/shard_map/all_to_all | solution.py:526
  94.7 2.4 %collective-permute-done.18.refs_2_ = bf16[528,256]{1,0:T(8,128)(2,1)S(1)} collective-permute-done((bf16[528,256]{1,0:T(8,128)(2,1)S(1)}, bf16[528,256]{1,0:T(8,128)(2,1)S(1)}, u32[]{:S(2)}, u32[]{:S(2)}) %collective-permute-start.18) | collective-permute-done | bytes 270368 | tf_op jit(solution)/shard_map/ppermute | solution.py:469
  97.2 1.1 %collective-permute-start.19 = (bf16[272,256]{1,0:T(8,128)(2,1)S(1)}, bf16[272,256]{1,0:T(8,128)(2,1)S(1)}, u32[]{:S(2)}, u32[]{:S(2)}) collective-permute-start(bf16[272,256]{1,0:T(8,128)(2,1)S(1)} %get-tuple-element.145), channel_id=1, source_target_pairs={{0,64},{8,72},{16,80},{24,88},{32,96},{40,104},{48,112},{56,120},{... | collective-permute-start | bytes 417800 | tf_op jit(solution)/shard_map/ppermute | solution.py:469
  98.3 4.0 %collective-permute-done.19.received_ref = bf16[272,256]{1,0:T(8,128)(2,1)S(1)} collective-permute-done((bf16[272,256]{1,0:T(8,128)(2,1)S(1)}, bf16[272,256]{1,0:T(8,128)(2,1)S(1)}, u32[]{:S(2)}, u32[]{:S(2)}) %collective-permute-start.19) | collective-permute-done | bytes 139296 | tf_op jit(solution)/shard_map/ppermute | solution.py:469
  (34 shorter events, 8.6 us)
Async XLA Ops:
  0.6 8.6 %collective-permute-start = (bf16[256,256]{1,0:T(8,128)(2,1)}, bf16[256,256]{1,0:T(8,128)(2,1)S(1)}, u32[]{:S(2)}, u32[]{:S(2)}) collective-permute-start(bf16[256,256]{1,0:T(8,128)(2,1)} %param.5), channel_id=1, source_target_pairs={{0,1},{1,0},{2,3},{3,2},{4,5},{5,4},{6,7},{7,6},{8,9},{9,8},{10,11... | collective-permute-start | bytes 393224 | tf_op jit(solution)/shard_map/ppermute | solution.py:469
  4.7 7.2 %collective-permute-start.1 = (bf16[256,256]{1,0:T(8,128)(2,1)}, bf16[256,256]{1,0:T(8,128)(2,1)S(1)}, u32[]{:S(2)}, u32[]{:S(2)}) collective-permute-start(bf16[256,256]{1,0:T(8,128)(2,1)} %param.6), channel_id=1, source_target_pairs={{0,64},{8,72},{16,80},{24,88},{32,96},{40,104},{48,112},{56,120},{... | collective-permute-start | bytes 393224 | tf_op jit(solution)/shard_map/ppermute | solution.py:469
  12.9 13.2 %collective-permute-start.4 = (bf16[512,256]{1,0:T(8,128)(2,1)S(1)}, bf16[512,256]{1,0:T(8,128)(2,1)S(1)}, u32[]{:S(2)}, u32[]{:S(2)}) collective-permute-start(bf16[512,256]{1,0:T(8,128)(2,1)S(1)} %get-tuple-element.79.refs_0_), channel_id=1, source_target_pairs={{0,6},{1,7},{2,0},{3,1},{4,2},{5,3},{6,4},{7,5},{8,14},{9,15},{10,... | collective-permute-start | bytes 786440 | tf_op jit(solution)/shard_map/ppermute | solution.py:469
  15.8 13.5 %collective-permute-start.3 = (bf16[512,256]{1,0:T(8,128)(2,1)S(1)}, bf16[512,256]{1,0:T(8,128)(2,1)S(1)}, u32[]{:S(2)}, u32[]{:S(2)}) collective-permute-start(bf16[512,256]{1,0:T(8,128)(2,1)S(1)} %get-tuple-element.79.refs_0_), channel_id=1, source_target_pairs={{0,4},{1,5},{2,6},{3,7},{4,0},{5,1},{6,2},{7,3},{8,12},{9,13},{10,... | collective-permute-start | bytes 786440 | tf_op jit(solution)/shard_map/ppermute | solution.py:469
  16.6 13.2 %collective-permute-start.2 = (bf16[512,256]{1,0:T(8,128)(2,1)S(1)}, bf16[512,256]{1,0:T(8,128)(2,1)S(1)}, u32[]{:S(2)}, u32[]{:S(2)}) collective-permute-start(bf16[512,256]{1,0:T(8,128)(2,1)S(1)} %get-tuple-element.79.refs_0_), channel_id=1, source_target_pairs={{0,2},{1,3},{2,4},{3,5},{4,6},{5,7},{6,0},{7,1},{8,10},{9,11},{10,... | collective-permute-start | bytes 786440 | tf_op jit(solution)/shard_map/ppermute | solution.py:469
  17.4 12.3 %collective-permute-start.6 = (bf16[512,256]{1,0:T(8,128)(2,1)S(1)}, bf16[512,256]{1,0:T(8,128)(2,1)S(1)}, u32[]{:S(2)}, u32[]{:S(2)}) collective-permute-start(bf16[512,256]{1,0:T(8,128)(2,1)S(1)} %get-tuple-element.83.refs_4_), channel_id=1, source_target_pairs={{0,48},{8,56},{16,0},{24,8},{32,16},{40,24},{48,32},{56,40},{64,11... | collective-permute-start | bytes 786440 | tf_op jit(solution)/shard_map/ppermute | solution.py:469
  20.5 10.1 %collective-permute-start.5 = (bf16[512,256]{1,0:T(8,128)(2,1)S(1)}, bf16[512,256]{1,0:T(8,128)(2,1)S(1)}, u32[]{:S(2)}, u32[]{:S(2)}) collective-permute-start(bf16[512,256]{1,0:T(8,128)(2,1)S(1)} %get-tuple-element.83.refs_4_), channel_id=1, source_target_pairs={{0,16},{8,24},{16,32},{24,40},{32,48},{40,56},{48,0},{56,8},{64,80... | collective-permute-start | bytes 786440 | tf_op jit(solution)/shard_map/ppermute | solution.py:469
  26.1 13.5 %collective-permute-start.7 = (bf16[512,256]{1,0:T(8,128)(2,1)S(1)}, bf16[512,256]{1,0:T(8,128)(2,1)S(1)}, u32[]{:S(2)}, u32[]{:S(2)}) collective-permute-start(bf16[512,256]{1,0:T(8,128)(2,1)S(1)} %get-tuple-element.83.refs_4_), channel_id=1, source_target_pairs={{0,32},{8,40},{16,48},{24,56},{32,0},{40,8},{48,16},{56,24},{64,96... | collective-permute-start | bytes 786440 | tf_op jit(solution)/shard_map/ppermute | solution.py:469
  36.9 2.6 %copy-start = (bf16[1536,2048]{1,0:T(8,128)(2,1)}, bf16[1536,2048]{1,0:T(8,128)(2,1)S(1)}, u32[]{:S(2)}) copy-start(bf16[1536,2048]{1,0:T(8,128)(2,1)S(1)} %get-tuple-element.128.refs_6_.refs_7_.refs_8_) | copy-start | bytes 18874372
  39.6 2.9 %collective-permute-start.8 = (bf16[2048,256]{1,0:T(8,128)(2,1)S(1)}, bf16[2048,256]{1,0:T(8,128)(2,1)S(1)}, u32[]{:S(2)}, u32[]{:S(2)}) collective-permute-start(bf16[2048,256]{1,0:T(8,128)(2,1)S(1)} %pad_maximum_fusion), channel_id=1, source_target_pairs={{0,8},{8,0},{16,24},{24,16},{32,40},{40,32},{48,56},{56,48},{64,72... | collective-permute-start | bytes 3145736 | tf_op jit(solution)/shard_map/ppermute | solution.py:469
  51.6 5.2 %collective-permute-start.9 = (f32[32,128]{1,0:T(8,128)S(1)}, f32[32,128]{1,0:T(8,128)S(1)}, u32[]{:S(2)}, u32[]{:S(2)}) collective-permute-start(f32[32,128]{1,0:T(8,128)S(1)} %get-tuple-element.102.own_ref), channel_id=1, source_target_pairs={{0,1},{1,0},{2,3},{3,2},{4,5},{5,4},{6,7},{7,6},{8,9},{9,8},{10,11... | collective-permute-start | bytes 49160 | tf_op jit(solution)/shard_map/ppermute | solution.py:469
  52.7 15.8 %copy-start.2 = (f32[2048]{0:T(1024)S(1)}, f32[2048]{0:T(1024)}, u32[]{:S(2)}) copy-start(f32[2048]{0:T(1024)} %param.9) | copy-start | bytes 24580
  56.8 9.1 %collective-permute-start.12 = (f32[32,128]{1,0:T(8,128)S(1)}, f32[32,128]{1,0:T(8,128)S(1)}, u32[]{:S(2)}, u32[]{:S(2)}) collective-permute-start(f32[32,128]{1,0:T(8,128)S(1)} %join_stats.1.refs_6_), channel_id=1, source_target_pairs={{0,6},{1,7},{2,0},{3,1},{4,2},{5,3},{6,4},{7,5},{8,14},{9,15},{10,... | collective-permute-start | bytes 49160 | tf_op jit(solution)/shard_map/ppermute | solution.py:469
  59.6 6.4 %collective-permute-start.11 = (f32[32,128]{1,0:T(8,128)S(1)}, f32[32,128]{1,0:T(8,128)S(1)}, u32[]{:S(2)}, u32[]{:S(2)}) collective-permute-start(f32[32,128]{1,0:T(8,128)S(1)} %join_stats.1.refs_6_), channel_id=1, source_target_pairs={{0,4},{1,5},{2,6},{3,7},{4,0},{5,1},{6,2},{7,3},{8,12},{9,13},{10,... | collective-permute-start | bytes 49160 | tf_op jit(solution)/shard_map/ppermute | solution.py:469
  63.6 4.9 %collective-permute-start.10 = (f32[32,128]{1,0:T(8,128)S(1)}, f32[32,128]{1,0:T(8,128)S(1)}, u32[]{:S(2)}, u32[]{:S(2)}) collective-permute-start(f32[32,128]{1,0:T(8,128)S(1)} %join_stats.1.refs_6_), channel_id=1, source_target_pairs={{0,2},{1,3},{2,4},{3,5},{4,6},{5,7},{6,0},{7,1},{8,10},{9,11},{10,... | collective-permute-start | bytes 49160 | tf_op jit(solution)/shard_map/ppermute | solution.py:469
  71.6 2.2 %collective-permute-start.13 = (bf16[528,256]{1,0:T(8,128)(2,1)S(1)}, bf16[528,256]{1,0:T(8,128)(2,1)S(1)}, u32[]{:S(2)}, u32[]{:S(2)}) collective-permute-start(bf16[528,256]{1,0:T(8,128)(2,1)S(1)} %get-tuple-element.123), channel_id=1, source_target_pairs={{0,8},{8,0},{16,24},{24,16},{32,40},{40,32},{48,56},{56,48},{64,72... | collective-permute-start | bytes 811016 | tf_op jit(solution)/shard_map/ppermute | solution.py:469
  73.8 11.3 %collective-permute-start.16 = (bf16[1536,256]{1,0:T(8,128)(2,1)S(1)}, bf16[1536,256]{1,0:T(8,128)(2,1)}, u32[]{:S(2)}, u32[]{:S(2)}) collective-permute-start(bf16[1536,256]{1,0:T(8,128)(2,1)S(1)} %grads_far.1), channel_id=1, source_target_pairs={{0,8},{8,0},{16,24},{24,16},{32,40},{40,32},{48,56},{56,48},{64,72... | collective-permute-start | bytes 2359304 | tf_op jit(solution)/shard_map/ppermute | solution.py:469
  74.4 20.4 %all-to-all-start = ((bf16[8,256,256]{2,1,0:T(8,128)(2,1)}), bf16[8,256,256]{2,1,0:T(8,128)(2,1)S(1)}, u32[]{:S(2)}, u32[]{:S(2)}) async-start(bf16[8,256,256]{2,1,0:T(8,128)(2,1)} %bitcast.3), calls=%async_computation | async-start | bytes 2097152 | tf_op jit(solution)/shard_map/all_to_all | solution.py:526
  78.0 7.1 %collective-permute-start.14 = (bf16[272,256]{1,0:T(8,128)(2,1)S(1)}, bf16[272,256]{1,0:T(8,128)(2,1)S(1)}, u32[]{:S(2)}, u32[]{:S(2)}) collective-permute-start(bf16[272,256]{1,0:T(8,128)(2,1)S(1)} %get-tuple-element.130), channel_id=1, source_target_pairs={{0,48},{8,56},{16,0},{24,8},{32,16},{40,24},{48,32},{56,40},{64,11... | collective-permute-start | bytes 417800 | tf_op jit(solution)/shard_map/ppermute | solution.py:469
  78.4 6.6 %collective-permute-start.15 = (bf16[256,256]{1,0:T(8,128)(2,1)S(1)}, bf16[256,256]{1,0:T(8,128)(2,1)S(1)}, u32[]{:S(2)}, u32[]{:S(2)}) collective-permute-start(bf16[256,256]{1,0:T(8,128)(2,1)S(1)} %get-tuple-element.131), channel_id=1, source_target_pairs={{0,16},{8,24},{16,32},{24,40},{32,48},{40,56},{48,0},{56,8},{64,80... | collective-permute-start | bytes 393224 | tf_op jit(solution)/shard_map/ppermute | solution.py:469
  80.1 2.8 %copy-start.1 = (bf16[1536,2048]{1,0:T(8,128)(2,1)S(1)}, bf16[1536,2048]{1,0:T(8,128)(2,1)}, u32[]{:S(2)}) copy-start(bf16[1536,2048]{1,0:T(8,128)(2,1)} %copy-done) | copy-start | bytes 18874372
  86.4 8.3 %collective-permute-start.17 = (bf16[528,256]{1,0:T(8,128)(2,1)S(1)}, bf16[528,256]{1,0:T(8,128)(2,1)S(1)}, u32[]{:S(2)}, u32[]{:S(2)}) collective-permute-start(bf16[528,256]{1,0:T(8,128)(2,1)S(1)} %get-tuple-element.137), channel_id=1, source_target_pairs={{0,48},{8,56},{16,0},{24,8},{32,16},{40,24},{48,32},{56,40},{64,11... | collective-permute-start | bytes 811016 | tf_op jit(solution)/shard_map/ppermute | solution.py:469
  88.0 9.1 %collective-permute-start.18 = (bf16[528,256]{1,0:T(8,128)(2,1)S(1)}, bf16[528,256]{1,0:T(8,128)(2,1)S(1)}, u32[]{:S(2)}, u32[]{:S(2)}) collective-permute-start(bf16[528,256]{1,0:T(8,128)(2,1)S(1)} %get-tuple-element.138), channel_id=1, source_target_pairs={{0,16},{8,24},{16,32},{24,40},{32,48},{40,56},{48,0},{56,8},{64,80... | collective-permute-start | bytes 811016 | tf_op jit(solution)/shard_map/ppermute | solution.py:469
  97.2 5.1 %collective-permute-start.19 = (bf16[272,256]{1,0:T(8,128)(2,1)S(1)}, bf16[272,256]{1,0:T(8,128)(2,1)S(1)}, u32[]{:S(2)}, u32[]{:S(2)}) collective-permute-start(bf16[272,256]{1,0:T(8,128)(2,1)S(1)} %get-tuple-element.145), channel_id=1, source_target_pairs={{0,64},{8,72},{16,80},{24,88},{32,96},{40,104},{48,112},{56,120},{... | collective-permute-start | bytes 417800 | tf_op jit(solution)/shard_map/ppermute | solution.py:469

commit v10 on v9

--- a/solution.py
+++ b/solution.py
@@ -13,7 +13,7 @@
 LOG2E = 1.4426950408889634
 LN2 = 0.6931471805599453
 NX, NZ, NY, NC = 4, 2, 4, 2
-VMEM_LIMIT = 24 * 2**20
+VMEM_LIMIT = 15 * 2**20
 
 
 def params():
@@ -94,7 +94,7 @@
         (staged, users_t), refs = refs[:2], refs[2:]
     if last_call:
         (stats_ref,), refs = refs[:1], refs[1:]
-    ads_all, logc_all, s0, s1, *late = refs
+    ads_all, logc_all, s0, s1 = refs
 
     if first_call:
         stage_users(user_refs, staged, inv)
@@ -138,8 +138,8 @@
             hit_ref[:, self.cols] = hit if first_call else hit + hit_in[:, self.cols]
 
     class Exps:
-        def __init__(self, tile, src, extra):
-            self.cols, self.src, self.extra = columns(tile), src, extra
+        def __init__(self, tile, src):
+            self.cols, self.src = columns(tile), src
             self.top = top_ref[:, self.cols]
             self.total = jnp.zeros((8, T), F32)
 
@@ -147,9 +147,7 @@
             for r in range(c * T, (c + 1) * T, 16):
                 e = jnp.exp2(self.src[r : r + 16, :] - self.top)
                 self.total += e[:8] + e[8:]
-                e = e.astype(BF16)
-                p_ref[r : r + 16, self.cols] = e
-                self.extra[r : r + 16, :] = e
+                p_ref[r : r + 16, self.cols] = e.astype(BF16)
 
         def end(self):
             cols, top = self.cols, self.top
@@ -162,20 +160,20 @@
                 m_ref[:, cols] = m
                 total_ref[:, cols] = total_in[:, cols] * jnp.exp2(m_in[:, cols] - m) + total * jnp.exp2(top - m)
 
-    def gather(tile, e):
+    def gather(tile):
         cols = columns(tile)
-        new = jnp.dot(ads_t[...], e[...], preferred_element_type=F32)
+        new = jnp.dot(ads_t[...], p_ref[:, cols], preferred_element_type=F32)
         if first_call:
             acc_ref[:, cols] = new
         else:
             m = m_ref[:, cols]
             acc_ref[:, cols] = acc_in[:, cols] * jnp.exp2(m_in[:, cols] - m) + new * jnp.exp2(top_ref[:, cols] - m)
 
-    def turn(tile, src, dst, e_now, e_before):
+    def turn(tile, src, dst):
         if tile:
-            gather(tile - 1, e_before)
+            gather(tile - 1)
         product = Product(tile + 1, dst) if tile + 1 < n else None
-        exps = Exps(tile, src, e_now)
+        exps = Exps(tile, src)
         for c in range(chunks):
             if product:
                 product.chunk(c)
@@ -190,10 +188,10 @@
     opening.end()
     for tile in range(n):
         if tile % 2:
-            turn(tile, s1, s0, late[1], late[0])
+            turn(tile, s1, s0)
         else:
-            turn(tile, s0, s1, late[0], late[1])
-    gather(n - 1, late[(n - 1) % 2])
+            turn(tile, s0, s1)
+    gather(n - 1)
     if last_call:
         lse = m_ref[...] + jnp.log2(total_ref[...])
         width = n * T // LANES
@@ -232,8 +230,6 @@
         pltpu.VMEM((count, LANES), F32),
         pltpu.VMEM((count, T), F32),
         pltpu.VMEM((count, T), F32),
-        pltpu.VMEM((count, T), BF16),
-        pltpu.VMEM((count, T), BF16),
     ]
     return call(
         lambda *refs: logits_kernel(group, len(ads), count, inv, *refs),

time: 104 us -> 104 us (level)
  no operation moved by 1% of the time
where the time goes in v10:
time: 104 us; the launch traced here: 103 us
  starting transfers between devices  33.5 us (32%)
  Pallas kernels  32.4 us (31%)
  waiting for transfers between devices  28.9 us (28%)
  local copies, waits for them, and re-layouts  5.41 us (5%)
  other arithmetic  2.5 us (2%)
    pallas_call x14, Pallas kernels, call(): pl.pallas_call(kernel, in_specs=[vmem] * len(args), out_specs=[vmem] * le...  32.4 us
    ppermute x20, starting transfers between devices, move(): lax.ppermute(x, axis, [(i, target(i)) for i in range(lax.axis_size(axis))])  29.9 us
    ppermute x20, waiting for transfers between devices, move(): lax.ppermute(x, axis, [(i, target(i)) for i in range(lax.axis_size(axis))])  22.6 us
    all_to_all x1, waiting for transfers between devices, local(): du = lax.all_to_all(du, 'aa', split_axis=0, concat_axis=0, tiled=True)  6.22 us
    unnamed x6, local copies, waits for them, and re-layouts  5.41 us
    all_to_all x1, starting transfers between devices, local(): du = lax.all_to_all(du, 'aa', split_axis=0, concat_axis=0, tiled=True)  3.56 us
  transfers between devices with their start and end apart: 21, of which 11 were waited for; matrix products, arithmetic and copies ran while one was open for 1% of the time, Pallas kernels for 19%

profile of v10, /device:TPU:0, one launch (start us, length us, event | category | flops | bytes accessed | tf_op | source)
XLA Modules:
  0.0 103.5 jit_solution(5682485317243470944)
XLA Ops:
  0.6 4.0 %collective-permute-start = (bf16[256,256]{1,0:T(8,128)(2,1)}, bf16[256,256]{1,0:T(8,128)(2,1)S(1)}, u32[]{:S(2)}, u32[]{:S(2)}) collective-permute-start(bf16[256,256]{1,0:T(8,128)(2,1)} %param.5), channel_id=1, source_target_pairs={{0,1},{1,0},{2,3},{3,2},{4,5},{5,4},{6,7},{7,6},{8,9},{9,8},{10,11... | collective-permute-start | bytes 393224 | tf_op jit(solution)/shard_map/ppermute | solution.py:465
  4.7 1.0 collective-permute-start.1
  7.1 2.1 %collective-permute-done = bf16[256,256]{1,0:T(8,128)(2,1)S(1)} collective-permute-done((bf16[256,256]{1,0:T(8,128)(2,1)}, bf16[256,256]{1,0:T(8,128)(2,1)S(1)}, u32[]{:S(2)}, u32[]{:S(2)}) %collective-permute-start) | collective-permute-done | bytes 131104 | tf_op jit(solution)/shard_map/ppermute | solution.py:465
  9.2 2.7 %collective-permute-done.1 = bf16[256,256]{1,0:T(8,128)(2,1)S(1)} collective-permute-done((bf16[256,256]{1,0:T(8,128)(2,1)}, bf16[256,256]{1,0:T(8,128)(2,1)S(1)}, u32[]{:S(2)}, u32[]{:S(2)}) %collective-permute-start.1) | collective-permute-done | bytes 131104 | tf_op jit(solution)/shard_map/ppermute | solution.py:465
  12.9 2.8 %collective-permute-start.4 = (bf16[512,256]{1,0:T(8,128)(2,1)S(1)}, bf16[512,256]{1,0:T(8,128)(2,1)S(1)}, u32[]{:S(2)}, u32[]{:S(2)}) collective-permute-start(bf16[512,256]{1,0:T(8,128)(2,1)S(1)} %get-tuple-element.79.refs_0_), channel_id=1, source_target_pairs={{0,6},{1,7},{2,0},{3,1},{4,2},{5,3},{6,4},{7,5},{8,14},{9,15},{10,... | collective-permute-start | bytes 786440 | tf_op jit(solution)/shard_map/ppermute | solution.py:465
  17.4 3.0 %collective-permute-start.6 = (bf16[512,256]{1,0:T(8,128)(2,1)S(1)}, bf16[512,256]{1,0:T(8,128)(2,1)S(1)}, u32[]{:S(2)}, u32[]{:S(2)}) collective-permute-start(bf16[512,256]{1,0:T(8,128)(2,1)S(1)} %get-tuple-element.83.refs_4_), channel_id=1, source_target_pairs={{0,48},{8,56},{16,0},{24,8},{32,16},{40,24},{48,32},{56,40},{64,11... | collective-permute-start | bytes 786440 | tf_op jit(solution)/shard_map/ppermute | solution.py:465
  20.5 5.6 %collective-permute-done.4.refs_3_ = bf16[512,256]{1,0:T(8,128)(2,1)S(1)} collective-permute-done((bf16[512,256]{1,0:T(8,128)(2,1)S(1)}, bf16[512,256]{1,0:T(8,128)(2,1)S(1)}, u32[]{:S(2)}, u32[]{:S(2)}) %collective-permute-start.4) | collective-permute-done | bytes 262176 | tf_op jit(solution)/shard_map/ppermute | solution.py:465
  26.1 3.2 %collective-permute-start.7 = (bf16[512,256]{1,0:T(8,128)(2,1)S(1)}, bf16[512,256]{1,0:T(8,128)(2,1)S(1)}, u32[]{:S(2)}, u32[]{:S(2)}) collective-permute-start(bf16[512,256]{1,0:T(8,128)(2,1)S(1)} %get-tuple-element.83.refs_4_), channel_id=1, source_target_pairs={{0,32},{8,40},{16,48},{24,56},{32,0},{40,8},{48,16},{56,24},{64,96... | collective-permute-start | bytes 786440 | tf_op jit(solution)/shard_map/ppermute | solution.py:465
  30.5 6.5 %logits_near.1 = (bf16[1536,2048]{1,0:T(8,128)(2,1)S(1)}, f32[1,2048]{1,0:T(1,128)S(1)}, bf16[256,1536]{1,0:T(8,128)(2,1)S(1)}, f32[256,2048]{1,0:T(8,128)S(1)},...) custom-call(bf16[512,256]{1,0:T(8,128)(2,1)S(1)} %get-tuple-element., ...), custom_call_target="tpu_custom_call" | custom-call | flops 100663296 | bytes 393216 | tf_op jit(solution)/shard_map/logits_near/pallas_call | solution.py:25
  37.0 2.6 %copy-done = bf16[1536,2048]{1,0:T(8,128)(2,1)} copy-done((bf16[1536,2048]{1,0:T(8,128)(2,1)}, bf16[1536,2048]{1,0:T(8,128)(2,1)S(1)}, u32[]{:S(2)}) %copy-start) | copy-done | bytes 6291480
  40.0 2.4 %logits_two.1 = (bf16[512,2048]{1,0:T(8,128)(2,1)S(1)}, f32[1,2048]{1,0:T(1,128)S(1)}, bf16[256,512]{1,0:T(8,128)(2,1)S(1)}, f32[256,2048]{1,0:T(8,128)S(1)}, f3...) custom-call(bf16[256,2048]{1,0:T(8,128)(2,1)S(1)} %get-tuple-element.87.refs_0_, ...), custom_call_target="tpu_custom_call" | custom-call | flops 33554432 | bytes 131072 | tf_op jit(solution)/shard_map/logits_two/pallas_call | solution.py:25
  42.6 9.1 %logits_far.1 = (bf16[2048,2048]{1,0:T(8,128)(2,1)S(1)}, f32[1,2048]{1,0:T(1,128)S(1)}, bf16[256,2048]{1,0:T(8,128)(2,1)S(1)}, f32[256,2048]{1,0:T(8,128)S(1)}, ...) custom-call(bf16[256,2048]{1,0:T(8,128)(2,1)S(1)} %get-tuple-element.87.refs_0_, ...), custom_call_target="tpu_custom_call" | custom-call | flops 134217728 | bytes 524288 | tf_op jit(solution)/shard_map/logits_far/pallas_call | solution.py:25
  51.8 1.2 %collective-permute-start.9 = (f32[32,128]{1,0:T(8,128)S(1)}, f32[32,128]{1,0:T(8,128)S(1)}, u32[]{:S(2)}, u32[]{:S(2)}) collective-permute-start(f32[32,128]{1,0:T(8,128)S(1)} %get-tuple-element.102.own_ref), channel_id=1, source_target_pairs={{0,1},{1,0},{2,3},{3,2},{4,5},{5,4},{6,7},{7,6},{8,9},{9,8},{10,11... | collective-permute-start | bytes 49160 | tf_op jit(solution)/shard_map/ppermute | solution.py:465
  52.9 2.3 %positive_rows.2.refs_2_ = bf16[256,1024]{1,0:T(8,128)(2,1)S(1)} custom-call(bf16[256,1536]{1,0:T(8,128)(2,1)S(1)} %get-tuple-element.103.refs_0_, bf16[256,512]{1,0:T(8,128)(2,1)S(1)} %get-tuple-element.104.refs_1_, bf16[256,2048]{1,0:T(8,128)(2,1)S(1)} %get-tuple-element.105.refs_2_, s32[1,2048]{1,0:T(1,128)S(1)} %bitcast.10), custom_call_target="tpu_custom_call" | custom-call | flops 134217728 | bytes 524288 | tf_op jit(solution)/shard_map/positive_rows/pallas_call | solution.py:25
  55.3 1.7 %collective-permute-done.9.other_ref = f32[32,128]{1,0:T(8,128)S(1)} collective-permute-done((f32[32,128]{1,0:T(8,128)S(1)}, f32[32,128]{1,0:T(8,128)S(1)}, u32[]{:S(2)}, u32[]{:S(2)}) %collective-permute-start.9) | collective-permute-done | bytes 16416 | tf_op jit(solution)/shard_map/ppermute | solution.py:465
  57.0 2.7 %collective-permute-start.12 = (f32[32,128]{1,0:T(8,128)S(1)}, f32[32,128]{1,0:T(8,128)S(1)}, u32[]{:S(2)}, u32[]{:S(2)}) collective-permute-start(f32[32,128]{1,0:T(8,128)S(1)} %join_stats.1.refs_6_), channel_id=1, source_target_pairs={{0,6},{1,7},{2,0},{3,1},{4,2},{5,3},{6,4},{7,5},{8,14},{9,15},{10,... | collective-permute-start | bytes 49160 | tf_op jit(solution)/shard_map/ppermute | solution.py:465
  59.8 4.0 %collective-permute-start.11 = (f32[32,128]{1,0:T(8,128)S(1)}, f32[32,128]{1,0:T(8,128)S(1)}, u32[]{:S(2)}, u32[]{:S(2)}) collective-permute-start(f32[32,128]{1,0:T(8,128)S(1)} %join_stats.1.refs_6_), channel_id=1, source_target_pairs={{0,4},{1,5},{2,6},{3,7},{4,0},{5,1},{6,2},{7,3},{8,12},{9,13},{10,... | collective-permute-start | bytes 49160 | tf_op jit(solution)/shard_map/ppermute | solution.py:465
  63.8 2.3 %positive_rows.3.refs_3_ = bf16[256,1024]{1,0:T(8,128)(2,1)S(1)} custom-call(bf16[256,1536]{1,0:T(8,128)(2,1)S(1)} %get-tuple-element.103.refs_0_, bf16[256,512]{1,0:T(8,128)(2,1)S(1)} %get-tuple-element.104.refs_1_, bf16[256,2048]{1,0:T(8,128)(2,1)S(1)} %get-tuple-element.105.refs_2_, s32[1,2048]{1,0:T(1,128)S(1)} %bitcast.11), custom_call_target="tpu_custom_call" | custom-call | flops 134217728 | bytes 524288 | tf_op jit(solution)/shard_map/positive_rows/pallas_call | solution.py:25
  66.1 2.6 %collective-permute-done.10.refs_7_ = f32[32,128]{1,0:T(8,128)S(1)} collective-permute-done((f32[32,128]{1,0:T(8,128)S(1)}, f32[32,128]{1,0:T(8,128)S(1)}, u32[]{:S(2)}, u32[]{:S(2)}) %collective-permute-start.10) | collective-permute-done | bytes 16416 | tf_op jit(solution)/shard_map/ppermute | solution.py:465
  68.7 1.6 %grad_users.1 = (bf16[2048,256]{1,0:T(8,128)(2,1)}, f32[1,2048]{1,0:T(1,128)S(1)}, f32[1,2048]{1,0:T(1,128)S(1)}, bf16[16,256]{1,0:T(8,128)(2,1)S(1)}) custom-call(f32[256,2048]{1,0:T(8,128)S(1)} %get-tuple-element.100.refs_0_, f32[1,2048]{1,0:T(1,128)S(1)} %get-tuple-element.101.refs_1_, bf16[256,1024]{1,0:T(8,128)(2,1)S(1)} %positive_rows.2.refs_2_, ...), custom_call_target="tpu_custom_call" | custom-call | tf_op jit(solution)/shard_map/grad_users/pallas_call | solution.py:25
  70.3 1.4 %grads_mid.1 = (bf16[528,256]{1,0:T(8,128)(2,1)S(1)}, bf16[528,256]{1,0:T(8,128)(2,1)S(1)}) custom-call(bf16[2048,256]{1,0:T(8,128)(2,1)S(1)} %get-tuple-element.127.refs_0_, f32[1,2048]{1,0:T(1,128)S(1)} %get-tuple-element.113.refs_1_, f32[1,2048]{1,0:T(1,128)S(1)} %get-tuple-element.114.refs_2_, f32[1,2048]{1,0:T(1,128)S(1)} %bitcast.19, ...), custom_call_target="tpu_custom_call" | custom-call | flops 67108864 | bytes 262144 | tf_op jit(solution)/shard_map/grads_mid/pallas_call | solution.py:25
  71.8 2.1 %grads_far.1 = bf16[1536,256]{1,0:T(8,128)(2,1)S(1)} custom-call(bf16[2048,256]{1,0:T(8,128)(2,1)S(1)} %get-tuple-element.127.refs_0_, f32[1,2048]{1,0:T(1,128)S(1)} %get-tuple-element.113.refs_1_, f32[1,2048]{1,0:T(1,128)S(1)} %get-tuple-element.114.refs_2_, f32[1,2048]{1,0:T(1,128)S(1)} %bitcast.20, s32[1,2048]{1,0:T(1,128)S(1)} %bitcast.13, ...), custom_call_target="tpu_custom_call" | custom-call | flops 100663296 | bytes 393216 | tf_op jit(solution)/shard_map/grads_far/pallas_call | solution.py:25
  74.6 3.6 %all-to-all-start = ((bf16[8,256,256]{2,1,0:T(8,128)(2,1)}), bf16[8,256,256]{2,1,0:T(8,128)(2,1)S(1)}, u32[]{:S(2)}, u32[]{:S(2)}) async-start(bf16[8,256,256]{2,1,0:T(8,128)(2,1)} %bitcast.3), calls=%async_computation | async-start | bytes 2097152 | tf_op jit(solution)/shard_map/all_to_all | solution.py:522
  78.6 1.7 %collective-permute-start.15 = (bf16[256,256]{1,0:T(8,128)(2,1)S(1)}, bf16[256,256]{1,0:T(8,128)(2,1)S(1)}, u32[]{:S(2)}, u32[]{:S(2)}) collective-permute-start(bf16[256,256]{1,0:T(8,128)(2,1)S(1)} %get-tuple-element.131), channel_id=1, source_target_pairs={{0,16},{8,24},{16,32},{24,40},{32,48},{40,56},{48,0},{56,8},{64,80... | collective-permute-start | bytes 393224 | tf_op jit(solution)/shard_map/ppermute | solution.py:465
  80.3 2.8 %copy-done.1 = bf16[1536,2048]{1,0:T(8,128)(2,1)S(1)} copy-done((bf16[1536,2048]{1,0:T(8,128)(2,1)S(1)}, bf16[1536,2048]{1,0:T(8,128)(2,1)}, u32[]{:S(2)}) %copy-start.1) | copy-done | bytes 6291480
  83.1 2.2 %grads_near.1.near_ref = bf16[1536,256]{1,0:T(8,128)(2,1)S(1)} custom-call(bf16[2048,256]{1,0:T(8,128)(2,1)S(1)} %get-tuple-element.127.refs_0_, f32[1,2048]{1,0:T(1,128)S(1)} %get-tuple-element.113.refs_1_, f32[1,2048]{1,0:T(1,128)S(1)} %get-tuple-element.114.refs_2_, f32[1,2048]{1,0:T(1,128)S(1)} %bitcast.21, s32[1,2048]{1,0:T(1,128)S(1)} %bitcast.14, ...), custom_call_target="tpu_custom_call" | custom-call | flops 100663296 | bytes 393216 | tf_op jit(solution)/shard_map/grads_near/pallas_call | solution.py:25
  85.3 1.3 %add_near.1 = (f32[528,256]{1,0:T(8,128)S(1)}, bf16[528,256]{1,0:T(8,128)(2,1)S(1)}, bf16[528,256]{1,0:T(8,128)(2,1)S(1)}) custom-call(bf16[1536,256]{1,0:T(8,128)(2,1)S(1)} %grads_near.1.near_ref, bf16[1536,256]{1,0:T(8,128)(2,1)} %collective-permute-done.16.back_ref, bf16[16,256]{1,0:T(8,128)(2,1)S(1)} %get-tuple-element.134.both_ref, ...), custom_call_target="tpu_custom_call" | custom-call | tf_op jit(solution)/shard_map/add_near/pallas_call | solution.py:25
  86.6 1.6 %collective-permute-start.17 = (bf16[528,256]{1,0:T(8,128)(2,1)S(1)}, bf16[528,256]{1,0:T(8,128)(2,1)S(1)}, u32[]{:S(2)}, u32[]{:S(2)}) collective-permute-start(bf16[528,256]{1,0:T(8,128)(2,1)S(1)} %get-tuple-element.137), channel_id=1, source_target_pairs={{0,48},{8,56},{16,0},{24,8},{32,16},{40,24},{48,32},{56,40},{64,11... | collective-permute-start | bytes 811016 | tf_op jit(solution)/shard_map/ppermute | solution.py:465
  88.7 6.2 %all-to-all-done = bf16[8,256,256]{2,1,0:T(8,128)(2,1)S(1)} async-done(((bf16[8,256,256]{2,1,0:T(8,128)(2,1)}), bf16[8,256,256]{2,1,0:T(8,128)(2,1)S(1)}, u32[]{:S(2)}, u32[]{:S(2)}) %all-to-all-start) | async-done | bytes 1048608 | tf_op jit(solution)/shard_map/all_to_all | solution.py:522
  94.9 2.4 %collective-permute-done.18.refs_2_ = bf16[528,256]{1,0:T(8,128)(2,1)S(1)} collective-permute-done((bf16[528,256]{1,0:T(8,128)(2,1)S(1)}, bf16[528,256]{1,0:T(8,128)(2,1)S(1)}, u32[]{:S(2)}, u32[]{:S(2)}) %collective-permute-start.18) | collective-permute-done | bytes 270368 | tf_op jit(solution)/shard_map/ppermute | solution.py:465
  97.4 1.1 %collective-permute-start.19 = (bf16[272,256]{1,0:T(8,128)(2,1)S(1)}, bf16[272,256]{1,0:T(8,128)(2,1)S(1)}, u32[]{:S(2)}, u32[]{:S(2)}) collective-permute-start(bf16[272,256]{1,0:T(8,128)(2,1)S(1)} %get-tuple-element.145), channel_id=1, source_target_pairs={{0,64},{8,72},{16,80},{24,88},{32,96},{40,104},{48,112},{56,120},{... | collective-permute-start | bytes 417800 | tf_op jit(solution)/shard_map/ppermute | solution.py:465
  98.5 4.0 %collective-permute-done.19.received_ref = bf16[272,256]{1,0:T(8,128)(2,1)S(1)} collective-permute-done((bf16[272,256]{1,0:T(8,128)(2,1)S(1)}, bf16[272,256]{1,0:T(8,128)(2,1)S(1)}, u32[]{:S(2)}, u32[]{:S(2)}) %collective-permute-start.19) | collective-permute-done | bytes 139296 | tf_op jit(solution)/shard_map/ppermute | solution.py:465
  (34 shorter events, 8.6 us)
Async XLA Ops:
  0.6 8.6 %collective-permute-start = (bf16[256,256]{1,0:T(8,128)(2,1)}, bf16[256,256]{1,0:T(8,128)(2,1)S(1)}, u32[]{:S(2)}, u32[]{:S(2)}) collective-permute-start(bf16[256,256]{1,0:T(8,128)(2,1)} %param.5), channel_id=1, source_target_pairs={{0,1},{1,0},{2,3},{3,2},{4,5},{5,4},{6,7},{7,6},{8,9},{9,8},{10,11... | collective-permute-start | bytes 393224 | tf_op jit(solution)/shard_map/ppermute | solution.py:465
  4.7 7.2 %collective-permute-start.1 = (bf16[256,256]{1,0:T(8,128)(2,1)}, bf16[256,256]{1,0:T(8,128)(2,1)S(1)}, u32[]{:S(2)}, u32[]{:S(2)}) collective-permute-start(bf16[256,256]{1,0:T(8,128)(2,1)} %param.6), channel_id=1, source_target_pairs={{0,64},{8,72},{16,80},{24,88},{32,96},{40,104},{48,112},{56,120},{... | collective-permute-start | bytes 393224 | tf_op jit(solution)/shard_map/ppermute | solution.py:465
  12.9 13.2 %collective-permute-start.4 = (bf16[512,256]{1,0:T(8,128)(2,1)S(1)}, bf16[512,256]{1,0:T(8,128)(2,1)S(1)}, u32[]{:S(2)}, u32[]{:S(2)}) collective-permute-start(bf16[512,256]{1,0:T(8,128)(2,1)S(1)} %get-tuple-element.79.refs_0_), channel_id=1, source_target_pairs={{0,6},{1,7},{2,0},{3,1},{4,2},{5,3},{6,4},{7,5},{8,14},{9,15},{10,... | collective-permute-start | bytes 786440 | tf_op jit(solution)/shard_map/ppermute | solution.py:465
  15.8 13.5 %collective-permute-start.3 = (bf16[512,256]{1,0:T(8,128)(2,1)S(1)}, bf16[512,256]{1,0:T(8,128)(2,1)S(1)}, u32[]{:S(2)}, u32[]{:S(2)}) collective-permute-start(bf16[512,256]{1,0:T(8,128)(2,1)S(1)} %get-tuple-element.79.refs_0_), channel_id=1, source_target_pairs={{0,4},{1,5},{2,6},{3,7},{4,0},{5,1},{6,2},{7,3},{8,12},{9,13},{10,... | collective-permute-start | bytes 786440 | tf_op jit(solution)/shard_map/ppermute | solution.py:465
  16.6 13.2 %collective-permute-start.2 = (bf16[512,256]{1,0:T(8,128)(2,1)S(1)}, bf16[512,256]{1,0:T(8,128)(2,1)S(1)}, u32[]{:S(2)}, u32[]{:S(2)}) collective-permute-start(bf16[512,256]{1,0:T(8,128)(2,1)S(1)} %get-tuple-element.79.refs_0_), channel_id=1, source_target_pairs={{0,2},{1,3},{2,4},{3,5},{4,6},{5,7},{6,0},{7,1},{8,10},{9,11},{10,... | collective-permute-start | bytes 786440 | tf_op jit(solution)/shard_map/ppermute | solution.py:465
  17.4 12.3 %collective-permute-start.6 = (bf16[512,256]{1,0:T(8,128)(2,1)S(1)}, bf16[512,256]{1,0:T(8,128)(2,1)S(1)}, u32[]{:S(2)}, u32[]{:S(2)}) collective-permute-start(bf16[512,256]{1,0:T(8,128)(2,1)S(1)} %get-tuple-element.83.refs_4_), channel_id=1, source_target_pairs={{0,48},{8,56},{16,0},{24,8},{32,16},{40,24},{48,32},{56,40},{64,11... | collective-permute-start | bytes 786440 | tf_op jit(solution)/shard_map/ppermute | solution.py:465
  20.5 10.1 %collective-permute-start.5 = (bf16[512,256]{1,0:T(8,128)(2,1)S(1)}, bf16[512,256]{1,0:T(8,128)(2,1)S(1)}, u32[]{:S(2)}, u32[]{:S(2)}) collective-permute-start(bf16[512,256]{1,0:T(8,128)(2,1)S(1)} %get-tuple-element.83.refs_4_), channel_id=1, source_target_pairs={{0,16},{8,24},{16,32},{24,40},{32,48},{40,56},{48,0},{56,8},{64,80... | collective-permute-start | bytes 786440 | tf_op jit(solution)/shard_map/ppermute | solution.py:465
  26.1 13.5 %collective-permute-start.7 = (bf16[512,256]{1,0:T(8,128)(2,1)S(1)}, bf16[512,256]{1,0:T(8,128)(2,1)S(1)}, u32[]{:S(2)}, u32[]{:S(2)}) collective-permute-start(bf16[512,256]{1,0:T(8,128)(2,1)S(1)} %get-tuple-element.83.refs_4_), channel_id=1, source_target_pairs={{0,32},{8,40},{16,48},{24,56},{32,0},{40,8},{48,16},{56,24},{64,96... | collective-permute-start | bytes 786440 | tf_op jit(solution)/shard_map/ppermute | solution.py:465
  37.0 2.6 %copy-start = (bf16[1536,2048]{1,0:T(8,128)(2,1)}, bf16[1536,2048]{1,0:T(8,128)(2,1)S(1)}, u32[]{:S(2)}) copy-start(bf16[1536,2048]{1,0:T(8,128)(2,1)S(1)} %get-tuple-element.128.refs_6_.refs_7_.refs_8_) | copy-start | bytes 18874372
  39.7 2.9 %collective-permute-start.8 = (bf16[2048,256]{1,0:T(8,128)(2,1)S(1)}, bf16[2048,256]{1,0:T(8,128)(2,1)S(1)}, u32[]{:S(2)}, u32[]{:S(2)}) collective-permute-start(bf16[2048,256]{1,0:T(8,128)(2,1)S(1)} %pad_maximum_fusion), channel_id=1, source_target_pairs={{0,8},{8,0},{16,24},{24,16},{32,40},{40,32},{48,56},{56,48},{64,72... | collective-permute-start | bytes 3145736 | tf_op jit(solution)/shard_map/ppermute | solution.py:465
  51.8 5.2 %collective-permute-start.9 = (f32[32,128]{1,0:T(8,128)S(1)}, f32[32,128]{1,0:T(8,128)S(1)}, u32[]{:S(2)}, u32[]{:S(2)}) collective-permute-start(f32[32,128]{1,0:T(8,128)S(1)} %get-tuple-element.102.own_ref), channel_id=1, source_target_pairs={{0,1},{1,0},{2,3},{3,2},{4,5},{5,4},{6,7},{7,6},{8,9},{9,8},{10,11... | collective-permute-start | bytes 49160 | tf_op jit(solution)/shard_map/ppermute | solution.py:465
  52.9 15.8 %copy-start.2 = (f32[2048]{0:T(1024)S(1)}, f32[2048]{0:T(1024)}, u32[]{:S(2)}) copy-start(f32[2048]{0:T(1024)} %param.9) | copy-start | bytes 24580
  57.0 9.1 %collective-permute-start.12 = (f32[32,128]{1,0:T(8,128)S(1)}, f32[32,128]{1,0:T(8,128)S(1)}, u32[]{:S(2)}, u32[]{:S(2)}) collective-permute-start(f32[32,128]{1,0:T(8,128)S(1)} %join_stats.1.refs_6_), channel_id=1, source_target_pairs={{0,6},{1,7},{2,0},{3,1},{4,2},{5,3},{6,4},{7,5},{8,14},{9,15},{10,... | collective-permute-start | bytes 49160 | tf_op jit(solution)/shard_map/ppermute | solution.py:465
  59.8 6.4 %collective-permute-start.11 = (f32[32,128]{1,0:T(8,128)S(1)}, f32[32,128]{1,0:T(8,128)S(1)}, u32[]{:S(2)}, u32[]{:S(2)}) collective-permute-start(f32[32,128]{1,0:T(8,128)S(1)} %join_stats.1.refs_6_), channel_id=1, source_target_pairs={{0,4},{1,5},{2,6},{3,7},{4,0},{5,1},{6,2},{7,3},{8,12},{9,13},{10,... | collective-permute-start | bytes 49160 | tf_op jit(solution)/shard_map/ppermute | solution.py:465
  63.8 4.9 %collective-permute-start.10 = (f32[32,128]{1,0:T(8,128)S(1)}, f32[32,128]{1,0:T(8,128)S(1)}, u32[]{:S(2)}, u32[]{:S(2)}) collective-permute-start(f32[32,128]{1,0:T(8,128)S(1)} %join_stats.1.refs_6_), channel_id=1, source_target_pairs={{0,2},{1,3},{2,4},{3,5},{4,6},{5,7},{6,0},{7,1},{8,10},{9,11},{10,... | collective-permute-start | bytes 49160 | tf_op jit(solution)/shard_map/ppermute | solution.py:465
  71.7 2.2 %collective-permute-start.13 = (bf16[528,256]{1,0:T(8,128)(2,1)S(1)}, bf16[528,256]{1,0:T(8,128)(2,1)S(1)}, u32[]{:S(2)}, u32[]{:S(2)}) collective-permute-start(bf16[528,256]{1,0:T(8,128)(2,1)S(1)} %get-tuple-element.123), channel_id=1, source_target_pairs={{0,8},{8,0},{16,24},{24,16},{32,40},{40,32},{48,56},{56,48},{64,72... | collective-permute-start | bytes 811016 | tf_op jit(solution)/shard_map/ppermute | solution.py:465
  74.0 11.3 %collective-permute-start.16 = (bf16[1536,256]{1,0:T(8,128)(2,1)S(1)}, bf16[1536,256]{1,0:T(8,128)(2,1)}, u32[]{:S(2)}, u32[]{:S(2)}) collective-permute-start(bf16[1536,256]{1,0:T(8,128)(2,1)S(1)} %grads_far.1), channel_id=1, source_target_pairs={{0,8},{8,0},{16,24},{24,16},{32,40},{40,32},{48,56},{56,48},{64,72... | collective-permute-start | bytes 2359304 | tf_op jit(solution)/shard_map/ppermute | solution.py:465
  74.6 20.4 %all-to-all-start = ((bf16[8,256,256]{2,1,0:T(8,128)(2,1)}), bf16[8,256,256]{2,1,0:T(8,128)(2,1)S(1)}, u32[]{:S(2)}, u32[]{:S(2)}) async-start(bf16[8,256,256]{2,1,0:T(8,128)(2,1)} %bitcast.3), calls=%async_computation | async-start | bytes 2097152 | tf_op jit(solution)/shard_map/all_to_all | solution.py:522
  78.2 7.1 %collective-permute-start.14 = (bf16[272,256]{1,0:T(8,128)(2,1)S(1)}, bf16[272,256]{1,0:T(8,128)(2,1)S(1)}, u32[]{:S(2)}, u32[]{:S(2)}) collective-permute-start(bf16[272,256]{1,0:T(8,128)(2,1)S(1)} %get-tuple-element.130), channel_id=1, source_target_pairs={{0,48},{8,56},{16,0},{24,8},{32,16},{40,24},{48,32},{56,40},{64,11... | collective-permute-start | bytes 417800 | tf_op jit(solution)/shard_map/ppermute | solution.py:465
  78.6 6.7 %collective-permute-start.15 = (bf16[256,256]{1,0:T(8,128)(2,1)S(1)}, bf16[256,256]{1,0:T(8,128)(2,1)S(1)}, u32[]{:S(2)}, u32[]{:S(2)}) collective-permute-start(bf16[256,256]{1,0:T(8,128)(2,1)S(1)} %get-tuple-element.131), channel_id=1, source_target_pairs={{0,16},{8,24},{16,32},{24,40},{32,48},{40,56},{48,0},{56,8},{64,80... | collective-permute-start | bytes 393224 | tf_op jit(solution)/shard_map/ppermute | solution.py:465
  80.3 2.8 %copy-start.1 = (bf16[1536,2048]{1,0:T(8,128)(2,1)S(1)}, bf16[1536,2048]{1,0:T(8,128)(2,1)}, u32[]{:S(2)}) copy-start(bf16[1536,2048]{1,0:T(8,128)(2,1)} %copy-done) | copy-start | bytes 18874372
  86.6 8.3 %collective-permute-start.17 = (bf16[528,256]{1,0:T(8,128)(2,1)S(1)}, bf16[528,256]{1,0:T(8,128)(2,1)S(1)}, u32[]{:S(2)}, u32[]{:S(2)}) collective-permute-start(bf16[528,256]{1,0:T(8,128)(2,1)S(1)} %get-tuple-element.137), channel_id=1, source_target_pairs={{0,48},{8,56},{16,0},{24,8},{32,16},{40,24},{48,32},{56,40},{64,11... | collective-permute-start | bytes 811016 | tf_op jit(solution)/shard_map/ppermute | solution.py:465
  88.2 9.1 %collective-permute-start.18 = (bf16[528,256]{1,0:T(8,128)(2,1)S(1)}, bf16[528,256]{1,0:T(8,128)(2,1)S(1)}, u32[]{:S(2)}, u32[]{:S(2)}) collective-permute-start(bf16[528,256]{1,0:T(8,128)(2,1)S(1)} %get-tuple-element.138), channel_id=1, source_target_pairs={{0,16},{8,24},{16,32},{24,40},{32,48},{40,56},{48,0},{56,8},{64,80... | collective-permute-start | bytes 811016 | tf_op jit(solution)/shard_map/ppermute | solution.py:465
  97.4 5.1 %collective-permute-start.19 = (bf16[272,256]{1,0:T(8,128)(2,1)S(1)}, bf16[272,256]{1,0:T(8,128)(2,1)S(1)}, u32[]{:S(2)}, u32[]{:S(2)}) collective-permute-start(bf16[272,256]{1,0:T(8,128)(2,1)S(1)} %get-tuple-element.145), channel_id=1, source_target_pairs={{0,64},{8,72},{16,80},{24,88},{32,96},{40,104},{48,112},{56,120},{... | collective-permute-start | bytes 417800 | tf_op jit(solution)/shard_map/ppermute | solution.py:465

commit v11 on v8

--- a/solution.py
+++ b/solution.py
@@ -94,7 +94,7 @@
         (staged, users_t), refs = refs[:2], refs[2:]
     if last_call:
         (stats_ref,), refs = refs[:1], refs[1:]
-    ads_all, logc_all, s0, s1, *late = refs
+    ads_all, logc_all, s0, s1 = refs
 
     if first_call:
         stage_users(user_refs, staged, inv)
@@ -138,8 +138,8 @@
             hit_ref[:, self.cols] = hit if first_call else hit + hit_in[:, self.cols]
 
     class Exps:
-        def __init__(self, tile, src, extra):
-            self.cols, self.src, self.extra = columns(tile), src, extra
+        def __init__(self, tile, src):
+            self.cols, self.src = columns(tile), src
             self.top = top_ref[:, self.cols]
             self.total = jnp.zeros((8, T), F32)
 
@@ -147,9 +147,7 @@
             for r in range(c * T, (c + 1) * T, 16):
                 e = jnp.exp2(self.src[r : r + 16, :] - self.top)
                 self.total += e[:8] + e[8:]
-                e = e.astype(BF16)
-                p_ref[r : r + 16, self.cols] = e
-                self.extra[r : r + 16, :] = e
+                p_ref[r : r + 16, self.cols] = e.astype(BF16)
 
         def end(self):
             cols, top = self.cols, self.top
@@ -162,20 +160,20 @@
                 m_ref[:, cols] = m
                 total_ref[:, cols] = total_in[:, cols] * jnp.exp2(m_in[:, cols] - m) + total * jnp.exp2(top - m)
 
-    def gather(tile, e):
+    def gather(tile):
         cols = columns(tile)
-        new = jnp.dot(ads_t[...], e[...], preferred_element_type=F32)
+        new = jnp.dot(ads_t[...], p_ref[:, cols], preferred_element_type=F32)
         if first_call:
             acc_ref[:, cols] = new
         else:
             m = m_ref[:, cols]
             acc_ref[:, cols] = acc_in[:, cols] * jnp.exp2(m_in[:, cols] - m) + new * jnp.exp2(top_ref[:, cols] - m)
 
-    def turn(tile, src, dst, e_now, e_before):
+    def turn(tile, src, dst):
         if tile:
-            gather(tile - 1, e_before)
+            gather(tile - 1)
         product = Product(tile + 1, dst) if tile + 1 < n else None
-        exps = Exps(tile, src, e_now)
+        exps = Exps(tile, src)
         for c in range(chunks):
             if product:
                 product.chunk(c)
@@ -190,10 +188,10 @@
     opening.end()
     for tile in range(n):
         if tile % 2:
-            turn(tile, s1, s0, late[1], late[0])
+            turn(tile, s1, s0)
         else:
-            turn(tile, s0, s1, late[0], late[1])
-    gather(n - 1, late[(n - 1) % 2])
+            turn(tile, s0, s1)
+    gather(n - 1)
     if last_call:
         lse = m_ref[...] + jnp.log2(total_ref[...])
         width = n * T // LANES
@@ -232,8 +230,6 @@
         pltpu.VMEM((count, LANES), F32),
         pltpu.VMEM((count, T), F32),
         pltpu.VMEM((count, T), F32),
-        pltpu.VMEM((count, T), BF16),
-        pltpu.VMEM((count, T), BF16),
     ]
     return call(
         lambda *refs: logits_kernel(group, len(ads), count, inv, *refs),
@@ -560,15 +556,16 @@
     back_2 = swap_core(pay_2)
     da_2, staged = lax.optimization_barrier((da_2, staged))
     (da_far,) = run_grads("far", [("far", i, p_far, top_far) for i in range(3)], staged, *tail)
-    da_far, back_2, du_2a, du_2b = lax.optimization_barrier((da_far, back_2, du_2a, du_2b))
-    du_1, du_3 = add_halves(du_1, du_3, du_2a, du_2b)
+    da_far, back_2 = lax.optimization_barrier((da_far, back_2))
     back = swap_core(da_far)
     first, second, both = add_mid(da_2, back_2)
-    first, second, du_1, du_3, staged = lax.optimization_barrier((first, second, du_1, du_3, staged))
+    first, second, staged = lax.optimization_barrier((first, second, staged))
     first, second = shift_y(first, -1), shift_y(second, 1)
+    (da_near,) = run_grads("near", [("near", i, p_near, top_near) for i in range(3)], staged, *tail)
+    da_near, du_2a, du_2b = lax.optimization_barrier((da_near, du_2a, du_2b))
+    du_1, du_3 = add_halves(du_1, du_3, du_2a, du_2b)
+    da_near, du_1, du_3 = lax.optimization_barrier((da_near, du_1, du_3))
     du_1, du_3 = shift_x(du_1, 1), shift_x(du_3, -1)
-    (da_near,) = run_grads("near", [("near", i, p_near, top_near) for i in range(3)], staged, *tail)
-    da_near, first, second, du_1, du_3 = lax.optimization_barrier((da_near, first, second, du_1, du_3))
     kept, one, three = add_near(da_near, back, both, first, second)
     one, three = shift_y(one, -1), shift_y(three, 1)
     keep_u, send_u = add_users((du_0, du_1, du_3))

time: 102 us -> 101 us (level)
  waiting for transfers between devices: 30.5 us -> 28.1 us
    ppermute x25, waiting for transfers between devices: 30.5 us -> 28.1 us  [move(): lax.ppermute(x, axis, [(i, target(i)) for i in range(lax.axis_size(axis))])]
  transfers between devices with their start and end apart: 25 -> 25, of which waited for: 13 -> 11; matrix products, arithmetic and copies ran while one was open for 1% -> 1% of each run, Pallas kernels for 18% -> 18%
where the time goes in v11:
time: 101 us; the launch traced here: 100 us
  starting transfers between devices  38.1 us (38%)
  Pallas kernels  30.6 us (30%)
  waiting for transfers between devices  28.1 us (28%)
  other arithmetic  2.5 us (2%)
    ppermute x25, starting transfers between devices, move(): lax.ppermute(x, axis, [(i, target(i)) for i in range(lax.axis_size(axis))])  38.1 us
    pallas_call x16, Pallas kernels, call(): pl.pallas_call(kernel, in_specs=[vmem] * len(args), out_specs=[vmem] * le...  30.6 us
    ppermute x25, waiting for transfers between devices, move(): lax.ppermute(x, axis, [(i, target(i)) for i in range(lax.axis_size(axis))])  28.1 us
  transfers between devices with their start and end apart: 25, of which 11 were waited for; matrix products, arithmetic and copies ran while one was open for 1% of the time, Pallas kernels for 18%

profile of v11, /device:TPU:0, one launch (start us, length us, event | category | flops | bytes accessed | tf_op | source)
XLA Modules:
  0.0 100.2 jit_solution(5903510920728269504)
XLA Ops:
  0.6 4.0 %collective-permute-start = (bf16[256,256]{1,0:T(8,128)(2,1)}, bf16[256,256]{1,0:T(8,128)(2,1)S(1)}, u32[]{:S(2)}, u32[]{:S(2)}) collective-permute-start(bf16[256,256]{1,0:T(8,128)(2,1)} %param.5), channel_id=1, source_target_pairs={{0,1},{1,0},{2,3},{3,2},{4,5},{5,4},{6,7},{7,6},{8,9},{9,8},{10,11... | collective-permute-start | bytes 393224 | tf_op jit(solution)/shard_map/ppermute | solution.py:495
  4.7 1.0 %collective-permute-start.1 = (bf16[256,256]{1,0:T(8,128)(2,1)}, bf16[256,256]{1,0:T(8,128)(2,1)S(1)}, u32[]{:S(2)}, u32[]{:S(2)}) collective-permute-start(bf16[256,256]{1,0:T(8,128)(2,1)} %param.6), channel_id=1, source_target_pairs={{0,64},{8,72},{16,80},{24,88},{32,96},{40,104},{48,112},{56,120},{... | collective-permute-start | bytes 393224 | tf_op jit(solution)/shard_map/ppermute | solution.py:495
  7.1 2.1 %collective-permute-done = bf16[256,256]{1,0:T(8,128)(2,1)S(1)} collective-permute-done((bf16[256,256]{1,0:T(8,128)(2,1)}, bf16[256,256]{1,0:T(8,128)(2,1)S(1)}, u32[]{:S(2)}, u32[]{:S(2)}) %collective-permute-start) | collective-permute-done | bytes 131104 | tf_op jit(solution)/shard_map/ppermute | solution.py:495
  9.2 2.7 %collective-permute-done.1 = bf16[256,256]{1,0:T(8,128)(2,1)S(1)} collective-permute-done((bf16[256,256]{1,0:T(8,128)(2,1)}, bf16[256,256]{1,0:T(8,128)(2,1)S(1)}, u32[]{:S(2)}, u32[]{:S(2)}) %collective-permute-start.1) | collective-permute-done | bytes 131104 | tf_op jit(solution)/shard_map/ppermute | solution.py:495
  11.9 1.0 %pad_maximum_fusion.1 = (bf16[512,256]{1,0:T(8,128)(2,1)S(1)}, bf16[512,256]{1,0:T(8,128)(2,1)S(1)}) fusion(bf16[256,256]{1,0:T(8,128)(2,1)S(1)} %collective-permute-done, bf16[256,256]{1,0:T(8,128)(2,1)} %param.5, bf16[256,256]{1,0:T(8,128)(2,1)S(1)} %collective-permute-done.1, bf16[256,256]{1,0:T(8,128)(2,1)} %param.6), kind=kLoop, calls=%fused_computation.1 | loop fusion | flops 1048576 | bytes 1048576 | tf_op jit(solution)/shard_map/concatenate | solution.py:524
  12.9 2.8 %collective-permute-start.4 = (bf16[512,256]{1,0:T(8,128)(2,1)S(1)}, bf16[512,256]{1,0:T(8,128)(2,1)S(1)}, u32[]{:S(2)}, u32[]{:S(2)}) collective-permute-start(bf16[512,256]{1,0:T(8,128)(2,1)S(1)} %get-tuple-element.90.refs_0_), channel_id=1, source_target_pairs={{0,6},{1,7},{2,0},{3,1},{4,2},{5,3},{6,4},{7,5},{8,14},{9,15},{10,... | collective-permute-start | bytes 786440 | tf_op jit(solution)/shard_map/ppermute | solution.py:495
  17.4 3.0 %collective-permute-start.6 = (bf16[512,256]{1,0:T(8,128)(2,1)S(1)}, bf16[512,256]{1,0:T(8,128)(2,1)S(1)}, u32[]{:S(2)}, u32[]{:S(2)}) collective-permute-start(bf16[512,256]{1,0:T(8,128)(2,1)S(1)} %get-tuple-element.94.refs_4_), channel_id=1, source_target_pairs={{0,48},{8,56},{16,0},{24,8},{32,16},{40,24},{48,32},{56,40},{64,11... | collective-permute-start | bytes 786440 | tf_op jit(solution)/shard_map/ppermute | solution.py:495
  20.5 5.6 %collective-permute-done.4.refs_3_ = bf16[512,256]{1,0:T(8,128)(2,1)S(1)} collective-permute-done((bf16[512,256]{1,0:T(8,128)(2,1)S(1)}, bf16[512,256]{1,0:T(8,128)(2,1)S(1)}, u32[]{:S(2)}, u32[]{:S(2)}) %collective-permute-start.4) | collective-permute-done | bytes 262176 | tf_op jit(solution)/shard_map/ppermute | solution.py:495
  26.1 3.2 %collective-permute-start.7 = (bf16[512,256]{1,0:T(8,128)(2,1)S(1)}, bf16[512,256]{1,0:T(8,128)(2,1)S(1)}, u32[]{:S(2)}, u32[]{:S(2)}) collective-permute-start(bf16[512,256]{1,0:T(8,128)(2,1)S(1)} %get-tuple-element.94.refs_4_), channel_id=1, source_target_pairs={{0,32},{8,40},{16,48},{24,56},{32,0},{40,8},{48,16},{56,24},{64,96... | collective-permute-start | bytes 786440 | tf_op jit(solution)/shard_map/ppermute | solution.py:495
  30.5 6.3 %logits_near.1 = (bf16[1536,2048]{1,0:T(8,128)(2,1)S(1)}, f32[1,2048]{1,0:T(1,128)S(1)}, bf16[256,1536]{1,0:T(8,128)(2,1)S(1)}, f32[256,2048]{1,0:T(8,128)S(1)},...) custom-call(bf16[512,256]{1,0:T(8,128)(2,1)S(1)} %get-tuple-element., ...), custom_call_target="tpu_custom_call" | custom-call | flops 100663296 | bytes 393216 | tf_op jit(solution)/shard_map/logits_near/pallas_call | solution.py:25
  37.2 2.3 %logits_two.1 = (bf16[512,2048]{1,0:T(8,128)(2,1)S(1)}, f32[1,2048]{1,0:T(1,128)S(1)}, bf16[256,512]{1,0:T(8,128)(2,1)S(1)}, f32[256,2048]{1,0:T(8,128)S(1)}, f3...) custom-call(bf16[256,2048]{1,0:T(8,128)(2,1)S(1)} %get-tuple-element.97.refs_0_, ...), custom_call_target="tpu_custom_call" | custom-call | flops 33554432 | bytes 131072 | tf_op jit(solution)/shard_map/logits_two/pallas_call | solution.py:25
  39.9 9.4 %logits_far.1 = (bf16[2048,2048]{1,0:T(8,128)(2,1)S(1)}, f32[1,2048]{1,0:T(1,128)S(1)}, bf16[256,2048]{1,0:T(8,128)(2,1)S(1)}, f32[256,2048]{1,0:T(8,128)S(1)}, ...) custom-call(bf16[256,2048]{1,0:T(8,128)(2,1)S(1)} %get-tuple-element.97.refs_0_, ...), custom_call_target="tpu_custom_call" | custom-call | flops 134217728 | bytes 524288 | tf_op jit(solution)/shard_map/logits_far/pallas_call | solution.py:25
  49.3 1.2 %collective-permute-start.9 = (f32[32,128]{1,0:T(8,128)S(1)}, f32[32,128]{1,0:T(8,128)S(1)}, u32[]{:S(2)}, u32[]{:S(2)}) collective-permute-start(f32[32,128]{1,0:T(8,128)S(1)} %get-tuple-element.112.own_ref), channel_id=1, source_target_pairs={{0,1},{1,0},{2,3},{3,2},{4,5},{5,4},{6,7},{7,6},{8,9},{9,8},{10,11... | collective-permute-start | bytes 49160 | tf_op jit(solution)/shard_map/ppermute | solution.py:495
  50.5 2.3 %positive_rows.2.refs_2_ = bf16[256,1024]{1,0:T(8,128)(2,1)S(1)} custom-call(bf16[256,1536]{1,0:T(8,128)(2,1)S(1)} %get-tuple-element.113.refs_0_, bf16[256,512]{1,0:T(8,128)(2,1)S(1)} %get-tuple-element.114.refs_1_, bf16[256,2048]{1,0:T(8,128)(2,1)S(1)} %get-tuple-element.115.refs_2_, s32[1,2048]{1,0:T(1,128)S(1)} %bitcast.7), custom_call_target="tpu_custom_call" | custom-call | flops 134217728 | bytes 524288 | tf_op jit(solution)/shard_map/positive_rows/pallas_call | solution.py:25
  52.8 1.7 %collective-permute-done.9.other_ref = f32[32,128]{1,0:T(8,128)S(1)} collective-permute-done((f32[32,128]{1,0:T(8,128)S(1)}, f32[32,128]{1,0:T(8,128)S(1)}, u32[]{:S(2)}, u32[]{:S(2)}) %collective-permute-start.9) | collective-permute-done | bytes 16416 | tf_op jit(solution)/shard_map/ppermute | solution.py:495
  54.6 2.7 %collective-permute-start.12 = (f32[32,128]{1,0:T(8,128)S(1)}, f32[32,128]{1,0:T(8,128)S(1)}, u32[]{:S(2)}, u32[]{:S(2)}) collective-permute-start(f32[32,128]{1,0:T(8,128)S(1)} %join_stats.1.refs_6_), channel_id=1, source_target_pairs={{0,6},{1,7},{2,0},{3,1},{4,2},{5,3},{6,4},{7,5},{8,14},{9,15},{10,... | collective-permute-start | bytes 49160 | tf_op jit(solution)/shard_map/ppermute | solution.py:495
  57.3 4.0 %collective-permute-start.11 = (f32[32,128]{1,0:T(8,128)S(1)}, f32[32,128]{1,0:T(8,128)S(1)}, u32[]{:S(2)}, u32[]{:S(2)}) collective-permute-start(f32[32,128]{1,0:T(8,128)S(1)} %join_stats.1.refs_6_), channel_id=1, source_target_pairs={{0,4},{1,5},{2,6},{3,7},{4,0},{5,1},{6,2},{7,3},{8,12},{9,13},{10,... | collective-permute-start | bytes 49160 | tf_op jit(solution)/shard_map/ppermute | solution.py:495
  61.3 2.3 %positive_rows.3.refs_3_ = bf16[256,1024]{1,0:T(8,128)(2,1)S(1)} custom-call(bf16[256,1536]{1,0:T(8,128)(2,1)S(1)} %get-tuple-element.113.refs_0_, bf16[256,512]{1,0:T(8,128)(2,1)S(1)} %get-tuple-element.114.refs_1_, bf16[256,2048]{1,0:T(8,128)(2,1)S(1)} %get-tuple-element.115.refs_2_, s32[1,2048]{1,0:T(1,128)S(1)} %bitcast.8), custom_call_target="tpu_custom_call" | custom-call | flops 134217728 | bytes 524288 | tf_op jit(solution)/shard_map/positive_rows/pallas_call | solution.py:25
  63.7 2.6 %collective-permute-done.10.refs_7_ = f32[32,128]{1,0:T(8,128)S(1)} collective-permute-done((f32[32,128]{1,0:T(8,128)S(1)}, f32[32,128]{1,0:T(8,128)S(1)}, u32[]{:S(2)}, u32[]{:S(2)}) %collective-permute-start.10) | collective-permute-done | bytes 16416 | tf_op jit(solution)/shard_map/ppermute | solution.py:495
  66.9 1.5 %grads_mid.1 = (bf16[528,256]{1,0:T(8,128)(2,1)S(1)}, bf16[528,256]{1,0:T(8,128)(2,1)S(1)}) custom-call(bf16[2048,256]{1,0:T(8,128)(2,1)S(1)} %get-tuple-element.139.refs_0_, f32[1,2048]{1,0:T(1,128)S(1)} %get-tuple-element.125.refs_1_, f32[1,2048]{1,0:T(1,128)S(1)} %get-tuple-element.126.refs_2_, f32[1,2048]{1,0:T(1,128)S(1)} %bitcast.16, ...), custom_call_target="tpu_custom_call" | custom-call | flops 67108864 | bytes 262144 | tf_op jit(solution)/shard_map/grads_mid/pallas_call | solution.py:25
  68.5 2.1 %grads_far.1 = bf16[1536,256]{1,0:T(8,128)(2,1)S(1)} custom-call(bf16[2048,256]{1,0:T(8,128)(2,1)S(1)} %get-tuple-element.139.refs_0_, f32[1,2048]{1,0:T(1,128)S(1)} %get-tuple-element.125.refs_1_, f32[1,2048]{1,0:T(1,128)S(1)} %get-tuple-element.126.refs_2_, f32[1,2048]{1,0:T(1,128)S(1)} %bitcast.17, s32[1,2048]{1,0:T(1,128)S(1)} %bitcast.10, ...), custom_call_target="tpu_custom_call" | custom-call | flops 100663296 | bytes 393216 | tf_op jit(solution)/shard_map/grads_far/pallas_call | solution.py:25
  71.2 3.2 %collective-permute-start.15 = (bf16[256,256]{1,0:T(8,128)(2,1)S(1)}, bf16[256,256]{1,0:T(8,128)(2,1)S(1)}, u32[]{:S(2)}, u32[]{:S(2)}) collective-permute-start(bf16[256,256]{1,0:T(8,128)(2,1)S(1)} %get-tuple-element.143), channel_id=1, source_target_pairs={{0,6},{1,7},{2,0},{3,1},{4,2},{5,3},{6,4},{7,5},{8,14},{9,15},{10,... | collective-permute-start | bytes 393224 | tf_op jit(solution)/shard_map/ppermute | solution.py:495
  74.9 1.7 %collective-permute-start.20 = (bf16[256,256]{1,0:T(8,128)(2,1)S(1)}, bf16[256,256]{1,0:T(8,128)(2,1)S(1)}, u32[]{:S(2)}, u32[]{:S(2)}) collective-permute-start(bf16[256,256]{1,0:T(8,128)(2,1)S(1)} %get-tuple-element.158), channel_id=1, source_target_pairs={{0,16},{8,24},{16,32},{24,40},{32,48},{40,56},{48,0},{56,8},{64,80... | collective-permute-start | bytes 393224 | tf_op jit(solution)/shard_map/ppermute | solution.py:495
  76.6 2.1 %grads_near.1.near_ref = bf16[1536,256]{1,0:T(8,128)(2,1)S(1)} custom-call(bf16[2048,256]{1,0:T(8,128)(2,1)S(1)} %get-tuple-element.139.refs_0_, f32[1,2048]{1,0:T(1,128)S(1)} %get-tuple-element.125.refs_1_, f32[1,2048]{1,0:T(1,128)S(1)} %get-tuple-element.126.refs_2_, f32[1,2048]{1,0:T(1,128)S(1)} %bitcast.18, s32[1,2048]{1,0:T(1,128)S(1)} %bitcast.11, ...), custom_call_target="tpu_custom_call" | custom-call | flops 100663296 | bytes 393216 | tf_op jit(solution)/shard_map/grads_near/pallas_call | solution.py:25
  78.9 3.2 %collective-permute-start.17 = (bf16[512,256]{1,0:T(8,128)(2,1)S(1)}, bf16[512,256]{1,0:T(8,128)(2,1)S(1)}, u32[]{:S(2)}, u32[]{:S(2)}) collective-permute-start(bf16[512,256]{1,0:T(8,128)(2,1)S(1)} %get-tuple-element.152), channel_id=1, source_target_pairs={{0,6},{1,7},{2,0},{3,1},{4,2},{5,3},{6,4},{7,5},{8,14},{9,15},{10,... | collective-permute-start | bytes 786440 | tf_op jit(solution)/shard_map/ppermute | solution.py:495
  82.4 1.6 %collective-permute-start.21 = (bf16[528,256]{1,0:T(8,128)(2,1)S(1)}, bf16[528,256]{1,0:T(8,128)(2,1)S(1)}, u32[]{:S(2)}, u32[]{:S(2)}) collective-permute-start(bf16[528,256]{1,0:T(8,128)(2,1)S(1)} %get-tuple-element.159), channel_id=1, source_target_pairs={{0,48},{8,56},{16,0},{24,8},{32,16},{40,24},{48,32},{56,40},{64,11... | collective-permute-start | bytes 811016 | tf_op jit(solution)/shard_map/ppermute | solution.py:495
  84.5 2.8 %collective-permute-done.16.refs_1_ = bf16[512,256]{1,0:T(8,128)(2,1)S(1)} collective-permute-done((bf16[512,256]{1,0:T(8,128)(2,1)S(1)}, bf16[512,256]{1,0:T(8,128)(2,1)S(1)}, u32[]{:S(2)}, u32[]{:S(2)}) %collective-permute-start.16) | collective-permute-done | bytes 262176 | tf_op jit(solution)/shard_map/ppermute | solution.py:495
  87.4 1.3 %collective-permute-start.23 = (bf16[256,256]{1,0:T(8,128)(2,1)S(1)}, bf16[256,256]{1,0:T(8,128)(2,1)S(1)}, u32[]{:S(2)}, u32[]{:S(2)}) collective-permute-start(bf16[256,256]{1,0:T(8,128)(2,1)S(1)} %get-tuple-element.161), channel_id=1, source_target_pairs={{0,1},{1,0},{2,3},{3,2},{4,5},{5,4},{6,7},{7,6},{8,9},{9,8},{10,11... | collective-permute-start | bytes 393224 | tf_op jit(solution)/shard_map/ppermute | solution.py:495
  88.7 5.3 %collective-permute-done.23.received_u_ref = bf16[256,256]{1,0:T(8,128)(2,1)S(1)} collective-permute-done((bf16[256,256]{1,0:T(8,128)(2,1)S(1)}, bf16[256,256]{1,0:T(8,128)(2,1)S(1)}, u32[]{:S(2)}, u32[]{:S(2)}) %collective-permute-start.23) | collective-permute-done | bytes 131104 | tf_op jit(solution)/shard_map/ppermute | solution.py:495
  94.1 1.5 %collective-permute-start.24 = (bf16[272,256]{1,0:T(8,128)(2,1)S(1)}, bf16[272,256]{1,0:T(8,128)(2,1)S(1)}, u32[]{:S(2)}, u32[]{:S(2)}) collective-permute-start(bf16[272,256]{1,0:T(8,128)(2,1)S(1)} %get-tuple-element.167), channel_id=1, source_target_pairs={{0,64},{8,72},{16,80},{24,88},{32,96},{40,104},{48,112},{56,120},{... | collective-permute-start | bytes 417800 | tf_op jit(solution)/shard_map/ppermute | solution.py:495
  95.6 3.6 %collective-permute-done.24.received_ref = bf16[272,256]{1,0:T(8,128)(2,1)S(1)} collective-permute-done((bf16[272,256]{1,0:T(8,128)(2,1)S(1)}, bf16[272,256]{1,0:T(8,128)(2,1)S(1)}, u32[]{:S(2)}, u32[]{:S(2)}) %collective-permute-start.24) | collective-permute-done | bytes 139296 | tf_op jit(solution)/shard_map/ppermute | solution.py:495
  99.2 0.9 finish.1
  (40 shorter events, 7.9 us)
Async XLA Ops:
  0.6 8.6 %collective-permute-start = (bf16[256,256]{1,0:T(8,128)(2,1)}, bf16[256,256]{1,0:T(8,128)(2,1)S(1)}, u32[]{:S(2)}, u32[]{:S(2)}) collective-permute-start(bf16[256,256]{1,0:T(8,128)(2,1)} %param.5), channel_id=1, source_target_pairs={{0,1},{1,0},{2,3},{3,2},{4,5},{5,4},{6,7},{7,6},{8,9},{9,8},{10,11... | collective-permute-start | bytes 393224 | tf_op jit(solution)/shard_map/ppermute | solution.py:495
  4.7 7.2 %collective-permute-start.1 = (bf16[256,256]{1,0:T(8,128)(2,1)}, bf16[256,256]{1,0:T(8,128)(2,1)S(1)}, u32[]{:S(2)}, u32[]{:S(2)}) collective-permute-start(bf16[256,256]{1,0:T(8,128)(2,1)} %param.6), channel_id=1, source_target_pairs={{0,64},{8,72},{16,80},{24,88},{32,96},{40,104},{48,112},{56,120},{... | collective-permute-start | bytes 393224 | tf_op jit(solution)/shard_map/ppermute | solution.py:495
  12.9 13.2 %collective-permute-start.4 = (bf16[512,256]{1,0:T(8,128)(2,1)S(1)}, bf16[512,256]{1,0:T(8,128)(2,1)S(1)}, u32[]{:S(2)}, u32[]{:S(2)}) collective-permute-start(bf16[512,256]{1,0:T(8,128)(2,1)S(1)} %get-tuple-element.90.refs_0_), channel_id=1, source_target_pairs={{0,6},{1,7},{2,0},{3,1},{4,2},{5,3},{6,4},{7,5},{8,14},{9,15},{10,... | collective-permute-start | bytes 786440 | tf_op jit(solution)/shard_map/ppermute | solution.py:495
  15.8 13.5 %collective-permute-start.3 = (bf16[512,256]{1,0:T(8,128)(2,1)S(1)}, bf16[512,256]{1,0:T(8,128)(2,1)S(1)}, u32[]{:S(2)}, u32[]{:S(2)}) collective-permute-start(bf16[512,256]{1,0:T(8,128)(2,1)S(1)} %get-tuple-element.90.refs_0_), channel_id=1, source_target_pairs={{0,4},{1,5},{2,6},{3,7},{4,0},{5,1},{6,2},{7,3},{8,12},{9,13},{10,... | collective-permute-start | bytes 786440 | tf_op jit(solution)/shard_map/ppermute | solution.py:495
  16.6 13.2 %collective-permute-start.2 = (bf16[512,256]{1,0:T(8,128)(2,1)S(1)}, bf16[512,256]{1,0:T(8,128)(2,1)S(1)}, u32[]{:S(2)}, u32[]{:S(2)}) collective-permute-start(bf16[512,256]{1,0:T(8,128)(2,1)S(1)} %get-tuple-element.90.refs_0_), channel_id=1, source_target_pairs={{0,2},{1,3},{2,4},{3,5},{4,6},{5,7},{6,0},{7,1},{8,10},{9,11},{10,... | collective-permute-start | bytes 786440 | tf_op jit(solution)/shard_map/ppermute | solution.py:495
  17.4 12.3 %collective-permute-start.6 = (bf16[512,256]{1,0:T(8,128)(2,1)S(1)}, bf16[512,256]{1,0:T(8,128)(2,1)S(1)}, u32[]{:S(2)}, u32[]{:S(2)}) collective-permute-start(bf16[512,256]{1,0:T(8,128)(2,1)S(1)} %get-tuple-element.94.refs_4_), channel_id=1, source_target_pairs={{0,48},{8,56},{16,0},{24,8},{32,16},{40,24},{48,32},{56,40},{64,11... | collective-permute-start | bytes 786440 | tf_op jit(solution)/shard_map/ppermute | solution.py:495
  20.5 10.1 %collective-permute-start.5 = (bf16[512,256]{1,0:T(8,128)(2,1)S(1)}, bf16[512,256]{1,0:T(8,128)(2,1)S(1)}, u32[]{:S(2)}, u32[]{:S(2)}) collective-permute-start(bf16[512,256]{1,0:T(8,128)(2,1)S(1)} %get-tuple-element.94.refs_4_), channel_id=1, source_target_pairs={{0,16},{8,24},{16,32},{24,40},{32,48},{40,56},{48,0},{56,8},{64,80... | collective-permute-start | bytes 786440 | tf_op jit(solution)/shard_map/ppermute | solution.py:495
  26.1 10.8 %collective-permute-start.7 = (bf16[512,256]{1,0:T(8,128)(2,1)S(1)}, bf16[512,256]{1,0:T(8,128)(2,1)S(1)}, u32[]{:S(2)}, u32[]{:S(2)}) collective-permute-start(bf16[512,256]{1,0:T(8,128)(2,1)S(1)} %get-tuple-element.94.refs_4_), channel_id=1, source_target_pairs={{0,32},{8,40},{16,48},{24,56},{32,0},{40,8},{48,16},{56,24},{64,96... | collective-permute-start | bytes 786440 | tf_op jit(solution)/shard_map/ppermute | solution.py:495
  37.0 2.9 %collective-permute-start.8 = (bf16[2048,256]{1,0:T(8,128)(2,1)S(1)}, bf16[2048,256]{1,0:T(8,128)(2,1)S(1)}, u32[]{:S(2)}, u32[]{:S(2)}) collective-permute-start(bf16[2048,256]{1,0:T(8,128)(2,1)S(1)} %pad_maximum_fusion), channel_id=1, source_target_pairs={{0,8},{8,0},{16,24},{24,16},{32,40},{40,32},{48,56},{56,48},{64,72... | collective-permute-start | bytes 3145736 | tf_op jit(solution)/shard_map/ppermute | solution.py:495
  49.3 5.2 %collective-permute-start.9 = (f32[32,128]{1,0:T(8,128)S(1)}, f32[32,128]{1,0:T(8,128)S(1)}, u32[]{:S(2)}, u32[]{:S(2)}) collective-permute-start(f32[32,128]{1,0:T(8,128)S(1)} %get-tuple-element.112.own_ref), channel_id=1, source_target_pairs={{0,1},{1,0},{2,3},{3,2},{4,5},{5,4},{6,7},{7,6},{8,9},{9,8},{10,11... | collective-permute-start | bytes 49160 | tf_op jit(solution)/shard_map/ppermute | solution.py:495
  50.5 15.8 %copy-start = (f32[2048]{0:T(1024)S(1)}, f32[2048]{0:T(1024)}, u32[]{:S(2)}) copy-start(f32[2048]{0:T(1024)} %param.9) | copy-start | bytes 24580
  54.6 9.1 %collective-permute-start.12 = (f32[32,128]{1,0:T(8,128)S(1)}, f32[32,128]{1,0:T(8,128)S(1)}, u32[]{:S(2)}, u32[]{:S(2)}) collective-permute-start(f32[32,128]{1,0:T(8,128)S(1)} %join_stats.1.refs_6_), channel_id=1, source_target_pairs={{0,6},{1,7},{2,0},{3,1},{4,2},{5,3},{6,4},{7,5},{8,14},{9,15},{10,... | collective-permute-start | bytes 49160 | tf_op jit(solution)/shard_map/ppermute | solution.py:495
  57.3 6.4 %collective-permute-start.11 = (f32[32,128]{1,0:T(8,128)S(1)}, f32[32,128]{1,0:T(8,128)S(1)}, u32[]{:S(2)}, u32[]{:S(2)}) collective-permute-start(f32[32,128]{1,0:T(8,128)S(1)} %join_stats.1.refs_6_), channel_id=1, source_target_pairs={{0,4},{1,5},{2,6},{3,7},{4,0},{5,1},{6,2},{7,3},{8,12},{9,13},{10,... | collective-permute-start | bytes 49160 | tf_op jit(solution)/shard_map/ppermute | solution.py:495
  61.3 4.9 %collective-permute-start.10 = (f32[32,128]{1,0:T(8,128)S(1)}, f32[32,128]{1,0:T(8,128)S(1)}, u32[]{:S(2)}, u32[]{:S(2)}) collective-permute-start(f32[32,128]{1,0:T(8,128)S(1)} %join_stats.1.refs_6_), channel_id=1, source_target_pairs={{0,2},{1,3},{2,4},{3,5},{4,6},{5,7},{6,0},{7,1},{8,10},{9,11},{10,... | collective-permute-start | bytes 49160 | tf_op jit(solution)/shard_map/ppermute | solution.py:495
  68.4 2.2 %collective-permute-start.13 = (bf16[528,256]{1,0:T(8,128)(2,1)S(1)}, bf16[528,256]{1,0:T(8,128)(2,1)S(1)}, u32[]{:S(2)}, u32[]{:S(2)}) collective-permute-start(bf16[528,256]{1,0:T(8,128)(2,1)S(1)} %get-tuple-element.135), channel_id=1, source_target_pairs={{0,8},{8,0},{16,24},{24,16},{32,40},{40,32},{48,56},{56,48},{64,72... | collective-permute-start | bytes 811016 | tf_op jit(solution)/shard_map/ppermute | solution.py:495
  70.6 11.5 %collective-permute-start.18 = (bf16[1536,256]{1,0:T(8,128)(2,1)S(1)}, bf16[1536,256]{1,0:T(8,128)(2,1)S(1)}, u32[]{:S(2)}, u32[]{:S(2)}) collective-permute-start(bf16[1536,256]{1,0:T(8,128)(2,1)S(1)} %grads_far.1), channel_id=1, source_target_pairs={{0,8},{8,0},{16,24},{24,16},{32,40},{40,32},{48,56},{56,48},{64,72... | collective-permute-start | bytes 2359304 | tf_op jit(solution)/shard_map/ppermute | solution.py:495
  71.2 7.5 %collective-permute-start.14 = (bf16[256,256]{1,0:T(8,128)(2,1)S(1)}, bf16[256,256]{1,0:T(8,128)(2,1)S(1)}, u32[]{:S(2)}, u32[]{:S(2)}) collective-permute-start(bf16[256,256]{1,0:T(8,128)(2,1)S(1)} %get-tuple-element.142), channel_id=1, source_target_pairs={{0,2},{1,3},{2,4},{3,5},{4,6},{5,7},{6,0},{7,1},{8,10},{9,11},{10,... | collective-permute-start | bytes 393224 | tf_op jit(solution)/shard_map/ppermute | solution.py:495
  71.2 7.6 %collective-permute-start.15 = (bf16[256,256]{1,0:T(8,128)(2,1)S(1)}, bf16[256,256]{1,0:T(8,128)(2,1)S(1)}, u32[]{:S(2)}, u32[]{:S(2)}) collective-permute-start(bf16[256,256]{1,0:T(8,128)(2,1)S(1)} %get-tuple-element.143), channel_id=1, source_target_pairs={{0,6},{1,7},{2,0},{3,1},{4,2},{5,3},{6,4},{7,5},{8,14},{9,15},{10,... | collective-permute-start | bytes 393224 | tf_op jit(solution)/shard_map/ppermute | solution.py:495
  74.5 7.6 %collective-permute-start.19 = (bf16[272,256]{1,0:T(8,128)(2,1)S(1)}, bf16[272,256]{1,0:T(8,128)(2,1)S(1)}, u32[]{:S(2)}, u32[]{:S(2)}) collective-permute-start(bf16[272,256]{1,0:T(8,128)(2,1)S(1)} %get-tuple-element.157), channel_id=1, source_target_pairs={{0,48},{8,56},{16,0},{24,8},{32,16},{40,24},{48,32},{56,40},{64,11... | collective-permute-start | bytes 417800 | tf_op jit(solution)/shard_map/ppermute | solution.py:495
  74.9 7.3 %collective-permute-start.20 = (bf16[256,256]{1,0:T(8,128)(2,1)S(1)}, bf16[256,256]{1,0:T(8,128)(2,1)S(1)}, u32[]{:S(2)}, u32[]{:S(2)}) collective-permute-start(bf16[256,256]{1,0:T(8,128)(2,1)S(1)} %get-tuple-element.158), channel_id=1, source_target_pairs={{0,16},{8,24},{16,32},{24,40},{32,48},{40,56},{48,0},{56,8},{64,80... | collective-permute-start | bytes 393224 | tf_op jit(solution)/shard_map/ppermute | solution.py:495
  78.9 8.5 %collective-permute-start.16 = (bf16[512,256]{1,0:T(8,128)(2,1)S(1)}, bf16[512,256]{1,0:T(8,128)(2,1)S(1)}, u32[]{:S(2)}, u32[]{:S(2)}) collective-permute-start(bf16[512,256]{1,0:T(8,128)(2,1)S(1)} %get-tuple-element.151), channel_id=1, source_target_pairs={{0,2},{1,3},{2,4},{3,5},{4,6},{5,7},{6,0},{7,1},{8,10},{9,11},{10,... | collective-permute-start | bytes 786440 | tf_op jit(solution)/shard_map/ppermute | solution.py:495
  78.9 8.4 %collective-permute-start.17 = (bf16[512,256]{1,0:T(8,128)(2,1)S(1)}, bf16[512,256]{1,0:T(8,128)(2,1)S(1)}, u32[]{:S(2)}, u32[]{:S(2)}) collective-permute-start(bf16[512,256]{1,0:T(8,128)(2,1)S(1)} %get-tuple-element.152), channel_id=1, source_target_pairs={{0,6},{1,7},{2,0},{3,1},{4,2},{5,3},{6,4},{7,5},{8,14},{9,15},{10,... | collective-permute-start | bytes 786440 | tf_op jit(solution)/shard_map/ppermute | solution.py:495
  82.4 11.6 %collective-permute-start.21 = (bf16[528,256]{1,0:T(8,128)(2,1)S(1)}, bf16[528,256]{1,0:T(8,128)(2,1)S(1)}, u32[]{:S(2)}, u32[]{:S(2)}) collective-permute-start(bf16[528,256]{1,0:T(8,128)(2,1)S(1)} %get-tuple-element.159), channel_id=1, source_target_pairs={{0,48},{8,56},{16,0},{24,8},{32,16},{40,24},{48,32},{56,40},{64,11... | collective-permute-start | bytes 811016 | tf_op jit(solution)/shard_map/ppermute | solution.py:495
  84.0 10.0 %collective-permute-start.22 = (bf16[528,256]{1,0:T(8,128)(2,1)S(1)}, bf16[528,256]{1,0:T(8,128)(2,1)S(1)}, u32[]{:S(2)}, u32[]{:S(2)}) collective-permute-start(bf16[528,256]{1,0:T(8,128)(2,1)S(1)} %get-tuple-element.160), channel_id=1, source_target_pairs={{0,16},{8,24},{16,32},{24,40},{32,48},{40,56},{48,0},{56,8},{64,80... | collective-permute-start | bytes 811016 | tf_op jit(solution)/shard_map/ppermute | solution.py:495
  87.4 6.6 %collective-permute-start.23 = (bf16[256,256]{1,0:T(8,128)(2,1)S(1)}, bf16[256,256]{1,0:T(8,128)(2,1)S(1)}, u32[]{:S(2)}, u32[]{:S(2)}) collective-permute-start(bf16[256,256]{1,0:T(8,128)(2,1)S(1)} %get-tuple-element.161), channel_id=1, source_target_pairs={{0,1},{1,0},{2,3},{3,2},{4,5},{5,4},{6,7},{7,6},{8,9},{9,8},{10,11... | collective-permute-start | bytes 393224 | tf_op jit(solution)/shard_map/ppermute | solution.py:495
  94.1 5.1 %collective-permute-start.24 = (bf16[272,256]{1,0:T(8,128)(2,1)S(1)}, bf16[272,256]{1,0:T(8,128)(2,1)S(1)}, u32[]{:S(2)}, u32[]{:S(2)}) collective-permute-start(bf16[272,256]{1,0:T(8,128)(2,1)S(1)} %get-tuple-element.167), channel_id=1, source_target_pairs={{0,64},{8,72},{16,80},{24,88},{32,96},{40,104},{48,112},{56,120},{... | collective-permute-start | bytes 417800 | tf_op jit(solution)/shard_map/ppermute | solution.py:495
